TPU v7x, 32 devices: a whole 2x2x4 slice. The times are simulated.
32 devices in a mesh: loop: 2 (over x), dp: 16 (over z, y, core).
Axes of the slice: x: 2, y: 2, z: 4, core: 2. Of those that a mesh axis runs over, the one named last changes fastest.
Arguments:
- layer_input_stream: bfloat16 [2, 2048, 2048], P('loop', 'dp'), may hold values from -6 to 6
- layer_output_gradient: bfloat16 [2, 2048, 2048], P('loop', 'dp'), may hold values from -6 to 6
- attention_in_weight: bfloat16 [2048, 2560], P('dp'), may hold values from -0.125 to 0.125
- attention_out_weight: bfloat16 [2048, 2048], P('dp'), may hold values from -1.5 to 1.5
- feedforward_weight: bfloat16 [16384, 3, 2048], P('dp'), may hold values from -0.125 to 0.125
- layer_norm_gains: float32 [2, 2048], replicated, may hold values from 0.5 to 1.5
- adapter_first_factors: bfloat16 [2, 2048, 1536], P('loop'), may hold values from -0.125 to 0.125
- adapter_second_factors: bfloat16 [2, 256, 6656], P('loop'), may hold values from -0.15625 to 0.15625
- adapter_hidden_factors: bfloat16 [2, 16384, 768], P('loop'), may hold values from -0.09375 to 0.09375
- group_sequence_lengths: int32 [2, 8], P('loop'), may hold values from 1 to 1529, as said below
- token_per_row: int32 [2, 2048], P('loop'), may hold values from -1 to 1535, as said below
- token_exit_depth: int32 [2, 2048], P('loop', 'dp'), may hold values from 0 to 2
Outputs:
- hidden_out: bfloat16 [2, 2048, 2048], P('loop', 'dp')
- hidden_grad: float32 [2, 2048, 2048], P('loop', 'dp')
- attn_in_grad: float32 [2048, 2560], P('dp')
- attn_out_grad: float32 [2048, 2048], P('dp')
- mlp_grad: float32 [16384, 3, 2048], P('dp')
- gains_grad: float32 [2, 2048], P(None, 'dp')
- lora_in_grad: float32 [2, 2048, 1536], P('loop', 'dp')
- lora_out_grad: float32 [2, 256, 6656], P('loop', None, 'dp')
- lora_ff_grad: float32 [2, 16384, 768], P('loop', 'dp')
- exit_counts: int32 [3], replicated
- mean_confidence: float32 [], replicated
Inputs may be any that keep to these rules, and one draw needn't show every extreme that they name: `group_sequence_lengths`: in each loop group the 8 lengths add up to 1536 and the longest is exactly 1529. `token_per_row`: in each loop group every token index from 0 to 1535 stands in exactly one row, sequences following one another in the order of group_sequence_lengths; -1 marks an unused row. A device's used rows are its first rows, and some device uses all 128.
All inputs are finite; a program needn't handle non-finite values.
Results may differ from a plain program's by a relative error of at most 0.019.
Values may be sent and summed in bfloat16 or wider, within the bound.
A program may use at most 512 MiB of HBM per device.

v0:
```python
import jax
import jax.numpy as jnp
from jax import lax
from jax.sharding import PartitionSpec as P

MODEL_WIDTH = 2048
HEADS = 8
HEAD_SIZE = 256
ADAPTER_RANK = 256
QUERY_WIDTH = 2048
PROJECTED_WIDTH = 2560


EPSILON = 1e-06
FLOOR_SCORE = -1e30


def matrix_product(left, right):
    return jnp.dot(left, right, preferred_element_type=jnp.float32)


def inner_rows(left, right):
    return lax.dot_general(
        left, right, (((0,), (0,)), ((), ())), preferred_element_type=jnp.float32
    )


def outer_columns(left, right):
    return lax.dot_general(
        left, right, (((1,), (1,)), ((), ())), preferred_element_type=jnp.float32
    )


def norm_rows(values, gain):
    return values * lax.rsqrt(jnp.mean(values * values, axis=-1, keepdims=True) + EPSILON) * gain


def rotate(values, positions):
    half_dim = values.shape[-1] // 2
    freqs = 10000.0 ** (-jnp.arange(half_dim, dtype=jnp.float32) / half_dim)
    angles = positions.astype(jnp.float32)[:, None, None] * freqs
    cosine = jnp.cos(angles)
    sine = jnp.sin(angles)
    first_half = values[..., :half_dim]
    second_half = values[..., half_dim:]
    return jnp.concatenate(
        [first_half * cosine - second_half * sine, first_half * sine + second_half * cosine],
        axis=-1,
    )


def rotate_back(grads, positions):

    def turned(values):
        return rotate(values, positions)

    return jax.vjp(turned, jnp.zeros_like(grads))[1](grads)[0]


def geglu(gate_values, up_projection_value):
    return jax.nn.gelu(gate_values, approximate=True) * up_projection_value


def root_mean(values):
    return jnp.sqrt(jnp.mean(values * values, axis=-1) + EPSILON)


def token_facts(row_of_tokens, sequence_length):
    row_total = row_of_tokens.shape[0]
    live_row = row_of_tokens >= 0
    seq_ends = jnp.cumsum(sequence_length)
    seq_index = jnp.sum((row_of_tokens[:, None] >= seq_ends[None, :]).astype(jnp.int32), axis=1)
    seq_starts = seq_ends - sequence_length
    own_start = jnp.sum(
        jnp.where(
            seq_index[:, None] == jnp.arange(sequence_length.shape[0], dtype=jnp.int32)[None, :],
            seq_starts[None, :],
            0,
        ),
        axis=1,
    )
    row_ids = jnp.arange(row_total, dtype=jnp.int32)
    sequence = jnp.where(live_row, seq_index, -1 - row_ids)
    ordering = jnp.where(live_row, row_of_tokens, 0)
    positions = jnp.where(live_row, row_of_tokens - own_start, 0)
    return (live_row, sequence, ordering, positions)


def per_device(
    layer_input_stream,
    layer_output_gradient,
    attention_in_weight,
    attention_out_weight,
    feedforward_weight,
    layer_norm_gains,
    adapter_first_factors,
    adapter_second_factors,
    adapter_hidden_factors,
    group_sequence_lengths,
    token_per_row,
    token_exit_depth,
):
    current_loop = lax.axis_index("loop")
    dp_index = lax.axis_index("dp")
    loop_count = lax.axis_size("loop")
    local_rows = layer_input_stream.shape[1]
    ffn_rows = feedforward_weight.shape[0]
    scale = HEAD_SIZE ** (-0.5)
    live_all, seq_all, order_all, pos_all = token_facts(token_per_row[0], group_sequence_lengths[0])
    first_row = dp_index * local_rows

    def own_slice(values):
        return lax.dynamic_slice_in_dim(values, first_row, local_rows, 0)

    live_own = own_slice(live_all)
    seq_own = own_slice(seq_all)
    order_own = own_slice(order_all)
    pos_own = own_slice(pos_all)
    active_mask = (live_own & (token_exit_depth[0] > current_loop)).astype(jnp.float32)[:, None]
    residual_stream = layer_input_stream[0].astype(jnp.float32)
    adapter_first = adapter_first_factors[0]
    adapter_second = adapter_second_factors[0]
    adapter_feedforward = adapter_hidden_factors[0]
    ffn_own = lax.dynamic_slice_in_dim(adapter_feedforward, dp_index * ffn_rows, ffn_rows, 0)
    input_weight, output_weight = (
        lax.all_gather(attention_in_weight, "dp", axis=0, tiled=True),
        lax.all_gather(attention_out_weight, "dp", axis=0, tiled=True),
    )
    normed_input = norm_rows(residual_stream, layer_norm_gains[0]).astype(jnp.bfloat16)
    lowrank_projection = matrix_product(normed_input, adapter_first[:, : 3 * ADAPTER_RANK]).astype(
        jnp.bfloat16
    )
    adapter_query_key_value = jnp.concatenate(
        [
            matrix_product(lowrank_projection[:, :ADAPTER_RANK], adapter_second[:, :QUERY_WIDTH]),
            matrix_product(
                lowrank_projection[:, ADAPTER_RANK : 2 * ADAPTER_RANK],
                adapter_second[:, QUERY_WIDTH : QUERY_WIDTH + HEAD_SIZE],
            ),
            matrix_product(
                lowrank_projection[:, 2 * ADAPTER_RANK :],
                adapter_second[:, QUERY_WIDTH + HEAD_SIZE : PROJECTED_WIDTH],
            ),
        ],
        axis=1,
    )
    query_key_value_linear = matrix_product(normed_input, input_weight) + adapter_query_key_value
    queries = rotate(
        query_key_value_linear[:, :QUERY_WIDTH].reshape(local_rows, HEADS, HEAD_SIZE), pos_own
    ).astype(jnp.bfloat16)
    key_rot = rotate(
        query_key_value_linear[:, QUERY_WIDTH : QUERY_WIDTH + HEAD_SIZE].reshape(
            local_rows, 1, HEAD_SIZE
        ),
        pos_own,
    )[:, 0]
    kv_send = jnp.concatenate(
        [key_rot, query_key_value_linear[:, QUERY_WIDTH + HEAD_SIZE :]], axis=1
    ).astype(jnp.bfloat16)
    kv_all = lax.all_gather(kv_send, "dp", axis=0, tiled=True)
    keys = kv_all[:, :HEAD_SIZE]
    values = kv_all[:, HEAD_SIZE:]
    key_total = kv_all.shape[0]
    allowed = ((seq_own[:, None] == seq_all[None, :]) & (order_all[None, :] <= order_own[:, None]))[
        :, None, :
    ]
    query_rows = queries.reshape(local_rows * HEADS, HEAD_SIZE)

    def score_rows():
        raw_scores = (outer_columns(query_rows, keys) * scale).reshape(local_rows, HEADS, key_total)
        return jnp.where(allowed, raw_scores, FLOOR_SCORE)

    scores = score_rows()
    top_score = jnp.max(scores, axis=-1, keepdims=True)
    expo = jnp.exp(scores - top_score)
    mass = jnp.sum(expo, axis=-1, keepdims=True)
    prob_low = (expo / mass).astype(jnp.bfloat16)
    attended_rows = (
        matrix_product(prob_low.reshape(local_rows * HEADS, key_total), values)
        .reshape(local_rows, QUERY_WIDTH)
        .astype(jnp.bfloat16)
    )
    output_projection = matrix_product(
        attended_rows, adapter_first[:, 3 * ADAPTER_RANK : 4 * ADAPTER_RANK]
    ).astype(jnp.bfloat16)
    branch_output = matrix_product(attended_rows, output_weight) + matrix_product(
        output_projection, adapter_second[:, PROJECTED_WIDTH : PROJECTED_WIDTH + MODEL_WIDTH]
    )
    middle_state = residual_stream + active_mask * branch_output
    second_normed_input = norm_rows(middle_state, layer_norm_gains[1]).astype(jnp.bfloat16)
    feedforward_projection = matrix_product(
        second_normed_input, adapter_first[:, 4 * ADAPTER_RANK :]
    ).astype(jnp.bfloat16)
    normed_all, proj_all = (
        lax.all_gather(second_normed_input, "dp", axis=0, tiled=True),
        lax.all_gather(feedforward_projection, "dp", axis=0, tiled=True),
    )
    gate_own = outer_columns(normed_all, feedforward_weight[:, 0, :]) + outer_columns(
        proj_all[:, :ADAPTER_RANK], ffn_own[:, ADAPTER_RANK : 2 * ADAPTER_RANK]
    )
    up_own = outer_columns(normed_all, feedforward_weight[:, 1, :]) + outer_columns(
        proj_all[:, ADAPTER_RANK:], ffn_own[:, 2 * ADAPTER_RANK :]
    )
    units_own = geglu(gate_own, up_own).astype(jnp.bfloat16)
    ffn_sum, low_sum = (
        lax.psum_scatter(
            matrix_product(units_own, feedforward_weight[:, 2, :]),
            "dp",
            scatter_dimension=0,
            tiled=True,
        ),
        lax.psum_scatter(
            matrix_product(units_own, ffn_own[:, :ADAPTER_RANK]),
            "dp",
            scatter_dimension=0,
            tiled=True,
        ),
    )
    down_lowrank = low_sum.astype(jnp.bfloat16)
    complete_output = middle_state + active_mask * (
        ffn_sum + matrix_product(down_lowrank, adapter_second[:, PROJECTED_WIDTH + MODEL_WIDTH :])
    )
    confidence = root_mean(residual_stream) / (
        root_mean(residual_stream) + root_mean(complete_output - residual_stream)
    )
    conf_sum = jnp.sum(jnp.where(live_own, confidence, 0.0))
    depth_hits = (
        (token_exit_depth[0][:, None] == jnp.arange(loop_count + 1, dtype=jnp.int32)[None, :])
        & live_own[:, None]
    ).astype(jnp.float32)
    conf_total, depth_total = lax.psum((conf_sum, jnp.sum(depth_hits, axis=0)), ("loop", "dp"))
    mean_confidence = conf_total / jnp.sum(depth_total)
    exit_counts = depth_total.astype(jnp.int32)
    grad_out = layer_output_gradient[0].astype(jnp.float32)
    feedforward_gradient = (active_mask * grad_out).astype(jnp.bfloat16)
    lowrank_gradient = outer_columns(
        feedforward_gradient, adapter_second[:, PROJECTED_WIDTH + MODEL_WIDTH :]
    ).astype(jnp.bfloat16)
    grad_ffn_all, grad_low_all = (
        lax.all_gather(feedforward_gradient, "dp", axis=0, tiled=True),
        lax.all_gather(lowrank_gradient, "dp", axis=0, tiled=True),
    )
    hidden_unit_gradient = outer_columns(grad_ffn_all, feedforward_weight[:, 2, :]) + outer_columns(
        grad_low_all, ffn_own[:, :ADAPTER_RANK]
    )
    grad_gate_own, grad_up_own = jax.vjp(geglu, gate_own, up_own)[1](hidden_unit_gradient)
    grad_gate_own = grad_gate_own.astype(jnp.bfloat16)
    grad_up_own = grad_up_own.astype(jnp.bfloat16)
    input_terms = matrix_product(grad_gate_own, feedforward_weight[:, 0, :]) + matrix_product(
        grad_up_own, feedforward_weight[:, 1, :]
    )
    proj_terms = jnp.concatenate(
        [
            matrix_product(grad_gate_own, ffn_own[:, ADAPTER_RANK : 2 * ADAPTER_RANK]),
            matrix_product(grad_up_own, ffn_own[:, 2 * ADAPTER_RANK :]),
        ],
        axis=1,
    )
    grad_norm_base, grad_proj = (
        lax.psum_scatter(input_terms, "dp", scatter_dimension=0, tiled=True),
        lax.psum_scatter(proj_terms, "dp", scatter_dimension=0, tiled=True),
    )
    ffn_grad = jnp.concatenate(
        [
            inner_rows(grad_gate_own, normed_all),
            inner_rows(grad_up_own, normed_all),
            inner_rows(units_own, grad_ffn_all),
            inner_rows(units_own, grad_low_all),
            inner_rows(grad_gate_own, proj_all[:, :ADAPTER_RANK]),
            inner_rows(grad_up_own, proj_all[:, ADAPTER_RANK:]),
        ],
        axis=1,
    )
    lowrank_projection_gradient = grad_proj.astype(jnp.bfloat16)
    second_normed_gradient = grad_norm_base + outer_columns(
        lowrank_projection_gradient, adapter_first[:, 4 * ADAPTER_RANK :]
    )
    grad_middle_part, grad_gain_two = jax.vjp(norm_rows, middle_state, layer_norm_gains[1])[1](
        second_normed_gradient
    )
    grad_middle = grad_out + grad_middle_part
    branch_gradient = (active_mask * grad_middle).astype(jnp.bfloat16)
    output_projection_gradient = outer_columns(
        branch_gradient, adapter_second[:, PROJECTED_WIDTH : PROJECTED_WIDTH + MODEL_WIDTH]
    ).astype(jnp.bfloat16)
    grad_attended = (
        outer_columns(branch_gradient, output_weight)
        + outer_columns(
            output_projection_gradient, adapter_first[:, 3 * ADAPTER_RANK : 4 * ADAPTER_RANK]
        )
    ).astype(jnp.bfloat16)
    grad_att_rows = grad_attended.reshape(local_rows * HEADS, HEAD_SIZE)
    prob = jnp.exp(score_rows() - top_score) / mass
    grad_prob = outer_columns(grad_att_rows, values).reshape(local_rows, HEADS, key_total)
    centre = jnp.sum(prob * grad_prob, axis=-1, keepdims=True)
    grad_scores = (
        (prob * (grad_prob - centre)).astype(jnp.bfloat16).reshape(local_rows * HEADS, key_total)
    )
    grad_queries = (matrix_product(grad_scores, keys) * scale).reshape(local_rows, HEADS, HEAD_SIZE)
    prob_again = prob.astype(jnp.bfloat16).reshape(local_rows * HEADS, key_total)
    kv_terms = jnp.concatenate(
        [inner_rows(grad_scores, query_rows) * scale, inner_rows(prob_again, grad_att_rows)], axis=1
    )
    grad_kv = lax.psum_scatter(kv_terms, "dp", scatter_dimension=0, tiled=True)
    query_linear_gradient = (
        rotate_back(grad_queries, pos_own).reshape(local_rows, QUERY_WIDTH).astype(jnp.bfloat16)
    )
    key_linear_gradient = rotate_back(grad_kv[:, None, :HEAD_SIZE], pos_own)[:, 0].astype(
        jnp.bfloat16
    )
    value_linear_gradient = grad_kv[:, HEAD_SIZE:].astype(jnp.bfloat16)
    query_key_value_gradient = jnp.concatenate(
        [query_linear_gradient, key_linear_gradient, value_linear_gradient], axis=1
    )
    attention_projection_gradient = jnp.concatenate(
        [
            outer_columns(query_linear_gradient, adapter_second[:, :QUERY_WIDTH]),
            outer_columns(
                key_linear_gradient, adapter_second[:, QUERY_WIDTH : QUERY_WIDTH + HEAD_SIZE]
            ),
            outer_columns(
                value_linear_gradient, adapter_second[:, QUERY_WIDTH + HEAD_SIZE : PROJECTED_WIDTH]
            ),
        ],
        axis=1,
    ).astype(jnp.bfloat16)
    normed_gradient = outer_columns(query_key_value_gradient, input_weight) + outer_columns(
        attention_projection_gradient, adapter_first[:, : 3 * ADAPTER_RANK]
    )
    grad_resid_part, grad_gain_one = jax.vjp(norm_rows, residual_stream, layer_norm_gains[0])[1](
        normed_gradient
    )
    hidden_grad = grad_middle + grad_resid_part
    grad_w_in = inner_rows(normed_input, query_key_value_gradient)
    grad_w_out = inner_rows(attended_rows, branch_gradient)
    grad_gains = jnp.stack([grad_gain_one, grad_gain_two])
    adapter_first_gradient = jnp.concatenate(
        [
            inner_rows(normed_input, attention_projection_gradient),
            inner_rows(attended_rows, output_projection_gradient),
            inner_rows(second_normed_input, lowrank_projection_gradient),
        ],
        axis=1,
    )
    adapter_second_gradient = jnp.concatenate(
        [
            inner_rows(lowrank_projection[:, :ADAPTER_RANK], query_linear_gradient),
            inner_rows(lowrank_projection[:, ADAPTER_RANK : 2 * ADAPTER_RANK], key_linear_gradient),
            inner_rows(lowrank_projection[:, 2 * ADAPTER_RANK :], value_linear_gradient),
            inner_rows(output_projection, branch_gradient),
            inner_rows(down_lowrank, feedforward_gradient),
        ],
        axis=1,
    )
    input_portion, output_portion, gain_portion, adapter_first_grads, adapter_second_grads = (
        lax.psum_scatter(grad_w_in, "dp", scatter_dimension=0, tiled=True),
        lax.psum_scatter(grad_w_out, "dp", scatter_dimension=0, tiled=True),
        lax.psum_scatter(grad_gains, "dp", scatter_dimension=1, tiled=True),
        lax.psum_scatter(adapter_first_gradient, "dp", scatter_dimension=0, tiled=True),
        lax.psum_scatter(adapter_second_gradient, "dp", scatter_dimension=1, tiled=True),
    )
    mlp_part = ffn_grad[:, : 3 * MODEL_WIDTH].reshape(ffn_rows, 3, MODEL_WIDTH)
    sum_in, sum_out, sum_gains, sum_mlp = (
        lax.psum(input_portion.astype(jnp.bfloat16), "loop").astype(jnp.float32),
        lax.psum(output_portion.astype(jnp.bfloat16), "loop").astype(jnp.float32),
        lax.psum(gain_portion.astype(jnp.bfloat16), "loop").astype(jnp.float32),
        lax.psum(mlp_part.astype(jnp.bfloat16), "loop").astype(jnp.float32),
    )
    return (
        complete_output.astype(jnp.bfloat16)[None],
        hidden_grad[None],
        sum_in,
        sum_out,
        sum_mlp,
        sum_gains,
        adapter_first_grads[None],
        adapter_second_grads[None],
        ffn_grad[:, 3 * MODEL_WIDTH :][None],
        exit_counts,
        mean_confidence,
    )


def solution(mesh):
    return jax.shard_map(
        per_device,
        mesh=mesh,
        in_specs=(
            P("loop", "dp", None),
            P("loop", "dp", None),
            P("dp", None),
            P("dp", None),
            P("dp", None, None),
            P(),
            P("loop", None, None),
            P("loop", None, None),
            P("loop", None, None),
            P("loop", None),
            P("loop", None),
            P("loop", "dp"),
        ),
        out_specs=(
            P("loop", "dp", None),
            P("loop", "dp", None),
            P("dp", None),
            P("dp", None),
            P("dp", None, None),
            P(None, "dp"),
            P("loop", "dp", None),
            P("loop", None, "dp"),
            P("loop", "dp", None),
            P(),
            P(),
        ),
        check_vma=False,
    )
```

profile of v0, /device:TPU:0, one launch (start us, length us, event | category | flops | bytes accessed | tf_op | source)
XLA Modules:
  0.0 2127.0 jit_solution(12081901270876605554)
XLA Ops:
  22.8 78.1 %all-gather.8.cloned.1.call-done = bf16[2048,2560]{1,0:T(8,128)(2,1)} async-done(((bf16[128,2560]{1,0:T(8,128)(2,1)}), bf16[2048,2560]{1,0:T(8,128)(2,1)}) %all-gather.8.cloned.1.call-update) | async-done | bytes 10485776 | tf_op jit(solution)/shard_map/all_gather | solution.py:126
  113.7 33.9 %all-gather.10.cloned.1.call-done = bf16[2048,512]{1,0:T(8,128)(2,1)} async-done(((bf16[128,512]{1,0:T(8,128)(2,1)}), bf16[2048,512]{1,0:T(8,128)(2,1)}) %all-gather.10.cloned.1.call-update) | async-done | bytes 2097168 | tf_op jit(solution)/shard_map/all_gather | solution.py:160
  164.3 59.1 %all-gather.12.cloned.1.call-done = bf16[2048,2048]{1,0:T(8,128)(2,1)} async-done(((bf16[128,2048]{1,0:T(8,128)(2,1)}), bf16[2048,2048]{1,0:T(8,128)(2,1)}) %all-gather.12.cloned.1.call-update) | async-done | bytes 8388624 | tf_op jit(solution)/shard_map/all_gather | solution.py:127
  238.2 61.0 %all-gather.18.cloned.1.call-done = bf16[2048,2048]{1,0:T(8,128)(2,1)} async-done(((bf16[128,2048]{1,0:T(8,128)(2,1)}), bf16[2048,2048]{1,0:T(8,128)(2,1)}) %all-gather.18.cloned.1.call-update) | async-done | bytes 8388624 | tf_op jit(solution)/shard_map/all_gather | solution.py:240
  299.2 14.5 fusion.14
  313.8 61.2 %all-gather.14.cloned.1.call-done = bf16[2048,2048]{1,0:T(8,128)(2,1)} async-done(((bf16[128,2048]{1,0:T(8,128)(2,1)}), bf16[2048,2048]{1,0:T(8,128)(2,1)}) %all-gather.14.cloned.1.call-update) | async-done | bytes 8388624 | tf_op jit(solution)/shard_map/all_gather | solution.py:195
  375.0 14.6 fusion.19
  389.6 13.2 fusion.23
  402.8 14.5 all-gather.16.cloned.1.call-done
  430.6 25.6 %all-gather.20.cloned.1.call-done = bf16[2048,256]{1,0:T(8,128)(2,1)} async-done(((bf16[128,256]{1,0:T(8,128)(2,1)}), bf16[2048,256]{1,0:T(8,128)(2,1)}) %all-gather.20.cloned.1.call-update) | async-done | bytes 1048592 | tf_op jit(solution)/shard_map/all_gather | solution.py:241
  456.2 14.6 multiply_convert_fusion.1
  476.6 15.5 fusion.21
  492.0 18.9 convolution_add_fusion
  511.9 36.0 %reduce-scatter.21.cloned.1.call-done = f32[128,512]{0,1:T(8,128)} async-done(((f32[2048,512]{0,1:T(8,128)}), f32[128,512]{0,1:T(8,128)}) %reduce-scatter.21.cloned.1.call-update) | async-done | bytes 262160 | tf_op jit(solution)/shard_map/reduce_scatter | solution.py:261
  547.9 182.9 %reduce-scatter.19.cloned.1.call-done = f32[128,2048]{1,0:T(8,128)} async-done(((f32[2048,2048]{1,0:T(8,128)}), f32[128,2048]{1,0:T(8,128)}) %reduce-scatter.19.cloned.1.call-update) | async-done | bytes 1048592 | tf_op jit(solution)/shard_map/reduce_scatter | solution.py:260
  745.3 10.6 multiply_reduce_fusion
  755.9 11.3 multiply_convert_fusion
  779.9 15.9 fusion.16
  813.0 33.6 %reduce-scatter.23.cloned.1.call-done = f32[128,512]{1,0:T(8,128)} async-done(((f32[2048,512]{1,0:T(8,128)}), f32[128,512]{1,0:T(8,128)}) %reduce-scatter.23.cloned.1.call-update) | async-done | bytes 262160 | tf_op jit(solution)/shard_map/reduce_scatter | solution.py:304
  874.1 37.4 %reduce-scatter.17.cloned.1.call-done = f32[128,256]{1,0:T(8,128)} async-done(((f32[2048,256]{1,0:T(8,128)}), f32[128,256]{1,0:T(8,128)}) %reduce-scatter.17.cloned.1.call-update) | async-done | bytes 131088 | tf_op jit(solution)/shard_map/reduce_scatter | solution.py:212
  911.5 182.1 %reduce-scatter.15.cloned.1.call-done = f32[128,2048]{1,0:T(8,128)} async-done(((f32[2048,2048]{1,0:T(8,128)}), f32[128,2048]{1,0:T(8,128)}) %reduce-scatter.15.cloned.1.call-update) | async-done | bytes 1048592 | tf_op jit(solution)/shard_map/reduce_scatter | solution.py:206
  1127.8 13.0 convolution_convert_fusion.1
  1140.9 11.9 convolution_convert_fusion.2
  1162.8 11.3 pad_maximum_fusion
  1174.1 16.7 copy.102
  1190.8 85.0 %reduce-scatter.27.cloned.1.call-done = f32[128,2048]{1,0:T(8,128)} async-done(((f32[2048,2048]{1,0:T(8,128)}), f32[128,2048]{1,0:T(8,128)}) %reduce-scatter.27.cloned.1.call-update) | async-done | bytes 1048592 | tf_op jit(solution)/shard_map/reduce_scatter | solution.py:357
  1277.9 212.9 %reduce-scatter.25.cloned.1.call-done = f32[128,2560]{1,0:T(8,128)} async-done(((f32[2048,2560]{1,0:T(8,128)}), f32[128,2560]{1,0:T(8,128)}) %reduce-scatter.25.cloned.1.call-update) | async-done | bytes 1310736 | tf_op jit(solution)/shard_map/reduce_scatter | solution.py:356
  1507.8 40.0 %all-reduce.4 = (f32[3]{0:T(128)S(1)}, f32[]{:T(128)}) all-reduce(f32[3]{0:T(128)S(1)} %convert_reduce_fusion.1, f32[]{:T(128)} %get-tuple-element.93), channel_id=1, replica_groups=mesh['loop'=2,'dp'=16] {'loop','dp'}, use_global_device_ids=true, to_apply=%region_27.28 | all-reduce | flops 4 | bytes 32 | tf_op jit(solution)/shard_map/psum | solution.py:231
  1559.7 83.3 %reduce-scatter.33.cloned.1.call-done = f32[416,256]{1,0:T(8,128)} async-done(((f32[6656,256]{1,0:T(8,128)}), f32[416,256]{1,0:T(8,128)}) %reduce-scatter.33.cloned.1.call-update) | async-done | bytes 426000
  1645.2 136.4 %reduce-scatter.29.cloned.1.call-done = f32[128,1536]{0,1:T(8,128)} async-done(((f32[2048,1536]{0,1:T(8,128)}), f32[128,1536]{0,1:T(8,128)}) %reduce-scatter.29.cloned.1.call-update) | async-done | bytes 786448 | tf_op jit(solution)/shard_map/reduce_scatter | solution.py:359
  1783.9 314.3 %all-reduce.8.cloned.1.call-done = (bf16[1024,3,2048]{0,2,1:T(8,128)(2,1)}, bf16[128,2560]{1,0:T(8,128)(2,1)}, bf16[128,2048]{1,0:T(8,128)(2,1)}) async-done(((bf16[1024,3,2048]{0,2,1:T(8,128)(2,1)}, bf16[128,2560]{1,0:T(8,128)(2,1)}, bf16[128,2048]{1,0:T(8,128)(2,1)}), (bf16[1024,3,2048]{0,2,1:T(8,128)(2,1)}, bf16[128,2560]{1,0:T(8,128)(2,1)}, bf16[128,2048]{1,0:T(8,128)(2,1)})) %all-reduce.8.cloned.1.call-update) | async-done | bytes 13762576 | tf_op jit(solution)/shard_map/psum | solution.py:367
  2098.2 18.2 copy.105
  (310 shorter events, 231.0 us)
Async XLA Ops:
  7.2 93.7 %copy-start = (bf16[1,128,2048]{2,1,0:T(8,128)(2,1)S(1)}, bf16[1,128,2048]{2,1,0:T(8,128)(2,1)}, u32[]{:S(2)}) copy-start(bf16[1,128,2048]{2,1,0:T(8,128)(2,1)} %param.12) | copy-start | bytes 1572868
  7.2 93.7 %all-gather.8.cloned.1.call-start = ((), (), s32[]{:S(2)}) async-start(), calls=%async_computation.10 | async-start | bytes 11141120 | tf_op jit(solution)/shard_map/all_gather | solution.py:126
  7.9 139.6 %all-gather.10.cloned.1.call-start = ((), (), s32[]{:S(2)}) async-start(), calls=%async_computation.11 | async-start | bytes 2228224 | tf_op jit(solution)/shard_map/all_gather | solution.py:160
  8.8 101.0 %copy-start.54 = (f32[128]{0:T(128)}, f32[128]{0:T(128)S(1)}, u32[]{:S(2)}) copy-start(f32[128]{0:T(128)S(1)} %multiply_power_fusion) | copy-start | bytes 1540
  12.2 94.5 %copy-start.46 = (f32[128]{0:T(128)}, f32[128]{0:T(128)S(1)}, u32[]{:S(2)}) copy-start(f32[128]{0:T(128)S(1)} %fusion.158) | copy-start | bytes 1540
  13.6 93.1 %copy-start.56 = (pred[128]{0:T(512)(128)(4,1)}, pred[128]{0:T(512)(128)(4,1)S(1)}, u32[]{:S(2)}) copy-start(pred[128]{0:T(512)(128)(4,1)S(1)} %get-tuple-element.66) | copy-start | bytes 388
  13.6 720.2 %copy-start.49 = (f32[128]{0:T(128)}, f32[128]{0:T(128)S(1)}, u32[]{:S(2)}) copy-start(f32[128]{0:T(128)S(1)} %get-tuple-element.65) | copy-start | bytes 1540
  14.4 95.4 %copy-start.52 = (f32[128]{0:T(128)}, f32[128]{0:T(128)S(1)}, u32[]{:S(2)}) copy-start(f32[128]{0:T(128)S(1)} %get-tuple-element.86) | copy-start | bytes 1540
  15.2 91.5 %copy-start.24 = (f32[1,2048]{1,0:T(1,128)}, f32[1,2048]{1,0:T(1,128)S(1)}, u32[]{:S(2)}) copy-start(f32[1,2048]{1,0:T(1,128)S(1)} %get-tuple-element.84) | copy-start | bytes 24580
  15.2 718.6 %copy-start.39 = (f32[1,2048]{1,0:T(1,128)}, f32[1,2048]{1,0:T(1,128)S(1)}, u32[]{:S(2)}) copy-start(f32[1,2048]{1,0:T(1,128)S(1)} %get-tuple-element.83) | copy-start | bytes 24580
  17.9 88.8 %copy-start.27 = (bf16[128,768]{1,0:T(8,128)(2,1)}, bf16[128,768]{1,0:T(8,128)(2,1)S(1)}, u32[]{:S(2)}) copy-start(bf16[128,768]{1,0:T(8,128)(2,1)S(1)} %fusion.56) | copy-start | bytes 589828
  22.8 85.8 %copy-start.7 = (bf16[1,128,2048]{2,1,0:T(8,128)(2,1)S(1)}, bf16[1,128,2048]{2,1,0:T(8,128)(2,1)}, u32[]{:S(2)}) copy-start(bf16[1,128,2048]{2,1,0:T(8,128)(2,1)} %param.13) | copy-start | bytes 1572868
  22.8 87.4 %copy-start.41 = (s32[1,2048]{1,0:T(1,128)S(1)}, s32[1,2048]{1,0:T(1,128)}, u32[]{:S(2)}) copy-start(s32[1,2048]{1,0:T(1,128)} %param.22) | copy-start | bytes 24580
  107.8 115.6 %all-gather.12.cloned.1.call-start = ((), (), s32[]{:S(2)}) async-start(), calls=%async_computation.12 | async-start | bytes 8912896 | tf_op jit(solution)/shard_map/all_gather | solution.py:127
  108.6 190.6 %all-gather.18.cloned.1.call-start = ((), (), s32[]{:S(2)}) async-start(), calls=%async_computation.17 | async-start | bytes 8912896 | tf_op jit(solution)/shard_map/all_gather | solution.py:240
  109.6 265.4 %all-gather.14.cloned.1.call-start = ((), (), s32[]{:S(2)}) async-start(), calls=%async_computation.13 | async-start | bytes 8912896 | tf_op jit(solution)/shard_map/all_gather | solution.py:195
  229.9 503.9 %copy-start.50 = (f32[128]{0:T(128)}, f32[128]{0:T(128)S(1)}, u32[]{:S(2)}) copy-start(f32[128]{0:T(128)S(1)} %fusion.151) | copy-start | bytes 1540
  230.9 186.4 %all-gather.16.cloned.1.call-start = ((), (), s32[]{:S(2)}) async-start(), calls=%async_computation.14 | async-start | bytes 2228224 | tf_op jit(solution)/shard_map/all_gather | solution.py:196
  234.0 222.1 %all-gather.20.cloned.1.call-start = ((), (), s32[]{:S(2)}) async-start(), calls=%async_computation.18 | async-start | bytes 1114112 | tf_op jit(solution)/shard_map/all_gather | solution.py:241
  236.4 311.5 %reduce-scatter.21.cloned.1.call-start = ((), (), s32[]{:S(2)}) async-start(), calls=%async_computation.20 | async-start | bytes 4456448 | tf_op jit(solution)/shard_map/reduce_scatter | solution.py:261
  238.2 233.8 %copy-start.11 = (bf16[1024,768]{1,0:T(8,128)(2,1)}, bf16[1024,768]{1,0:T(8,128)(2,1)S(1)}, u32[]{:S(2)}) copy-start(bf16[1024,768]{1,0:T(8,128)(2,1)S(1)} %dynamic-slice_bitcast_fusion) | copy-start | bytes 4718596
  476.5 254.3 %reduce-scatter.19.cloned.1.call-start = ((), (), s32[]{:S(2)}) async-start(), calls=%async_computation.19 | async-start | bytes 17825792 | tf_op jit(solution)/shard_map/reduce_scatter | solution.py:260
  510.9 223.8 %copy-start.8 = (bf16[1,128,2048]{2,1,0:T(8,128)(2,1)S(1)}, bf16[1,128,2048]{2,1,0:T(8,128)(2,1)}, u32[]{:S(2)}) copy-start(bf16[1,128,2048]{2,1,0:T(8,128)(2,1)} %param.13) | copy-start | bytes 1572868
  511.0 335.6 %reduce-scatter.23.cloned.1.call-start = ((), (), s32[]{:S(2)}) async-start(), calls=%async_computation.21 | async-start | bytes 4456448 | tf_op jit(solution)/shard_map/reduce_scatter | solution.py:304
  774.9 136.6 %reduce-scatter.17.cloned.1.call-start = ((), (), s32[]{:S(2)}) async-start(), calls=%async_computation.16 | async-start | bytes 2228224 | tf_op jit(solution)/shard_map/reduce_scatter | solution.py:212
  779.9 313.7 %reduce-scatter.15.cloned.1.call-start = ((), (), s32[]{:S(2)}) async-start(), calls=%async_computation.15 | async-start | bytes 17825792 | tf_op jit(solution)/shard_map/reduce_scatter | solution.py:206
  795.8 480.0 %reduce-scatter.27.cloned.1.call-start = ((), (), s32[]{:S(2)}) async-start(), calls=%async_computation.23 | async-start | bytes 17825792 | tf_op jit(solution)/shard_map/reduce_scatter | solution.py:357
  805.4 685.4 %reduce-scatter.25.cloned.1.call-start = ((), (), s32[]{:S(2)}) async-start(), calls=%async_computation.22 | async-start | bytes 22282240 | tf_op jit(solution)/shard_map/reduce_scatter | solution.py:356
  858.9 694.2 %reduce-scatter.31.cloned.1.call-start = ((), (), s32[]{:S(2)}) async-start(), calls=%async_computation.25 | async-start | bytes 1114112
  1105.4 537.7 %reduce-scatter.33.cloned.1.call-start = ((), (), s32[]{:S(2)}) async-start(), calls=%async_computation.26 | async-start | bytes 7241728
  1117.4 664.2 %reduce-scatter.29.cloned.1.call-start = ((), (), s32[]{:S(2)}) async-start(), calls=%async_computation.24 | async-start | bytes 13369344 | tf_op jit(solution)/shard_map/reduce_scatter | solution.py:359
  1127.7 970.5 %all-reduce.8.cloned.1.call-start = ((), (), s32[]{:S(2)}) async-start(), calls=%async_computation.27 | async-start | bytes 27525120 | tf_op jit(solution)/shard_map/psum | solution.py:367
  (64 other events, 1101.5 us)
Sparse Core Ops, SparseCore 0:
  10.3 90.5 all-gather.7
  108.0 39.5 all-gather.9
  149.7 73.6 all-gather.11
  226.0 73.1 all-gather.17
  301.8 73.1 all-gather.13
  377.6 39.6 all-gather.15
  419.4 36.6 all-gather.19
  476.6 71.2 reduce-scatter.20
  553.2 177.6 reduce-scatter.18
  775.0 71.4 reduce-scatter.22
  850.9 60.6 reduce-scatter.16
  916.0 177.5 reduce-scatter.14
  1098.3 177.4 reduce-scatter.26
  1280.9 209.8 reduce-scatter.24
  1495.3 56.4 reduce-scatter.30
  1555.6 87.4 reduce-scatter.32
  1647.5 134.0 reduce-scatter.28
  1784.2 313.9 all-reduce.7
where the time goes:
time: 2130 us
  waiting for transfers between devices  1640 us (77%)
  matrix products  282 us (13%)
  local copies, waits for them, and re-layouts  75.8 us (4%)
  other arithmetic  65.6 us (3%)
  blocking collectives  45.1 us (2%)
    psum x1, waiting for transfers between devices, per_device(): lax.psum(mlp_part.astype(jnp.bfloat16), 'loop').astype(jnp.float32)  314 us
    reduce_scatter x1, waiting for transfers between devices, per_device(): lax.psum_scatter(grad_w_in, 'dp', scatter_dimension=0, tiled=True)  213 us
    reduce_scatter x1, waiting for transfers between devices, per_device(): lax.psum_scatter(input_terms, 'dp', scatter_dimension=0, tiled=True)  183 us
    reduce_scatter x1, waiting for transfers between devices, per_device(): lax.psum_scatter(matrix_product(units_own, feedforward_weight[:, 2, :]),...  182 us
    reduce_scatter x1, waiting for transfers between devices, per_device(): lax.psum_scatter(adapter_first_gradient, 'dp', scatter_dimension=0, tiled...  136 us
    dot_general x18, matrix products, outer_columns(): lax.dot_general(left, right, (((1,), (1,)), ((), ())), preferred_element_...  113 us
    dot_general x18, matrix products, matrix_product(): return jnp.dot(left, right, preferred_element_type=jnp.float32)  91.8 us
    reduce_scatter x1, waiting for transfers between devices, per_device(): lax.psum_scatter(grad_w_out, 'dp', scatter_dimension=0, tiled=True)  85 us
  transfers between devices with their start and end apart: 18, of which 17 were waited for; matrix products, arithmetic and copies ran while one was open for 15% of the time, Pallas kernels for 0%

commit v1 on v0

v1 whole, which is shorter than its diff:
```python
import functools

import jax
import jax.numpy as jnp
from jax import lax
from jax.experimental import pallas as pl
from jax.experimental.pallas import tpu as pltpu
from jax.sharding import PartitionSpec as P

MODEL_WIDTH = 2048
HEADS = 8
HEAD_SIZE = 256
ADAPTER_RANK = 256
QUERY_WIDTH = 2048
PROJECTED_WIDTH = 2560


EPSILON = 1e-06
FLOOR_SCORE = -1e30
MESH = pl.DeviceIdType.MESH
VMEM_LIMIT = 60 * 1024 * 1024
LINE_DEVICES = 16


def matrix_product(left, right):
    return jnp.dot(left, right, preferred_element_type=jnp.float32)


def inner_rows(left, right):
    return lax.dot_general(
        left, right, (((0,), (0,)), ((), ())), preferred_element_type=jnp.float32
    )


def outer_columns(left, right):
    return lax.dot_general(
        left, right, (((1,), (1,)), ((), ())), preferred_element_type=jnp.float32
    )


def norm_rows(values, gain):
    return values * lax.rsqrt(jnp.mean(values * values, axis=-1, keepdims=True) + EPSILON) * gain


def rotate(values, positions):
    half_dim = values.shape[-1] // 2
    freqs = 10000.0 ** (-jnp.arange(half_dim, dtype=jnp.float32) / half_dim)
    angles = positions.astype(jnp.float32)[:, None, None] * freqs
    cosine = jnp.cos(angles)
    sine = jnp.sin(angles)
    first_half = values[..., :half_dim]
    second_half = values[..., half_dim:]
    return jnp.concatenate(
        [first_half * cosine - second_half * sine, first_half * sine + second_half * cosine],
        axis=-1,
    )


def rotate_back(grads, positions):

    def turned(values):
        return rotate(values, positions)

    return jax.vjp(turned, jnp.zeros_like(grads))[1](grads)[0]


def geglu(gate_values, up_projection_value):
    return jax.nn.gelu(gate_values, approximate=True) * up_projection_value


def root_mean(values):
    return jnp.sqrt(jnp.mean(values * values, axis=-1) + EPSILON)


def token_facts(row_of_tokens, sequence_length):
    row_total = row_of_tokens.shape[0]
    live_row = row_of_tokens >= 0
    seq_ends = jnp.cumsum(sequence_length)
    seq_index = jnp.sum((row_of_tokens[:, None] >= seq_ends[None, :]).astype(jnp.int32), axis=1)
    seq_starts = seq_ends - sequence_length
    own_start = jnp.sum(
        jnp.where(
            seq_index[:, None] == jnp.arange(sequence_length.shape[0], dtype=jnp.int32)[None, :],
            seq_starts[None, :],
            0,
        ),
        axis=1,
    )
    row_ids = jnp.arange(row_total, dtype=jnp.int32)
    sequence = jnp.where(live_row, seq_index, -1 - row_ids)
    ordering = jnp.where(live_row, row_of_tokens, 0)
    positions = jnp.where(live_row, row_of_tokens - own_start, 0)
    return (live_row, sequence, ordering, positions)


def place(count):
    me = lax.axis_index("dp")
    return me, count // 4, me // 4, (me // 2) % 2, me % 2


def greet(count):
    me, depth, z, y, c = place(count)
    barrier = pltpu.get_barrier_semaphore()

    def signal(where):
        pl.semaphore_signal(barrier, inc=1, device_id={"dp": where}, device_id_type=MESH)

    signal(me + 1 - 2 * c)
    signal(me + 2 - 4 * y)

    @pl.when(z > 0)
    def _():
        signal(me - 4)

    @pl.when(z < depth - 1)
    def _():
        signal(me + 4)

    ends = jnp.where((z > 0) & (z < depth - 1), 4, 3)
    pl.semaphore_wait(barrier, ends)


def gather_body(count, parts, arrays, *refs):
    own = refs[:arrays]
    full = refs[arrays : 2 * arrays]
    keep, recv, send_core, send_pair, send_right, send_left = refs[2 * arrays :]
    me, depth, z, y, c = place(count)
    greet(count)

    def spans(a):
        rows = own[a].shape[0]
        step = rows // parts
        return [(s, pl.ds(s * step, step)) for s in range(parts)]

    def copy(a, block, span, target, sem, first=False):
        s, rows = span
        source = own[a].at[rows] if first else full[a].at[block, rows]
        return pltpu.make_async_remote_copy(
            src_ref=source,
            dst_ref=full[a].at[block, rows],
            send_sem=sem,
            recv_sem=recv.at[a, block, s],
            device_id={"dp": target},
            device_id_type=MESH,
        )

    def to_core(a, block, span, first=False):
        return copy(a, block, span, me + 1 - 2 * c, send_core.at[a, block // 2, span[0]], first)

    def to_pair(a, block, span, first=False):
        return copy(a, block, span, me + 2 - 4 * y, send_pair.at[a, block // 4, span[0]], first)

    def to_right(a, block, span, first=False):
        return copy(a, block, span, me + 4, send_right.at[a, block // 4, span[0]], first)

    def to_left(a, block, span, first=False):
        return copy(a, block, span, me - 4, send_left.at[a, block // 4, span[0]], first)

    local = [
        pltpu.make_async_copy(own[a], full[a].at[me], keep.at[a]) for a in range(arrays)
    ]
    units = [(a, span) for a in range(arrays) for span in spans(a)]
    for a, span in units:

        @pl.when(z < depth - 1)
        def _(a=a, span=span):
            to_right(a, me, span, True).start()

        @pl.when(z > 0)
        def _(a=a, span=span):
            to_left(a, me, span, True).start()

        to_pair(a, me, span, True).start()
        to_core(a, me, span, True).start()
    for item in local:
        item.start()
    mate = me + 2 - 4 * y
    for k in range(1, depth):
        for a, span in units:

            @pl.when(z - k >= 0)
            def _(a=a, span=span):
                block = me - 4 * k
                to_right(a, block, span).wait_recv()

                @pl.when(z < depth - 1)
                def _():
                    to_right(a, block, span).start()

                to_pair(a, block, span).start()
                to_core(a, block, span).start()

            @pl.when(z + k < depth)
            def _(a=a, span=span):
                block = me + 4 * k
                to_left(a, block, span).wait_recv()

                @pl.when(z > 0)
                def _():
                    to_left(a, block, span).start()

                to_pair(a, block, span).start()
                to_core(a, block, span).start()

    def from_pair(a, block, span):
        to_pair(a, block, span).wait_recv()
        to_core(a, block, span).start()

    for a, span in units:
        from_pair(a, mate, span)
    for k in range(1, depth):
        for a, span in units:

            @pl.when(z - k >= 0)
            def _(a=a, span=span):
                from_pair(a, mate - 4 * k, span)

            @pl.when(z + k < depth)
            def _(a=a, span=span):
                from_pair(a, mate + 4 * k, span)

    for a, span in units:
        for j in range(count // 2):
            to_core(a, 2 * j + 1 - c, span).wait_recv()
    for item in local:
        item.wait()
    for a, span in units:
        for j in range(count // 2):
            to_core(a, 2 * j + c, span).wait_send()
        for j in range(depth):
            block = 4 * j + 2 * y + c
            to_pair(a, block, span).wait_send()

            @pl.when((z >= j) & (z < depth - 1))
            def _():
                to_right(a, block, span).wait_send()

            @pl.when((z <= j) & (z > 0))
            def _():
                to_left(a, block, span).wait_send()


def gather_rows(count, ident, *arrays, parts=2):
    if count != LINE_DEVICES:
        return [lax.all_gather(item, "dp", axis=0, tiled=True) for item in arrays]
    number = len(arrays)
    depth = count // 4
    sem = pltpu.SemaphoreType.DMA
    full = pl.pallas_call(
        functools.partial(gather_body, count, parts, number),
        out_shape=[
            jax.ShapeDtypeStruct((count,) + item.shape, item.dtype) for item in arrays
        ],
        in_specs=[pl.BlockSpec(memory_space=pl.ANY)] * number,
        out_specs=[pl.BlockSpec(memory_space=pl.ANY)] * number,
        scratch_shapes=[
            sem((number,)),
            sem((number, count, parts)),
            sem((number, count // 2, parts)),
            sem((number, depth, parts)),
            sem((number, depth, parts)),
            sem((number, depth, parts)),
        ],
        compiler_params=pltpu.CompilerParams(
            collective_id=ident, has_side_effects=True, vmem_limit_bytes=VMEM_LIMIT
        ),
        name="gather_rows",
    )(*arrays)
    return [
        item.reshape((count * item.shape[1],) + item.shape[2:]) for item in full
    ]


def scatter_body(count, parts, arrays, *refs):
    terms = refs[:arrays]
    total = refs[arrays : 2 * arrays]
    scratch = refs[2 * arrays :]
    held, loaded, core_in, pair_in, line_in = [
        scratch[i * arrays : (i + 1) * arrays] for i in range(5)
    ]
    (load_sem, core_send, core_recv, pair_send, pair_recv, line_send, line_recv) = scratch[
        5 * arrays :
    ]
    me, depth, z, y, c = place(count)
    greet(count)
    near = z < depth // 2

    def turn(k):
        even = depth - 1 - k // 2 if k % 2 == 0 else k // 2
        return jnp.where(near, even, depth - 1 - even)

    def rows_of(a, s):
        step = terms[a].shape[1] // parts[a]
        return pl.ds(s * step, step)

    def to_core(a, s, line, pair):
        slot = 2 * line + pair
        return pltpu.make_async_remote_copy(
            src_ref=terms[a].at[2 * slot + 1 - c, rows_of(a, s)],
            dst_ref=core_in[a].at[slot, rows_of(a, s)],
            send_sem=core_send.at[a, slot, s],
            recv_sem=core_recv.at[a, slot, s],
            device_id={"dp": me + 1 - 2 * c},
            device_id_type=MESH,
        )

    def load(a, s, line, pair):
        slot = 2 * line + pair
        return pltpu.make_async_copy(
            terms[a].at[2 * slot + c, rows_of(a, s)],
            loaded[a].at[slot, rows_of(a, s)],
            load_sem.at[a, slot, s],
        )

    def to_pair(a, s, line):
        return pltpu.make_async_remote_copy(
            src_ref=loaded[a].at[2 * line + 1 - y, rows_of(a, s)],
            dst_ref=pair_in[a].at[line, rows_of(a, s)],
            send_sem=pair_send.at[a, line, s],
            recv_sem=pair_recv.at[a, line, s],
            device_id={"dp": me + 2 - 4 * y},
            device_id_type=MESH,
        )

    def along(a, s, line, slot, target):
        return pltpu.make_async_remote_copy(
            src_ref=loaded[a].at[2 * line + y, rows_of(a, s)],
            dst_ref=line_in[a].at[slot, rows_of(a, s)],
            send_sem=line_send.at[a, line, s],
            recv_sem=line_recv.at[a, slot, s],
            device_id={"dp": target},
            device_id_type=MESH,
        )

    def to_right(a, s, line):
        return along(a, s, line, line, me + 4)

    def to_left(a, s, line):
        return along(a, s, line, jnp.where(line == z - 1, depth, line), me - 4)

    def from_right(a, s, line):
        return along(a, s, line, jnp.where(line == z, depth, line), me)

    order = [turn(k) for k in range(depth)]
    units = [(a, s) for a in range(arrays) for s in range(parts[a])]
    for pair in (1 - y, y):
        for line in order:
            for a, s in units:
                to_core(a, s, line, pair).start()
                load(a, s, line, pair).start()

    for line in order:
        for a, s in units:
            slot = 2 * line + 1 - y
            rows = rows_of(a, s)
            load(a, s, line, 1 - y).wait()
            to_core(a, s, line, 1 - y).wait_recv()
            loaded[a][slot, rows] = loaded[a][slot, rows] + core_in[a][slot, rows]
            to_pair(a, s, line).start()

    def own_sum(a, s, line):
        slot = 2 * line + y
        rows = rows_of(a, s)
        load(a, s, line, y).wait()
        to_core(a, s, line, y).wait_recv()
        to_pair(a, s, line).wait_recv()
        part = loaded[a][slot, rows].astype(jnp.float32)
        part += core_in[a][slot, rows].astype(jnp.float32)
        held[a][...] = part + pair_in[a][line, rows].astype(jnp.float32)

    def add_line(a, s, slot):
        along(a, s, z, slot, me).wait_recv()
        held[a][...] += line_in[a][slot, rows_of(a, s)].astype(jnp.float32)

    for line in order:
        for a, s in units:

            @pl.when(line != z)
            def _(a=a, s=s, line=line):
                own_sum(a, s, line)

                @pl.when(((line > z) & (z > 0)) | ((line < z) & (z < depth - 1)))
                def _():
                    add_line(a, s, line)

                loaded[a][2 * line + y, rows_of(a, s)] = held[a][...].astype(loaded[a].dtype)

                @pl.when(line > z)
                def _():
                    to_right(a, s, line).start()

                @pl.when(line < z)
                def _():
                    to_left(a, s, line).start()

    for a, s in units:
        own_sum(a, s, z)

        @pl.when(z > 0)
        def _(a=a, s=s):
            add_line(a, s, z)

        @pl.when(z < depth - 1)
        def _(a=a, s=s):
            add_line(a, s, depth)

        total[a][rows_of(a, s)] = held[a][...]

    for a, s in units:
        for line in range(depth):
            for pair in range(2):
                to_core(a, s, line, pair).wait_send()
            to_pair(a, s, line).wait_send()

            @pl.when(z != line)
            def _():
                to_right(a, s, line).wait_send()


def scatter_rows(count, ident, *arrays):
    if count != LINE_DEVICES:
        return [
            lax.psum_scatter(
                item.astype(jnp.float32), "dp", scatter_dimension=0, tiled=True
            )
            for item in arrays
        ]
    depth = count // 4
    number = len(arrays)
    blocks = [
        item.reshape(count, item.shape[0] // count, item.shape[1]) for item in arrays
    ]
    parts = [2 if item.shape[1] % 32 == 0 and item.shape[1] > 32 else 1 for item in blocks]
    most = max(parts)

    def room(slots):
        return [pltpu.VMEM((slots,) + item.shape[1:], item.dtype) for item in blocks]

    def sems(slots):
        return pltpu.SemaphoreType.DMA((number, slots, most))

    return pl.pallas_call(
        functools.partial(scatter_body, count, parts, number),
        out_shape=[jax.ShapeDtypeStruct(item.shape[1:], jnp.float32) for item in blocks],
        in_specs=[pl.BlockSpec(memory_space=pl.ANY)] * number,
        out_specs=[pl.BlockSpec(memory_space=pltpu.VMEM)] * number,
        scratch_shapes=[
            pltpu.VMEM((item.shape[1] // part, item.shape[2]), jnp.float32)
            for item, part in zip(blocks, parts)
        ]
        + room(2 * depth)
        + room(2 * depth)
        + room(depth)
        + room(depth + 1)
        + [
            sems(2 * depth),
            sems(2 * depth),
            sems(2 * depth),
            sems(depth),
            sems(depth),
            sems(depth),
            sems(depth + 1),
        ],
        compiler_params=pltpu.CompilerParams(
            collective_id=ident, has_side_effects=True, vmem_limit_bytes=VMEM_LIMIT
        ),
        name="scatter_rows",
    )(*blocks)


def swap_loops(values):
    if lax.axis_size("loop") == 1:
        return values
    return lax.ppermute(values, "loop", [(0, 1), (1, 0)])


def both_loops(values):
    if lax.axis_size("loop") != 2:
        return lax.psum(values.astype(jnp.float32), "loop")
    return values.astype(jnp.float32) + swap_loops(values).astype(jnp.float32)


def per_device(
    layer_input_stream,
    layer_output_gradient,
    attention_in_weight,
    attention_out_weight,
    feedforward_weight,
    layer_norm_gains,
    adapter_first_factors,
    adapter_second_factors,
    adapter_hidden_factors,
    group_sequence_lengths,
    token_per_row,
    token_exit_depth,
):
    current_loop = lax.axis_index("loop")
    dp_index = lax.axis_index("dp")
    loop_count = lax.axis_size("loop")
    count = lax.axis_size("dp")
    local_rows = layer_input_stream.shape[1]
    ffn_rows = feedforward_weight.shape[0]
    weight_rows = attention_in_weight.shape[0]
    low = jnp.bfloat16
    rank = ADAPTER_RANK
    scale = HEAD_SIZE ** (-0.5)
    key_at = QUERY_WIDTH
    value_at = QUERY_WIDTH + HEAD_SIZE
    down_at = PROJECTED_WIDTH + MODEL_WIDTH
    live_all, seq_all, order_all, pos_all = token_facts(token_per_row[0], group_sequence_lengths[0])
    first_row = dp_index * local_rows

    def own_slice(values):
        return lax.dynamic_slice_in_dim(values, first_row, local_rows, 0)

    live_own = own_slice(live_all)
    seq_own = own_slice(seq_all)
    order_own = own_slice(order_all)
    pos_own = own_slice(pos_all)
    active_mask = (live_own & (token_exit_depth[0] > current_loop)).astype(jnp.float32)[:, None]
    residual_stream = layer_input_stream[0].astype(jnp.float32)
    grad_out = layer_output_gradient[0].astype(jnp.float32)
    adapter_first = adapter_first_factors[0]
    adapter_second = adapter_second_factors[0]
    ffn_own = lax.dynamic_slice_in_dim(adapter_hidden_factors[0], dp_index * ffn_rows, ffn_rows, 0)
    first_own = lax.dynamic_slice_in_dim(adapter_first, dp_index * weight_rows, weight_rows, 0)
    second_query = adapter_second[:, :key_at]
    second_key = adapter_second[:, key_at:value_at]
    second_value = adapter_second[:, value_at:PROJECTED_WIDTH]
    second_output = adapter_second[:, PROJECTED_WIDTH:down_at]
    second_down = adapter_second[:, down_at:]

    in_own = (
        attention_in_weight.astype(jnp.float32)
        + jnp.concatenate(
            [
                matrix_product(first_own[:, :rank], second_query),
                matrix_product(first_own[:, rank : 2 * rank], second_key),
                matrix_product(first_own[:, 2 * rank : 3 * rank], second_value),
            ],
            axis=1,
        )
    ).astype(low)
    out_own = (
        attention_out_weight.astype(jnp.float32)
        + matrix_product(first_own[:, 3 * rank : 4 * rank], second_output)
    ).astype(low)
    down_factor = ffn_own[:, :rank]
    gate_factor = ffn_own[:, rank : 2 * rank]
    up_factor = ffn_own[:, 2 * rank :]
    first_gate = adapter_first[:, 4 * rank : 5 * rank]
    first_up = adapter_first[:, 5 * rank :]
    gate_weight = (
        feedforward_weight[:, 0, :].astype(jnp.float32) + outer_columns(gate_factor, first_gate)
    ).astype(low)
    up_weight = (
        feedforward_weight[:, 1, :].astype(jnp.float32) + outer_columns(up_factor, first_up)
    ).astype(low)
    down_weight = (
        feedforward_weight[:, 2, :].astype(jnp.float32) + matrix_product(down_factor, second_down)
    ).astype(low)

    feedforward_gradient = (active_mask * grad_out).astype(low)
    normed_input = norm_rows(residual_stream, layer_norm_gains[0]).astype(low)
    input_weight, output_weight, grad_ffn_all = gather_rows(
        count, 1, in_own, out_own, feedforward_gradient
    )
    query_key_value_linear = matrix_product(normed_input, input_weight)
    queries = rotate(
        query_key_value_linear[:, :QUERY_WIDTH].reshape(local_rows, HEADS, HEAD_SIZE), pos_own
    ).astype(low)
    key_rot = rotate(
        query_key_value_linear[:, key_at:value_at].reshape(local_rows, 1, HEAD_SIZE), pos_own
    )[:, 0]
    kv_send = jnp.concatenate([key_rot, query_key_value_linear[:, value_at:]], axis=1).astype(low)
    (kv_all,) = gather_rows(count, 2, kv_send)
    keys = kv_all[:, :HEAD_SIZE]
    values = kv_all[:, HEAD_SIZE:]
    key_total = kv_all.shape[0]
    allowed = ((seq_own[:, None] == seq_all[None, :]) & (order_all[None, :] <= order_own[:, None]))[
        :, None, :
    ]
    query_rows = queries.reshape(local_rows * HEADS, HEAD_SIZE)

    def score_rows():
        raw_scores = (outer_columns(query_rows, keys) * scale).reshape(local_rows, HEADS, key_total)
        return jnp.where(allowed, raw_scores, FLOOR_SCORE)

    scores = score_rows()
    top_score = jnp.max(scores, axis=-1, keepdims=True)
    expo = jnp.exp(scores - top_score)
    mass = jnp.sum(expo, axis=-1, keepdims=True)
    prob_low = (expo / mass).astype(low)
    attended_rows = (
        matrix_product(prob_low.reshape(local_rows * HEADS, key_total), values)
        .reshape(local_rows, QUERY_WIDTH)
        .astype(low)
    )
    branch_output = matrix_product(attended_rows, output_weight)
    middle_state = residual_stream + active_mask * branch_output
    second_normed_input = norm_rows(middle_state, layer_norm_gains[1]).astype(low)
    (normed_all,) = gather_rows(count, 3, second_normed_input)

    gate_own = outer_columns(normed_all, gate_weight)
    up_own = outer_columns(normed_all, up_weight)
    hidden_unit_gradient = outer_columns(grad_ffn_all, down_weight)
    units_own = geglu(gate_own, up_own).astype(low)
    grad_gate_own, grad_up_own = jax.vjp(geglu, gate_own, up_own)[1](hidden_unit_gradient)
    grad_gate_own = grad_gate_own.astype(low)
    grad_up_own = grad_up_own.astype(low)
    gate_grad = inner_rows(grad_gate_own, normed_all).astype(low)
    up_grad = inner_rows(grad_up_own, normed_all).astype(low)
    down_grad = inner_rows(units_own, grad_ffn_all).astype(low)
    gate_other, up_other, down_other = (
        swap_loops(gate_grad),
        swap_loops(up_grad),
        swap_loops(down_grad),
    )
    ffn_terms = matrix_product(units_own, down_weight).astype(low)
    input_terms = (
        matrix_product(grad_gate_own, gate_weight) + matrix_product(grad_up_own, up_weight)
    ).astype(low)
    ffn_sum, second_normed_gradient = scatter_rows(count, 4, ffn_terms, input_terms)
    complete_output = middle_state + active_mask * ffn_sum
    confidence = root_mean(residual_stream) / (
        root_mean(residual_stream) + root_mean(complete_output - residual_stream)
    )
    conf_sum = jnp.sum(jnp.where(live_own, confidence, 0.0))
    depth_hits = (
        (token_exit_depth[0][:, None] == jnp.arange(loop_count + 1, dtype=jnp.int32)[None, :])
        & live_own[:, None]
    ).astype(jnp.float32)
    stats = jnp.concatenate([conf_sum[None], jnp.sum(depth_hits, axis=0)])

    adapter_hidden_gradient = jnp.concatenate(
        [
            outer_columns(down_grad, second_down),
            matrix_product(gate_grad, first_gate),
            matrix_product(up_grad, first_up),
        ],
        axis=1,
    )
    first_terms = jnp.concatenate(
        [inner_rows(gate_grad, gate_factor), inner_rows(up_grad, up_factor)], axis=1
    ).astype(low)
    grad_middle_part, grad_gain_two = jax.vjp(norm_rows, middle_state, layer_norm_gains[1])[1](
        second_normed_gradient
    )
    grad_middle = grad_out + grad_middle_part
    branch_gradient = (active_mask * grad_middle).astype(low)
    grad_attended = outer_columns(branch_gradient, output_weight).astype(low)
    grad_att_rows = grad_attended.reshape(local_rows * HEADS, HEAD_SIZE)
    prob = jnp.exp(score_rows() - top_score) / mass
    grad_prob = outer_columns(grad_att_rows, values).reshape(local_rows, HEADS, key_total)
    centre = jnp.sum(prob * grad_prob, axis=-1, keepdims=True)
    grad_scores = (
        (prob * (grad_prob - centre)).astype(low).reshape(local_rows * HEADS, key_total)
    )
    prob_again = prob.astype(low).reshape(local_rows * HEADS, key_total)
    kv_terms = jnp.concatenate(
        [inner_rows(grad_scores, query_rows) * scale, inner_rows(prob_again, grad_att_rows)], axis=1
    ).astype(low)
    grad_kv, first_grad_hidden = scatter_rows(count, 5, kv_terms, first_terms)
    grad_queries = (matrix_product(grad_scores, keys) * scale).reshape(local_rows, HEADS, HEAD_SIZE)
    query_linear_gradient = (
        rotate_back(grad_queries, pos_own).reshape(local_rows, QUERY_WIDTH).astype(low)
    )
    key_linear_gradient = rotate_back(grad_kv[:, None, :HEAD_SIZE], pos_own)[:, 0].astype(low)
    value_linear_gradient = grad_kv[:, HEAD_SIZE:].astype(low)
    query_key_value_gradient = jnp.concatenate(
        [query_linear_gradient, key_linear_gradient, value_linear_gradient], axis=1
    )
    normed_gradient = outer_columns(query_key_value_gradient, input_weight)
    grad_resid_part, grad_gain_one = jax.vjp(norm_rows, residual_stream, layer_norm_gains[0])[1](
        normed_gradient
    )
    hidden_grad = grad_middle + grad_resid_part

    lowrank_projection = matrix_product(normed_input, adapter_first[:, : 3 * rank]).astype(low)
    output_projection = matrix_product(
        attended_rows, adapter_first[:, 3 * rank : 4 * rank]
    ).astype(low)
    second_terms = jnp.concatenate(
        [
            inner_rows(query_linear_gradient, lowrank_projection[:, :rank]),
            inner_rows(key_linear_gradient, lowrank_projection[:, rank : 2 * rank]),
            inner_rows(value_linear_gradient, lowrank_projection[:, 2 * rank :]),
            inner_rows(branch_gradient, output_projection),
            inner_rows(down_grad, down_factor),
        ],
        axis=0,
    ).astype(low)
    in_terms = inner_rows(normed_input, query_key_value_gradient).astype(low)
    out_terms = inner_rows(attended_rows, branch_gradient).astype(low)
    width_own = MODEL_WIDTH // count
    gain_rows = jnp.stack([grad_gain_one, grad_gain_two]).reshape(2, count, width_own)
    small = jnp.zeros((count, 8, 128), jnp.float32)
    small = small.at[:, :2, :width_own].set(jnp.swapaxes(gain_rows, 0, 1))
    small = small.at[:, 2, : loop_count + 2].set(stats[None])
    in_portion, out_portion, second_grad, small_sum = scatter_rows(
        count, 6, in_terms, out_terms, second_terms, small.reshape(count * 8, 128)
    )
    in_low = in_portion.astype(low)
    out_low = out_portion.astype(low)
    adapter_first_gradient = jnp.concatenate(
        [
            outer_columns(in_low[:, :key_at], second_query),
            outer_columns(in_low[:, key_at:value_at], second_key),
            outer_columns(in_low[:, value_at:], second_value),
            outer_columns(out_low, second_output),
            first_grad_hidden,
        ],
        axis=1,
    )
    small_total = both_loops(small_sum)
    sum_gains = small_total[:2, :width_own]
    depth_total = small_total[2, 1 : loop_count + 2]
    mean_confidence = small_total[2, 0] / jnp.sum(depth_total)
    exit_counts = depth_total.astype(jnp.int32)
    sum_mlp = jnp.stack(
        [
            gate_grad.astype(jnp.float32) + gate_other.astype(jnp.float32),
            up_grad.astype(jnp.float32) + up_other.astype(jnp.float32),
            down_grad.astype(jnp.float32) + down_other.astype(jnp.float32),
        ],
        axis=1,
    )
    return (
        complete_output.astype(low)[None],
        hidden_grad[None],
        both_loops(in_low),
        both_loops(out_low),
        sum_mlp,
        sum_gains,
        adapter_first_gradient[None],
        jnp.swapaxes(second_grad, 0, 1)[None],
        adapter_hidden_gradient[None],
        exit_counts,
        mean_confidence,
    )


def solution(mesh):
    return jax.shard_map(
        per_device,
        mesh=mesh,
        in_specs=(
            P("loop", "dp", None),
            P("loop", "dp", None),
            P("dp", None),
            P("dp", None),
            P("dp", None, None),
            P(),
            P("loop", None, None),
            P("loop", None, None),
            P("loop", None, None),
            P("loop", None),
            P("loop", None),
            P("loop", "dp"),
        ),
        out_specs=(
            P("loop", "dp", None),
            P("loop", "dp", None),
            P("dp", None),
            P("dp", None),
            P("dp", None, None),
            P(None, "dp"),
            P("loop", "dp", None),
            P("loop", None, "dp"),
            P("loop", "dp", None),
            P(),
            P(),
        ),
        check_vma=False,
    )
```

time: 2130 us -> 885 us (0.42)
  waiting for transfers between devices: 1640 us -> 5.02 us
  Pallas kernels: 0 us -> 501 us
  local copies, waits for them, and re-layouts: 75.8 us -> 29.1 us
  blocking collectives: 45.1 us -> 0 us
  matrix products: 282 us -> 252 us
    reduce_scatter x8 -> x0, waiting for transfers between devices: 906 us -> none  [the longest x1 213 us: per_device(): lax.psum_scatter(grad_w_in, 'dp', scatter_dimension=0, tiled=True)]
    pallas_call x0 -> x6, Pallas kernels: none -> 501 us  [the longest x3 275 us: scatter_rows(): pl.pallas_call(functools.partial(scatter_body, count, parts, number), out...]
    all_gather x7 -> x0, waiting for transfers between devices: 333 us -> none  [the longest x1 78.1 us: per_device(): lax.all_gather(attention_in_weight, 'dp', axis=0, tiled=True)]
    psum x1 -> x0, waiting for transfers between devices: 314 us -> none  [per_device(): lax.psum(mlp_part.astype(jnp.bfloat16), 'loop').astype(jnp.float32)]
    unnamed x20 -> x0, waiting for transfers between devices: 85 us -> none
    psum x2 -> x0, blocking collectives: 45.1 us -> none  [the longest x1 40 us: per_device(): lax.psum((conf_sum, jnp.sum(depth_hits, axis=0)), ('loop', 'dp'))]
    unnamed x166 -> x177, local copies, waits for them, and re-layouts: 50.1 us -> 10.7 us
    another operation x4 -> x8, other arithmetic: 1.93 us -> 33 us  [the longest x4 31.6 us: per_device(): jnp.stack([gate_grad.astype(jnp.float32) + gate_other.astype(jnp.float32)...]
  transfers between devices with their start and end apart: 18 -> 6, of which waited for: 17 -> 1; matrix products, arithmetic and copies ran while one was open for 15% -> 23% of each run, Pallas kernels for 0% -> 31%
where the time goes in v1:
time: 885 us; the launch traced here: 876 us
  Pallas kernels  501 us (57%)
  matrix products  252 us (28%)
  other arithmetic  77.7 us (9%)
  local copies, waits for them, and re-layouts  29.1 us (3%)
    pallas_call x3, Pallas kernels, scatter_rows(): pl.pallas_call(functools.partial(scatter_body, count, parts, number), out...  275 us
    pallas_call x3, Pallas kernels, gather_rows(): pl.pallas_call(functools.partial(gather_body, count, parts, number), out_...  226 us
    dot_general x14, matrix products, outer_columns(): lax.dot_general(left, right, (((1,), (1,)), ((), ())), preferred_element_...  102 us
    dot_general x15, matrix products, matrix_product(): return jnp.dot(left, right, preferred_element_type=jnp.float32)  75.2 us
    dot_general x14, matrix products, inner_rows(): lax.dot_general(left, right, (((0,), (0,)), ((), ())), preferred_element_...  74.9 us
    another operation x4, other arithmetic, per_device(): jnp.stack([gate_grad.astype(jnp.float32) + gate_other.astype(jnp.float32)...  31.6 us
  transfers between devices with their start and end apart: 6, of which 1 were waited for; matrix products, arithmetic and copies ran while one was open for 23% of the time, Pallas kernels for 31%

profile of v1, /device:TPU:0, one launch (start us, length us, event | category | flops | bytes accessed | tf_op | source)
XLA Modules:
  0.0 876.2 jit_solution(7058119635912306740)
XLA Ops:
  13.8 154.8 %gather_rows.3 = (bf16[16,128,2560]{2,1,0:T(8,128)(2,1)}, bf16[16,128,2048]{2,1,0:T(8,128)(2,1)}, bf16[16,128,2048]{2,1,0:T(8,128)(2,1)}) custom-call(bf16[128,2560]{1,0:T(8,128)(2,1)} %fusion.38.refs_0_, bf16[128,2048]{1,0:T(8,128)(2,1)} %fusion.26.refs_1_, bf16[128,2048]{1,0:T(8,128)(2,1)} %fusion.54.refs_2_), custom_call_target="tpu_custom_call" | custom-call | tf_op jit(solution)/shard_map/gather_rows/pallas_call | solution.py:249
  168.6 5.5 fusion.81
  176.2 6.4 fusion.8
  182.6 5.8 fusion.9
  188.4 5.9 fusion.7
  196.4 20.6 %gather_rows.4 = bf16[16,128,512]{2,1,0:T(8,128)(2,1)} custom-call(bf16[128,512]{1,0:T(8,128)(2,1)} %pad_maximum_fusion.6.refs_0_), custom_call_target="tpu_custom_call" | custom-call | tf_op jit(solution)/shard_map/gather_rows/pallas_call | solution.py:249
  224.5 5.0 multiply_bitcast_fusion
  233.0 5.0 multiply_reduce_fusion.3
  240.0 50.5 %gather_rows.5 = bf16[16,128,2048]{2,1,0:T(8,128)(2,1)} custom-call(bf16[128,2048]{1,0:T(8,128)(2,1)} %multiply_convert_fusion.4.refs_0_), custom_call_target="tpu_custom_call" | custom-call | tf_op jit(solution)/shard_map/gather_rows/pallas_call | solution.py:249
  290.5 14.7 %fusion.150 = f32[2048,1024]{1,0:T(8,128)} fusion(bf16[2048,2048]{1,0:T(8,128)(2,1)} %bitcast.222, bf16[1024,2048]{1,0:T(8,128)(2,1)} %fusion.8), kind=kOutput, calls=%fused_computation.250 | convolution fusion | flops 8589934592 | bytes 20971520 | tf_op jit(solution)/shard_map/dot_general | solution.py:36
  305.3 11.2 %fusion.149 = f32[2048,1024]{1,0:T(8,128)} fusion(bf16[2048,2048]{1,0:T(8,128)(2,1)S(1)} %bitcast.225, bf16[1024,2048]{1,0:T(8,128)(2,1)S(1)} %copy-done.77), kind=kOutput, calls=%fused_computation.249 | convolution fusion | flops 8589934592 | bytes 20971520 | tf_op jit(solution)/shard_map/dot_general | solution.py:36
  316.4 25.9 %multiply_convert_fusion.1 = (bf16[2048,1024]{1,0:T(8,128)(2,1)}, bf16[2048,1024]{1,0:T(8,128)(2,1)}, bf16[2048,1024]{1,0:T(8,128)(2,1)}) fusion(f32[2048,1024]{1,0:T(8,128)} %fusion.149, f32[2048,1024]{1,0:T(8,128)} %fusion.150, bf16[2048,2048]{1,0:T(8,128)(2,1)} %bitcast.278, bf16[1024,2048]{1,0:T(8,128)(2,1)} %fusion.7), kind=kOutput, calls=%fused_computation.27 | convolution fusion | flops 8644460544 | bytes 41943040 | tf_op jit(solution)/shard_map/dot_general | solution.py:36
  342.3 14.2 %convolution_convert_fusion.5 = bf16[1024,2048]{1,0:T(8,128)(2,1)} fusion(bf16[2048,1024]{1,0:T(8,128)(2,1)} %get-tuple-element.98, bf16[2048,2048]{1,0:T(8,128)(2,1)} %bitcast.223), kind=kOutput, calls=%fused_computation.43 | convolution fusion | flops 8592031744 | bytes 16777216 | tf_op jit(solution)/shard_map/dot_general | solution.py:30
  358.0 13.5 %convolution_convert_fusion.4 = bf16[1024,2048]{1,0:T(8,128)(2,1)} fusion(bf16[2048,1024]{1,0:T(8,128)(2,1)S(1)} %copy-done.79, bf16[2048,2048]{1,0:T(8,128)(2,1)} %bitcast.224), kind=kOutput, calls=%fused_computation.42 | convolution fusion | flops 8592031744 | bytes 16777216 | tf_op jit(solution)/shard_map/dot_general | solution.py:30
  372.2 11.0 %convolution_convert_fusion.3 = bf16[1024,2048]{1,0:T(8,128)(2,1)} fusion(bf16[2048,1024]{1,0:T(8,128)(2,1)S(1)} %copy-done.81, bf16[2048,2048]{1,0:T(8,128)(2,1)S(1)} %bitcast.281), kind=kOutput, calls=%fused_computation.41 | convolution fusion | flops 8592031744 | bytes 16777216 | tf_op jit(solution)/shard_map/dot_general | solution.py:30
  384.6 11.8 %fusion.151 = f32[2048,2048]{1,0:T(8,128)} fusion(bf16[2048,1024]{1,0:T(8,128)(2,1)S(1)} %copy-done.82, bf16[1024,2048]{1,0:T(8,128)(2,1)S(1)} %copy-done.78), kind=kOutput, calls=%fused_computation.251 | convolution fusion | flops 8589934592 | bytes 25165824 | tf_op jit(solution)/shard_map/dot_general | solution.py:26
  396.4 11.3 %convolution_convert_fusion.1 = bf16[2048,2048]{1,0:T(8,128)(2,1)} fusion(bf16[2048,1024]{1,0:T(8,128)(2,1)S(1)} %copy-done.81, bf16[1024,2048]{1,0:T(8,128)(2,1)S(1)} %copy-done.76), kind=kOutput, calls=%fused_computation.34 | convolution fusion | flops 8594128896 | bytes 16777216 | tf_op jit(solution)/shard_map/dot_general | solution.py:26
  417.1 13.9 %add_convert_fusion = bf16[2048,2048]{1,0:T(8,128)(2,1)} fusion(f32[2048,2048]{1,0:T(8,128)} %fusion.151, bf16[2048,1024]{1,0:T(8,128)(2,1)S(1)} %copy-done.80, bf16[1024,2048]{1,0:T(8,128)(2,1)S(1)} %copy-done.75), kind=kOutput, calls=%fused_computation.1 | convolution fusion | flops 8598323200 | bytes 33554432 | tf_op jit(solution)/shard_map/dot_general | solution.py:26
  431.0 103.8 %scatter_rows.3 = (f32[128,2048]{1,0:T(8,128)}, f32[128,2048]{1,0:T(8,128)}) custom-call(bf16[16,128,2048]{2,1,0:T(8,128)(2,1)} %bitcast.226, bf16[16,128,2048]{2,1,0:T(8,128)(2,1)} %bitcast.227), custom_call_target="tpu_custom_call" | custom-call | tf_op jit(solution)/shard_map/scatter_rows/pallas_call | solution.py:442
  539.6 6.3 convolution_convert_fusion.11
  546.7 10.8 %multiply_reduce_fusion = (f32[128,8]{0,1:T(8,128)S(1)}, f32[128,8,2048]{2,0,1:T(8,128)S(1)}) fusion(f32[128,8]{0,1:T(8,128)} %copy.58, f32[128,8]{0,1:T(8,128)S(1)} %copy.57, f32[128,8,2048]{2,1,0:T(8,128)} %get-tuple-element.100, pred[128,2048]{1,0:T(8,128)(4,1)S(1)} %copy-done.18, bf16[2048,512]{1,0:T(8,128)(2,1)} %bitcast.236, ...), kind=kOutput, calls=%fused_computation.26 | convolution fusion | flops 1084226560 | bytes 18624512 | tf_op jit(solution)/shard_map/dot_general | solution.py:36
  557.5 7.6 multiply_convert_fusion
  572.0 6.4 copy.70
  584.4 33.1 %scatter_rows.4 = (f32[128,512]{1,0:T(8,128)}, f32[128,512]{1,0:T(8,128)}) custom-call(bf16[16,128,512]{2,1,0:T(8,128)(2,1)} %pad_maximum_fusion.1.refs_0_, bf16[16,128,512]{2,1,0:T(8,128)(2,1)} %pad_maximum_fusion.2.refs_1_), custom_call_target="tpu_custom_call" | custom-call | tf_op jit(solution)/shard_map/scatter_rows/pallas_call | solution.py:442
  622.6 5.7 convolution_convert_fusion.2
  632.1 8.8 %fusion.47 = (f32[2048]{0:T(1024)S(1)}, f32[128]{0:T(128)S(1)}, f32[128,2048]{1,0:T(8,128)}) fusion(bf16[1,128,2048]{2,1,0:T(8,128)(2,1)S(1)} %copy-done.3, f32[128]{0:T(128)S(1)} %copy-done.53, f32[2048]{0:T(1024)S(1)} %bitcast.254, bf16[2048,2560]{1,0:T(8,128)(2,1)} %bitcast.220, bf16[128,256]{0,1:T(8,128)(2,1)S(1)} %copy.67, ...), kind=kOutput, calls=%fused_computation.97 | convolution fusion | flops 1345976192 | bytes 12731392 | tf_op jit(solution)/shard_map/dot_general | solution.py:36
  640.9 6.6 convolution_convert_fusion
  661.2 138.5 %scatter_rows.5 = (f32[128,2560]{1,0:T(8,128)}, f32[128,2048]{1,0:T(8,128)}, f32[416,256]{1,0:T(8,128)}, f32[8,128]{1,0:T(8,128)}) custom-call(bf16[16,128,2560]{2,1,0:T(8,128)(2,1)} %bitcast.213, bf16[16,128,2048]{2,1,0:T(8,128)(2,1)} %bitcast.216, bf16[16,416,256]{2,1,0:T(8,128)(2,1)} %bitcast.51.refs_2_, f32[16,8,128]{2,1,0:T(8,128)} %copy-done.44), custom_call_target="tpu_custom_call" | custom-call | tf_op jit(solution)/shard_map/scatter_rows/pallas_call | solution.py:442
  842.4 5.4 add_bitcast_fusion.2
  847.8 5.4 add_bitcast_fusion.1
  853.2 8.7 add_bitcast_fusion
  861.9 12.1 %pad_maximum_fusion = f32[1024,3,2048]{2,0,1:T(8,128)} fusion(f32[1024,1,2048]{2,0,1:T(8,128)} %add_bitcast_fusion, f32[1024,1,2048]{2,0,1:T(8,128)S(1)} %add_bitcast_fusion.1, f32[1024,1,2048]{2,0,1:T(8,128)S(1)} %add_bitcast_fusion.2), kind=kLoop, calls=%fused_computation | loop fusion | flops 12582912 | bytes 50331648 | tf_op jit(solution)/shard_map/stack | solution.py:720
  (286 shorter events, 125.4 us)
Async XLA Ops:
  5.5 189.8 %copy-start.63 = (f32[128]{0:T(128)}, f32[128]{0:T(128)S(1)}, u32[]{:S(2)}) copy-start(f32[128]{0:T(128)S(1)} %multiply_power_fusion) | copy-start | bytes 1540
  11.0 163.1 %copy-start.39 = (f32[1,2048]{1,0:T(1,128)}, f32[1,2048]{1,0:T(1,128)S(1)}, u32[]{:S(2)}) copy-start(f32[1,2048]{1,0:T(1,128)S(1)} %get-tuple-element.116) | copy-start | bytes 24580
  11.1 227.1 %copy-start.46 = (f32[1,2048]{1,0:T(1,128)}, f32[1,2048]{1,0:T(1,128)S(1)}, u32[]{:S(2)}) copy-start(f32[1,2048]{1,0:T(1,128)S(1)} %get-tuple-element.115) | copy-start | bytes 24580
  11.3 162.9 %copy-start.52 = (f32[128]{0:T(128)}, f32[128]{0:T(128)S(1)}, u32[]{:S(2)}) copy-start(f32[128]{0:T(128)S(1)} %fusion.144) | copy-start | bytes 1540
  11.8 183.0 %copy-start.58 = (pred[128]{0:T(512)(128)(4,1)}, pred[128]{0:T(512)(128)(4,1)S(1)}, u32[]{:S(2)}) copy-start(pred[128]{0:T(512)(128)(4,1)S(1)} %get-tuple-element.96) | copy-start | bytes 388
  11.9 221.2 %copy-start.54 = (f32[128]{0:T(128)}, f32[128]{0:T(128)S(1)}, u32[]{:S(2)}) copy-start(f32[128]{0:T(128)S(1)} %and_convert_fusion) | copy-start | bytes 1540
  195.1 22.0 %copy-start.56 = (f32[128]{0:T(128)}, f32[128]{0:T(128)S(1)}, u32[]{:S(2)}) copy-start(f32[128]{0:T(128)S(1)} %get-tuple-element.118) | copy-start | bytes 1540
  195.4 26.2 %copy-start.35 = (f32[128,128]{1,0:T(8,128)}, f32[128,128]{1,0:T(8,128)S(1)}, u32[]{:S(2)}) copy-start(f32[128,128]{1,0:T(8,128)S(1)} %get-tuple-element.123) | copy-start | bytes 196612
  195.4 26.2 %copy-start.37 = (f32[128,128]{1,0:T(8,128)}, f32[128,128]{1,0:T(8,128)S(1)}, u32[]{:S(2)}) copy-start(f32[128,128]{1,0:T(8,128)S(1)} %get-tuple-element.124) | copy-start | bytes 196612
  238.1 52.4 %copy-start.71 = (f32[128]{0:T(128)}, f32[128]{0:T(128)S(1)}, u32[]{:S(2)}) copy-start(f32[128]{0:T(128)S(1)} %get-tuple-element.129) | copy-start | bytes 1540
  238.1 52.4 %copy-start.60 = (f32[128]{0:T(128)}, f32[128]{0:T(128)S(1)}, u32[]{:S(2)}) copy-start(f32[128]{0:T(128)S(1)} %fusion.139) | copy-start | bytes 1540
  290.5 14.7 %copy-start.6 = (bf16[16,128,2048]{2,1,0:T(8,128)(2,1)S(1)}, bf16[16,128,2048]{2,1,0:T(8,128)(2,1)}, u32[]{:S(2)}) copy-start(bf16[16,128,2048]{2,1,0:T(8,128)(2,1)} %gather_rows.5) | copy-start | bytes 25165828
  290.5 14.7 %copy-start.77 = (bf16[1024,2048]{1,0:T(8,128)(2,1)S(1)}, bf16[1024,2048]{1,0:T(8,128)(2,1)}, u32[]{:S(2)}) copy-start(bf16[1024,2048]{1,0:T(8,128)(2,1)} %fusion.9) | copy-start | bytes 12582916
  342.3 15.7 %copy-start.79 = (bf16[2048,1024]{1,0:T(8,128)(2,1)S(1)}, bf16[2048,1024]{1,0:T(8,128)(2,1)}, u32[]{:S(2)}) copy-start(bf16[2048,1024]{1,0:T(8,128)(2,1)} %get-tuple-element.97) | copy-start | bytes 12582916
  342.3 29.9 %slice-start.3 = ((s8[8388608]{0:T(1024)(128)(4,1)}), s8[4194304]{0:T(1024)(128)(4,1)S(1)}, s32[]{:S(2)}) async-start(s8[8388608]{0:T(1024)(128)(4,1)} %bitcast.279), calls=%async_computation.3 | async-start | bytes 8388608
  356.5 15.7 %slice-start.4 = ((s8[8388608]{0:T(1024)(128)(4,1)}), s8[4194304]{0:T(1024)(128)(4,1)S(1)}, s32[]{:S(2)}) async-start(s8[8388608]{0:T(1024)(128)(4,1)} %bitcast.279), calls=%async_computation.4 | async-start | bytes 8388608
  356.5 485.9 %collective-permute-start.2 = (bf16[1024,2048]{1,0:T(8,128)(2,1)}, bf16[1024,2048]{1,0:T(8,128)(2,1)}, u32[]{:S(2)}, u32[]{:S(2)}) collective-permute-start(bf16[1024,2048]{1,0:T(8,128)(2,1)} %convolution_convert_fusion.5), channel_id=1, source_target_pairs={{0,16},{16,0},{1,17},{17,1},{2,18},{18,2},{3,19},{19,3},{4,20},{20... | collective-permute-start | bytes 12582920 | tf_op jit(solution)/shard_map/ppermute | solution.py:474
  371.4 476.4 %collective-permute-start.3 = (bf16[1024,2048]{1,0:T(8,128)(2,1)}, bf16[1024,2048]{1,0:T(8,128)(2,1)}, u32[]{:S(2)}, u32[]{:S(2)}) collective-permute-start(bf16[1024,2048]{1,0:T(8,128)(2,1)} %convolution_convert_fusion.4), channel_id=1, source_target_pairs={{0,16},{16,0},{1,17},{17,1},{2,18},{18,2},{3,19},{19,3},{4,20},{20... | collective-permute-start | bytes 12582920 | tf_op jit(solution)/shard_map/ppermute | solution.py:474
  383.3 469.9 %collective-permute-start.4 = (bf16[1024,2048]{1,0:T(8,128)(2,1)}, bf16[1024,2048]{1,0:T(8,128)(2,1)}, u32[]{:S(2)}, u32[]{:S(2)}) collective-permute-start(bf16[1024,2048]{1,0:T(8,128)(2,1)} %convolution_convert_fusion.3), channel_id=1, source_target_pairs={{0,16},{16,0},{1,17},{17,1},{2,18},{18,2},{3,19},{19,3},{4,20},{20... | collective-permute-start | bytes 12582920 | tf_op jit(solution)/shard_map/ppermute | solution.py:474
  431.0 103.9 %copy-start.1 = (f32[128,2048]{1,0:T(8,128)S(1)}, f32[128,2048]{1,0:T(8,128)}, u32[]{:S(2)}) copy-start(f32[128,2048]{1,0:T(8,128)} %copy-done) | copy-start | bytes 3145732
  431.0 103.9 %copy-start.3 = (bf16[1,128,2048]{2,1,0:T(8,128)(2,1)S(1)}, bf16[1,128,2048]{2,1,0:T(8,128)(2,1)}, u32[]{:S(2)}) copy-start(bf16[1,128,2048]{2,1,0:T(8,128)(2,1)} %param.16) | copy-start | bytes 1572868
  431.0 103.9 %copy-start.47 = (f32[1,2048]{1,0:T(1,128)S(1)}, f32[1,2048]{1,0:T(1,128)}, u32[]{:S(2)}) copy-start(f32[1,2048]{1,0:T(1,128)} %copy-done.46) | copy-start | bytes 24580
  431.0 103.9 %copy-start.55 = (f32[128]{0:T(128)S(1)}, f32[128]{0:T(128)}, u32[]{:S(2)}) copy-start(f32[128]{0:T(128)} %copy-done.54) | copy-start | bytes 1540
  431.0 103.9 %copy-start.61 = (f32[128]{0:T(128)S(1)}, f32[128]{0:T(128)}, u32[]{:S(2)}) copy-start(f32[128]{0:T(128)} %copy-done.60) | copy-start | bytes 1540
  582.9 36.4 %copy-start.40 = (f32[1,2048]{1,0:T(1,128)S(1)}, f32[1,2048]{1,0:T(1,128)}, u32[]{:S(2)}) copy-start(f32[1,2048]{1,0:T(1,128)} %copy-done.39) | copy-start | bytes 24580
  582.9 36.4 %copy-start.53 = (f32[128]{0:T(128)S(1)}, f32[128]{0:T(128)}, u32[]{:S(2)}) copy-start(f32[128]{0:T(128)} %copy-done.52) | copy-start | bytes 1540
  584.4 38.1 %copy-start.8 = (bf16[128,2048]{1,0:T(8,128)(2,1)S(1)}, bf16[128,2048]{1,0:T(8,128)(2,1)}, u32[]{:S(2)}) copy-start(bf16[128,2048]{1,0:T(8,128)(2,1)} %copy-done.7) | copy-start | bytes 1572868
  584.4 38.1 %copy-start.13 = (bf16[128,2048]{1,0:T(8,128)(2,1)S(1)}, bf16[128,2048]{1,0:T(8,128)(2,1)}, u32[]{:S(2)}) copy-start(bf16[128,2048]{1,0:T(8,128)(2,1)} %copy-done.12) | copy-start | bytes 1572868
  799.7 24.1 %collective-permute-start.5 = (f32[8,128]{1,0:T(8,128)}, f32[8,128]{1,0:T(8,128)S(1)}, u32[]{:S(2)}, u32[]{:S(2)}) collective-permute-start(f32[8,128]{1,0:T(8,128)} %get-tuple-element.54), channel_id=1, source_target_pairs={{0,16},{16,0},{1,17},{17,1},{2,18},{18,2},{3,19},{19,3},{4,20},{20... | collective-permute-start | bytes 12296 | tf_op jit(solution)/shard_map/ppermute | solution.py:474
  802.6 30.4 %collective-permute-start.1 = (bf16[128,2048]{1,0:T(8,128)(2,1)}, bf16[128,2048]{1,0:T(8,128)(2,1)}, u32[]{:S(2)}, u32[]{:S(2)}) collective-permute-start(bf16[128,2048]{1,0:T(8,128)(2,1)} %convert_element_type.264), channel_id=1, source_target_pairs={{0,16},{16,0},{1,17},{17,1},{2,18},{18,2},{3,19},{19,3},{4,20},{20... | collective-permute-start | bytes 1572872 | tf_op jit(solution)/shard_map/ppermute | solution.py:474
  823.8 16.4 %collective-permute-start = (bf16[128,2560]{1,0:T(8,128)(2,1)S(1)}, bf16[128,2560]{1,0:T(8,128)(2,1)}, u32[]{:S(2)}, u32[]{:S(2)}) collective-permute-start(bf16[128,2560]{1,0:T(8,128)(2,1)S(1)} %convert_element_type.261), channel_id=1, source_target_pairs={{0,16},{16,0},{1,17},{17,1},{2,18},{18,2},{3,19},{19,3},{4,20},{20... | collective-permute-start | bytes 1966088 | tf_op jit(solution)/shard_map/ppermute | solution.py:474
  825.5 14.7 %copy-start.10 = (f32[128,2560]{1,0:T(8,128)S(1)}, f32[128,2560]{1,0:T(8,128)}, u32[]{:S(2)}) copy-start(f32[128,2560]{1,0:T(8,128)} %get-tuple-element.52) | copy-start | bytes 3932164
  (62 other events, 391.8 us)

commit v2 on v1

--- a/solution.py
+++ b/solution.py
@@ -120,23 +120,29 @@
     pl.semaphore_wait(barrier, ends)
 
 
-def gather_body(count, parts, arrays, *refs):
-    own = refs[:arrays]
-    full = refs[arrays : 2 * arrays]
-    keep, recv, send_core, send_pair, send_right, send_left = refs[2 * arrays :]
+def contract(left, right, left_axis, right_axis):
+    return lax.dot_general(
+        left,
+        right,
+        (((left_axis,), (right_axis,)), ((), ())),
+        preferred_element_type=jnp.float32,
+    )
+
+
+def gather_plan(count, parts, own, full, keep, recv, send_core, send_pair, send_right, send_left):
+    arrays = len(own)
     me, depth, z, y, c = place(count)
-    greet(count)
-
-    def spans(a):
-        rows = own[a].shape[0]
-        step = rows // parts
-        return [(s, pl.ds(s * step, step)) for s in range(parts)]
-
-    def copy(a, block, span, target, sem, first=False):
-        s, rows = span
-        source = own[a].at[rows] if first else full[a].at[block, rows]
+    mate = me + 2 - 4 * y
+
+    def rows_of(a, s):
+        step = own[a].shape[0] // parts
+        return pl.ds(s * step, step)
+
+    def copy(unit, block, target, sem, first=False):
+        a, s = unit
+        rows = rows_of(a, s)
         return pltpu.make_async_remote_copy(
-            src_ref=source,
+            src_ref=own[a].at[rows] if first else full[a].at[block, rows],
             dst_ref=full[a].at[block, rows],
             send_sem=sem,
             recv_sem=recv.at[a, block, s],
@@ -144,131 +150,275 @@
             device_id_type=MESH,
         )
 
-    def to_core(a, block, span, first=False):
-        return copy(a, block, span, me + 1 - 2 * c, send_core.at[a, block // 2, span[0]], first)
-
-    def to_pair(a, block, span, first=False):
-        return copy(a, block, span, me + 2 - 4 * y, send_pair.at[a, block // 4, span[0]], first)
-
-    def to_right(a, block, span, first=False):
-        return copy(a, block, span, me + 4, send_right.at[a, block // 4, span[0]], first)
-
-    def to_left(a, block, span, first=False):
-        return copy(a, block, span, me - 4, send_left.at[a, block // 4, span[0]], first)
-
-    local = [
-        pltpu.make_async_copy(own[a], full[a].at[me], keep.at[a]) for a in range(arrays)
+    def to_core(unit, block, first=False):
+        a, s = unit
+        return copy(unit, block, me + 1 - 2 * c, send_core.at[a, block // 2, s], first)
+
+    def to_pair(unit, block, first=False):
+        a, s = unit
+        return copy(unit, block, mate, send_pair.at[a, block // 4, s], first)
+
+    def to_right(unit, block, first=False):
+        a, s = unit
+        return copy(unit, block, me + 4, send_right.at[a, block // 4, s], first)
+
+    def to_left(unit, block, first=False):
+        a, s = unit
+        return copy(unit, block, me - 4, send_left.at[a, block // 4, s], first)
+
+    local = [pltpu.make_async_copy(own[a], full[a].at[me], keep.at[a]) for a in range(arrays)]
+    units = [(a, s) for a in range(arrays) for s in range(parts)]
+
+    def begin():
+        for unit in units:
+
+            @pl.when(z < depth - 1)
+            def _(unit=unit):
+                to_right(unit, me, True).start()
+
+            @pl.when(z > 0)
+            def _(unit=unit):
+                to_left(unit, me, True).start()
+
+            to_pair(unit, me, True).start()
+            to_core(unit, me, True).start()
+        for item in local:
+            item.start()
+
+    def from_line(k, unit):
+        @pl.when(z - k >= 0)
+        def _():
+            block = me - 4 * k
+            to_right(unit, block).wait_recv()
+
+            @pl.when(z < depth - 1)
+            def _():
+                to_right(unit, block).start()
+
+            to_pair(unit, block).start()
+            to_core(unit, block).start()
+
+        @pl.when(z + k < depth)
+        def _():
+            block = me + 4 * k
+            to_left(unit, block).wait_recv()
+
+            @pl.when(z > 0)
+            def _():
+                to_left(unit, block).start()
+
+            to_pair(unit, block).start()
+            to_core(unit, block).start()
+
+    def pass_on(unit, block):
+        to_pair(unit, block).wait_recv()
+        to_core(unit, block).start()
+
+    def from_pair(k, unit):
+        if k == 0:
+            pass_on(unit, mate)
+            return
+
+        @pl.when(z - k >= 0)
+        def _():
+            pass_on(unit, mate - 4 * k)
+
+        @pl.when(z + k < depth)
+        def _():
+            pass_on(unit, mate + 4 * k)
+
+    def arrive():
+        for unit in units:
+            for j in range(count // 2):
+                to_core(unit, 2 * j + 1 - c).wait_recv()
+        for item in local:
+            item.wait()
+
+    def finish():
+        for unit in units:
+            for j in range(count // 2):
+                to_core(unit, 2 * j + c).wait_send()
+            for j in range(depth):
+                block = 4 * j + 2 * y + c
+                to_pair(unit, block).wait_send()
+
+                @pl.when((z >= j) & (z < depth - 1))
+                def _():
+                    to_right(unit, block).wait_send()
+
+                @pl.when((z <= j) & (z > 0))
+                def _():
+                    to_left(unit, block).wait_send()
+
+    return units, begin, from_line, from_pair, arrive, finish
+
+
+def gather_sems(count, number, parts):
+    depth = count // 4
+    sem = pltpu.SemaphoreType.DMA
+    return [
+        sem((number,)),
+        sem((number, count, parts)),
+        sem((number, count // 2, parts)),
+        sem((number, depth, parts)),
+        sem((number, depth, parts)),
+        sem((number, depth, parts)),
     ]
-    units = [(a, span) for a in range(arrays) for span in spans(a)]
-    for a, span in units:
-
-        @pl.when(z < depth - 1)
-        def _(a=a, span=span):
-            to_right(a, me, span, True).start()
-
-        @pl.when(z > 0)
-        def _(a=a, span=span):
-            to_left(a, me, span, True).start()
-
-        to_pair(a, me, span, True).start()
-        to_core(a, me, span, True).start()
-    for item in local:
-        item.start()
-    mate = me + 2 - 4 * y
+
+
+def gather_body(count, parts, arrays, *refs):
+    depth = count // 4
+    greet(count)
+    units, begin, from_line, from_pair, arrive, finish = gather_plan(
+        count, parts, refs[:arrays], refs[arrays : 2 * arrays], *refs[2 * arrays :]
+    )
+    begin()
     for k in range(1, depth):
-        for a, span in units:
-
-            @pl.when(z - k >= 0)
-            def _(a=a, span=span):
-                block = me - 4 * k
-                to_right(a, block, span).wait_recv()
-
-                @pl.when(z < depth - 1)
-                def _():
-                    to_right(a, block, span).start()
-
-                to_pair(a, block, span).start()
-                to_core(a, block, span).start()
-
-            @pl.when(z + k < depth)
-            def _(a=a, span=span):
-                block = me + 4 * k
-                to_left(a, block, span).wait_recv()
-
-                @pl.when(z > 0)
-                def _():
-                    to_left(a, block, span).start()
-
-                to_pair(a, block, span).start()
-                to_core(a, block, span).start()
-
-    def from_pair(a, block, span):
-        to_pair(a, block, span).wait_recv()
-        to_core(a, block, span).start()
-
-    for a, span in units:
-        from_pair(a, mate, span)
-    for k in range(1, depth):
-        for a, span in units:
-
-            @pl.when(z - k >= 0)
-            def _(a=a, span=span):
-                from_pair(a, mate - 4 * k, span)
-
-            @pl.when(z + k < depth)
-            def _(a=a, span=span):
-                from_pair(a, mate + 4 * k, span)
-
-    for a, span in units:
-        for j in range(count // 2):
-            to_core(a, 2 * j + 1 - c, span).wait_recv()
-    for item in local:
-        item.wait()
-    for a, span in units:
-        for j in range(count // 2):
-            to_core(a, 2 * j + c, span).wait_send()
-        for j in range(depth):
-            block = 4 * j + 2 * y + c
-            to_pair(a, block, span).wait_send()
-
-            @pl.when((z >= j) & (z < depth - 1))
-            def _():
-                to_right(a, block, span).wait_send()
-
-            @pl.when((z <= j) & (z > 0))
-            def _():
-                to_left(a, block, span).wait_send()
+        for unit in units:
+            from_line(k, unit)
+        for unit in units:
+            from_pair(k - 1, unit)
+    for unit in units:
+        from_pair(depth - 1, unit)
+    arrive()
+    finish()
+
+
+def kernel_params(ident):
+    return pltpu.CompilerParams(
+        collective_id=ident, has_side_effects=True, vmem_limit_bytes=VMEM_LIMIT
+    )
 
 
 def gather_rows(count, ident, *arrays, parts=2):
     if count != LINE_DEVICES:
         return [lax.all_gather(item, "dp", axis=0, tiled=True) for item in arrays]
     number = len(arrays)
-    depth = count // 4
-    sem = pltpu.SemaphoreType.DMA
+    anywhere = pl.BlockSpec(memory_space=pl.ANY)
     full = pl.pallas_call(
         functools.partial(gather_body, count, parts, number),
         out_shape=[
             jax.ShapeDtypeStruct((count,) + item.shape, item.dtype) for item in arrays
         ],
-        in_specs=[pl.BlockSpec(memory_space=pl.ANY)] * number,
-        out_specs=[pl.BlockSpec(memory_space=pl.ANY)] * number,
-        scratch_shapes=[
-            sem((number,)),
-            sem((number, count, parts)),
-            sem((number, count // 2, parts)),
-            sem((number, depth, parts)),
-            sem((number, depth, parts)),
-            sem((number, depth, parts)),
-        ],
-        compiler_params=pltpu.CompilerParams(
-            collective_id=ident, has_side_effects=True, vmem_limit_bytes=VMEM_LIMIT
-        ),
+        in_specs=[anywhere] * number,
+        out_specs=[anywhere] * number,
+        scratch_shapes=gather_sems(count, number, parts),
+        compiler_params=kernel_params(ident),
         name="gather_rows",
     )(*arrays)
     return [
         item.reshape((count * item.shape[1],) + item.shape[2:]) for item in full
     ]
+
+
+def opening_body(count, parts, arrays, *refs):
+    own = refs[:arrays]
+    weights, factors, first, second = refs[arrays : arrays + 4]
+    full = refs[arrays + 4 : 2 * arrays + 4]
+    folded = refs[2 * arrays + 4]
+    scratch = refs[2 * arrays + 5 :]
+    bank, factor_bank, first_bank, second_bank, bank_sem, factor_sem, out_sem = scratch[:7]
+    me, depth, z, y, c = place(count)
+    rank = ADAPTER_RANK
+    width, wide = bank.shape[1:]
+    greet(count)
+    units, begin, from_line, from_pair, arrive, finish = gather_plan(
+        count, parts, own, full, *scratch[7:]
+    )
+    begin()
+    fills = [
+        pltpu.make_async_copy(weights.at[i], bank.at[i], bank_sem.at[i]) for i in range(3)
+    ]
+    sources = [
+        pltpu.make_async_copy(
+            factors.at[pl.ds(me * width, width)], factor_bank, factor_sem.at[0]
+        ),
+        pltpu.make_async_copy(
+            first.at[:, pl.ds(4 * rank, 2 * rank)], first_bank, factor_sem.at[1]
+        ),
+        pltpu.make_async_copy(
+            second.at[:, pl.ds(PROJECTED_WIDTH + MODEL_WIDTH, wide)], second_bank, factor_sem.at[2]
+        ),
+    ]
+    for item in sources + fills:
+        item.start()
+
+    def put(i):
+        return pltpu.make_async_copy(bank.at[i], folded.at[i], out_sem.at[i])
+
+    def fold(i):
+        high, tile = 256, 512
+
+        def inner(n, carry):
+            rows = pl.ds(pl.multiple_of((n // (wide // tile)) * high, high), high)
+            cols = pl.ds(pl.multiple_of((n % (wide // tile)) * tile, tile), tile)
+            if i == 2:
+                extra = contract(factor_bank[rows, :rank], second_bank[:, cols], 1, 0)
+            else:
+                extra = contract(
+                    factor_bank[rows, (i + 1) * rank : (i + 2) * rank],
+                    first_bank[cols, i * rank : (i + 1) * rank],
+                    1,
+                    1,
+                )
+            bank[i, rows, cols] = (bank[i, rows, cols].astype(jnp.float32) + extra).astype(
+                bank.dtype
+            )
+            return carry
+
+        lax.fori_loop(0, (width // high) * (wide // tile), inner, 0)
+        put(i).start()
+
+    for item in sources:
+        item.wait()
+    fills[0].wait()
+    fold(0)
+    for k in range(1, depth):
+        for unit in units:
+            from_line(k, unit)
+        if k < 3:
+            fills[k].wait()
+            fold(k)
+        for unit in units:
+            from_pair(k - 1, unit)
+    for unit in units:
+        from_pair(depth - 1, unit)
+    arrive()
+    finish()
+    for i in range(3):
+        put(i).wait()
+
+
+def opening(count, ident, arrays, weights, factors, first, second, parts=2):
+    number = len(arrays)
+    _, width, wide = weights.shape
+    low = jnp.bfloat16
+    sem = pltpu.SemaphoreType.DMA
+    anywhere = pl.BlockSpec(memory_space=pl.ANY)
+    out = pl.pallas_call(
+        functools.partial(opening_body, count, parts, number),
+        out_shape=[
+            jax.ShapeDtypeStruct((count,) + item.shape, item.dtype) for item in arrays
+        ]
+        + [jax.ShapeDtypeStruct(weights.shape, low)],
+        in_specs=[anywhere] * (number + 4),
+        out_specs=[anywhere] * (number + 1),
+        scratch_shapes=[
+            pltpu.VMEM(weights.shape, low),
+            pltpu.VMEM((width, factors.shape[1]), low),
+            pltpu.VMEM((wide, 2 * ADAPTER_RANK), low),
+            pltpu.VMEM((ADAPTER_RANK, wide), low),
+            sem((3,)),
+            sem((3,)),
+            sem((3,)),
+        ]
+        + gather_sems(count, number, parts),
+        compiler_params=kernel_params(ident),
+        name="opening",
+    )(*arrays, weights, factors, first, second)
+    return [
+        item.reshape((count * item.shape[1],) + item.shape[2:]) for item in out[:number]
+    ] + [out[number]]
 
 
 def scatter_body(count, parts, arrays, *refs):
@@ -461,11 +611,555 @@
             sems(depth),
             sems(depth + 1),
         ],
-        compiler_params=pltpu.CompilerParams(
-            collective_id=ident, has_side_effects=True, vmem_limit_bytes=VMEM_LIMIT
-        ),
+        compiler_params=kernel_params(ident),
         name="scatter_rows",
     )(*blocks)
+
+
+def line_order(z):
+    near = z < 2
+    return [z, z + 1 - 2 * (z % 2), jnp.where(near, 2, 1), jnp.where(near, 3, 0)]
+
+
+def unit_values(gate, up, grad):
+    slope = 0.7978845608028654
+    cubic = 0.044715
+    square = gate * gate
+    curve = jnp.tanh(slope * (gate + cubic * square * gate))
+    half = 0.5 * (1.0 + curve)
+    turned = gate * half
+    rise = half + 0.5 * gate * (1.0 - curve * curve) * slope * (1.0 + 3.0 * cubic * square)
+    low = jnp.bfloat16
+    return (turned * up).astype(low), (grad * up * rise).astype(low), (grad * turned).astype(low)
+
+
+def hidden_body(count, parts, own, grads, weights, units, gate_grads, up_grads, rows_out,
+                held, bank, coming, done, recv, send_core, send_pair, send_line, keep, bank_sem,
+                coming_sem, done_sem, rows_sem):
+    me, depth, z, y, c = place(count)
+    height = own.shape[0]
+    width = bank.shape[1]
+    step = height // parts
+    tile = 512
+    core, mate = me + 1 - 2 * c, me + 2 - 4 * y
+    lines = line_order(z)
+    greet(count)
+
+    def hop(block, s, target, sem, first=False):
+        rows = pl.ds(s * step, step)
+        return pltpu.make_async_remote_copy(
+            src_ref=own.at[rows] if first else held.at[block, rows],
+            dst_ref=held.at[block, rows],
+            send_sem=sem,
+            recv_sem=recv.at[block, s],
+            device_id={"dp": target},
+            device_id_type=MESH,
+        )
+
+    def to_core(block, s, first=False):
+        return hop(block, s, core, send_core.at[block // 2, s], first)
+
+    def to_pair(block, s, first=False):
+        return hop(block, s, mate, send_pair.at[block // 4, s], first)
+
+    def to_right(block, s, first=False):
+        return hop(block, s, me + 4, send_line.at[0, block // 4, s], first)
+
+    def to_left(block, s, first=False):
+        return hop(block, s, me - 4, send_line.at[1, block // 4, s], first)
+
+    for s in range(parts):
+
+        @pl.when(z > 0)
+        def _():
+            to_left(me, s, True).start()
+
+        @pl.when(z < depth - 1)
+        def _():
+            to_right(me, s, True).start()
+
+        to_core(me, s, True).start()
+        to_pair(me, s, True).start()
+    mine = pltpu.make_async_copy(own, held.at[me], keep)
+    mine.start()
+    fills = [
+        pltpu.make_async_copy(weights.at[i], bank.at[i], bank_sem.at[i]) for i in range(3)
+    ]
+    for fill in fills:
+        fill.start()
+
+    def first_of(line, pair):
+        return 4 * line + 2 * pair
+
+    def fetch(line, pair, slot):
+        return pltpu.make_async_copy(
+            grads.at[pl.ds(first_of(line, pair), 2)], coming.at[slot], coming_sem.at[slot]
+        )
+
+    def store(line, pair, slot):
+        rows = pl.ds(first_of(line, pair) * height, 2 * height)
+        return [
+            pltpu.make_async_copy(done.at[slot, i], out.at[rows], done_sem.at[slot, i])
+            for i, out in enumerate((units, gate_grads, up_grads))
+        ]
+
+    def keep_rows(line, pair):
+        some = pl.ds(first_of(line, pair), 2)
+        return pltpu.make_async_copy(held.at[some], rows_out.at[some], rows_sem.at[line, pair])
+
+    def from_line(line):
+        block = first_of(line, y) + c
+        for s in range(parts):
+            hop(block, s, core, send_core.at[block // 2, s]).wait_recv()
+
+            @pl.when((line < z) & (z < depth - 1))
+            def _():
+                to_right(block, s).start()
+
+            @pl.when((line > z) & (z > 0))
+            def _():
+                to_left(block, s).start()
+
+            to_pair(block, s).start()
+            to_core(block, s).start()
+
+    def from_pair(line):
+        block = first_of(line, 1 - y) + c
+        for s in range(parts):
+            to_core(block, s).wait_recv()
+            to_core(block, s).start()
+
+    steps = [(line, pair) for line in lines for pair in (y, 1 - y)]
+
+    def work(index):
+        line, pair = steps[index]
+        slot = index % 2
+        for s in range(parts):
+            to_core(first_of(line, pair) + 1 - c, s).wait_recv()
+        if index == 0:
+            mine.wait()
+            fetch(line, pair, slot).start()
+            for fill in fills:
+                fill.wait()
+        if index + 1 < len(steps):
+            fetch(*steps[index + 1], 1 - slot).start()
+        fetch(line, pair, slot).wait()
+        keep_rows(line, pair).start()
+        if index >= 2:
+            for item in store(*steps[index - 2], slot):
+                item.wait()
+        some = pl.ds(first_of(line, pair), 2)
+
+        def inner(n, carry):
+            cols = pl.ds(pl.multiple_of(n * tile, tile), tile)
+            block = held[some].reshape(2 * height, held.shape[2])
+            gate = contract(block, bank[0, cols], 1, 1)
+            up = contract(block, bank[1, cols], 1, 1)
+            grad = contract(coming[slot].reshape(2 * height, held.shape[2]), bank[2, cols], 1, 1)
+            for i, value in enumerate(unit_values(gate, up, grad)):
+                done[slot, i, :, cols] = value
+            return carry
+
+        lax.fori_loop(0, width // tile, inner, 0)
+        for item in store(line, pair, slot):
+            item.start()
+
+    work(0)
+    from_pair(lines[0])
+    from_line(lines[1])
+    work(1)
+    for k in range(1, depth):
+        from_pair(lines[k])
+        work(2 * k)
+        if k + 1 < depth:
+            from_line(lines[k + 1])
+        work(2 * k + 1)
+
+    for index in (len(steps) - 2, len(steps) - 1):
+        for item in store(*steps[index], index % 2):
+            item.wait()
+    for line, pair in steps:
+        keep_rows(line, pair).wait()
+    for j in range(depth):
+        block = first_of(j, y) + c
+        for s in range(parts):
+            to_core(block, s).wait_send()
+            to_core(first_of(j, 1 - y) + c, s).wait_send()
+            to_pair(block, s).wait_send()
+
+            @pl.when((z >= j) & (z < depth - 1))
+            def _():
+                to_right(block, s).wait_send()
+
+            @pl.when((z <= j) & (z > 0))
+            def _():
+                to_left(block, s).wait_send()
+
+
+def hidden_units(count, ident, own, grads, weights, parts=2):
+    height, wide = own.shape
+    width = weights.shape[1]
+    depth = count // 4
+    low = jnp.bfloat16
+    sem = pltpu.SemaphoreType.DMA
+    anywhere = pl.BlockSpec(memory_space=pl.ANY)
+    acts = jax.ShapeDtypeStruct((count * height, width), low)
+    return pl.pallas_call(
+        functools.partial(hidden_body, count, parts),
+        out_shape=[acts, acts, acts, jax.ShapeDtypeStruct((count, height, wide), low)],
+        in_specs=[anywhere] * 3,
+        out_specs=[anywhere] * 4,
+        scratch_shapes=[
+            pltpu.VMEM((count, height, wide), low),
+            pltpu.VMEM((3, width, wide), low),
+            pltpu.VMEM((2, 2, height, wide), low),
+            pltpu.VMEM((2, 3, 2 * height, width), low),
+            sem((count, parts)),
+            sem((2 * depth, parts)),
+            sem((depth, parts)),
+            sem((2, depth, parts)),
+            sem,
+            sem((3,)),
+            sem((2,)),
+            sem((2, 3)),
+            sem((depth, 2)),
+        ],
+        compiler_params=kernel_params(ident),
+        cost_estimate=pl.CostEstimate(
+            flops=6 * count * height * width * wide,
+            bytes_accessed=20 * width * wide,
+            transcendentals=0,
+        ),
+        name="hidden_units",
+    )(own, grads, weights)
+
+
+def unit_grads_body(count, parts, units, gate_grads, up_grads, weights, rows_all, grads_all,
+                    input_sum, output_sum, weight_grads,
+                    bank, rows_in, units_in, made, held, loaded, leaving, core_in, pair_in,
+                    line_in, bank_sem, rows_sem, fill_sems, units_sem, made_sem, core_send, core_recv,
+                    pair_send, pair_recv, line_send, line_recv):
+    me, depth, z, y, c = place(count)
+    height, wide = input_sum.shape
+    width = weights.shape[1]
+    step = height // parts
+    low = jnp.bfloat16
+    core, mate = me + 1 - 2 * c, me + 2 - 4 * y
+    near = z < 2
+    order = [jnp.where(near, 3, 0), jnp.where(near, 0, 3), jnp.where(near, 2, 1),
+             jnp.where(near, 1, 2)]
+    greet(count)
+
+    def fill(source, at):
+        return pltpu.make_async_copy(source, bank.at[at], bank_sem.at[at])
+
+    blocks = width // height
+
+    def fill_rows(source, half, at):
+        return [
+            pltpu.make_async_copy(
+                source.at[half * blocks + i],
+                bank.at[at, pl.ds(i * height, height)],
+                fill_sems.at[at, i],
+            )
+            for i in range(blocks)
+        ]
+
+    first_fills = [fill(weights.at[i], i) for i in range(3)]
+    for item in first_fills:
+        item.start()
+    grad_tail = fill_rows(grads_all, 1, 3)
+    steps = [(line, pair) for line in order for pair in (1 - y, y)]
+
+    def fetch(line, pair, slot, sources):
+        rows = pl.ds((4 * line + 2 * pair) * height, 2 * height)
+        return [
+            pltpu.make_async_copy(source.at[rows], rows_in.at[slot, i], rows_sem.at[slot, i])
+            for i, source in enumerate(sources)
+        ]
+
+    def rows_of(s):
+        return pl.ds(s * step, step)
+
+    def to_core(a, line, pair, slot, s):
+        at = 2 * line + pair
+        return pltpu.make_async_remote_copy(
+            src_ref=leaving.at[a, slot, rows_of(s)],
+            dst_ref=core_in.at[a, at, rows_of(s)],
+            send_sem=core_send.at[a, slot, s],
+            recv_sem=core_recv.at[a, at, s],
+            device_id={"dp": core},
+            device_id_type=MESH,
+        )
+
+    def to_pair(a, line, s):
+        return pltpu.make_async_remote_copy(
+            src_ref=loaded.at[a, 2 * line + 1 - y, rows_of(s)],
+            dst_ref=pair_in.at[a, line, rows_of(s)],
+            send_sem=pair_send.at[a, line, s],
+            recv_sem=pair_recv.at[a, line, s],
+            device_id={"dp": mate},
+            device_id_type=MESH,
+        )
+
+    def along(a, line, slot, s, target):
+        return pltpu.make_async_remote_copy(
+            src_ref=loaded.at[a, 2 * line + y, rows_of(s)],
+            dst_ref=line_in.at[a, slot, rows_of(s)],
+            send_sem=line_send.at[a, line, s],
+            recv_sem=line_recv.at[a, slot, s],
+            device_id={"dp": target},
+            device_id_type=MESH,
+        )
+
+    def product(a, index):
+        line, pair = steps[index]
+        slot = index % 2
+        sources = (gate_grads, up_grads) if a == 0 else (units,)
+        if index == 0:
+            for item in fetch(line, pair, slot, sources):
+                item.start()
+        if index + 1 < len(steps):
+            for item in fetch(*steps[index + 1], 1 - slot, sources):
+                item.start()
+        if index >= 2:
+            for s in range(parts):
+                to_core(a, *steps[index - 2], slot, s).wait_send()
+        for item in fetch(line, pair, slot, sources):
+            item.wait()
+        tile = 512
+
+        def inner(n, carry):
+            cols = pl.ds(pl.multiple_of(n * tile, tile), tile)
+            if a == 0:
+                value = contract(rows_in[slot, 0], bank[0, :, cols], 1, 0)
+                value += contract(rows_in[slot, 1], bank[1, :, cols], 1, 0)
+            else:
+                value = contract(rows_in[slot, 0], bank[2, :, cols], 1, 0)
+            value = value.astype(low)
+
+            @pl.when(c == 0)
+            def _():
+                loaded[a, 2 * line + pair, :, cols] = value[:height]
+                leaving[a, slot, :, cols] = value[height:]
+
+            @pl.when(c == 1)
+            def _():
+                loaded[a, 2 * line + pair, :, cols] = value[height:]
+                leaving[a, slot, :, cols] = value[:height]
+
+            return carry
+
+        lax.fori_loop(0, wide // tile, inner, 0)
+        for s in range(parts):
+            to_core(a, line, pair, slot, s).start()
+
+    def finish_sends(a):
+        for index in (len(steps) - 2, len(steps) - 1):
+            for s in range(parts):
+                to_core(a, *steps[index], index % 2, s).wait_send()
+
+    def pair_step(a, k):
+        line = order[k]
+        at = 2 * line + 1 - y
+        for s in range(parts):
+            to_core(a, line, 1 - y, 0, s).wait_recv()
+            loaded[a, at, rows_of(s)] = loaded[a, at, rows_of(s)] + core_in[a, at, rows_of(s)]
+            to_pair(a, line, s).start()
+
+    def own_sum(a, line, s):
+        at = 2 * line + y
+        to_core(a, line, y, 0, s).wait_recv()
+        to_pair(a, line, s).wait_recv()
+        part = loaded[a, at, rows_of(s)].astype(jnp.float32)
+        part += core_in[a, at, rows_of(s)].astype(jnp.float32)
+        held[...] = part + pair_in[a, line, rows_of(s)].astype(jnp.float32)
+
+    def add_line(a, slot, s):
+        along(a, z, slot, s, me + 4).wait_recv()
+        held[...] += line_in[a, slot, rows_of(s)].astype(jnp.float32)
+
+    def line_step(a, k):
+        line = order[k]
+
+        @pl.when(line != z)
+        def _():
+            for s in range(parts):
+                own_sum(a, line, s)
+
+                @pl.when(((line > z) & (z > 0)) | ((line < z) & (z < depth - 1)))
+                def _():
+                    add_line(a, line, s)
+
+                loaded[a, 2 * line + y, rows_of(s)] = held[...].astype(low)
+
+                @pl.when(line > z)
+                def _():
+                    along(a, line, line, s, me + 4).start()
+
+                @pl.when(line < z)
+                def _():
+                    along(a, line, jnp.where(line == z - 1, depth, line), s, me - 4).start()
+
+    def last_step(a, total):
+        for s in range(parts):
+            own_sum(a, z, s)
+
+            @pl.when(z > 0)
+            def _():
+                add_line(a, z, s)
+
+            @pl.when(z < depth - 1)
+            def _():
+                add_line(a, depth, s)
+
+            total[rows_of(s)] = held[...]
+
+    tall = units_in.shape[2]
+
+    def bring(g, slot):
+        source = (gate_grads, up_grads, units)[g // (width // tall)]
+        cols = pl.ds((g % (width // tall)) * tall, tall)
+        return pltpu.make_async_copy(source.at[:, cols], units_in.at[slot], units_sem.at[slot])
+
+    def put(g, slot):
+        rows = pl.ds((g % (width // tall)) * tall, tall)
+        return pltpu.make_async_copy(
+            made.at[slot], weight_grads.at[g // (width // tall), rows], made_sem.at[slot]
+        )
+
+    number = 3 * (width // tall)
+
+    def weight_product(g):
+        slot = g % 2
+        if g + 1 < number:
+            bring(g + 1, 1 - slot).start()
+        bring(g, slot).wait()
+        if g >= 2:
+            put(g - 2, slot).wait()
+        at = 0 if g < 2 * (width // tall) else 2
+        tile = 512
+
+        def inner(n, carry):
+            cols = pl.ds(pl.multiple_of(n * tile, tile), tile)
+            whole = bank[at : at + 2, :, cols].reshape(2 * width, tile)
+            made[slot, :, cols] = contract(units_in[slot], whole, 0, 0).astype(low)
+            return carry
+
+        lax.fori_loop(0, wide // tile, inner, 0)
+        put(g, slot).start()
+
+    for item in first_fills[:2]:
+        item.wait()
+    for index in range(8):
+        product(0, index)
+        if index >= 2 and index % 2 == 0:
+            pair_step(0, index // 2 - 1)
+    finish_sends(0)
+    row_fills = fill_rows(rows_all, 0, 0) + fill_rows(rows_all, 1, 1)
+    for item in row_fills:
+        item.start()
+    for item in grad_tail:
+        item.start()
+    first_fills[2].wait()
+    for index in range(8):
+        product(1, index)
+        if index == 0:
+            pair_step(0, 3)
+        if index >= 2 and index % 2 == 0:
+            pair_step(1, index // 2 - 1)
+        if index == 4:
+            line_step(0, 0)
+    finish_sends(1)
+    grad_fills = fill_rows(grads_all, 0, 2)
+    for item in grad_fills:
+        item.start()
+    bring(0, 0).start()
+    for item in row_fills:
+        item.wait()
+    weight_product(0)
+    pair_step(1, 3)
+    line_step(0, 1)
+    weight_product(1)
+    weight_product(2)
+    line_step(0, 2)
+    weight_product(3)
+    weight_product(4)
+    line_step(0, 3)
+    weight_product(5)
+    weight_product(6)
+    last_step(0, input_sum)
+    weight_product(7)
+    for item in grad_tail + grad_fills:
+        item.wait()
+    weight_product(8)
+    line_step(1, 0)
+    weight_product(9)
+    weight_product(10)
+    line_step(1, 1)
+    weight_product(11)
+    line_step(1, 2)
+    line_step(1, 3)
+    last_step(1, output_sum)
+
+    for g in (number - 2, number - 1):
+        put(g, g % 2).wait()
+    for a in range(2):
+        for line in range(depth):
+            for s in range(parts):
+                to_pair(a, line, s).wait_send()
+
+                @pl.when(z != line)
+                def _():
+                    along(a, line, line, s, me + 4).wait_send()
+
+
+def unit_grads(count, ident, units, gate_grads, up_grads, weights, rows_all, grads_all, parts=2):
+    width, wide = weights.shape[1:]
+    height = rows_all.shape[1]
+    depth = count // 4
+    low = jnp.bfloat16
+    sem = pltpu.SemaphoreType.DMA
+    anywhere = pl.BlockSpec(memory_space=pl.ANY)
+    inside = pl.BlockSpec(memory_space=pltpu.VMEM)
+    total = jax.ShapeDtypeStruct((height, wide), jnp.float32)
+
+    return pl.pallas_call(
+        functools.partial(unit_grads_body, count, parts),
+        out_shape=[total, total, jax.ShapeDtypeStruct((3, width, wide), low)],
+        in_specs=[anywhere] * 6,
+        out_specs=[inside, inside, anywhere],
+        scratch_shapes=[
+            pltpu.VMEM((4, width, wide), low),
+            pltpu.VMEM((2, 2, 2 * height, width), low),
+            pltpu.VMEM((2, count * height, 256), low),
+            pltpu.VMEM((2, 256, wide), low),
+            pltpu.VMEM((height // parts, wide), jnp.float32),
+            pltpu.VMEM((2, 2 * depth, height, wide), low),
+            pltpu.VMEM((2, 2, height, wide), low),
+            pltpu.VMEM((2, 2 * depth, height, wide), low),
+            pltpu.VMEM((2, depth, height, wide), low),
+            pltpu.VMEM((2, depth + 1, height, wide), low),
+            sem((4,)),
+            sem((2, 2)),
+            sem((4, width // height)),
+            sem((2,)),
+            sem((2,)),
+            sem((2, 2, parts)),
+            sem((2, 2 * depth, parts)),
+            sem((2, depth, parts)),
+            sem((2, depth, parts)),
+            sem((2, depth, parts)),
+            sem((2, depth + 1, parts)),
+        ],
+        compiler_params=kernel_params(ident),
+        cost_estimate=pl.CostEstimate(
+            flops=12 * count * height * width * wide,
+            bytes_accessed=40 * width * wide,
+            transcendentals=0,
+        ),
+        name="unit_grads",
+    )(units, gate_grads, up_grads, weights, rows_all, grads_all)
 
 
 def swap_loops(values):
@@ -550,21 +1244,29 @@
     up_factor = ffn_own[:, 2 * rank :]
     first_gate = adapter_first[:, 4 * rank : 5 * rank]
     first_up = adapter_first[:, 5 * rank :]
-    gate_weight = (
-        feedforward_weight[:, 0, :].astype(jnp.float32) + outer_columns(gate_factor, first_gate)
-    ).astype(low)
-    up_weight = (
-        feedforward_weight[:, 1, :].astype(jnp.float32) + outer_columns(up_factor, first_up)
-    ).astype(low)
-    down_weight = (
-        feedforward_weight[:, 2, :].astype(jnp.float32) + matrix_product(down_factor, second_down)
-    ).astype(low)
+    ffn_weight = jnp.swapaxes(feedforward_weight, 0, 1)
 
     feedforward_gradient = (active_mask * grad_out).astype(low)
     normed_input = norm_rows(residual_stream, layer_norm_gains[0]).astype(low)
-    input_weight, output_weight, grad_ffn_all = gather_rows(
-        count, 1, in_own, out_own, feedforward_gradient
-    )
+    if count == LINE_DEVICES:
+        input_weight, output_weight, ffn_folded = opening(
+            count, 1, (in_own, out_own), ffn_weight, adapter_hidden_factors[0],
+            adapter_first, adapter_second,
+        )
+    else:
+        input_weight, output_weight = gather_rows(count, 1, in_own, out_own)
+        extra = jnp.stack(
+            [
+                outer_columns(gate_factor, first_gate),
+                outer_columns(up_factor, first_up),
+                matrix_product(down_factor, second_down),
+            ]
+        )
+        ffn_folded = (ffn_weight.astype(jnp.float32) + extra).astype(low)
+    feedforward_gradient, input_weight = lax.optimization_barrier(
+        (feedforward_gradient, input_weight)
+    )
+    grad_ffn_all = lax.all_gather(feedforward_gradient, "dp", axis=0, tiled=True)
     query_key_value_linear = matrix_product(normed_input, input_weight)
     queries = rotate(
         query_key_value_linear[:, :QUERY_WIDTH].reshape(local_rows, HEADS, HEAD_SIZE), pos_own
@@ -599,28 +1301,35 @@
     branch_output = matrix_product(attended_rows, output_weight)
     middle_state = residual_stream + active_mask * branch_output
     second_normed_input = norm_rows(middle_state, layer_norm_gains[1]).astype(low)
-    (normed_all,) = gather_rows(count, 3, second_normed_input)
-
-    gate_own = outer_columns(normed_all, gate_weight)
-    up_own = outer_columns(normed_all, up_weight)
-    hidden_unit_gradient = outer_columns(grad_ffn_all, down_weight)
-    units_own = geglu(gate_own, up_own).astype(low)
-    grad_gate_own, grad_up_own = jax.vjp(geglu, gate_own, up_own)[1](hidden_unit_gradient)
-    grad_gate_own = grad_gate_own.astype(low)
-    grad_up_own = grad_up_own.astype(low)
-    gate_grad = inner_rows(grad_gate_own, normed_all).astype(low)
-    up_grad = inner_rows(grad_up_own, normed_all).astype(low)
-    down_grad = inner_rows(units_own, grad_ffn_all).astype(low)
-    gate_other, up_other, down_other = (
-        swap_loops(gate_grad),
-        swap_loops(up_grad),
-        swap_loops(down_grad),
-    )
-    ffn_terms = matrix_product(units_own, down_weight).astype(low)
-    input_terms = (
-        matrix_product(grad_gate_own, gate_weight) + matrix_product(grad_up_own, up_weight)
-    ).astype(low)
-    ffn_sum, second_normed_gradient = scatter_rows(count, 4, ffn_terms, input_terms)
+    if count == LINE_DEVICES:
+        grad_blocks = grad_ffn_all.reshape(count, local_rows, MODEL_WIDTH)
+        units_own, grad_gate_own, grad_up_own, normed_blocks = hidden_units(
+            count, 3, second_normed_input, grad_blocks, ffn_folded
+        )
+        second_normed_gradient, ffn_sum, weight_grads = unit_grads(
+            count, 4, units_own, grad_gate_own, grad_up_own, ffn_folded, normed_blocks, grad_blocks
+        )
+        gate_grad, up_grad, down_grad = weight_grads
+    else:
+        (normed_all,) = gather_rows(count, 3, second_normed_input)
+        gate_weight, up_weight, down_weight = ffn_folded
+        gate_own = outer_columns(normed_all, gate_weight)
+        up_own = outer_columns(normed_all, up_weight)
+        hidden_unit_gradient = outer_columns(grad_ffn_all, down_weight)
+        units_own = geglu(gate_own, up_own).astype(low)
+        grad_gate_own, grad_up_own = jax.vjp(geglu, gate_own, up_own)[1](hidden_unit_gradient)
+        grad_gate_own = grad_gate_own.astype(low)
+        grad_up_own = grad_up_own.astype(low)
+        gate_grad = inner_rows(grad_gate_own, normed_all).astype(low)
+        up_grad = inner_rows(grad_up_own, normed_all).astype(low)
+        down_grad = inner_rows(units_own, grad_ffn_all).astype(low)
+        ffn_terms = matrix_product(units_own, down_weight).astype(low)
+        input_terms = (
+            matrix_product(grad_gate_own, gate_weight) + matrix_product(grad_up_own, up_weight)
+        ).astype(low)
+        ffn_sum, second_normed_gradient = scatter_rows(count, 4, ffn_terms, input_terms)
+        weight_grads = jnp.stack([gate_grad, up_grad, down_grad])
+    weight_other = swap_loops(weight_grads)
     complete_output = middle_state + active_mask * ffn_sum
     confidence = root_mean(residual_stream) / (
         root_mean(residual_stream) + root_mean(complete_output - residual_stream)
@@ -717,13 +1426,8 @@
     depth_total = small_total[2, 1 : loop_count + 2]
     mean_confidence = small_total[2, 0] / jnp.sum(depth_total)
     exit_counts = depth_total.astype(jnp.int32)
-    sum_mlp = jnp.stack(
-        [
-            gate_grad.astype(jnp.float32) + gate_other.astype(jnp.float32),
-            up_grad.astype(jnp.float32) + up_other.astype(jnp.float32),
-            down_grad.astype(jnp.float32) + down_other.astype(jnp.float32),
-        ],
-        axis=1,
+    sum_mlp = jnp.swapaxes(
+        weight_grads.astype(jnp.float32) + weight_other.astype(jnp.float32), 0, 1
     )
     return (
         complete_output.astype(low)[None],

time: 885 us -> 774 us (0.87)
  matrix products: 252 us -> 104 us
  local copies, waits for them, and re-layouts: 29.1 us -> 55.6 us
  Pallas kernels: 501 us -> 519 us
  between operations: 4.53 us -> 17.9 us
  other arithmetic: 77.7 us -> 68.1 us
    pallas_call x0 -> x3, Pallas kernels: none -> 312 us  [the longest x1 126 us: unit_grads(): pl.pallas_call(functools.partial(unit_grads_body, count, parts), out_shap...]
    pallas_call x3 -> x1, Pallas kernels: 226 us -> 35 us  [gather_rows(): pl.pallas_call(functools.partial(gather_body, count, parts, number), out_...]
    pallas_call x3 -> x2, Pallas kernels: 275 us -> 171 us  [scatter_rows(): pl.pallas_call(functools.partial(scatter_body, count, parts, number), out...]
    dot_general x14 -> x9, matrix products: 102 us -> 36.8 us  [outer_columns(): lax.dot_general(left, right, (((1,), (1,)), ((), ())), preferred_element_...]
    dot_general x15 -> x11, matrix products: 75.2 us -> 31.2 us  [matrix_product(): return jnp.dot(left, right, preferred_element_type=jnp.float32)]
    dot_general x14 -> x11, matrix products: 74.9 us -> 36.1 us  [inner_rows(): lax.dot_general(left, right, (((0,), (0,)), ((), ())), preferred_element_...]
    another operation x8 -> x4, other arithmetic: 33 us -> 0.73 us  [the longest x4 31.6 us: per_device(): jnp.stack([gate_grad.astype(jnp.float32) + gate_other.astype(jnp.float32)...]
    dot_general x1 -> x4, local copies, waits for them, and re-layouts: 6.45 us -> 25.8 us  [inner_rows(): lax.dot_general(left, right, (((0,), (0,)), ((), ())), preferred_element_...]
  transfers between devices with their start and end apart: 6 -> 5, of which waited for: 1 -> 0; matrix products, arithmetic and copies ran while one was open for 23% -> 24% of each run, Pallas kernels for 31% -> 27%
where the time goes in v2:
time: 774 us; the launch traced here: 769 us
  Pallas kernels  519 us (67%)
  matrix products  104 us (13%)
  other arithmetic  68.1 us (9%)
  local copies, waits for them, and re-layouts  55.6 us (7%)
  between operations  17.9 us (2%)
    pallas_call x2, Pallas kernels, scatter_rows(): pl.pallas_call(functools.partial(scatter_body, count, parts, number), out...  171 us
    pallas_call x1, Pallas kernels, unit_grads(): pl.pallas_call(functools.partial(unit_grads_body, count, parts), out_shap...  126 us
    pallas_call x1, Pallas kernels, opening(): pl.pallas_call(functools.partial(opening_body, count, parts, number), out...  109 us
    pallas_call x1, Pallas kernels, hidden_units(): pl.pallas_call(functools.partial(hidden_body, count, parts), out_shape=[a...  76.9 us
    dot_general x9, matrix products, outer_columns(): lax.dot_general(left, right, (((1,), (1,)), ((), ())), preferred_element_...  36.8 us
    dot_general x11, matrix products, inner_rows(): lax.dot_general(left, right, (((0,), (0,)), ((), ())), preferred_element_...  36.1 us
    pallas_call x1, Pallas kernels, gather_rows(): pl.pallas_call(functools.partial(gather_body, count, parts, number), out_...  35 us
    dot_general x11, matrix products, matrix_product(): return jnp.dot(left, right, preferred_element_type=jnp.float32)  31.2 us
  transfers between devices with their start and end apart: 5, of which 0 were waited for; matrix products, arithmetic and copies ran while one was open for 24% of the time, Pallas kernels for 27%

profile of v2, /device:TPU:0, one launch (start us, length us, event | category | flops | bytes accessed | tf_op | source)
XLA Modules:
  0.0 768.7 jit_solution(12049199554868156766)
XLA Ops:
  16.9 109.3 %opening.1 = (bf16[16,128,2560]{2,1,0:T(8,128)(2,1)}, bf16[16,128,2048]{2,1,0:T(8,128)(2,1)}, bf16[3,1024,2048]{2,1,0:T(8,128)(2,1)}) custom-call(bf16[128,2560]{1,0:T(8,128)(2,1)} %fusion.40.refs_0_, bf16[128,2048]{1,0:T(8,128)(2,1)} %fusion.33.refs_1_, bf16[3,1024,2048]{2,1,0:T(8,128)(2,1)} %bitcast.185, bf16[16384,768]{1,0:T(8,128)(2,1)} %bitcast.181, ...), custom_call_target="tpu_custom_call" | custom-call | tf_op jit(solution)/shard_map/opening/pallas_call | solution.py:398
  127.0 5.6 fusion.129
  134.3 35.0 %gather_rows.1 = bf16[16,128,512]{2,1,0:T(8,128)(2,1)} custom-call(bf16[128,512]{1,0:T(8,128)(2,1)} %pad_maximum_fusion.5.refs_0_), custom_call_target="tpu_custom_call" | custom-call | tf_op jit(solution)/shard_map/gather_rows/pallas_call | solution.py:298
  171.0 4.5 fusion.3
  175.6 5.0 fusion.4
  180.7 7.2 multiply_bitcast_fusion
  194.6 6.4 copy.76
  201.7 2.9 dynamic-slice_bitcast_fusion
  204.6 5.2 multiply_reduce_fusion.3
  212.1 76.9 %hidden_units.1 = (bf16[2048,1024]{1,0:T(8,128)(2,1)}, bf16[2048,1024]{1,0:T(8,128)(2,1)}, bf16[2048,1024]{1,0:T(8,128)(2,1)}, bf16[16,128,2048]{2,1,0:T(8,128)(2,1)}) custom-call(bf16[128,2048]{1,0:T(8,128)(2,1)} %multiply_convert_fusion.2.own, bf16[16,128,2048]{2,1,0:T(8,128)(2,1)} %bitcast.237, bf16[3,1024,2048]{2,1,0:T(8,128)(2,1)} %get-tuple-element.57.weights), custom_call_target="tpu_custom_call" | custom-call | flops 25769803776 | bytes 41943040 | tf_op jit(solution)/shard_map/hidden_units/pallas_call | solution.py:807
  289.1 126.3 %unit_grads.1 = (f32[128,2048]{1,0:T(8,128)}, f32[128,2048]{1,0:T(8,128)}, bf16[3,1024,2048]{2,1,0:T(8,128)(2,1)}) custom-call(bf16[2048,1024]{1,0:T(8,128)(2,1)} %get-tuple-element.58.units, bf16[2048,1024]{1,0:T(8,128)(2,1)} %get-tuple-element.59.gate_grads, bf16[2048,1024]{1,0:T(8,128)(2,1)} %get-tuple-element.60.up_grads, ...), custom_call_target="tpu_custom_call" | custom-call | flops 51539607552 | bytes 83886080 | tf_op jit(solution)/shard_map/unit_grads/pallas_call | solution.py:1127
  415.4 3.5 multiply_reduce_fusion.1
  419.4 6.5 convolution_convert_fusion.4
  426.0 7.2 multiply_reduce_fusion
  433.2 7.6 multiply_convert_fusion
  442.9 3.4 fusion.37
  452.7 6.1 slice_bitcast_fusion.1
  458.8 6.4 copy.78
  465.2 6.8 copy.77
  472.1 3.7 convolution_convert_fusion.5
  485.1 33.1 %scatter_rows.2 = (f32[128,512]{1,0:T(8,128)}, f32[128,512]{1,0:T(8,128)}) custom-call(bf16[16,128,512]{2,1,0:T(8,128)(2,1)} %pad_maximum_fusion.refs_0_, bf16[16,128,512]{2,1,0:T(8,128)(2,1)} %pad_maximum_fusion.1.refs_1_), custom_call_target="tpu_custom_call" | custom-call | tf_op jit(solution)/shard_map/scatter_rows/pallas_call | solution.py:592
  521.3 8.8 %fusion.49 = (f32[2048]{0:T(1024)S(1)}, f32[128]{0:T(128)S(1)}, f32[128,2048]{1,0:T(8,128)}) fusion(bf16[1,128,2048]{2,1,0:T(8,128)(2,1)S(1)} %copy-done, f32[128]{0:T(128)} %copy-done.37, f32[2048]{0:T(1024)S(1)} %bitcast.219, bf16[2048,2560]{1,0:T(8,128)(2,1)} %bitcast.183, bf16[128,256]{0,1:T(8,128)(2,1)} %copy.73, bf16[128,256]{0,1:T(8,128)(2,1)S(1)} %copy.72, ...), kind=kOutput, calls=%fused_computation.83 | convolution fusion | flops 1345976192 | bytes 12731392 | tf_op jit(solution)/shard_map/dot_general | solution.py:36
  539.7 3.3 fusion.28
  543.0 6.7 convolution_convert_fusion.1
  549.8 6.6 convolution_convert_fusion
  556.4 4.7 fusion.29
  561.1 138.1 %scatter_rows.3 = (f32[128,2560]{1,0:T(8,128)}, f32[128,2048]{1,0:T(8,128)}, f32[416,256]{1,0:T(8,128)}, f32[8,128]{1,0:T(8,128)}) custom-call(bf16[16,128,2560]{2,1,0:T(8,128)(2,1)} %bitcast.175, bf16[16,128,2048]{2,1,0:T(8,128)(2,1)} %bitcast.178, bf16[16,416,256]{2,1,0:T(8,128)(2,1)} %bitcast.54.refs_2_, f32[16,8,128]{2,1,0:T(8,128)} %copy-done.27), custom_call_target="tpu_custom_call" | custom-call | tf_op jit(solution)/shard_map/scatter_rows/pallas_call | solution.py:592
  710.8 3.8 fusion.11
  714.6 3.8 fusion.9
  718.5 3.6 fusion.5
  728.7 3.6 copy.74
  741.1 18.6 %add_bitcast_fusion = f32[1024,3,2048]{2,0,1:T(8,128)} fusion(bf16[3,1024,2048]{2,1,0:T(8,128)(2,1)} %collective-permute-done.2, bf16[3,1024,2048]{2,1,0:T(8,128)(2,1)} %get-tuple-element.64), kind=kLoop, calls=%fused_computation | loop fusion | flops 18874368 | bytes 50331648 | tf_op jit(solution)/shard_map/transpose | solution.py:1429
  (238 shorter events, 80.6 us)
Async XLA Ops:
  7.2 8.7 %copy-start.23 = (bf16[128,2560]{1,0:T(8,128)(2,1)S(1)}, bf16[128,2560]{1,0:T(8,128)(2,1)}, u32[]{:S(2)}) copy-start(bf16[128,2560]{1,0:T(8,128)(2,1)} %param.18) | copy-start | bytes 1966084
  7.2 204.9 %all-gather.2.cloned.1.call-start = ((), (), s32[]{:S(2)}) async-start(), calls=%async_computation | async-start | bytes 8912896 | tf_op jit(solution)/shard_map/all_gather | solution.py:1269
  14.9 118.2 %copy-start.45 = (pred[128]{0:T(512)(128)(4,1)}, pred[128]{0:T(512)(128)(4,1)S(1)}, u32[]{:S(2)}) copy-start(pred[128]{0:T(512)(128)(4,1)S(1)} %get-tuple-element.110) | copy-start | bytes 388
  14.9 111.2 %copy-start.40 = (f32[128]{0:T(128)}, f32[128]{0:T(128)S(1)}, u32[]{:S(2)}) copy-start(f32[128]{0:T(128)S(1)} %and_convert_fusion) | copy-start | bytes 1540
  16.9 109.4 %copy-start = (bf16[1,128,2048]{2,1,0:T(8,128)(2,1)S(1)}, bf16[1,128,2048]{2,1,0:T(8,128)(2,1)}, u32[]{:S(2)}) copy-start(bf16[1,128,2048]{2,1,0:T(8,128)(2,1)} %param.16) | copy-start | bytes 1572868
  16.9 109.6 %copy-start.34 = (f32[2,2048]{1,0:T(2,128)S(1)}, f32[2,2048]{1,0:T(2,128)}, u32[]{:S(2)}) copy-start(f32[2,2048]{1,0:T(2,128)} %param.21) | copy-start | bytes 49156
  133.0 37.3 %copy-start.51 = (f32[128]{0:T(128)}, f32[128]{0:T(128)S(1)}, u32[]{:S(2)}) copy-start(f32[128]{0:T(128)S(1)} %multiply_power_fusion) | copy-start | bytes 1540
  133.3 37.1 %copy-start.43 = (f32[128]{0:T(128)}, f32[128]{0:T(128)S(1)}, u32[]{:S(2)}) copy-start(f32[128]{0:T(128)S(1)} %get-tuple-element.131) | copy-start | bytes 1540
  194.6 10.0 %copy-start.41 = (f32[128]{0:T(128)S(1)}, f32[128]{0:T(128)}, u32[]{:S(2)}) copy-start(f32[128]{0:T(128)} %copy-done.40) | copy-start | bytes 1540
  209.8 79.3 %copy-start.60 = (f32[128]{0:T(128)}, f32[128]{0:T(128)S(1)}, u32[]{:S(2)}) copy-start(f32[128]{0:T(128)S(1)} %get-tuple-element.142) | copy-start | bytes 1540
  209.8 79.2 %copy-start.48 = (f32[128]{0:T(128)}, f32[128]{0:T(128)S(1)}, u32[]{:S(2)}) copy-start(f32[128]{0:T(128)S(1)} %fusion.121) | copy-start | bytes 1540
  289.0 126.4 %copy-start.42 = (f32[128]{0:T(128)S(1)}, f32[128]{0:T(128)}, u32[]{:S(2)}) copy-start(f32[128]{0:T(128)} %copy-done.40) | copy-start | bytes 1540
  289.0 126.4 %copy-start.49 = (f32[128]{0:T(128)S(1)}, f32[128]{0:T(128)}, u32[]{:S(2)}) copy-start(f32[128]{0:T(128)} %copy-done.48) | copy-start | bytes 1540
  415.4 10.6 %slice-start = ((s8[8388608]{0:T(1024)(128)(4,1)}), s8[4194304]{0:T(1024)(128)(4,1)S(1)}, s32[]{:S(2)}) async-start(s8[8388608]{0:T(1024)(128)(4,1)} %bitcast.179), calls=%async_computation.1 | async-start | bytes 8388608
  425.9 315.2 %collective-permute-start.2 = (bf16[3,1024,2048]{2,1,0:T(8,128)(2,1)}, bf16[3,1024,2048]{2,1,0:T(8,128)(2,1)}, u32[]{:S(2)}, u32[]{:S(2)}) collective-permute-start(bf16[3,1024,2048]{2,1,0:T(8,128)(2,1)} %get-tuple-element.64), channel_id=1, source_target_pairs={{0,16},{16,0},{1,17},{17,1},{2,18},{18,2},{3,19},{19,3},{4,20},{20... | collective-permute-start | bytes 37748744 | tf_op jit(solution)/shard_map/ppermute | solution.py:1168
  483.5 36.5 %copy-start.44 = (f32[128]{0:T(128)S(1)}, f32[128]{0:T(128)}, u32[]{:S(2)}) copy-start(f32[128]{0:T(128)} %copy-done.43) | copy-start | bytes 1540
  483.5 36.5 %copy-start.52 = (f32[128]{0:T(128)S(1)}, f32[128]{0:T(128)}, u32[]{:S(2)}) copy-start(f32[128]{0:T(128)} %copy-done.51) | copy-start | bytes 1540
  520.5 9.6 %copy-start.28 = (bf16[128,256]{0,1:T(8,128)(2,1)}, bf16[128,256]{0,1:T(8,128)(2,1)S(1)}, u32[]{:S(2)}) copy-start(bf16[128,256]{0,1:T(8,128)(2,1)S(1)} %copy.72) | copy-start | bytes 196612
  521.3 8.8 %copy-start.33 = (f32[2048]{0:T(1024)S(1)}, f32[2048]{0:T(1024)}, u32[]{:S(2)}) copy-start(f32[2048]{0:T(1024)} %get-tuple-element.104) | copy-start | bytes 24580
  521.3 8.9 %copy-start.47 = (pred[128]{0:T(512)(128)(4,1)S(1)}, pred[128]{0:T(512)(128)(4,1)}, u32[]{:S(2)}) copy-start(pred[128]{0:T(512)(128)(4,1)} %copy-done.45) | copy-start | bytes 388
  521.3 8.9 %copy-start.57 = (f32[128]{0:T(128)S(1)}, f32[128]{0:T(128)}, u32[]{:S(2)}) copy-start(f32[128]{0:T(128)} %copy-done.56) | copy-start | bytes 1540
  521.3 8.9 %copy-start.59 = (f32[128]{0:T(128)S(1)}, f32[128]{0:T(128)}, u32[]{:S(2)}) copy-start(f32[128]{0:T(128)} %get-tuple-element.108) | copy-start | bytes 1540
  521.3 10.0 %copy-start.65 = (f32[3]{0:T(128)S(1)}, f32[3]{0:T(128)}, u32[]{:S(2)}) copy-start(f32[3]{0:T(128)} %convert_reduce_fusion.1) | copy-start | bytes 40
  521.3 16.7 %copy-start.26 = (f32[128,512]{1,0:T(8,128)S(1)}, f32[128,512]{1,0:T(8,128)}, u32[]{:S(2)}) copy-start(f32[128,512]{1,0:T(8,128)} %get-tuple-element.65) | copy-start | bytes 786436
  533.8 16.0 %copy-start.27 = (f32[16,8,128]{2,1,0:T(8,128)}, f32[16,8,128]{2,1,0:T(8,128)S(1)}, u32[]{:S(2)}) copy-start(f32[16,8,128]{2,1,0:T(8,128)S(1)} %scatter.9.refs_3_) | copy-start | bytes 196612
  699.2 9.9 %copy-start.2 = (bf16[1,256,6656]{2,1,0:T(8,128)(2,1)S(1)}, bf16[1,256,6656]{2,1,0:T(8,128)(2,1)}, u32[]{:S(2)}) copy-start(bf16[1,256,6656]{2,1,0:T(8,128)(2,1)} %param.23) | copy-start | bytes 10223620
  699.2 33.2 %collective-permute-start.3 = (f32[8,128]{1,0:T(8,128)}, f32[8,128]{1,0:T(8,128)}, u32[]{:S(2)}, u32[]{:S(2)}) collective-permute-start(f32[8,128]{1,0:T(8,128)} %get-tuple-element.68), channel_id=1, source_target_pairs={{0,16},{16,0},{1,17},{17,1},{2,18},{18,2},{3,19},{19,3},{4,20},{20... | collective-permute-start | bytes 12296 | tf_op jit(solution)/shard_map/ppermute | solution.py:1168
  704.7 32.0 %collective-permute-start.1 = (bf16[128,2048]{1,0:T(8,128)(2,1)}, bf16[128,2048]{1,0:T(8,128)(2,1)}, u32[]{:S(2)}, u32[]{:S(2)}) collective-permute-start(bf16[128,2048]{1,0:T(8,128)(2,1)} %convert_element_type.173), channel_id=1, source_target_pairs={{0,16},{16,0},{1,17},{17,1},{2,18},{18,2},{3,19},{19,3},{4,20},{20... | collective-permute-start | bytes 1572872 | tf_op jit(solution)/shard_map/ppermute | solution.py:1168
  704.9 33.9 %collective-permute-start = (bf16[128,2560]{1,0:T(8,128)(2,1)S(1)}, bf16[128,2560]{1,0:T(8,128)(2,1)}, u32[]{:S(2)}, u32[]{:S(2)}) collective-permute-start(bf16[128,2560]{1,0:T(8,128)(2,1)S(1)} %convert_element_type.170), channel_id=1, source_target_pairs={{0,16},{16,0},{1,17},{17,1},{2,18},{18,2},{3,19},{19,3},{4,20},{20... | collective-permute-start | bytes 1966088 | tf_op jit(solution)/shard_map/ppermute | solution.py:1168
  725.8 10.9 %copy-start.11 = (f32[128,2048]{1,0:T(8,128)S(1)}, f32[128,2048]{1,0:T(8,128)}, u32[]{:S(2)}) copy-start(f32[128,2048]{1,0:T(8,128)} %get-tuple-element.67) | copy-start | bytes 3145732
  728.7 10.1 %copy-start.4 = (f32[128,2560]{1,0:T(8,128)S(1)}, f32[128,2560]{1,0:T(8,128)}, u32[]{:S(2)}) copy-start(f32[128,2560]{1,0:T(8,128)} %get-tuple-element.66) | copy-start | bytes 3932164
  741.1 18.6 %copy-start.25 = (f32[416,256]{1,0:T(8,128)S(1)}, f32[416,256]{1,0:T(8,128)}, u32[]{:S(2)}) copy-start(f32[416,256]{1,0:T(8,128)} %get-tuple-element.70) | copy-start | bytes 1277956
  (43 other events, 208.6 us)
Sparse Core Ops, SparseCore 0:
  126.3 83.2 all-gather.1

commit v3 on v2

--- a/solution.py
+++ b/solution.py
@@ -98,7 +98,7 @@
     return me, count // 4, me // 4, (me // 2) % 2, me % 2
 
 
-def greet(count):
+def greet(count, across=False):
     me, depth, z, y, c = place(count)
     barrier = pltpu.get_barrier_semaphore()
 
@@ -107,6 +107,9 @@
 
     signal(me + 1 - 2 * c)
     signal(me + 2 - 4 * y)
+    if across:
+        other = 1 - lax.axis_index("loop")
+        pl.semaphore_signal(barrier, inc=1, device_id={"loop": other}, device_id_type=MESH)
 
     @pl.when(z > 0)
     def _():
@@ -117,7 +120,7 @@
         signal(me + 4)
 
     ends = jnp.where((z > 0) & (z < depth - 1), 4, 3)
-    pl.semaphore_wait(barrier, ends)
+    pl.semaphore_wait(barrier, ends + 1 if across else ends)
 
 
 def contract(left, right, left_axis, right_axis):
@@ -616,6 +619,9 @@
     )(*blocks)
 
 
+FAR_TILES = 3
+
+
 def line_order(z):
     near = z < 2
     return [z, z + 1 - 2 * (z % 2), jnp.where(near, 2, 1), jnp.where(near, 3, 0)]
@@ -825,20 +831,16 @@
             sem((depth, 2)),
         ],
         compiler_params=kernel_params(ident),
-        cost_estimate=pl.CostEstimate(
-            flops=6 * count * height * width * wide,
-            bytes_accessed=20 * width * wide,
-            transcendentals=0,
-        ),
         name="hidden_units",
     )(own, grads, weights)
 
 
 def unit_grads_body(count, parts, units, gate_grads, up_grads, weights, rows_all, grads_all,
-                    input_sum, output_sum, weight_grads,
+                    input_sum, output_sum, gate_out, up_out, down_out, gate_far,
                     bank, rows_in, units_in, made, held, loaded, leaving, core_in, pair_in,
                     line_in, bank_sem, rows_sem, fill_sems, units_sem, made_sem, core_send, core_recv,
-                    pair_send, pair_recv, line_send, line_recv):
+                    pair_send, pair_recv, line_send, line_recv,
+                    far_send, far_recv):
     me, depth, z, y, c = place(count)
     height, wide = input_sum.shape
     width = weights.shape[1]
@@ -848,7 +850,7 @@
     near = z < 2
     order = [jnp.where(near, 3, 0), jnp.where(near, 0, 3), jnp.where(near, 2, 1),
              jnp.where(near, 1, 2)]
-    greet(count)
+    greet(count, True)
 
     def fill(source, at):
         return pltpu.make_async_copy(source, bank.at[at], bank_sem.at[at])
@@ -1016,19 +1018,31 @@
             total[rows_of(s)] = held[...]
 
     tall = units_in.shape[2]
+    each = width // tall
 
     def bring(g, slot):
-        source = (gate_grads, up_grads, units)[g // (width // tall)]
-        cols = pl.ds((g % (width // tall)) * tall, tall)
+        source = (gate_grads, up_grads, units)[g // each]
+        cols = pl.ds((g % each) * tall, tall)
         return pltpu.make_async_copy(source.at[:, cols], units_in.at[slot], units_sem.at[slot])
 
     def put(g, slot):
-        rows = pl.ds((g % (width // tall)) * tall, tall)
+        rows = pl.ds((g % each) * tall, tall)
         return pltpu.make_async_copy(
-            made.at[slot], weight_grads.at[g // (width // tall), rows], made_sem.at[slot]
-        )
-
-    number = 3 * (width // tall)
+            made.at[slot], (gate_out, up_out, down_out)[g // each].at[rows], made_sem.at[slot]
+        )
+
+    def swap(g):
+        rows = pl.ds(g * tall, tall)
+        return pltpu.make_async_remote_copy(
+            src_ref=gate_out.at[rows],
+            dst_ref=gate_far.at[rows],
+            send_sem=far_send.at[g],
+            recv_sem=far_recv.at[g],
+            device_id={"loop": 1 - lax.axis_index("loop")},
+            device_id_type=MESH,
+        )
+
+    number = 3 * each
 
     def weight_product(g):
         slot = g % 2
@@ -1037,7 +1051,9 @@
         bring(g, slot).wait()
         if g >= 2:
             put(g - 2, slot).wait()
-        at = 0 if g < 2 * (width // tall) else 2
+            if g - 2 < FAR_TILES:
+                swap(g - 2).start()
+        at = 0 if g < 2 * each else 2
         tile = 512
 
         def inner(n, carry):
@@ -1061,42 +1077,43 @@
         item.start()
     for item in grad_tail:
         item.start()
+    bring(0, 0).start()
     first_fills[2].wait()
-    for index in range(8):
+    product(1, 0)
+    pair_step(0, 3)
+    product(1, 1)
+    for item in row_fills:
+        item.wait()
+    weight_product(0)
+    weight_product(1)
+    line_step(0, 0)
+    weight_product(2)
+    weight_product(3)
+    line_step(0, 1)
+    for index in range(2, 8):
         product(1, index)
-        if index == 0:
-            pair_step(0, 3)
-        if index >= 2 and index % 2 == 0:
+        if index % 2 == 0:
             pair_step(1, index // 2 - 1)
-        if index == 4:
-            line_step(0, 0)
+        if index == 6:
+            line_step(0, 2)
     finish_sends(1)
     grad_fills = fill_rows(grads_all, 0, 2)
     for item in grad_fills:
         item.start()
-    bring(0, 0).start()
-    for item in row_fills:
-        item.wait()
-    weight_product(0)
+    weight_product(4)
     pair_step(1, 3)
-    line_step(0, 1)
-    weight_product(1)
-    weight_product(2)
-    line_step(0, 2)
-    weight_product(3)
-    weight_product(4)
     line_step(0, 3)
     weight_product(5)
+    last_step(0, input_sum)
     weight_product(6)
-    last_step(0, input_sum)
     weight_product(7)
+    line_step(1, 0)
     for item in grad_tail + grad_fills:
         item.wait()
     weight_product(8)
-    line_step(1, 0)
     weight_product(9)
+    line_step(1, 1)
     weight_product(10)
-    line_step(1, 1)
     weight_product(11)
     line_step(1, 2)
     line_step(1, 3)
@@ -1104,6 +1121,8 @@
 
     for g in (number - 2, number - 1):
         put(g, g % 2).wait()
+    for g in range(FAR_TILES):
+        swap(g).wait()
     for a in range(2):
         for line in range(depth):
             for s in range(parts):
@@ -1126,9 +1145,10 @@
 
     return pl.pallas_call(
         functools.partial(unit_grads_body, count, parts),
-        out_shape=[total, total, jax.ShapeDtypeStruct((3, width, wide), low)],
+        out_shape=[total, total] + [jax.ShapeDtypeStruct((width, wide), low)] * 3
+        + [jax.ShapeDtypeStruct((FAR_TILES * 256, wide), low)],
         in_specs=[anywhere] * 6,
-        out_specs=[inside, inside, anywhere],
+        out_specs=[inside, inside] + [anywhere] * 4,
         scratch_shapes=[
             pltpu.VMEM((4, width, wide), low),
             pltpu.VMEM((2, 2, 2 * height, width), low),
@@ -1151,15 +1171,550 @@
             sem((2, depth, parts)),
             sem((2, depth, parts)),
             sem((2, depth + 1, parts)),
+            sem((FAR_TILES,)),
+            sem((FAR_TILES,)),
         ],
         compiler_params=kernel_params(ident),
-        cost_estimate=pl.CostEstimate(
-            flops=12 * count * height * width * wide,
-            bytes_accessed=40 * width * wide,
-            transcendentals=0,
-        ),
         name="unit_grads",
     )(units, gate_grads, up_grads, weights, rows_all, grads_all)
+
+
+OUT_SPLIT = 1536
+
+
+def sum_plan(count, parts, mine, theirs, core_in, pair_in, line_in, sems):
+    me, depth, z, y, c = place(count)
+    core_send, core_recv, pair_send, pair_recv, line_send, line_recv = sems
+    rows = core_in.shape[1]
+    step = rows // parts
+    near = z < 2
+    order = [
+        jnp.where(near, 3, 0),
+        jnp.where(near, 0, 3),
+        jnp.where(near, 2, 1),
+        jnp.where(near, 1, 2),
+    ]
+
+    def rows_of(s):
+        return pl.ds(s * step, step)
+
+    def to_core(line, pair, s):
+        at = 2 * line + pair
+        return pltpu.make_async_remote_copy(
+            src_ref=theirs(at, rows_of(s)),
+            dst_ref=core_in.at[at, rows_of(s)],
+            send_sem=core_send.at[at, s],
+            recv_sem=core_recv.at[at, s],
+            device_id={"dp": me + 1 - 2 * c},
+            device_id_type=MESH,
+        )
+
+    def to_pair(line, s):
+        return pltpu.make_async_remote_copy(
+            src_ref=mine(2 * line + 1 - y, rows_of(s)),
+            dst_ref=pair_in.at[line, rows_of(s)],
+            send_sem=pair_send.at[line, s],
+            recv_sem=pair_recv.at[line, s],
+            device_id={"dp": me + 2 - 4 * y},
+            device_id_type=MESH,
+        )
+
+    def along(line, slot, s, target):
+        return pltpu.make_async_remote_copy(
+            src_ref=mine(2 * line + y, rows_of(s)),
+            dst_ref=line_in.at[slot, rows_of(s)],
+            send_sem=line_send.at[line, s],
+            recv_sem=line_recv.at[slot, s],
+            device_id={"dp": target},
+            device_id_type=MESH,
+        )
+
+    def send_core(line, pair):
+        for s in range(parts):
+            to_core(line, pair, s).start()
+
+    def pair_step(k):
+        line = order[k]
+        at = 2 * line + 1 - y
+        for s in range(parts):
+            to_core(line, 1 - y, s).wait_recv()
+            block = mine(at, rows_of(s))
+            block[...] = block[...] + core_in[at, rows_of(s)]
+            to_pair(line, s).start()
+
+    def own_sum(line, s):
+        at = 2 * line + y
+        to_core(line, y, s).wait_recv()
+        to_pair(line, s).wait_recv()
+        part = mine(at, rows_of(s))[...].astype(jnp.float32)
+        part += core_in[at, rows_of(s)].astype(jnp.float32)
+        return part + pair_in[line, rows_of(s)].astype(jnp.float32)
+
+    def line_step(k):
+        line = order[k]
+
+        @pl.when(line != z)
+        def _():
+            for s in range(parts):
+                block = mine(2 * line + y, rows_of(s))
+                follows = ((line > z) & (z > 0)) | ((line < z) & (z < depth - 1))
+                part = own_sum(line, s)
+
+                @pl.when(follows)
+                def _():
+                    along(z, line, s, me + 4).wait_recv()
+                    extra = line_in[line, rows_of(s)].astype(jnp.float32)
+                    block[...] = (part + extra).astype(block.dtype)
+
+                @pl.when(jnp.logical_not(follows))
+                def _():
+                    block[...] = part.astype(block.dtype)
+
+                @pl.when(line > z)
+                def _():
+                    along(line, line, s, me + 4).start()
+
+                @pl.when(line < z)
+                def _():
+                    along(line, jnp.where(line == z - 1, depth, line), s, me - 4).start()
+
+    def last_step(total):
+        for s in range(parts):
+            total[rows_of(s)] = own_sum(z, s)
+
+            @pl.when(z > 0)
+            def _():
+                along(z, z, s, me + 4).wait_recv()
+                total[rows_of(s)] += line_in[z, rows_of(s)].astype(jnp.float32)
+
+            @pl.when(z < depth - 1)
+            def _():
+                along(z, depth, s, me + 4).wait_recv()
+                total[rows_of(s)] += line_in[depth, rows_of(s)].astype(jnp.float32)
+
+    def finish():
+        for line in range(depth):
+            for s in range(parts):
+                for pair in range(2):
+                    to_core(line, pair, s).wait_send()
+                to_pair(line, s).wait_send()
+
+                @pl.when(z != line)
+                def _():
+                    along(line, line, s, me + 4).wait_send()
+
+    return order, send_core, pair_step, line_step, last_step, finish
+
+
+def sum_sems(count, parts):
+    depth = count // 4
+    sem = pltpu.SemaphoreType.DMA
+    return [
+        sem((2 * depth, parts)),
+        sem((2 * depth, parts)),
+        sem((depth, parts)),
+        sem((depth, parts)),
+        sem((depth, parts)),
+        sem((depth + 1, parts)),
+    ]
+
+
+def sum_rooms(count, rows, cols, kind=jnp.bfloat16):
+    depth = count // 4
+    return [
+        pltpu.VMEM((2 * depth, rows, cols), kind),
+        pltpu.VMEM((depth, rows, cols), kind),
+        pltpu.VMEM((depth + 1, rows, cols), kind),
+    ]
+
+
+def sum_terms(count, parts, terms, rooms, sems):
+    me, depth, z, y, c = place(count)
+
+    def mine(at, rows):
+        return terms.at[2 * at + c, rows]
+
+    def theirs(at, rows):
+        return terms.at[2 * at + 1 - c, rows]
+
+    return sum_plan(count, parts, mine, theirs, *rooms, sems)
+
+
+def turn_back(values, cosine, sine):
+    half = values.shape[-1] // 2
+    first, second = values[:, :half], values[:, half:]
+    return jnp.concatenate(
+        [first * cosine + second * sine, second * cosine - first * sine], axis=1
+    )
+
+
+def attention_grads_body(count, attended, grad_rows, weight, queries, keys_values, level,
+                         cosine, sine, own_seq, own_order, all_seq, all_order,
+                         joint_grads, out_sum,
+                         weight_in, grad_att, allowed, kv_total, kv_terms, kv_sum, out_terms,
+                         out_core, out_pair, out_line, kv_core, kv_pair, kv_line,
+                         weight_sem, *sems):
+    me, depth, z, y, c = place(count)
+    height, wide = grad_rows.shape
+    size = HEAD_SIZE
+    scale = size ** (-0.5)
+    low = jnp.bfloat16
+    greet(count)
+    load = pltpu.make_async_copy(weight, weight_in, weight_sem)
+    load.start()
+    order, send_out, pair_out, line_out, last_out, finish_out = sum_terms(
+        count, 2, out_terms, (out_core, out_pair, out_line), sems[:6]
+    )
+    _, send_kv, pair_kv, line_kv, last_kv, finish_kv = sum_terms(
+        count, 1, kv_terms, (kv_core, kv_pair, kv_line), sems[6:]
+    )
+    feature, some = out_terms.shape[1:]
+
+    def out_product(line):
+        def inner(n, carry):
+            into = pl.ds(pl.multiple_of(n * 512, 512), 512)
+            cols = pl.ds(pl.multiple_of(line * 4 * feature, 4 * feature), 4 * feature)
+            value = contract(attended[:, cols], grad_rows[:, into], 0, 0).astype(low)
+            out_terms[pl.ds(4 * line, 4), :, into] = value.reshape(4, feature, 512)
+            return carry
+
+        lax.fori_loop(0, some // 512, inner, 0)
+        for pair in (1 - y, y):
+            send_out(line, pair)
+
+    for line in order:
+        out_product(line)
+    load.wait()
+    tile = 256
+
+    def product(n, carry):
+        cols = pl.ds(pl.multiple_of(n * tile, tile), tile)
+        grad_att[:, cols] = contract(grad_rows[...], weight_in[cols], 1, 1).astype(low)
+        return carry
+
+    lax.fori_loop(0, wide // tile, product, 0)
+    same = own_seq[...] == all_seq[...]
+    allowed[...] = jnp.where(same & (all_order[...] <= own_order[...]), 1.0, 0.0)
+    for k in range(depth):
+        pair_out(k)
+    keys = keys_values[:, :size]
+    values = keys_values[:, size:]
+
+    def heads(pair):
+        def both(ref):
+            return jnp.concatenate(
+                [
+                    ref[:, 2 * pair * size : (2 * pair + 1) * size],
+                    ref[:, (2 * pair + 1) * size : (2 * pair + 2) * size],
+                ],
+                axis=0,
+            )
+
+        query = both(queries)
+        grad = both(grad_att)
+        keep = jnp.concatenate([allowed[...], allowed[...]], axis=0) > 0.5
+        scores = jnp.where(keep, contract(query, keys, 1, 1) * scale, FLOOR_SCORE)
+        prob = jnp.exp(scores - level[pair][:, :1])
+        grad_prob = contract(grad, values, 1, 1)
+        centre = jnp.sum(prob * grad_prob, axis=-1, keepdims=True)
+        grad_scores = (prob * (grad_prob - centre)).astype(low)
+        back = contract(grad_scores, keys, 1, 0) * scale
+        for i in range(2):
+            part = turn_back(back[i * height : (i + 1) * height], cosine[...], sine[...])
+            joint_grads[:, (2 * pair + i) * size : (2 * pair + i + 1) * size] = part.astype(low)
+        key_part = contract(grad_scores, query, 0, 0) * scale
+        value_part = contract(prob.astype(low), grad, 0, 0)
+        if pair == 0:
+            kv_total[:, :size] = key_part
+            kv_total[:, size:] = value_part
+        else:
+            kv_total[:, :size] += key_part
+            kv_total[:, size:] += value_part
+
+    for pair in range(wide // size // 2):
+        heads(pair)
+    for block in range(count):
+        kv_terms[block] = kv_total[block * height : (block + 1) * height].astype(low)
+    for pair in (1 - y, y):
+        for line in order:
+            send_kv(line, pair)
+    for k in range(depth):
+        pair_kv(k)
+    for k in range(depth):
+        line_out(k)
+    for k in range(depth):
+        line_kv(k)
+    last_kv(kv_sum)
+    part = turn_back(kv_sum[:, :size], cosine[...], sine[...])
+    joint_grads[:, wide : wide + size] = part.astype(low)
+    joint_grads[:, wide + size :] = kv_sum[:, size:].astype(low)
+    last_out(out_sum)
+    finish_out()
+    finish_kv()
+
+
+def attention_grads(count, ident, attended, grad_rows, weight, queries, keys_values, level,
+                    cosine, sine, own_seq, own_order, all_seq, all_order):
+    height, wide = grad_rows.shape
+    total = keys_values.shape[0]
+    low = jnp.bfloat16
+    inside = pl.BlockSpec(memory_space=pltpu.VMEM)
+    anywhere = pl.BlockSpec(memory_space=pl.ANY)
+    feature = attended.shape[1] // count
+    both = 2 * HEAD_SIZE
+    return pl.pallas_call(
+        functools.partial(attention_grads_body, count),
+        out_shape=[
+            jax.ShapeDtypeStruct((height, wide + both), low),
+            jax.ShapeDtypeStruct((feature, OUT_SPLIT), jnp.float32),
+        ],
+        in_specs=[inside] * 2 + [anywhere] + [inside] * 9,
+        out_specs=[inside] * 2,
+        scratch_shapes=[
+            pltpu.VMEM(weight.shape, low),
+            pltpu.VMEM(attended.shape, low),
+            pltpu.VMEM((height, total), jnp.float32),
+            pltpu.VMEM((total, both), jnp.float32),
+            pltpu.VMEM((count, height, both), low),
+            pltpu.VMEM((height, both), jnp.float32),
+            pltpu.VMEM((count, feature, OUT_SPLIT), low),
+        ]
+        + sum_rooms(count, feature, OUT_SPLIT)
+        + sum_rooms(count, height, both)
+        + [pltpu.SemaphoreType.DMA]
+        + sum_sems(count, 2)
+        + sum_sems(count, 1),
+        compiler_params=kernel_params(ident),
+        name="attention_grads",
+    )(
+        attended, grad_rows, weight, queries, keys_values, level,
+        cosine, sine, own_seq, own_order, all_seq, all_order,
+    )
+
+
+def closing_body(count, normed, joint_grads, attended, grad_rows, lowrank, lowrank_out, stream,
+                 gain, grad_middle, small, weight, gate_grads, up_grads, down_grads, factors,
+                 first, second,
+                 in_sum, out_sum, second_sum, first_sum, small_sum, stream_grad, factor_grads,
+                 bank, factor_bank, first_bank, second_bank, made, in_terms, out_terms,
+                 second_terms, first_terms, small_terms, *scratch):
+    me, depth, z, y, c = place(count)
+    height, wide = normed.shape
+    rank = ADAPTER_RANK
+    width = gate_grads.shape[0]
+    low = jnp.bfloat16
+    rooms = [scratch[3 * i : 3 * i + 3] for i in range(5)]
+    weight_sem, grads_sem, factor_sem, made_sem = scratch[15:19]
+    sems = [scratch[19 + 6 * i : 25 + 6 * i] for i in range(5)]
+    greet(count)
+    halves = [
+        pltpu.make_async_copy(weight.at[pl.ds(i * width, width)], bank, weight_sem.at[i])
+        for i in range(wide // width)
+    ]
+    halves[0].start()
+    loads = [
+        pltpu.make_async_copy(
+            factors.at[pl.ds(me * width, width)], factor_bank, factor_sem.at[0]
+        ),
+        pltpu.make_async_copy(
+            first.at[:, pl.ds(4 * rank, 2 * rank)], first_bank, factor_sem.at[1]
+        ),
+        pltpu.make_async_copy(
+            second.at[:, pl.ds(PROJECTED_WIDTH + MODEL_WIDTH, wide)], second_bank, factor_sem.at[2]
+        ),
+    ]
+    for item in loads:
+        item.start()
+    terms = (in_terms, out_terms, second_terms, first_terms, small_terms)
+    parts = (2, 2, 1, 1, 1)
+    plans = [sum_terms(count, parts[i], terms[i], rooms[i], sems[i]) for i in range(5)]
+    order = plans[0][0]
+    send = [plan[1] for plan in plans]
+    pair_step = [plan[2] for plan in plans]
+    line_step = [plan[3] for plan in plans]
+    last_step = [plan[4] for plan in plans]
+    finish = [plan[5] for plan in plans]
+
+    def block_products(i, left, right, at):
+        feature, some = terms[i].shape[1:]
+
+        def product(line):
+            def inner(n, carry):
+                cols = pl.ds(pl.multiple_of(line * 4 * feature, 4 * feature), 4 * feature)
+                into = pl.ds(pl.multiple_of(n * 512, 512), 512)
+                from_ = pl.ds(pl.multiple_of(at + n * 512, 512), 512)
+                value = contract(left[:, cols], right[:, from_], 0, 0).astype(low)
+                terms[i][pl.ds(4 * line, 4), :, into] = value.reshape(4, feature, 512)
+                return carry
+
+            lax.fori_loop(0, some // 512, inner, 0)
+            for pair in (1 - y, y):
+                send[i](line, pair)
+
+        for line in order:
+            product(line)
+
+    def send_all(i):
+        for pair in (1 - y, y):
+            for line in order:
+                send[i](line, pair)
+        for k in range(depth):
+            pair_step[i](k)
+
+    def put_second(at, value):
+        size = second_terms.shape[1]
+        value = value.astype(low)
+        start = at
+        while start < at + value.shape[0]:
+            block, inner = start // size, start % size
+            rows = min(size - inner, at + value.shape[0] - start)
+            second_terms[block, inner : inner + rows, :] = value[start - at : start - at + rows]
+            start += rows
+
+    def half_product(i):
+        halves[i].wait()
+
+        def product(n, carry):
+            some = pl.ds(pl.multiple_of(n * 256, 256), 256)
+            cols = pl.ds(pl.multiple_of(i * width + n * 256, 256), 256)
+            stream_grad[:, cols] = contract(joint_grads[...], bank[some], 1, 1)
+            return carry
+
+        lax.fori_loop(0, width // 256, product, 0)
+        if i + 1 < len(halves):
+            halves[i + 1].start()
+
+    block_products(0, normed, joint_grads, 0)
+    for k in range(depth):
+        pair_step[0](k)
+    half_product(0)
+    block_products(1, attended, grad_rows, OUT_SPLIT)
+    for k in range(depth):
+        pair_step[1](k)
+    for i in range(1, len(halves)):
+        half_product(i)
+
+    rows = stream[...].astype(jnp.float32)
+    inverse = lax.rsqrt(jnp.mean(rows * rows, axis=-1, keepdims=True) + EPSILON)
+    grad = stream_grad[...]
+    unit = rows * inverse
+    gain_grad = jnp.sum(grad * unit, axis=0, keepdims=True)
+    scaled = grad * gain[...]
+    centre = jnp.mean(scaled * unit, axis=-1, keepdims=True)
+    stream_grad[...] = grad_middle[...] + inverse * (scaled - unit * centre)
+    small_terms[...] = small[...]
+    share = wide // count
+    for block in range(count):
+        small_terms[block, 0:1, :share] = gain_grad[:, block * share : (block + 1) * share]
+    send_all(4)
+
+    def bring(i):
+        source = (gate_grads, up_grads, down_grads)[i]
+        return pltpu.make_async_copy(source, bank.at[:, pl.ds(0, wide)], grads_sem.at[i])
+
+    bring(0).start()
+    line_step[0](0)
+    value_at = QUERY_WIDTH + HEAD_SIZE
+    for at, stop, left, own in (
+        (0, QUERY_WIDTH, joint_grads, lowrank[:, :rank]),
+        (QUERY_WIDTH, value_at, joint_grads, lowrank[:, rank : 2 * rank]),
+        (value_at, PROJECTED_WIDTH, joint_grads, lowrank[:, 2 * rank :]),
+    ):
+        put_second(at, contract(left[:, at:stop], own, 0, 0))
+    put_second(PROJECTED_WIDTH, contract(grad_rows[...], lowrank_out[...], 0, 0))
+    for item in loads:
+        item.wait()
+
+    def put_factor(slot, cols):
+        return pltpu.make_async_copy(
+            made.at[slot], factor_grads.at[:, pl.ds(cols * rank, rank)], made_sem.at[slot]
+        )
+
+    line_step[0](1)
+    held = bank.at[:, pl.ds(0, wide)]
+    for i in range(2):
+        bring(i).wait()
+        made[i] = contract(held[...], first_bank[:, i * rank : (i + 1) * rank], 1, 0)
+        put_factor(i, i + 1).start()
+        value = contract(held[...], factor_bank[:, (i + 1) * rank : (i + 2) * rank], 0, 0)
+        first_terms[:, :, i * rank : (i + 1) * rank] = value.astype(low).reshape(
+            count, wide // count, rank
+        )
+        bring(i + 1).start()
+        if i == 0:
+            line_step[0](2)
+    send_all(3)
+    bring(2).wait()
+    put_factor(0, 1).wait()
+    made[0] = contract(held[...], second_bank[...], 1, 1)
+    put_factor(0, 0).start()
+    put_second(
+        PROJECTED_WIDTH + MODEL_WIDTH, contract(held[...], factor_bank[:, :rank], 0, 0)
+    )
+    send_all(2)
+    line_step[0](3)
+    for k in range(depth):
+        line_step[1](k)
+    last_step[0](in_sum)
+    last_step[1](out_sum)
+    for i, total in ((4, small_sum), (3, first_sum), (2, second_sum)):
+        for k in range(depth):
+            line_step[i](k)
+        last_step[i](total)
+    for item in finish:
+        item()
+    put_factor(0, 0).wait()
+    put_factor(1, 2).wait()
+
+
+def closing(count, ident, normed, joint_grads, attended, grad_rows, lowrank, lowrank_out, stream,
+            gain, grad_middle, small, weight, gate_grads, up_grads, down_grads, factors, first,
+            second):
+    height, wide = normed.shape
+    width = gate_grads.shape[0]
+    low, high = jnp.bfloat16, jnp.float32
+    rank = ADAPTER_RANK
+    inside = pl.BlockSpec(memory_space=pltpu.VMEM)
+    anywhere = pl.BlockSpec(memory_space=pl.ANY)
+    share = wide // count
+    shapes = [
+        (share, joint_grads.shape[1], low),
+        (share, wide - OUT_SPLIT, low),
+        (second.shape[1] // count, rank, low),
+        (share, 2 * rank, low),
+        (8, 128, high),
+    ]
+    sem = pltpu.SemaphoreType.DMA
+    rooms, sems = [], []
+    for (rows, cols, kind), parts in zip(shapes, (2, 2, 1, 1, 1)):
+        rooms += sum_rooms(count, rows, cols, kind)
+        sems += sum_sems(count, parts)
+    return pl.pallas_call(
+        functools.partial(closing_body, count),
+        out_shape=[jax.ShapeDtypeStruct((rows, cols), high) for rows, cols, _ in shapes]
+        + [
+            jax.ShapeDtypeStruct((height, wide), high),
+            jax.ShapeDtypeStruct((width, 3 * rank), high),
+        ],
+        in_specs=[inside] * 10 + [anywhere] * 7,
+        out_specs=[inside] * 6 + [anywhere],
+        scratch_shapes=[
+            pltpu.VMEM((width, weight.shape[1]), low),
+            pltpu.VMEM((width, 3 * rank), low),
+            pltpu.VMEM((wide, 2 * rank), low),
+            pltpu.VMEM((rank, wide), low),
+            pltpu.VMEM((2, width, rank), high),
+        ]
+        + [pltpu.VMEM((count, rows, cols), kind) for rows, cols, kind in shapes]
+        + rooms
+        + [sem((wide // width,)), sem((3,)), sem((3,)), sem((2,))]
+        + sems,
+        compiler_params=kernel_params(ident),
+        name="closing",
+    )(
+        normed, joint_grads, attended, grad_rows, lowrank, lowrank_out, stream, gain, grad_middle,
+        small, weight, gate_grads, up_grads, down_grads, factors, first, second,
+    )
 
 
 def swap_loops(values):
@@ -1268,6 +1823,10 @@
     )
     grad_ffn_all = lax.all_gather(feedforward_gradient, "dp", axis=0, tiled=True)
     query_key_value_linear = matrix_product(normed_input, input_weight)
+    half = HEAD_SIZE // 2
+    freqs = 10000.0 ** (-jnp.arange(half, dtype=jnp.float32) / half)
+    angles = pos_own.astype(jnp.float32)[:, None] * freqs
+    cosine, sine = jnp.cos(angles), jnp.sin(angles)
     queries = rotate(
         query_key_value_linear[:, :QUERY_WIDTH].reshape(local_rows, HEADS, HEAD_SIZE), pos_own
     ).astype(low)
@@ -1283,6 +1842,7 @@
         :, None, :
     ]
     query_rows = queries.reshape(local_rows * HEADS, HEAD_SIZE)
+    queries_flat = queries.reshape(local_rows, QUERY_WIDTH)
 
     def score_rows():
         raw_scores = (outer_columns(query_rows, keys) * scale).reshape(local_rows, HEADS, key_total)
@@ -1292,6 +1852,7 @@
     top_score = jnp.max(scores, axis=-1, keepdims=True)
     expo = jnp.exp(scores - top_score)
     mass = jnp.sum(expo, axis=-1, keepdims=True)
+    level = (top_score + jnp.log(mass))[:, :, 0]
     prob_low = (expo / mass).astype(low)
     attended_rows = (
         matrix_product(prob_low.reshape(local_rows * HEADS, key_total), values)
@@ -1306,10 +1867,9 @@
         units_own, grad_gate_own, grad_up_own, normed_blocks = hidden_units(
             count, 3, second_normed_input, grad_blocks, ffn_folded
         )
-        second_normed_gradient, ffn_sum, weight_grads = unit_grads(
+        second_normed_gradient, ffn_sum, gate_grad, up_grad, down_grad, gate_other = unit_grads(
             count, 4, units_own, grad_gate_own, grad_up_own, ffn_folded, normed_blocks, grad_blocks
         )
-        gate_grad, up_grad, down_grad = weight_grads
     else:
         (normed_all,) = gather_rows(count, 3, second_normed_input)
         gate_weight, up_weight, down_weight = ffn_folded
@@ -1328,9 +1888,13 @@
             matrix_product(grad_gate_own, gate_weight) + matrix_product(grad_up_own, up_weight)
         ).astype(low)
         ffn_sum, second_normed_gradient = scatter_rows(count, 4, ffn_terms, input_terms)
-        weight_grads = jnp.stack([gate_grad, up_grad, down_grad])
-    weight_other = swap_loops(weight_grads)
-    complete_output = middle_state + active_mask * ffn_sum
+        gate_other = swap_loops(gate_grad)
+    if count == LINE_DEVICES:
+        gate_last = swap_loops(gate_grad[FAR_TILES * 256 :])
+        gate_other = jnp.concatenate([gate_other, gate_last], axis=0)
+    up_other = swap_loops(up_grad)
+    down_other = swap_loops(down_grad)
+    complete_output = middle_state + active_mask * ffn_sum.astype(jnp.float32)
     confidence = root_mean(residual_stream) / (
         root_mean(residual_stream) + root_mean(complete_output - residual_stream)
     )
@@ -1341,73 +1905,99 @@
     ).astype(jnp.float32)
     stats = jnp.concatenate([conf_sum[None], jnp.sum(depth_hits, axis=0)])
 
-    adapter_hidden_gradient = jnp.concatenate(
-        [
-            outer_columns(down_grad, second_down),
-            matrix_product(gate_grad, first_gate),
-            matrix_product(up_grad, first_up),
-        ],
-        axis=1,
-    )
-    first_terms = jnp.concatenate(
-        [inner_rows(gate_grad, gate_factor), inner_rows(up_grad, up_factor)], axis=1
-    ).astype(low)
     grad_middle_part, grad_gain_two = jax.vjp(norm_rows, middle_state, layer_norm_gains[1])[1](
         second_normed_gradient
     )
     grad_middle = grad_out + grad_middle_part
     branch_gradient = (active_mask * grad_middle).astype(low)
-    grad_attended = outer_columns(branch_gradient, output_weight).astype(low)
-    grad_att_rows = grad_attended.reshape(local_rows * HEADS, HEAD_SIZE)
-    prob = jnp.exp(score_rows() - top_score) / mass
-    grad_prob = outer_columns(grad_att_rows, values).reshape(local_rows, HEADS, key_total)
-    centre = jnp.sum(prob * grad_prob, axis=-1, keepdims=True)
-    grad_scores = (
-        (prob * (grad_prob - centre)).astype(low).reshape(local_rows * HEADS, key_total)
-    )
-    prob_again = prob.astype(low).reshape(local_rows * HEADS, key_total)
-    kv_terms = jnp.concatenate(
-        [inner_rows(grad_scores, query_rows) * scale, inner_rows(prob_again, grad_att_rows)], axis=1
-    ).astype(low)
-    grad_kv, first_grad_hidden = scatter_rows(count, 5, kv_terms, first_terms)
-    grad_queries = (matrix_product(grad_scores, keys) * scale).reshape(local_rows, HEADS, HEAD_SIZE)
-    query_linear_gradient = (
-        rotate_back(grad_queries, pos_own).reshape(local_rows, QUERY_WIDTH).astype(low)
-    )
-    key_linear_gradient = rotate_back(grad_kv[:, None, :HEAD_SIZE], pos_own)[:, 0].astype(low)
-    value_linear_gradient = grad_kv[:, HEAD_SIZE:].astype(low)
-    query_key_value_gradient = jnp.concatenate(
-        [query_linear_gradient, key_linear_gradient, value_linear_gradient], axis=1
-    )
-    normed_gradient = outer_columns(query_key_value_gradient, input_weight)
-    grad_resid_part, grad_gain_one = jax.vjp(norm_rows, residual_stream, layer_norm_gains[0])[1](
-        normed_gradient
-    )
-    hidden_grad = grad_middle + grad_resid_part
-
+    width_own = MODEL_WIDTH // count
+    small = jnp.zeros((count, 8, 128), jnp.float32)
+    small = small.at[:, 1, :width_own].set(grad_gain_two.reshape(count, width_own))
+    small = small.at[:, 2, : loop_count + 2].set(stats[None])
     lowrank_projection = matrix_product(normed_input, adapter_first[:, : 3 * rank]).astype(low)
     output_projection = matrix_product(
         attended_rows, adapter_first[:, 3 * rank : 4 * rank]
     ).astype(low)
-    second_terms = jnp.concatenate(
-        [
-            inner_rows(query_linear_gradient, lowrank_projection[:, :rank]),
-            inner_rows(key_linear_gradient, lowrank_projection[:, rank : 2 * rank]),
-            inner_rows(value_linear_gradient, lowrank_projection[:, 2 * rank :]),
-            inner_rows(branch_gradient, output_projection),
-            inner_rows(down_grad, down_factor),
-        ],
-        axis=0,
-    ).astype(low)
-    in_terms = inner_rows(normed_input, query_key_value_gradient).astype(low)
-    out_terms = inner_rows(attended_rows, branch_gradient).astype(low)
-    width_own = MODEL_WIDTH // count
-    gain_rows = jnp.stack([grad_gain_one, grad_gain_two]).reshape(2, count, width_own)
-    small = jnp.zeros((count, 8, 128), jnp.float32)
-    small = small.at[:, :2, :width_own].set(jnp.swapaxes(gain_rows, 0, 1))
-    small = small.at[:, 2, : loop_count + 2].set(stats[None])
-    in_portion, out_portion, second_grad, small_sum = scatter_rows(
-        count, 6, in_terms, out_terms, second_terms, small.reshape(count * 8, 128)
+    if count == LINE_DEVICES:
+        steps = jnp.transpose(level).reshape(HEADS // 2, 2 * local_rows, 1)
+        joint_grads, out_first = attention_grads(
+            count, 5, attended_rows, branch_gradient, output_weight, queries_flat, kv_all,
+            jnp.broadcast_to(steps, steps.shape[:2] + (128,)), cosine, sine, seq_own[:, None],
+            order_own[:, None], seq_all[None], order_all[None],
+        )
+        (
+            in_portion, out_last, second_grad, first_grad_hidden, small_sum, hidden_grad,
+            adapter_hidden_gradient,
+        ) = closing(
+            count, 6, normed_input, joint_grads, attended_rows, branch_gradient, lowrank_projection,
+            output_projection, layer_input_stream[0], layer_norm_gains[:1], grad_middle, small,
+            input_weight, gate_grad, up_grad, down_grad, adapter_hidden_factors[0], adapter_first,
+            adapter_second,
+        )
+        out_portion = jnp.concatenate([out_first, out_last], axis=1)
+    else:
+        grad_attended = outer_columns(branch_gradient, output_weight).astype(low)
+        grad_att_rows = grad_attended.reshape(local_rows * HEADS, HEAD_SIZE)
+        prob = jnp.exp(score_rows() - level[:, :, None])
+        grad_prob = outer_columns(grad_att_rows, values).reshape(local_rows, HEADS, key_total)
+        centre = jnp.sum(prob * grad_prob, axis=-1, keepdims=True)
+        grad_scores = (
+            (prob * (grad_prob - centre)).astype(low).reshape(local_rows * HEADS, key_total)
+        )
+        prob_again = prob.astype(low).reshape(local_rows * HEADS, key_total)
+        kv_terms = jnp.concatenate(
+            [inner_rows(grad_scores, query_rows) * scale, inner_rows(prob_again, grad_att_rows)],
+            axis=1,
+        ).astype(low)
+        (grad_kv,) = scatter_rows(count, 5, kv_terms)
+        grad_queries = (matrix_product(grad_scores, keys) * scale).reshape(
+            local_rows, HEADS, HEAD_SIZE
+        )
+        query_key_value_gradient = jnp.concatenate(
+            [
+                rotate_back(grad_queries, pos_own).reshape(local_rows, QUERY_WIDTH),
+                rotate_back(grad_kv[:, None, :HEAD_SIZE], pos_own)[:, 0],
+                grad_kv[:, HEAD_SIZE:],
+            ],
+            axis=1,
+        ).astype(low)
+        normed_gradient = outer_columns(query_key_value_gradient, input_weight)
+        grad_resid_part, grad_gain_one = jax.vjp(norm_rows, residual_stream, layer_norm_gains[0])[1](
+            normed_gradient
+        )
+        hidden_grad = grad_middle + grad_resid_part
+        small = small.at[:, 0, :width_own].set(grad_gain_one.reshape(count, width_own))
+        second_terms = jnp.concatenate(
+            [
+                inner_rows(query_key_value_gradient[:, :key_at], lowrank_projection[:, :rank]),
+                inner_rows(
+                    query_key_value_gradient[:, key_at:value_at],
+                    lowrank_projection[:, rank : 2 * rank],
+                ),
+                inner_rows(query_key_value_gradient[:, value_at:], lowrank_projection[:, 2 * rank :]),
+                inner_rows(branch_gradient, output_projection),
+                inner_rows(down_grad, down_factor),
+            ],
+            axis=0,
+        ).astype(low)
+        in_terms = inner_rows(normed_input, query_key_value_gradient).astype(low)
+        out_terms = inner_rows(attended_rows, branch_gradient).astype(low)
+        first_terms = jnp.concatenate(
+            [inner_rows(gate_grad, gate_factor), inner_rows(up_grad, up_factor)], axis=1
+        ).astype(low)
+        in_portion, out_portion, second_grad, first_grad_hidden, small_sum = scatter_rows(
+            count, 6, in_terms, out_terms, second_terms, first_terms, small.reshape(count * 8, 128)
+        )
+        adapter_hidden_gradient = jnp.concatenate(
+            [
+                outer_columns(down_grad, second_down),
+                matrix_product(gate_grad, first_gate),
+                matrix_product(up_grad, first_up),
+            ],
+            axis=1,
+        )
+    gate_other, up_other, down_other, small_sum = lax.optimization_barrier(
+        (gate_other, up_other, down_other, small_sum)
     )
     in_low = in_portion.astype(low)
     out_low = out_portion.astype(low)
@@ -1426,8 +2016,13 @@
     depth_total = small_total[2, 1 : loop_count + 2]
     mean_confidence = small_total[2, 0] / jnp.sum(depth_total)
     exit_counts = depth_total.astype(jnp.int32)
-    sum_mlp = jnp.swapaxes(
-        weight_grads.astype(jnp.float32) + weight_other.astype(jnp.float32), 0, 1
+    sum_mlp = jnp.stack(
+        [
+            gate_grad.astype(jnp.float32) + gate_other.astype(jnp.float32),
+            up_grad.astype(jnp.float32) + up_other.astype(jnp.float32),
+            down_grad.astype(jnp.float32) + down_other.astype(jnp.float32),
+        ],
+        axis=1,
     )
     return (
         complete_output.astype(low)[None],

time: 774 us -> 706 us (0.912)
  matrix products: 104 us -> 26.8 us
  local copies, waits for them, and re-layouts: 55.6 us -> 15.9 us
  waiting for transfers between devices: 0.03 us -> 34.1 us
  Pallas kernels: 519 us -> 550 us
  other arithmetic: 68.1 us -> 49 us
    pallas_call x2, Pallas kernels: 171 us -> 208 us  [the longest x1 133 us: closing(): pl.pallas_call(functools.partial(closing_body, count), out_shape=[jax.Sha...]
    dot_general x11 -> x0, matrix products: 36.1 us -> none  [inner_rows(): lax.dot_general(left, right, (((0,), (0,)), ((), ())), preferred_element_...]
    dot_general x9 -> x5, matrix products: 36.8 us -> 4.77 us  [outer_columns(): lax.dot_general(left, right, (((1,), (1,)), ((), ())), preferred_element_...]
    dot_general x4 -> x0, local copies, waits for them, and re-layouts: 25.8 us -> none  [inner_rows(): lax.dot_general(left, right, (((0,), (0,)), ((), ())), preferred_element_...]
    another operation x4 -> x8, other arithmetic: 0.73 us -> 25.8 us  [the longest x3 22.4 us: per_device(): jnp.stack([gate_grad.astype(jnp.float32) + gate_other.astype(jnp.float32)...]
    transpose x1 -> x0, other arithmetic: 18.6 us -> none  [per_device(): jnp.swapaxes(weight_grads.astype(jnp.float32) + weight_other.astype(jnp.f...]
    all_gather x1, waiting for transfers between devices: 0.01 us -> 18.5 us  [per_device(): lax.all_gather(feedforward_gradient, 'dp', axis=0, tiled=True)]
    ppermute x4 -> x6, waiting for transfers between devices: 0.01 us -> 15.6 us  [swap_loops(): return lax.ppermute(values, 'loop', [(0, 1), (1, 0)])]
  transfers between devices with their start and end apart: 5 -> 7, of which waited for: 0 -> 3; matrix products, arithmetic and copies ran while one was open for 24% -> 10% of each run, Pallas kernels for 27% -> 35%
where the time goes in v3:
time: 706 us; the launch traced here: 701 us
  Pallas kernels  550 us (78%)
  other arithmetic  49 us (7%)
  waiting for transfers between devices  34.1 us (5%)
  matrix products  26.8 us (4%)
  between operations  17.7 us (3%)
  local copies, waits for them, and re-layouts  15.9 us (2%)
  starting transfers between devices  7.84 us (1%)
    pallas_call x1, Pallas kernels, closing(): pl.pallas_call(functools.partial(closing_body, count), out_shape=[jax.Sha...  133 us
    pallas_call x1, Pallas kernels, unit_grads(): pl.pallas_call(functools.partial(unit_grads_body, count, parts), out_shap...  122 us
    pallas_call x1, Pallas kernels, opening(): pl.pallas_call(functools.partial(opening_body, count, parts, number), out...  109 us
    pallas_call x1, Pallas kernels, hidden_units(): pl.pallas_call(functools.partial(hidden_body, count, parts), out_shape=[a...  75.9 us
    pallas_call x1, Pallas kernels, attention_grads(): pl.pallas_call(functools.partial(attention_grads_body, count), out_shape=...  74.7 us
    pallas_call x1, Pallas kernels, gather_rows(): pl.pallas_call(functools.partial(gather_body, count, parts, number), out_...  34.9 us
    another operation x3, other arithmetic, per_device(): jnp.stack([gate_grad.astype(jnp.float32) + gate_other.astype(jnp.float32)...  22.4 us
    dot_general x9, matrix products, matrix_product(): return jnp.dot(left, right, preferred_element_type=jnp.float32)  22 us
  transfers between devices with their start and end apart: 7, of which 3 were waited for; matrix products, arithmetic and copies ran while one was open for 10% of the time, Pallas kernels for 35%

profile of v3, /device:TPU:0, one launch (start us, length us, event | category | flops | bytes accessed | tf_op | source)
XLA Modules:
  0.0 700.9 jit_solution(9997530252230601324)
XLA Ops:
  8.3 1.5 fusion.25
  12.0 2.5 fusion.6.refs_1_
  17.5 2.0 fusion.12
  20.5 109.3 %opening.1 = (bf16[16,128,2560]{2,1,0:T(8,128)(2,1)}, bf16[16,128,2048]{2,1,0:T(8,128)(2,1)}, bf16[3,1024,2048]{2,1,0:T(8,128)(2,1)}) custom-call(bf16[128,2560]{1,0:T(8,128)(2,1)} %fusion.7.refs_0_, bf16[128,2048]{1,0:T(8,128)(2,1)} %fusion.6.refs_1_, bf16[3,1024,2048]{2,1,0:T(8,128)(2,1)} %bitcast.112, bf16[16384,768]{1,0:T(8,128)(2,1)} %bitcast.87, ...), custom_call_target="tpu_custom_call" | custom-call | tf_op jit(solution)/shard_map/opening/pallas_call | solution.py:401
  130.3 5.7 fusion.63
  137.8 34.9 %gather_rows.1 = bf16[16,128,512]{2,1,0:T(8,128)(2,1)} custom-call(bf16[128,512]{1,0:T(8,128)(2,1)} %pad_maximum_fusion.4.refs_0_), custom_call_target="tpu_custom_call" | custom-call | tf_op jit(solution)/shard_map/gather_rows/pallas_call | solution.py:301
  173.5 3.4 fusion
  176.9 2.9 fusion.1
  179.9 2.7 fusion.8
  186.4 5.2 multiply_reduce_fusion.2
  194.8 18.5 %all-gather.2.cloned.1.call-done = bf16[2048,2048]{1,0:T(8,128)(2,1)} async-done(((bf16[128,2048]{1,0:T(8,128)(2,1)}), bf16[2048,2048]{1,0:T(8,128)(2,1)}) %all-gather.2.cloned.1.call-update) | async-done | bytes 8388624 | tf_op jit(solution)/shard_map/all_gather | solution.py:1824
  213.3 75.9 %hidden_units.1 = (bf16[2048,1024]{1,0:T(8,128)(2,1)}, bf16[2048,1024]{1,0:T(8,128)(2,1)}, bf16[2048,1024]{1,0:T(8,128)(2,1)}, bf16[16,128,2048]{2,1,0:T(8,128)(2,1)}) custom-call(bf16[128,2048]{1,0:T(8,128)(2,1)} %multiply_convert_fusion.1.own, bf16[16,128,2048]{2,1,0:T(8,128)(2,1)} %bitcast.93, bf16[3,1024,2048]{2,1,0:T(8,128)(2,1)} %get-tuple-element.67.weights), custom_call_target="tpu_custom_call" | custom-call | tf_op jit(solution)/shard_map/hidden_units/pallas_call | solution.py:813
  289.2 121.6 %unit_grads.1 = (f32[128,2048]{1,0:T(8,128)}, f32[128,2048]{1,0:T(8,128)}, bf16[1024,2048]{1,0:T(8,128)(2,1)}, bf16[1024,2048]{1,0:T(8,128)(2,1)}, bf16[1024,204...) custom-call(bf16[2048,1024]{1,0:T(8,128)(2,1)} %get-tuple-element.68.units, bf16[2048,1024]{1,0:T(8,128)(2,1)} %get-tuple-element.69.gate_grads, ...), custom_call_target="tpu_custom_call" | custom-call | tf_op jit(solution)/shard_map/unit_grads/pallas_call | solution.py:1146
  410.8 2.4 slice.153
  413.3 1.5 collective-permute-start.2
  415.3 1.5 collective-permute-start.4
  416.7 2.7 multiply_reduce_fusion
  421.2 1.5 multiply_convert_fusion
  423.7 74.7 %attention_grads.1 = (bf16[128,2560]{1,0:T(8,128)(2,1)}, f32[128,1536]{1,0:T(8,128)}) custom-call(bf16[128,2048]{1,0:T(8,128)(2,1)} %convert_element_type.126.attended, bf16[128,2048]{1,0:T(8,128)(2,1)} %get-tuple-element.94.grad_rows, bf16[2048,2048]{1,0:T(8,128)(2,1)} %bitcast.92, bf16[128,2048]{1,0:T(8,128)(2,1)} %bitcast.119, ...), custom_call_target="tpu_custom_call" | custom-call | tf_op jit(solution)/shard_map/attention_grads/pallas_call | solution.py:1465
  498.5 133.1 %closing.1 = (f32[128,2560]{1,0:T(8,128)}, f32[128,512]{1,0:T(8,128)}, f32[416,256]{1,0:T(8,128)}, f32[128,512]{1,0:T(8,128)}, f32[8,128]{1,0:T(8,128)}, /*index=5*/f32[128,2048]{1,0:T(8,128)}, f32[1024,768]{1,0:T(8,128)}) custom-call(bf16[128,2048]{1,0:T(8,128)(2,1)} %copy-done.7, bf16[128,2560]{1,0:T(8,128)(2,1)} %get-tuple-element.74.joint_grads, ...), custom_call_target="tpu_custom_call" | custom-call | tf_op jit(solution)/shard_map/closing/pallas_call | solution.py:1692
  631.6 1.5 convert_element_type.134
  635.3 2.4 collective-permute-start.1
  639.3 9.6 %collective-permute-done.1 = bf16[128,2048]{1,0:T(8,128)(2,1)S(1)} collective-permute-done((bf16[128,2048]{1,0:T(8,128)(2,1)S(1)}, bf16[128,2048]{1,0:T(8,128)(2,1)S(1)}, u32[]{:S(2)}, u32[]{:S(2)}) %collective-permute-start.1) | collective-permute-done | bytes 524320 | tf_op jit(solution)/shard_map/ppermute | solution.py:1723
  650.0 5.9 collective-permute-done
  657.2 1.6 pad_maximum_fusion.1
  658.8 1.8 collective-permute-start.5
  660.6 1.9 add_bitcast_fusion.2
  662.6 8.3 %add_bitcast_fusion = (f32[1024,1,2048]{2,0,1:T(8,128)S(1)}, f32[1024,1,2048]{2,0,1:T(8,128)}) fusion(bf16[1024,2048]{1,0:T(8,128)(2,1)} %collective-permute-done.4, bf16[1024,2048]{1,0:T(8,128)(2,1)} %get-tuple-element.77.down_grads, bf16[1024,2048]{1,0:T(8,128)(2,1)} %collective-permute-done.3, bf16[1024,2048]{1,0:T(8,128)(2,1)S(1)} %copy-done.2), kind=kLoop, calls=%fused_computation.1 | loop fusion | flops 12582912 | bytes 33554432 | tf_op jit(solution)/shard_map/stack | solution.py:2019
  670.8 12.2 %pad_maximum_fusion = f32[1024,3,2048]{2,0,1:T(8,128)} fusion(f32[1024,1,2048]{2,0,1:T(8,128)S(1)} %get-tuple-element.117, f32[1024,1,2048]{2,0,1:T(8,128)} %get-tuple-element.118, f32[1024,1,2048]{2,0,1:T(8,128)S(1)} %add_bitcast_fusion.2), kind=kLoop, calls=%fused_computation | loop fusion | flops 12582912 | bytes 50331648 | tf_op jit(solution)/shard_map/stack | solution.py:2019
  686.6 2.3 copy.43
  688.9 1.8 copy.44
  690.7 1.7 copy.45
  (132 shorter events, 28.6 us)
Async XLA Ops:
  7.2 12.3 %copy-start.14 = (bf16[128,2560]{1,0:T(8,128)(2,1)S(1)}, bf16[128,2560]{1,0:T(8,128)(2,1)}, u32[]{:S(2)}) copy-start(bf16[128,2560]{1,0:T(8,128)(2,1)} %param.18) | copy-start | bytes 1966084
  7.2 206.1 %all-gather.2.cloned.1.call-start = ((), (), s32[]{:S(2)}) async-start(), calls=%async_computation | async-start | bytes 8912896 | tf_op jit(solution)/shard_map/all_gather | solution.py:1824
  20.5 109.4 %copy-start.3 = (bf16[1,128,2048]{2,1,0:T(8,128)(2,1)S(1)}, bf16[1,128,2048]{2,1,0:T(8,128)(2,1)}, u32[]{:S(2)}) copy-start(bf16[1,128,2048]{2,1,0:T(8,128)(2,1)} %param.16) | copy-start | bytes 1572868
  20.5 109.6 %copy-start.23 = (f32[2,2048]{1,0:T(2,128)S(1)}, f32[2,2048]{1,0:T(2,128)}, u32[]{:S(2)}) copy-start(f32[2,2048]{1,0:T(2,128)} %param.21) | copy-start | bytes 49156
  130.1 6.0 copy-start.20
  130.3 5.8 copy-start.7
  130.3 6.2 copy-start.27
  130.3 6.3 copy-start.19
  173.2 6.7 copy-start.21
  173.2 6.7 copy-start.22
  179.9 6.4 copy-start.25
  183.8 7.8 %slice-start = ((s8[6291456]{0:T(1024)(128)(4,1)}), s8[2097152]{0:T(1024)(128)(4,1)S(1)}, s32[]{:S(2)}) async-start(s8[6291456]{0:T(1024)(128)(4,1)} %bitcast.97), calls=%async_computation.1 | async-start | bytes 4194304
  186.4 5.3 copy-start.5
  186.4 6.2 copy-start.8
  289.2 127.5 %copy-start.4 = (bf16[1,128,2048]{2,1,0:T(8,128)(2,1)S(1)}, bf16[1,128,2048]{2,1,0:T(8,128)(2,1)}, u32[]{:S(2)}) copy-start(bf16[1,128,2048]{2,1,0:T(8,128)(2,1)} %param.16) | copy-start | bytes 1572868
  410.8 10.4 %copy-start.10 = (f32[128,2048]{1,0:T(8,128)S(1)}, f32[128,2048]{1,0:T(8,128)}, u32[]{:S(2)}) copy-start(f32[128,2048]{1,0:T(8,128)} %get-tuple-element.73) | copy-start | bytes 3145732
  410.8 10.4 %copy-start.13 = (bf16[1,128,2048]{2,1,0:T(8,128)(2,1)S(1)}, bf16[1,128,2048]{2,1,0:T(8,128)(2,1)}, u32[]{:S(2)}) copy-start(bf16[1,128,2048]{2,1,0:T(8,128)(2,1)} %param.17) | copy-start | bytes 1572868
  413.3 243.9 %collective-permute-start.2 = (bf16[256,2048]{1,0:T(8,128)(2,1)}, bf16[256,2048]{1,0:T(8,128)(2,1)}, u32[]{:S(2)}, u32[]{:S(2)}) collective-permute-start(bf16[256,2048]{1,0:T(8,128)(2,1)} %slice.153), channel_id=1, source_target_pairs={{0,16},{16,0},{1,17},{17,1},{2,18},{18,2},{3,19},{19,3},{4,20},{20... | collective-permute-start | bytes 3145736 | tf_op jit(solution)/shard_map/ppermute | solution.py:1723
  414.7 244.1 %collective-permute-start.3 = (bf16[1024,2048]{1,0:T(8,128)(2,1)}, bf16[1024,2048]{1,0:T(8,128)(2,1)}, u32[]{:S(2)}, u32[]{:S(2)}) collective-permute-start(bf16[1024,2048]{1,0:T(8,128)(2,1)} %get-tuple-element.76.up_grads), channel_id=1, source_target_pairs={{0,16},{16,0},{1,17},{17,1},{2,18},{18,2},{3,19},{19,3},{4,20},{20... | collective-permute-start | bytes 12582920 | tf_op jit(solution)/shard_map/ppermute | solution.py:1723
  415.3 243.5 %collective-permute-start.4 = (bf16[1024,2048]{1,0:T(8,128)(2,1)}, bf16[1024,2048]{1,0:T(8,128)(2,1)}, u32[]{:S(2)}, u32[]{:S(2)}) collective-permute-start(bf16[1024,2048]{1,0:T(8,128)(2,1)} %get-tuple-element.77.down_grads), channel_id=1, source_target_pairs={{0,16},{16,0},{1,17},{17,1},{2,18},{18,2},{3,19},{19,3},{4,20},{20... | collective-permute-start | bytes 12582920 | tf_op jit(solution)/shard_map/ppermute | solution.py:1723
  421.2 77.3 %copy-start.17 = (f32[16,8,128]{2,1,0:T(8,128)}, f32[16,8,128]{2,1,0:T(8,128)S(1)}, u32[]{:S(2)}) copy-start(f32[16,8,128]{2,1,0:T(8,128)S(1)} %scatter.9.small) | copy-start | bytes 196612
  498.5 139.4 %copy-start = (bf16[1,256,6656]{2,1,0:T(8,128)(2,1)S(1)}, bf16[1,256,6656]{2,1,0:T(8,128)(2,1)}, u32[]{:S(2)}) copy-start(bf16[1,256,6656]{2,1,0:T(8,128)(2,1)} %param.23) | copy-start | bytes 10223620
  631.6 7.6 %copy-start.18 = (f32[128,512]{1,0:T(8,128)S(1)}, f32[128,512]{1,0:T(8,128)}, u32[]{:S(2)}) copy-start(f32[128,512]{1,0:T(8,128)} %get-tuple-element.88) | copy-start | bytes 786436
  631.6 24.4 %copy-start.9 = (f32[128,2560]{1,0:T(8,128)S(1)}, f32[128,2560]{1,0:T(8,128)}, u32[]{:S(2)}) copy-start(f32[128,2560]{1,0:T(8,128)} %get-tuple-element.79) | copy-start | bytes 3932164
  635.3 21.9 %copy-start.12 = (bf16[768,2048]{1,0:T(8,128)(2,1)S(1)}, bf16[768,2048]{1,0:T(8,128)(2,1)}, u32[]{:S(2)}) copy-start(bf16[768,2048]{1,0:T(8,128)(2,1)} %get-tuple-element.82) | copy-start | bytes 9437188
  635.3 13.6 %collective-permute-start.1 = (bf16[128,2048]{1,0:T(8,128)(2,1)S(1)}, bf16[128,2048]{1,0:T(8,128)(2,1)S(1)}, u32[]{:S(2)}, u32[]{:S(2)}) collective-permute-start(bf16[128,2048]{1,0:T(8,128)(2,1)S(1)} %pad_maximum_fusion.3), channel_id=1, source_target_pairs={{0,16},{16,0},{1,17},{17,1},{2,18},{18,2},{3,19},{19,3},{4,20},{20... | collective-permute-start | bytes 1572872 | tf_op jit(solution)/shard_map/ppermute | solution.py:1723
  637.8 18.2 %collective-permute-start = (bf16[128,2560]{1,0:T(8,128)(2,1)S(1)}, bf16[128,2560]{1,0:T(8,128)(2,1)S(1)}, u32[]{:S(2)}, u32[]{:S(2)}) collective-permute-start(bf16[128,2560]{1,0:T(8,128)(2,1)S(1)} %convert_element_type.134), channel_id=1, source_target_pairs={{0,16},{16,0},{1,17},{17,1},{2,18},{18,2},{3,19},{19,3},{4,20},{20... | collective-permute-start | bytes 1966088 | tf_op jit(solution)/shard_map/ppermute | solution.py:1723
  639.3 19.5 %copy-start.26 = (f32[128,1536]{1,0:T(8,128)}, f32[128,1536]{1,0:T(8,128)S(1)}, u32[]{:S(2)}) copy-start(f32[128,1536]{1,0:T(8,128)S(1)} %constant_dynamic-update-slice_fusion) | copy-start | bytes 2359300
  650.0 8.8 %copy-start.24 = (f32[8,128]{1,0:T(8,128)S(1)}, f32[8,128]{1,0:T(8,128)}, u32[]{:S(2)}) copy-start(f32[8,128]{1,0:T(8,128)} %get-tuple-element.87) | copy-start | bytes 12292
  650.0 10.6 %copy-start.1 = (bf16[1024,2048]{1,0:T(8,128)(2,1)S(1)}, bf16[1024,2048]{1,0:T(8,128)(2,1)}, u32[]{:S(2)}) copy-start(bf16[1024,2048]{1,0:T(8,128)(2,1)} %get-tuple-element.75.gate_grads) | copy-start | bytes 12582916
  658.8 24.2 %collective-permute-start.5 = (f32[8,128]{1,0:T(8,128)S(1)}, f32[8,128]{1,0:T(8,128)S(1)}, u32[]{:S(2)}, u32[]{:S(2)}) collective-permute-start(f32[8,128]{1,0:T(8,128)S(1)} %copy-done.24), channel_id=1, source_target_pairs={{0,16},{16,0},{1,17},{17,1},{2,18},{18,2},{3,19},{19,3},{4,20},{20... | collective-permute-start | bytes 12296 | tf_op jit(solution)/shard_map/ppermute | solution.py:1723
  670.8 19.9 %copy-start.11 = (f32[1024,768]{1,0:T(8,128)S(1)}, f32[1024,768]{1,0:T(8,128)}, u32[]{:S(2)}) copy-start(f32[1024,768]{1,0:T(8,128)} %get-tuple-element.90) | copy-start | bytes 9437188
  (5 other events, 19.8 us)
Sparse Core Ops, SparseCore 0:
  130.0 83.2 all-gather.1

commit v4 on v3

--- a/solution.py
+++ b/solution.py
@@ -20,6 +20,10 @@
 MESH = pl.DeviceIdType.MESH
 VMEM_LIMIT = 60 * 1024 * 1024
 LINE_DEVICES = 16
+FAR_TILES = 3
+OUT_SPLIT = 1536
+IN_SHARE = 48
+OUT_SHARE = 32
 
 
 def matrix_product(left, right):
@@ -132,18 +136,16 @@
     )
 
 
-def gather_plan(count, parts, own, full, keep, recv, send_core, send_pair, send_right, send_left):
+def gather_plan(count, spans, own, full, sems, far_sems=None):
+    keep, recv, send_core, send_pair, send_right, send_left = sems
     arrays = len(own)
     me, depth, z, y, c = place(count)
     mate = me + 2 - 4 * y
-
-    def rows_of(a, s):
-        step = own[a].shape[0] // parts
-        return pl.ds(s * step, step)
+    core = me + 1 - 2 * c
 
     def copy(unit, block, target, sem, first=False):
         a, s = unit
-        rows = rows_of(a, s)
+        rows = pl.ds(*spans[a][s])
         return pltpu.make_async_remote_copy(
             src_ref=own[a].at[rows] if first else full[a].at[block, rows],
             dst_ref=full[a].at[block, rows],
@@ -155,7 +157,7 @@
 
     def to_core(unit, block, first=False):
         a, s = unit
-        return copy(unit, block, me + 1 - 2 * c, send_core.at[a, block // 2, s], first)
+        return copy(unit, block, core, send_core.at[a, block // 2, s], first)
 
     def to_pair(unit, block, first=False):
         a, s = unit
@@ -169,8 +171,34 @@
         a, s = unit
         return copy(unit, block, me - 4, send_left.at[a, block // 4, s], first)
 
+    def to_far(a, block):
+        rows = pl.ds(*spans[a][0])
+        return pltpu.make_async_remote_copy(
+            src_ref=full[a].at[block, rows],
+            dst_ref=full[a].at[block, rows],
+            send_sem=far_sems[0].at[a, block // 2],
+            recv_sem=far_sems[1].at[a, block],
+            device_id={"loop": 1 - lax.axis_index("loop")},
+            device_id_type=MESH,
+        )
+
+    def far_core(a, block, first=False):
+        rows = pl.ds(*spans[a][2])
+        return pltpu.make_async_remote_copy(
+            src_ref=own[a].at[rows] if first else full[a].at[block, rows],
+            dst_ref=full[a].at[block, rows],
+            send_sem=far_sems[2].at[a, block // 2],
+            recv_sem=far_sems[3].at[a, block],
+            device_id={"dp": core},
+            device_id_type=MESH,
+        )
+
+    def cross(unit, block):
+        if far_sems is not None and unit[1] == 0:
+            to_far(unit[0], block).start()
+
     local = [pltpu.make_async_copy(own[a], full[a].at[me], keep.at[a]) for a in range(arrays)]
-    units = [(a, s) for a in range(arrays) for s in range(parts)]
+    units = [(a, s) for a in range(arrays) for s in range(2 if far_sems else len(spans[a]))]
 
     def begin():
         for unit in units:
@@ -185,6 +213,9 @@
 
             to_pair(unit, me, True).start()
             to_core(unit, me, True).start()
+        if far_sems is not None:
+            for a in range(arrays):
+                far_core(a, me, True).start()
         for item in local:
             item.start()
 
@@ -200,6 +231,7 @@
 
             to_pair(unit, block).start()
             to_core(unit, block).start()
+            cross(unit, block)
 
         @pl.when(z + k < depth)
         def _():
@@ -212,10 +244,12 @@
 
             to_pair(unit, block).start()
             to_core(unit, block).start()
+            cross(unit, block)
 
     def pass_on(unit, block):
         to_pair(unit, block).wait_recv()
         to_core(unit, block).start()
+        cross(unit, block)
 
     def from_pair(k, unit):
         if k == 0:
@@ -230,10 +264,33 @@
         def _():
             pass_on(unit, mate + 4 * k)
 
+    def far_on(a, block):
+        to_far(a, block).wait_recv()
+        far_core(a, block).start()
+
+    def from_far(k, a):
+        if k == 0:
+            far_on(a, mate)
+            return
+
+        @pl.when(z - k >= 0)
+        def _():
+            far_on(a, me - 4 * k)
+            far_on(a, mate - 4 * k)
+
+        @pl.when(z + k < depth)
+        def _():
+            far_on(a, me + 4 * k)
+            far_on(a, mate + 4 * k)
+
     def arrive():
         for unit in units:
             for j in range(count // 2):
                 to_core(unit, 2 * j + 1 - c).wait_recv()
+        if far_sems is not None:
+            for a in range(arrays):
+                for j in range(count // 2):
+                    far_core(a, 2 * j + 1 - c).wait_recv()
         for item in local:
             item.wait()
 
@@ -253,7 +310,16 @@
                 def _():
                     to_left(unit, block).wait_send()
 
-    return units, begin, from_line, from_pair, arrive, finish
+        if far_sems is not None:
+            for a in range(arrays):
+                for j in range(count // 2):
+                    far_core(a, 2 * j + c).wait_send()
+
+                    @pl.when(2 * j + c != me)
+                    def _():
+                        to_far(a, 2 * j + c).wait_send()
+
+    return units, begin, from_line, from_pair, from_far, arrive, finish
 
 
 def gather_sems(count, number, parts):
@@ -269,22 +335,8 @@
     ]
 
 
-def gather_body(count, parts, arrays, *refs):
-    depth = count // 4
-    greet(count)
-    units, begin, from_line, from_pair, arrive, finish = gather_plan(
-        count, parts, refs[:arrays], refs[arrays : 2 * arrays], *refs[2 * arrays :]
-    )
-    begin()
-    for k in range(1, depth):
-        for unit in units:
-            from_line(k, unit)
-        for unit in units:
-            from_pair(k - 1, unit)
-    for unit in units:
-        from_pair(depth - 1, unit)
-    arrive()
-    finish()
+def even_spans(rows, parts):
+    return [(s * (rows // parts), rows // parts) for s in range(parts)]
 
 
 def kernel_params(ident):
@@ -293,54 +345,47 @@
     )
 
 
-def gather_rows(count, ident, *arrays, parts=2):
-    if count != LINE_DEVICES:
-        return [lax.all_gather(item, "dp", axis=0, tiled=True) for item in arrays]
-    number = len(arrays)
-    anywhere = pl.BlockSpec(memory_space=pl.ANY)
-    full = pl.pallas_call(
-        functools.partial(gather_body, count, parts, number),
-        out_shape=[
-            jax.ShapeDtypeStruct((count,) + item.shape, item.dtype) for item in arrays
-        ],
-        in_specs=[anywhere] * number,
-        out_specs=[anywhere] * number,
-        scratch_shapes=gather_sems(count, number, parts),
-        compiler_params=kernel_params(ident),
-        name="gather_rows",
-    )(*arrays)
-    return [
-        item.reshape((count * item.shape[1],) + item.shape[2:]) for item in full
-    ]
-
-
-def opening_body(count, parts, arrays, *refs):
+def opening_body(count, shares, arrays, stream, gain, *refs):
     own = refs[:arrays]
     weights, factors, first, second = refs[arrays : arrays + 4]
     full = refs[arrays + 4 : 2 * arrays + 4]
-    folded = refs[2 * arrays + 4]
-    scratch = refs[2 * arrays + 5 :]
-    bank, factor_bank, first_bank, second_bank, bank_sem, factor_sem, out_sem = scratch[:7]
+    folded, normed, lowrank = refs[2 * arrays + 4 : 2 * arrays + 7]
+    scratch = refs[2 * arrays + 7 :]
+    (bank, factor_bank, first_bank, in_bank, second_bank, bank_sem, factor_sem, out_sem) = scratch[
+        :8
+    ]
     me, depth, z, y, c = place(count)
     rank = ADAPTER_RANK
     width, wide = bank.shape[1:]
-    greet(count)
-    units, begin, from_line, from_pair, arrive, finish = gather_plan(
-        count, parts, own, full, *scratch[7:]
+    loop = lax.axis_index("loop")
+    greet(count, True)
+    spans = []
+    for a in range(arrays):
+        rows, share = own[a].shape[0], shares[a]
+        spans.append(
+            [
+                (pl.multiple_of(loop * (rows - share), 16), share),
+                (share, rows - 2 * share),
+                (pl.multiple_of((1 - loop) * (rows - share), 16), share),
+            ]
+        )
+    units, begin, from_line, from_pair, from_far, arrive, finish = gather_plan(
+        count, spans, own, full, scratch[8:14], scratch[14:18]
     )
     begin()
     fills = [
         pltpu.make_async_copy(weights.at[i], bank.at[i], bank_sem.at[i]) for i in range(3)
     ]
     sources = [
+        pltpu.make_async_copy(first.at[:, pl.ds(0, 3 * rank)], in_bank, factor_sem.at[0]),
         pltpu.make_async_copy(
-            factors.at[pl.ds(me * width, width)], factor_bank, factor_sem.at[0]
+            factors.at[pl.ds(me * width, width)], factor_bank, factor_sem.at[1]
         ),
         pltpu.make_async_copy(
-            first.at[:, pl.ds(4 * rank, 2 * rank)], first_bank, factor_sem.at[1]
+            first.at[:, pl.ds(4 * rank, 2 * rank)], first_bank, factor_sem.at[2]
         ),
         pltpu.make_async_copy(
-            second.at[:, pl.ds(PROJECTED_WIDTH + MODEL_WIDTH, wide)], second_bank, factor_sem.at[2]
+            second.at[:, pl.ds(PROJECTED_WIDTH + MODEL_WIDTH, wide)], second_bank, factor_sem.at[3]
         ),
     ]
     for item in sources + fills:
@@ -372,254 +417,264 @@
         lax.fori_loop(0, (width // high) * (wide // tile), inner, 0)
         put(i).start()
 
-    for item in sources:
+    rows = stream[...].astype(jnp.float32)
+    inverse = lax.rsqrt(jnp.mean(rows * rows, axis=-1, keepdims=True) + EPSILON)
+    normed[...] = (rows * inverse * gain[...]).astype(normed.dtype)
+    sources[0].wait()
+    lowrank[...] = contract(normed[...], in_bank[...], 1, 0).astype(lowrank.dtype)
+    for item in sources[1:]:
         item.wait()
-    fills[0].wait()
-    fold(0)
     for k in range(1, depth):
-        for unit in units:
-            from_line(k, unit)
-        if k < 3:
-            fills[k].wait()
-            fold(k)
-        for unit in units:
-            from_pair(k - 1, unit)
+        for a in range(arrays):
+            for unit in units:
+                if unit[0] == a:
+                    from_line(k, unit)
+                    from_pair(k - 1, unit)
+            if k > 1 or a > 0:
+                stage = (k - 1) * arrays + a - 1
+                from_far(stage // arrays, stage % arrays)
+        fills[k - 1].wait()
+        fold(k - 1)
     for unit in units:
         from_pair(depth - 1, unit)
+    for stage in range((depth - 1) * arrays - 1, depth * arrays):
+        from_far(stage // arrays, stage % arrays)
     arrive()
     finish()
     for i in range(3):
         put(i).wait()
 
 
-def opening(count, ident, arrays, weights, factors, first, second, parts=2):
+def opening(count, ident, stream, gain, arrays, shares, weights, factors, first, second):
     number = len(arrays)
     _, width, wide = weights.shape
     low = jnp.bfloat16
+    rank = ADAPTER_RANK
     sem = pltpu.SemaphoreType.DMA
     anywhere = pl.BlockSpec(memory_space=pl.ANY)
+    inside = pl.BlockSpec(memory_space=pltpu.VMEM)
     out = pl.pallas_call(
-        functools.partial(opening_body, count, parts, number),
+        functools.partial(opening_body, count, shares, number),
         out_shape=[
             jax.ShapeDtypeStruct((count,) + item.shape, item.dtype) for item in arrays
         ]
-        + [jax.ShapeDtypeStruct(weights.shape, low)],
-        in_specs=[anywhere] * (number + 4),
-        out_specs=[anywhere] * (number + 1),
+        + [
+            jax.ShapeDtypeStruct(weights.shape, low),
+            jax.ShapeDtypeStruct(stream.shape, low),
+            jax.ShapeDtypeStruct((stream.shape[0], 3 * rank), low),
+        ],
+        in_specs=[inside] * 2 + [anywhere] * (number + 4),
+        out_specs=[anywhere] * (number + 1) + [inside] * 2,
         scratch_shapes=[
             pltpu.VMEM(weights.shape, low),
             pltpu.VMEM((width, factors.shape[1]), low),
-            pltpu.VMEM((wide, 2 * ADAPTER_RANK), low),
-            pltpu.VMEM((ADAPTER_RANK, wide), low),
+            pltpu.VMEM((wide, 2 * rank), low),
+            pltpu.VMEM((wide, 3 * rank), low),
+            pltpu.VMEM((rank, wide), low),
             sem((3,)),
-            sem((3,)),
+            sem((4,)),
             sem((3,)),
         ]
-        + gather_sems(count, number, parts),
+        + gather_sems(count, number, 2)
+        + [
+            sem((number, count // 2)),
+            sem((number, count)),
+            sem((number, count // 2)),
+            sem((number, count)),
+        ],
         compiler_params=kernel_params(ident),
         name="opening",
-    )(*arrays, weights, factors, first, second)
+    )(stream, gain, *arrays, weights, factors, first, second)
     return [
         item.reshape((count * item.shape[1],) + item.shape[2:]) for item in out[:number]
-    ] + [out[number]]
-
-
-def scatter_body(count, parts, arrays, *refs):
-    terms = refs[:arrays]
-    total = refs[arrays : 2 * arrays]
-    scratch = refs[2 * arrays :]
-    held, loaded, core_in, pair_in, line_in = [
-        scratch[i * arrays : (i + 1) * arrays] for i in range(5)
+    ] + list(out[number:])
+
+
+def turn(values, cosine, sine):
+    half = values.shape[-1] // 2
+    first, second = values[:, :half], values[:, half:]
+    return jnp.concatenate(
+        [first * cosine - second * sine, first * sine + second * cosine], axis=1
+    )
+
+
+def attention_body(count, normed, lowrank, stream, active, gain, cosine, sine, own_seq, own_order,
+                   all_seq, all_order, in_weight, out_weight, first, second, grads,
+                   queries, attended, lowrank_out, level, middle, normed_next, keys_values, grads_all,
+                   in_bank, out_bank, in_second, out_second, out_first, allowed, kv_own, kv_full,
+                   load_sem, put_sem, *sems):
+    me, depth, z, y, c = place(count)
+    height, wide = normed.shape
+    size = HEAD_SIZE
+    scale = size ** (-0.5)
+    rank = ADAPTER_RANK
+    low = jnp.bfloat16
+    greet(count)
+    kv_units, kv_begin, kv_line, kv_pair, _, kv_arrive, kv_finish = gather_plan(
+        count, [even_spans(height, 1)], (kv_own,), (kv_full,), sems[:6]
+    )
+    units, begin, from_line, from_pair, _, arrive, finish = gather_plan(
+        count, [even_spans(height, 2)], (grads,), (grads_all,), sems[6:]
+    )
+    loads = [
+        pltpu.make_async_copy(source, bank, load_sem.at[i])
+        for i, (source, bank) in enumerate(
+            (
+                (in_weight, in_bank),
+                (second.at[:, pl.ds(0, PROJECTED_WIDTH)], in_second),
+                (out_weight, out_bank),
+                (second.at[:, pl.ds(PROJECTED_WIDTH, MODEL_WIDTH)], out_second),
+                (first.at[:, pl.ds(3 * rank, rank)], out_first),
+            )
+        )
     ]
-    (load_sem, core_send, core_recv, pair_send, pair_recv, line_send, line_recv) = scratch[
-        5 * arrays :
-    ]
-    me, depth, z, y, c = place(count)
-    greet(count)
-    near = z < depth // 2
-
-    def turn(k):
-        even = depth - 1 - k // 2 if k % 2 == 0 else k // 2
-        return jnp.where(near, even, depth - 1 - even)
-
-    def rows_of(a, s):
-        step = terms[a].shape[1] // parts[a]
-        return pl.ds(s * step, step)
-
-    def to_core(a, s, line, pair):
-        slot = 2 * line + pair
-        return pltpu.make_async_remote_copy(
-            src_ref=terms[a].at[2 * slot + 1 - c, rows_of(a, s)],
-            dst_ref=core_in[a].at[slot, rows_of(a, s)],
-            send_sem=core_send.at[a, slot, s],
-            recv_sem=core_recv.at[a, slot, s],
-            device_id={"dp": me + 1 - 2 * c},
-            device_id_type=MESH,
+    for item in loads:
+        item.start()
+    loads[0].wait()
+    loads[1].wait()
+
+    def head(at, part):
+        value = contract(normed[...], in_bank[:, at : at + size], 1, 0)
+        return value + contract(
+            lowrank[:, part * rank : (part + 1) * rank], in_second[:, at : at + size], 1, 0
         )
 
-    def load(a, s, line, pair):
-        slot = 2 * line + pair
-        return pltpu.make_async_copy(
-            terms[a].at[2 * slot + c, rows_of(a, s)],
-            loaded[a].at[slot, rows_of(a, s)],
-            load_sem.at[a, slot, s],
+    kv_own[:, :size] = turn(head(QUERY_WIDTH, 1), cosine[...], sine[...]).astype(low)
+    kv_own[:, size:] = head(QUERY_WIDTH + size, 2).astype(low)
+    kv_begin()
+    begin()
+    heads = wide // size
+
+    def some_heads(start, stop):
+        for i in range(start, stop):
+            value = turn(head(i * size, 0), cosine[...], sine[...])
+            queries[:, i * size : (i + 1) * size] = value.astype(low)
+
+    some_heads(0, 4)
+    (kv_unit,) = kv_units
+    kv_line(1, kv_unit)
+    kv_pair(0, kv_unit)
+    some_heads(4, heads)
+    same = own_seq[...] == all_seq[...]
+    allowed[...] = jnp.where(same & (all_order[...] <= own_order[...]), 1.0, 0.0)
+    kv_line(2, kv_unit)
+    kv_pair(1, kv_unit)
+    kv_line(3, kv_unit)
+    kv_pair(2, kv_unit)
+    kv_pair(3, kv_unit)
+    for unit in units:
+        from_line(1, unit)
+        from_pair(0, unit)
+    kv_arrive()
+    put_kv = pltpu.make_async_copy(kv_full, keys_values, put_sem)
+    put_kv.start()
+    total = count * height
+    keys = kv_full[:, :, :size].reshape(total, size)
+    values = kv_full[:, :, size:].reshape(total, size)
+
+    def attend(pair):
+        query = jnp.concatenate(
+            [
+                queries[:, 2 * pair * size : (2 * pair + 1) * size],
+                queries[:, (2 * pair + 1) * size : (2 * pair + 2) * size],
+            ],
+            axis=0,
         )
-
-    def to_pair(a, s, line):
-        return pltpu.make_async_remote_copy(
-            src_ref=loaded[a].at[2 * line + 1 - y, rows_of(a, s)],
-            dst_ref=pair_in[a].at[line, rows_of(a, s)],
-            send_sem=pair_send.at[a, line, s],
-            recv_sem=pair_recv.at[a, line, s],
-            device_id={"dp": me + 2 - 4 * y},
-            device_id_type=MESH,
-        )
-
-    def along(a, s, line, slot, target):
-        return pltpu.make_async_remote_copy(
-            src_ref=loaded[a].at[2 * line + y, rows_of(a, s)],
-            dst_ref=line_in[a].at[slot, rows_of(a, s)],
-            send_sem=line_send.at[a, line, s],
-            recv_sem=line_recv.at[a, slot, s],
-            device_id={"dp": target},
-            device_id_type=MESH,
-        )
-
-    def to_right(a, s, line):
-        return along(a, s, line, line, me + 4)
-
-    def to_left(a, s, line):
-        return along(a, s, line, jnp.where(line == z - 1, depth, line), me - 4)
-
-    def from_right(a, s, line):
-        return along(a, s, line, jnp.where(line == z, depth, line), me)
-
-    order = [turn(k) for k in range(depth)]
-    units = [(a, s) for a in range(arrays) for s in range(parts[a])]
-    for pair in (1 - y, y):
-        for line in order:
-            for a, s in units:
-                to_core(a, s, line, pair).start()
-                load(a, s, line, pair).start()
-
-    for line in order:
-        for a, s in units:
-            slot = 2 * line + 1 - y
-            rows = rows_of(a, s)
-            load(a, s, line, 1 - y).wait()
-            to_core(a, s, line, 1 - y).wait_recv()
-            loaded[a][slot, rows] = loaded[a][slot, rows] + core_in[a][slot, rows]
-            to_pair(a, s, line).start()
-
-    def own_sum(a, s, line):
-        slot = 2 * line + y
-        rows = rows_of(a, s)
-        load(a, s, line, y).wait()
-        to_core(a, s, line, y).wait_recv()
-        to_pair(a, s, line).wait_recv()
-        part = loaded[a][slot, rows].astype(jnp.float32)
-        part += core_in[a][slot, rows].astype(jnp.float32)
-        held[a][...] = part + pair_in[a][line, rows].astype(jnp.float32)
-
-    def add_line(a, s, slot):
-        along(a, s, z, slot, me).wait_recv()
-        held[a][...] += line_in[a][slot, rows_of(a, s)].astype(jnp.float32)
-
-    for line in order:
-        for a, s in units:
-
-            @pl.when(line != z)
-            def _(a=a, s=s, line=line):
-                own_sum(a, s, line)
-
-                @pl.when(((line > z) & (z > 0)) | ((line < z) & (z < depth - 1)))
-                def _():
-                    add_line(a, s, line)
-
-                loaded[a][2 * line + y, rows_of(a, s)] = held[a][...].astype(loaded[a].dtype)
-
-                @pl.when(line > z)
-                def _():
-                    to_right(a, s, line).start()
-
-                @pl.when(line < z)
-                def _():
-                    to_left(a, s, line).start()
-
-    for a, s in units:
-        own_sum(a, s, z)
-
-        @pl.when(z > 0)
-        def _(a=a, s=s):
-            add_line(a, s, z)
-
-        @pl.when(z < depth - 1)
-        def _(a=a, s=s):
-            add_line(a, s, depth)
-
-        total[a][rows_of(a, s)] = held[a][...]
-
-    for a, s in units:
-        for line in range(depth):
-            for pair in range(2):
-                to_core(a, s, line, pair).wait_send()
-            to_pair(a, s, line).wait_send()
-
-            @pl.when(z != line)
-            def _():
-                to_right(a, s, line).wait_send()
-
-
-def scatter_rows(count, ident, *arrays):
-    if count != LINE_DEVICES:
-        return [
-            lax.psum_scatter(
-                item.astype(jnp.float32), "dp", scatter_dimension=0, tiled=True
-            )
-            for item in arrays
+        keep = jnp.concatenate([allowed[...], allowed[...]], axis=0) > 0.5
+        scores = jnp.where(keep, contract(query, keys, 1, 1) * scale, FLOOR_SCORE)
+        top = jnp.max(scores, axis=-1, keepdims=True)
+        expo = jnp.exp(scores - top)
+        mass = jnp.sum(expo, axis=-1, keepdims=True)
+        level[pair] = jnp.broadcast_to(top + jnp.log(mass), level.shape[1:])
+        value = contract((expo / mass).astype(low), values, 1, 0).astype(low)
+        for i in range(2):
+            attended[:, (2 * pair + i) * size : (2 * pair + i + 1) * size] = value[
+                i * height : (i + 1) * height
+            ]
+
+    for pair in range(heads // 2):
+        attend(pair)
+        if pair == 0:
+            for unit in units:
+                from_line(2, unit)
+        if pair == 1:
+            for unit in units:
+                from_pair(1, unit)
+        if pair == 2:
+            for unit in units:
+                from_line(3, unit)
+        if pair == 3:
+            for unit in units:
+                from_pair(2, unit)
+    for item in loads[2:]:
+        item.wait()
+    lowrank_out[...] = contract(attended[...], out_first[...], 1, 0).astype(low)
+    tile = 256
+
+    def product(n, carry):
+        cols = pl.ds(pl.multiple_of(n * tile, tile), tile)
+        value = contract(attended[...], out_bank[:, cols], 1, 0)
+        value += contract(lowrank_out[...], out_second[:, cols], 1, 0)
+        middle[:, cols] = stream[:, cols].astype(jnp.float32) + active[...] * value
+        return carry
+
+    lax.fori_loop(0, wide // tile, product, 0)
+    rows = middle[...]
+    inverse = lax.rsqrt(jnp.mean(rows * rows, axis=-1, keepdims=True) + EPSILON)
+    normed_next[...] = (rows * inverse * gain[...]).astype(low)
+    for unit in units:
+        from_pair(3, unit)
+    arrive()
+    finish()
+    kv_finish()
+    put_kv.wait()
+
+
+def attention(count, ident, normed, lowrank, stream, active, gain, cosine, sine, own_seq,
+              own_order, all_seq, all_order, in_weight, out_weight, first, second, grads):
+    height, wide = normed.shape
+    low, high = jnp.bfloat16, jnp.float32
+    inside = pl.BlockSpec(memory_space=pltpu.VMEM)
+    anywhere = pl.BlockSpec(memory_space=pl.ANY)
+    rank = ADAPTER_RANK
+    both = 2 * HEAD_SIZE
+    total = count * height
+    sem = pltpu.SemaphoreType.DMA
+    shape = jax.ShapeDtypeStruct
+    return pl.pallas_call(
+        functools.partial(attention_body, count),
+        out_shape=[
+            shape((height, wide), low),
+            shape((height, wide), low),
+            shape((height, rank), low),
+            shape((wide // both, 2 * height, 128), high),
+            shape((height, wide), high),
+            shape((height, wide), low),
+            shape((count, height, both), low),
+            shape((count, height, wide), low),
+        ],
+        in_specs=[inside] * 11 + [anywhere] * 5,
+        out_specs=[inside] * 6 + [anywhere] * 2,
+        scratch_shapes=[
+            pltpu.VMEM(in_weight.shape, low),
+            pltpu.VMEM(out_weight.shape, low),
+            pltpu.VMEM((rank, PROJECTED_WIDTH), low),
+            pltpu.VMEM((rank, wide), low),
+            pltpu.VMEM((wide, rank), low),
+            pltpu.VMEM((height, total), high),
+            pltpu.VMEM((height, both), low),
+            pltpu.VMEM((count, height, both), low),
+            sem((5,)),
+            sem,
         ]
-    depth = count // 4
-    number = len(arrays)
-    blocks = [
-        item.reshape(count, item.shape[0] // count, item.shape[1]) for item in arrays
-    ]
-    parts = [2 if item.shape[1] % 32 == 0 and item.shape[1] > 32 else 1 for item in blocks]
-    most = max(parts)
-
-    def room(slots):
-        return [pltpu.VMEM((slots,) + item.shape[1:], item.dtype) for item in blocks]
-
-    def sems(slots):
-        return pltpu.SemaphoreType.DMA((number, slots, most))
-
-    return pl.pallas_call(
-        functools.partial(scatter_body, count, parts, number),
-        out_shape=[jax.ShapeDtypeStruct(item.shape[1:], jnp.float32) for item in blocks],
-        in_specs=[pl.BlockSpec(memory_space=pl.ANY)] * number,
-        out_specs=[pl.BlockSpec(memory_space=pltpu.VMEM)] * number,
-        scratch_shapes=[
-            pltpu.VMEM((item.shape[1] // part, item.shape[2]), jnp.float32)
-            for item, part in zip(blocks, parts)
-        ]
-        + room(2 * depth)
-        + room(2 * depth)
-        + room(depth)
-        + room(depth + 1)
-        + [
-            sems(2 * depth),
-            sems(2 * depth),
-            sems(2 * depth),
-            sems(depth),
-            sems(depth),
-            sems(depth),
-            sems(depth + 1),
-        ],
+        + gather_sems(count, 1, 1)
+        + gather_sems(count, 1, 2),
         compiler_params=kernel_params(ident),
-        name="scatter_rows",
-    )(*blocks)
-
-
-FAR_TILES = 3
+        name="attention",
+    )(
+        normed, lowrank, stream, active, gain, cosine, sine, own_seq, own_order, all_seq,
+        all_order, in_weight, out_weight, first, second, grads,
+    )
 
 
 def line_order(z):
@@ -1179,9 +1234,6 @@
     )(units, gate_grads, up_grads, weights, rows_all, grads_all)
 
 
-OUT_SPLIT = 1536
-
-
 def sum_plan(count, parts, mine, theirs, core_in, pair_in, line_in, sems):
     me, depth, z, y, c = place(count)
     core_send, core_recv, pair_send, pair_recv, line_send, line_recv = sems
@@ -1349,9 +1401,9 @@
 
 
 def attention_grads_body(count, attended, grad_rows, weight, queries, keys_values, level,
-                         cosine, sine, own_seq, own_order, all_seq, all_order,
-                         joint_grads, out_sum,
-                         weight_in, grad_att, allowed, kv_total, kv_terms, kv_sum, out_terms,
+                         cosine, sine, own_seq, own_order, all_seq, all_order, first, second,
+                         joint_grads, lowrank_grads, out_sum,
+                         weight_in, out_first, both_second, grad_att, allowed, kv_total, kv_terms, kv_sum, out_terms,
                          out_core, out_pair, out_line, kv_core, kv_pair, kv_line,
                          weight_sem, *sems):
     me, depth, z, y, c = place(count)
@@ -1360,8 +1412,19 @@
     scale = size ** (-0.5)
     low = jnp.bfloat16
     greet(count)
-    load = pltpu.make_async_copy(weight, weight_in, weight_sem)
-    load.start()
+    rank = ADAPTER_RANK
+    loads = [
+        pltpu.make_async_copy(source, bank, weight_sem.at[i])
+        for i, (source, bank) in enumerate(
+            (
+                (weight, weight_in),
+                (first.at[:, pl.ds(3 * rank, rank)], out_first),
+                (second.at[:, pl.ds(0, PROJECTED_WIDTH + wide)], both_second),
+            )
+        )
+    ]
+    for item in loads:
+        item.start()
     order, send_out, pair_out, line_out, last_out, finish_out = sum_terms(
         count, 2, out_terms, (out_core, out_pair, out_line), sems[:6]
     )
@@ -1384,12 +1447,16 @@
 
     for line in order:
         out_product(line)
-    load.wait()
+    for item in loads:
+        item.wait()
     tile = 256
+    back_out = contract(grad_rows[...], both_second[:, PROJECTED_WIDTH:], 1, 1).astype(low)
 
     def product(n, carry):
         cols = pl.ds(pl.multiple_of(n * tile, tile), tile)
-        grad_att[:, cols] = contract(grad_rows[...], weight_in[cols], 1, 1).astype(low)
+        value = contract(grad_rows[...], weight_in[cols], 1, 1)
+        value += contract(back_out, out_first[cols], 1, 1)
+        grad_att[:, cols] = value.astype(low)
         return carry
 
     lax.fori_loop(0, wide // tile, product, 0)
@@ -1448,13 +1515,18 @@
     part = turn_back(kv_sum[:, :size], cosine[...], sine[...])
     joint_grads[:, wide : wide + size] = part.astype(low)
     joint_grads[:, wide + size :] = kv_sum[:, size:].astype(low)
+    for i, (at, stop) in enumerate(
+        ((0, wide), (wide, wide + size), (wide + size, wide + 2 * size))
+    ):
+        value = contract(joint_grads[:, at:stop], both_second[:, at:stop], 1, 1)
+        lowrank_grads[:, i * rank : (i + 1) * rank] = value.astype(low)
     last_out(out_sum)
     finish_out()
     finish_kv()
 
 
 def attention_grads(count, ident, attended, grad_rows, weight, queries, keys_values, level,
-                    cosine, sine, own_seq, own_order, all_seq, all_order):
+                    cosine, sine, own_seq, own_order, all_seq, all_order, first, second):
     height, wide = grad_rows.shape
     total = keys_values.shape[0]
     low = jnp.bfloat16
@@ -1466,12 +1538,15 @@
         functools.partial(attention_grads_body, count),
         out_shape=[
             jax.ShapeDtypeStruct((height, wide + both), low),
+            jax.ShapeDtypeStruct((height, 3 * ADAPTER_RANK), low),
             jax.ShapeDtypeStruct((feature, OUT_SPLIT), jnp.float32),
         ],
-        in_specs=[inside] * 2 + [anywhere] + [inside] * 9,
-        out_specs=[inside] * 2,
+        in_specs=[inside] * 2 + [anywhere] + [inside] * 9 + [anywhere] * 2,
+        out_specs=[inside] * 3,
         scratch_shapes=[
             pltpu.VMEM(weight.shape, low),
+            pltpu.VMEM((wide, ADAPTER_RANK), low),
+            pltpu.VMEM((ADAPTER_RANK, PROJECTED_WIDTH + wide), low),
             pltpu.VMEM(attended.shape, low),
             pltpu.VMEM((height, total), jnp.float32),
             pltpu.VMEM((total, both), jnp.float32),
@@ -1481,22 +1556,22 @@
         ]
         + sum_rooms(count, feature, OUT_SPLIT)
         + sum_rooms(count, height, both)
-        + [pltpu.SemaphoreType.DMA]
+        + [pltpu.SemaphoreType.DMA((3,))]
         + sum_sems(count, 2)
         + sum_sems(count, 1),
         compiler_params=kernel_params(ident),
         name="attention_grads",
     )(
         attended, grad_rows, weight, queries, keys_values, level,
-        cosine, sine, own_seq, own_order, all_seq, all_order,
+        cosine, sine, own_seq, own_order, all_seq, all_order, first, second,
     )
 
 
 def closing_body(count, normed, joint_grads, attended, grad_rows, lowrank, lowrank_out, stream,
-                 gain, grad_middle, small, weight, gate_grads, up_grads, down_grads, factors,
+                 gain, grad_middle, small, lowrank_grads, weight, gate_grads, up_grads, down_grads, factors,
                  first, second,
                  in_sum, out_sum, second_sum, first_sum, small_sum, stream_grad, factor_grads,
-                 bank, factor_bank, first_bank, second_bank, made, in_terms, out_terms,
+                 bank, in_bank, factor_bank, second_bank, made, in_terms, out_terms,
                  second_terms, first_terms, small_terms, *scratch):
     me, depth, z, y, c = place(count)
     height, wide = normed.shape
@@ -1504,8 +1579,8 @@
     width = gate_grads.shape[0]
     low = jnp.bfloat16
     rooms = [scratch[3 * i : 3 * i + 3] for i in range(5)]
-    weight_sem, grads_sem, factor_sem, made_sem = scratch[15:19]
-    sems = [scratch[19 + 6 * i : 25 + 6 * i] for i in range(5)]
+    weight_sem, grads_sem, factor_sem, made_sem, side_sem = scratch[15:20]
+    sems = [scratch[20 + 6 * i : 26 + 6 * i] for i in range(5)]
     greet(count)
     halves = [
         pltpu.make_async_copy(weight.at[pl.ds(i * width, width)], bank, weight_sem.at[i])
@@ -1514,16 +1589,22 @@
     halves[0].start()
     loads = [
         pltpu.make_async_copy(
-            factors.at[pl.ds(me * width, width)], factor_bank, factor_sem.at[0]
-        ),
-        pltpu.make_async_copy(
-            first.at[:, pl.ds(4 * rank, 2 * rank)], first_bank, factor_sem.at[1]
+            factors.at[pl.ds(me * width, width), pl.ds(0, rank)], factor_bank, factor_sem.at[0]
         ),
         pltpu.make_async_copy(
             second.at[:, pl.ds(PROJECTED_WIDTH + MODEL_WIDTH, wide)], second_bank, factor_sem.at[2]
         ),
     ]
-    for item in loads:
+    in_load = pltpu.make_async_copy(first.at[:, pl.ds(0, 3 * rank)], in_bank, factor_sem.at[3])
+    first_load = pltpu.make_async_copy(
+        first.at[:, pl.ds(4 * rank, 2 * rank)], in_bank.at[:, pl.ds(0, 2 * rank)], factor_sem.at[1]
+    )
+    side_load = pltpu.make_async_copy(
+        factors.at[pl.ds(me * width, width), pl.ds(rank, 2 * rank)],
+        bank.at[:, pl.ds(wide, 2 * rank)],
+        side_sem,
+    )
+    for item in [in_load] + loads:
         item.start()
     terms = (in_terms, out_terms, second_terms, first_terms, small_terms)
     parts = (2, 2, 1, 1, 1)
@@ -1577,7 +1658,8 @@
         def product(n, carry):
             some = pl.ds(pl.multiple_of(n * 256, 256), 256)
             cols = pl.ds(pl.multiple_of(i * width + n * 256, 256), 256)
-            stream_grad[:, cols] = contract(joint_grads[...], bank[some], 1, 1)
+            value = contract(joint_grads[...], bank[some], 1, 1)
+            stream_grad[:, cols] = value + contract(lowrank_grads[...], in_bank[cols], 1, 1)
             return carry
 
         lax.fori_loop(0, width // 256, product, 0)
@@ -1587,12 +1669,15 @@
     block_products(0, normed, joint_grads, 0)
     for k in range(depth):
         pair_step[0](k)
+    in_load.wait()
     half_product(0)
     block_products(1, attended, grad_rows, OUT_SPLIT)
     for k in range(depth):
         pair_step[1](k)
     for i in range(1, len(halves)):
         half_product(i)
+    first_load.start()
+    side_load.start()
 
     rows = stream[...].astype(jnp.float32)
     inverse = lax.rsqrt(jnp.mean(rows * rows, axis=-1, keepdims=True) + EPSILON)
@@ -1622,21 +1707,23 @@
     ):
         put_second(at, contract(left[:, at:stop], own, 0, 0))
     put_second(PROJECTED_WIDTH, contract(grad_rows[...], lowrank_out[...], 0, 0))
-    for item in loads:
+    for item in loads + [first_load, side_load]:
         item.wait()
 
-    def put_factor(slot, cols):
+    def put_factor(cols):
         return pltpu.make_async_copy(
-            made.at[slot], factor_grads.at[:, pl.ds(cols * rank, rank)], made_sem.at[slot]
+            made, factor_grads.at[:, pl.ds(cols * rank, rank)], made_sem.at[cols]
         )
 
     line_step[0](1)
     held = bank.at[:, pl.ds(0, wide)]
     for i in range(2):
         bring(i).wait()
-        made[i] = contract(held[...], first_bank[:, i * rank : (i + 1) * rank], 1, 0)
-        put_factor(i, i + 1).start()
-        value = contract(held[...], factor_bank[:, (i + 1) * rank : (i + 2) * rank], 0, 0)
+        if i > 0:
+            put_factor(i).wait()
+        made[...] = contract(held[...], in_bank[:, i * rank : (i + 1) * rank], 1, 0)
+        put_factor(i + 1).start()
+        value = contract(held[...], bank[:, wide + i * rank : wide + (i + 1) * rank], 0, 0)
         first_terms[:, :, i * rank : (i + 1) * rank] = value.astype(low).reshape(
             count, wide // count, rank
         )
@@ -1645,11 +1732,11 @@
             line_step[0](2)
     send_all(3)
     bring(2).wait()
-    put_factor(0, 1).wait()
-    made[0] = contract(held[...], second_bank[...], 1, 1)
-    put_factor(0, 0).start()
+    put_factor(2).wait()
+    made[...] = contract(held[...], second_bank[...], 1, 1)
+    put_factor(0).start()
     put_second(
-        PROJECTED_WIDTH + MODEL_WIDTH, contract(held[...], factor_bank[:, :rank], 0, 0)
+        PROJECTED_WIDTH + MODEL_WIDTH, contract(held[...], factor_bank[...], 0, 0)
     )
     send_all(2)
     line_step[0](3)
@@ -1663,12 +1750,11 @@
         last_step[i](total)
     for item in finish:
         item()
-    put_factor(0, 0).wait()
-    put_factor(1, 2).wait()
+    put_factor(0).wait()
 
 
 def closing(count, ident, normed, joint_grads, attended, grad_rows, lowrank, lowrank_out, stream,
-            gain, grad_middle, small, weight, gate_grads, up_grads, down_grads, factors, first,
+            gain, grad_middle, small, lowrank_grads, weight, gate_grads, up_grads, down_grads, factors, first,
             second):
     height, wide = normed.shape
     width = gate_grads.shape[0]
@@ -1696,36 +1782,32 @@
             jax.ShapeDtypeStruct((height, wide), high),
             jax.ShapeDtypeStruct((width, 3 * rank), high),
         ],
-        in_specs=[inside] * 10 + [anywhere] * 7,
+        in_specs=[inside] * 11 + [anywhere] * 7,
         out_specs=[inside] * 6 + [anywhere],
         scratch_shapes=[
             pltpu.VMEM((width, weight.shape[1]), low),
-            pltpu.VMEM((width, 3 * rank), low),
-            pltpu.VMEM((wide, 2 * rank), low),
+            pltpu.VMEM((wide, 3 * rank), low),
+            pltpu.VMEM((width, rank), low),
             pltpu.VMEM((rank, wide), low),
-            pltpu.VMEM((2, width, rank), high),
+            pltpu.VMEM((width, rank), high),
         ]
         + [pltpu.VMEM((count, rows, cols), kind) for rows, cols, kind in shapes]
         + rooms
-        + [sem((wide // width,)), sem((3,)), sem((3,)), sem((2,))]
+        + [sem((wide // width,)), sem((3,)), sem((4,)), sem((3,)), sem]
         + sems,
         compiler_params=kernel_params(ident),
         name="closing",
     )(
         normed, joint_grads, attended, grad_rows, lowrank, lowrank_out, stream, gain, grad_middle,
-        small, weight, gate_grads, up_grads, down_grads, factors, first, second,
+        small, lowrank_grads, weight, gate_grads, up_grads, down_grads, factors, first, second,
     )
 
 
 def swap_loops(values):
-    if lax.axis_size("loop") == 1:
-        return values
     return lax.ppermute(values, "loop", [(0, 1), (1, 0)])
 
 
 def both_loops(values):
-    if lax.axis_size("loop") != 2:
-        return lax.psum(values.astype(jnp.float32), "loop")
     return values.astype(jnp.float32) + swap_loops(values).astype(jnp.float32)
 
 
@@ -1748,11 +1830,7 @@
     loop_count = lax.axis_size("loop")
     count = lax.axis_size("dp")
     local_rows = layer_input_stream.shape[1]
-    ffn_rows = feedforward_weight.shape[0]
-    weight_rows = attention_in_weight.shape[0]
     low = jnp.bfloat16
-    rank = ADAPTER_RANK
-    scale = HEAD_SIZE ** (-0.5)
     key_at = QUERY_WIDTH
     value_at = QUERY_WIDTH + HEAD_SIZE
     down_at = PROJECTED_WIDTH + MODEL_WIDTH
@@ -1767,134 +1845,42 @@
     order_own = own_slice(order_all)
     pos_own = own_slice(pos_all)
     active_mask = (live_own & (token_exit_depth[0] > current_loop)).astype(jnp.float32)[:, None]
-    residual_stream = layer_input_stream[0].astype(jnp.float32)
+    stream = layer_input_stream[0]
+    residual_stream = stream.astype(jnp.float32)
     grad_out = layer_output_gradient[0].astype(jnp.float32)
     adapter_first = adapter_first_factors[0]
     adapter_second = adapter_second_factors[0]
-    ffn_own = lax.dynamic_slice_in_dim(adapter_hidden_factors[0], dp_index * ffn_rows, ffn_rows, 0)
-    first_own = lax.dynamic_slice_in_dim(adapter_first, dp_index * weight_rows, weight_rows, 0)
-    second_query = adapter_second[:, :key_at]
-    second_key = adapter_second[:, key_at:value_at]
-    second_value = adapter_second[:, value_at:PROJECTED_WIDTH]
-    second_output = adapter_second[:, PROJECTED_WIDTH:down_at]
-    second_down = adapter_second[:, down_at:]
-
-    in_own = (
-        attention_in_weight.astype(jnp.float32)
-        + jnp.concatenate(
-            [
-                matrix_product(first_own[:, :rank], second_query),
-                matrix_product(first_own[:, rank : 2 * rank], second_key),
-                matrix_product(first_own[:, 2 * rank : 3 * rank], second_value),
-            ],
-            axis=1,
-        )
-    ).astype(low)
-    out_own = (
-        attention_out_weight.astype(jnp.float32)
-        + matrix_product(first_own[:, 3 * rank : 4 * rank], second_output)
-    ).astype(low)
-    down_factor = ffn_own[:, :rank]
-    gate_factor = ffn_own[:, rank : 2 * rank]
-    up_factor = ffn_own[:, 2 * rank :]
-    first_gate = adapter_first[:, 4 * rank : 5 * rank]
-    first_up = adapter_first[:, 5 * rank :]
     ffn_weight = jnp.swapaxes(feedforward_weight, 0, 1)
-
     feedforward_gradient = (active_mask * grad_out).astype(low)
-    normed_input = norm_rows(residual_stream, layer_norm_gains[0]).astype(low)
-    if count == LINE_DEVICES:
-        input_weight, output_weight, ffn_folded = opening(
-            count, 1, (in_own, out_own), ffn_weight, adapter_hidden_factors[0],
-            adapter_first, adapter_second,
-        )
-    else:
-        input_weight, output_weight = gather_rows(count, 1, in_own, out_own)
-        extra = jnp.stack(
-            [
-                outer_columns(gate_factor, first_gate),
-                outer_columns(up_factor, first_up),
-                matrix_product(down_factor, second_down),
-            ]
-        )
-        ffn_folded = (ffn_weight.astype(jnp.float32) + extra).astype(low)
-    feedforward_gradient, input_weight = lax.optimization_barrier(
-        (feedforward_gradient, input_weight)
-    )
-    grad_ffn_all = lax.all_gather(feedforward_gradient, "dp", axis=0, tiled=True)
-    query_key_value_linear = matrix_product(normed_input, input_weight)
+
+    input_weight, output_weight, ffn_folded, normed_input, lowrank_projection = opening(
+        count, 1, stream, layer_norm_gains[:1], (attention_in_weight, attention_out_weight),
+        (IN_SHARE, OUT_SHARE), ffn_weight, adapter_hidden_factors[0], adapter_first,
+        adapter_second,
+    )
     half = HEAD_SIZE // 2
     freqs = 10000.0 ** (-jnp.arange(half, dtype=jnp.float32) / half)
     angles = pos_own.astype(jnp.float32)[:, None] * freqs
     cosine, sine = jnp.cos(angles), jnp.sin(angles)
-    queries = rotate(
-        query_key_value_linear[:, :QUERY_WIDTH].reshape(local_rows, HEADS, HEAD_SIZE), pos_own
-    ).astype(low)
-    key_rot = rotate(
-        query_key_value_linear[:, key_at:value_at].reshape(local_rows, 1, HEAD_SIZE), pos_own
-    )[:, 0]
-    kv_send = jnp.concatenate([key_rot, query_key_value_linear[:, value_at:]], axis=1).astype(low)
-    (kv_all,) = gather_rows(count, 2, kv_send)
-    keys = kv_all[:, :HEAD_SIZE]
-    values = kv_all[:, HEAD_SIZE:]
-    key_total = kv_all.shape[0]
-    allowed = ((seq_own[:, None] == seq_all[None, :]) & (order_all[None, :] <= order_own[:, None]))[
-        :, None, :
-    ]
-    query_rows = queries.reshape(local_rows * HEADS, HEAD_SIZE)
-    queries_flat = queries.reshape(local_rows, QUERY_WIDTH)
-
-    def score_rows():
-        raw_scores = (outer_columns(query_rows, keys) * scale).reshape(local_rows, HEADS, key_total)
-        return jnp.where(allowed, raw_scores, FLOOR_SCORE)
-
-    scores = score_rows()
-    top_score = jnp.max(scores, axis=-1, keepdims=True)
-    expo = jnp.exp(scores - top_score)
-    mass = jnp.sum(expo, axis=-1, keepdims=True)
-    level = (top_score + jnp.log(mass))[:, :, 0]
-    prob_low = (expo / mass).astype(low)
-    attended_rows = (
-        matrix_product(prob_low.reshape(local_rows * HEADS, key_total), values)
-        .reshape(local_rows, QUERY_WIDTH)
-        .astype(low)
-    )
-    branch_output = matrix_product(attended_rows, output_weight)
-    middle_state = residual_stream + active_mask * branch_output
-    second_normed_input = norm_rows(middle_state, layer_norm_gains[1]).astype(low)
-    if count == LINE_DEVICES:
-        grad_blocks = grad_ffn_all.reshape(count, local_rows, MODEL_WIDTH)
-        units_own, grad_gate_own, grad_up_own, normed_blocks = hidden_units(
-            count, 3, second_normed_input, grad_blocks, ffn_folded
-        )
-        second_normed_gradient, ffn_sum, gate_grad, up_grad, down_grad, gate_other = unit_grads(
-            count, 4, units_own, grad_gate_own, grad_up_own, ffn_folded, normed_blocks, grad_blocks
-        )
-    else:
-        (normed_all,) = gather_rows(count, 3, second_normed_input)
-        gate_weight, up_weight, down_weight = ffn_folded
-        gate_own = outer_columns(normed_all, gate_weight)
-        up_own = outer_columns(normed_all, up_weight)
-        hidden_unit_gradient = outer_columns(grad_ffn_all, down_weight)
-        units_own = geglu(gate_own, up_own).astype(low)
-        grad_gate_own, grad_up_own = jax.vjp(geglu, gate_own, up_own)[1](hidden_unit_gradient)
-        grad_gate_own = grad_gate_own.astype(low)
-        grad_up_own = grad_up_own.astype(low)
-        gate_grad = inner_rows(grad_gate_own, normed_all).astype(low)
-        up_grad = inner_rows(grad_up_own, normed_all).astype(low)
-        down_grad = inner_rows(units_own, grad_ffn_all).astype(low)
-        ffn_terms = matrix_product(units_own, down_weight).astype(low)
-        input_terms = (
-            matrix_product(grad_gate_own, gate_weight) + matrix_product(grad_up_own, up_weight)
-        ).astype(low)
-        ffn_sum, second_normed_gradient = scatter_rows(count, 4, ffn_terms, input_terms)
-        gate_other = swap_loops(gate_grad)
-    if count == LINE_DEVICES:
-        gate_last = swap_loops(gate_grad[FAR_TILES * 256 :])
-        gate_other = jnp.concatenate([gate_other, gate_last], axis=0)
+    facts = (cosine, sine, seq_own[:, None], order_own[:, None], seq_all[None], order_all[None])
+    (
+        queries, attended_rows, output_projection, level, middle_state, second_normed_input,
+        kv_blocks, grad_blocks,
+    ) = attention(
+        count, 2, normed_input, lowrank_projection, stream, active_mask, layer_norm_gains[1:],
+        *facts, input_weight, output_weight, adapter_first, adapter_second, feedforward_gradient,
+    )
+    units_own, grad_gate_own, grad_up_own, normed_blocks = hidden_units(
+        count, 3, second_normed_input, grad_blocks, ffn_folded
+    )
+    second_normed_gradient, ffn_sum, gate_grad, up_grad, down_grad, gate_other = unit_grads(
+        count, 4, units_own, grad_gate_own, grad_up_own, ffn_folded, normed_blocks, grad_blocks
+    )
+    gate_last = swap_loops(gate_grad[FAR_TILES * 256 :])
     up_other = swap_loops(up_grad)
     down_other = swap_loops(down_grad)
-    complete_output = middle_state + active_mask * ffn_sum.astype(jnp.float32)
+
+    complete_output = middle_state + active_mask * ffn_sum
     confidence = root_mean(residual_stream) / (
         root_mean(residual_stream) + root_mean(complete_output - residual_stream)
     )
@@ -1904,109 +1890,41 @@
         & live_own[:, None]
     ).astype(jnp.float32)
     stats = jnp.concatenate([conf_sum[None], jnp.sum(depth_hits, axis=0)])
-
     grad_middle_part, grad_gain_two = jax.vjp(norm_rows, middle_state, layer_norm_gains[1])[1](
         second_normed_gradient
     )
     grad_middle = grad_out + grad_middle_part
     branch_gradient = (active_mask * grad_middle).astype(low)
+    joint_grads, lowrank_grads, out_first = attention_grads(
+        count, 5, attended_rows, branch_gradient, output_weight, queries,
+        kv_blocks.reshape(count * local_rows, 2 * HEAD_SIZE), level, *facts, adapter_first,
+        adapter_second,
+    )
     width_own = MODEL_WIDTH // count
     small = jnp.zeros((count, 8, 128), jnp.float32)
     small = small.at[:, 1, :width_own].set(grad_gain_two.reshape(count, width_own))
     small = small.at[:, 2, : loop_count + 2].set(stats[None])
-    lowrank_projection = matrix_product(normed_input, adapter_first[:, : 3 * rank]).astype(low)
-    output_projection = matrix_product(
-        attended_rows, adapter_first[:, 3 * rank : 4 * rank]
-    ).astype(low)
-    if count == LINE_DEVICES:
-        steps = jnp.transpose(level).reshape(HEADS // 2, 2 * local_rows, 1)
-        joint_grads, out_first = attention_grads(
-            count, 5, attended_rows, branch_gradient, output_weight, queries_flat, kv_all,
-            jnp.broadcast_to(steps, steps.shape[:2] + (128,)), cosine, sine, seq_own[:, None],
-            order_own[:, None], seq_all[None], order_all[None],
-        )
-        (
-            in_portion, out_last, second_grad, first_grad_hidden, small_sum, hidden_grad,
-            adapter_hidden_gradient,
-        ) = closing(
-            count, 6, normed_input, joint_grads, attended_rows, branch_gradient, lowrank_projection,
-            output_projection, layer_input_stream[0], layer_norm_gains[:1], grad_middle, small,
-            input_weight, gate_grad, up_grad, down_grad, adapter_hidden_factors[0], adapter_first,
-            adapter_second,
-        )
-        out_portion = jnp.concatenate([out_first, out_last], axis=1)
-    else:
-        grad_attended = outer_columns(branch_gradient, output_weight).astype(low)
-        grad_att_rows = grad_attended.reshape(local_rows * HEADS, HEAD_SIZE)
-        prob = jnp.exp(score_rows() - level[:, :, None])
-        grad_prob = outer_columns(grad_att_rows, values).reshape(local_rows, HEADS, key_total)
-        centre = jnp.sum(prob * grad_prob, axis=-1, keepdims=True)
-        grad_scores = (
-            (prob * (grad_prob - centre)).astype(low).reshape(local_rows * HEADS, key_total)
-        )
-        prob_again = prob.astype(low).reshape(local_rows * HEADS, key_total)
-        kv_terms = jnp.concatenate(
-            [inner_rows(grad_scores, query_rows) * scale, inner_rows(prob_again, grad_att_rows)],
-            axis=1,
-        ).astype(low)
-        (grad_kv,) = scatter_rows(count, 5, kv_terms)
-        grad_queries = (matrix_product(grad_scores, keys) * scale).reshape(
-            local_rows, HEADS, HEAD_SIZE
-        )
-        query_key_value_gradient = jnp.concatenate(
-            [
-                rotate_back(grad_queries, pos_own).reshape(local_rows, QUERY_WIDTH),
-                rotate_back(grad_kv[:, None, :HEAD_SIZE], pos_own)[:, 0],
-                grad_kv[:, HEAD_SIZE:],
-            ],
-            axis=1,
-        ).astype(low)
-        normed_gradient = outer_columns(query_key_value_gradient, input_weight)
-        grad_resid_part, grad_gain_one = jax.vjp(norm_rows, residual_stream, layer_norm_gains[0])[1](
-            normed_gradient
-        )
-        hidden_grad = grad_middle + grad_resid_part
-        small = small.at[:, 0, :width_own].set(grad_gain_one.reshape(count, width_own))
-        second_terms = jnp.concatenate(
-            [
-                inner_rows(query_key_value_gradient[:, :key_at], lowrank_projection[:, :rank]),
-                inner_rows(
-                    query_key_value_gradient[:, key_at:value_at],
-                    lowrank_projection[:, rank : 2 * rank],
-                ),
-                inner_rows(query_key_value_gradient[:, value_at:], lowrank_projection[:, 2 * rank :]),
-                inner_rows(branch_gradient, output_projection),
-                inner_rows(down_grad, down_factor),
-            ],
-            axis=0,
-        ).astype(low)
-        in_terms = inner_rows(normed_input, query_key_value_gradient).astype(low)
-        out_terms = inner_rows(attended_rows, branch_gradient).astype(low)
-        first_terms = jnp.concatenate(
-            [inner_rows(gate_grad, gate_factor), inner_rows(up_grad, up_factor)], axis=1
-        ).astype(low)
-        in_portion, out_portion, second_grad, first_grad_hidden, small_sum = scatter_rows(
-            count, 6, in_terms, out_terms, second_terms, first_terms, small.reshape(count * 8, 128)
-        )
-        adapter_hidden_gradient = jnp.concatenate(
-            [
-                outer_columns(down_grad, second_down),
-                matrix_product(gate_grad, first_gate),
-                matrix_product(up_grad, first_up),
-            ],
-            axis=1,
-        )
-    gate_other, up_other, down_other, small_sum = lax.optimization_barrier(
-        (gate_other, up_other, down_other, small_sum)
-    )
+    (
+        in_portion, out_last, second_grad, first_grad_hidden, small_sum, hidden_grad,
+        adapter_hidden_gradient,
+    ) = closing(
+        count, 6, normed_input, joint_grads, attended_rows, branch_gradient, lowrank_projection,
+        output_projection, stream, layer_norm_gains[:1], grad_middle, small, lowrank_grads,
+        input_weight, gate_grad, up_grad, down_grad, adapter_hidden_factors[0], adapter_first,
+        adapter_second,
+    )
+    gate_other, gate_last, up_other, down_other, small_sum = lax.optimization_barrier(
+        (gate_other, gate_last, up_other, down_other, small_sum)
+    )
+    gate_other = jnp.concatenate([gate_other, gate_last], axis=0)
     in_low = in_portion.astype(low)
-    out_low = out_portion.astype(low)
+    out_low = jnp.concatenate([out_first, out_last], axis=1).astype(low)
     adapter_first_gradient = jnp.concatenate(
         [
-            outer_columns(in_low[:, :key_at], second_query),
-            outer_columns(in_low[:, key_at:value_at], second_key),
-            outer_columns(in_low[:, value_at:], second_value),
-            outer_columns(out_low, second_output),
+            outer_columns(in_low[:, :key_at], adapter_second[:, :key_at]),
+            outer_columns(in_low[:, key_at:value_at], adapter_second[:, key_at:value_at]),
+            outer_columns(in_low[:, value_at:], adapter_second[:, value_at:PROJECTED_WIDTH]),
+            outer_columns(out_low, adapter_second[:, PROJECTED_WIDTH:down_at]),
             first_grad_hidden,
         ],
         axis=1,
@@ -2039,9 +1957,304 @@
     )
 
 
+def per_device_any(
+    layer_input_stream,
+    layer_output_gradient,
+    attention_in_weight,
+    attention_out_weight,
+    feedforward_weight,
+    layer_norm_gains,
+    adapter_first_factors,
+    adapter_second_factors,
+    adapter_hidden_factors,
+    group_sequence_lengths,
+    token_per_row,
+    token_exit_depth,
+):
+    current_loop = lax.axis_index("loop")
+    dp_index = lax.axis_index("dp")
+    loop_count = lax.axis_size("loop")
+    local_rows = layer_input_stream.shape[1]
+    ffn_rows = feedforward_weight.shape[0]
+    scale = HEAD_SIZE ** (-0.5)
+    live_all, seq_all, order_all, pos_all = token_facts(token_per_row[0], group_sequence_lengths[0])
+    first_row = dp_index * local_rows
+
+    def own_slice(values):
+        return lax.dynamic_slice_in_dim(values, first_row, local_rows, 0)
+
+    live_own = own_slice(live_all)
+    seq_own = own_slice(seq_all)
+    order_own = own_slice(order_all)
+    pos_own = own_slice(pos_all)
+    active_mask = (live_own & (token_exit_depth[0] > current_loop)).astype(jnp.float32)[:, None]
+    residual_stream = layer_input_stream[0].astype(jnp.float32)
+    adapter_first = adapter_first_factors[0]
+    adapter_second = adapter_second_factors[0]
+    adapter_feedforward = adapter_hidden_factors[0]
+    ffn_own = lax.dynamic_slice_in_dim(adapter_feedforward, dp_index * ffn_rows, ffn_rows, 0)
+    input_weight, output_weight = (
+        lax.all_gather(attention_in_weight, "dp", axis=0, tiled=True),
+        lax.all_gather(attention_out_weight, "dp", axis=0, tiled=True),
+    )
+    normed_input = norm_rows(residual_stream, layer_norm_gains[0]).astype(jnp.bfloat16)
+    lowrank_projection = matrix_product(normed_input, adapter_first[:, : 3 * ADAPTER_RANK]).astype(
+        jnp.bfloat16
+    )
+    adapter_query_key_value = jnp.concatenate(
+        [
+            matrix_product(lowrank_projection[:, :ADAPTER_RANK], adapter_second[:, :QUERY_WIDTH]),
+            matrix_product(
+                lowrank_projection[:, ADAPTER_RANK : 2 * ADAPTER_RANK],
+                adapter_second[:, QUERY_WIDTH : QUERY_WIDTH + HEAD_SIZE],
+            ),
+            matrix_product(
+                lowrank_projection[:, 2 * ADAPTER_RANK :],
+                adapter_second[:, QUERY_WIDTH + HEAD_SIZE : PROJECTED_WIDTH],
+            ),
+        ],
+        axis=1,
+    )
+    query_key_value_linear = matrix_product(normed_input, input_weight) + adapter_query_key_value
+    queries = rotate(
+        query_key_value_linear[:, :QUERY_WIDTH].reshape(local_rows, HEADS, HEAD_SIZE), pos_own
+    ).astype(jnp.bfloat16)
+    key_rot = rotate(
+        query_key_value_linear[:, QUERY_WIDTH : QUERY_WIDTH + HEAD_SIZE].reshape(
+            local_rows, 1, HEAD_SIZE
+        ),
+        pos_own,
+    )[:, 0]
+    kv_send = jnp.concatenate(
+        [key_rot, query_key_value_linear[:, QUERY_WIDTH + HEAD_SIZE :]], axis=1
+    ).astype(jnp.bfloat16)
+    kv_all = lax.all_gather(kv_send, "dp", axis=0, tiled=True)
+    keys = kv_all[:, :HEAD_SIZE]
+    values = kv_all[:, HEAD_SIZE:]
+    key_total = kv_all.shape[0]
+    allowed = ((seq_own[:, None] == seq_all[None, :]) & (order_all[None, :] <= order_own[:, None]))[
+        :, None, :
+    ]
+    query_rows = queries.reshape(local_rows * HEADS, HEAD_SIZE)
+
+    def score_rows():
+        raw_scores = (outer_columns(query_rows, keys) * scale).reshape(local_rows, HEADS, key_total)
+        return jnp.where(allowed, raw_scores, FLOOR_SCORE)
+
+    scores = score_rows()
+    top_score = jnp.max(scores, axis=-1, keepdims=True)
+    expo = jnp.exp(scores - top_score)
+    mass = jnp.sum(expo, axis=-1, keepdims=True)
+    prob_low = (expo / mass).astype(jnp.bfloat16)
+    attended_rows = (
+        matrix_product(prob_low.reshape(local_rows * HEADS, key_total), values)
+        .reshape(local_rows, QUERY_WIDTH)
+        .astype(jnp.bfloat16)
+    )
+    output_projection = matrix_product(
+        attended_rows, adapter_first[:, 3 * ADAPTER_RANK : 4 * ADAPTER_RANK]
+    ).astype(jnp.bfloat16)
+    branch_output = matrix_product(attended_rows, output_weight) + matrix_product(
+        output_projection, adapter_second[:, PROJECTED_WIDTH : PROJECTED_WIDTH + MODEL_WIDTH]
+    )
+    middle_state = residual_stream + active_mask * branch_output
+    second_normed_input = norm_rows(middle_state, layer_norm_gains[1]).astype(jnp.bfloat16)
+    feedforward_projection = matrix_product(
+        second_normed_input, adapter_first[:, 4 * ADAPTER_RANK :]
+    ).astype(jnp.bfloat16)
+    normed_all, proj_all = (
+        lax.all_gather(second_normed_input, "dp", axis=0, tiled=True),
+        lax.all_gather(feedforward_projection, "dp", axis=0, tiled=True),
+    )
+    gate_own = outer_columns(normed_all, feedforward_weight[:, 0, :]) + outer_columns(
+        proj_all[:, :ADAPTER_RANK], ffn_own[:, ADAPTER_RANK : 2 * ADAPTER_RANK]
+    )
+    up_own = outer_columns(normed_all, feedforward_weight[:, 1, :]) + outer_columns(
+        proj_all[:, ADAPTER_RANK:], ffn_own[:, 2 * ADAPTER_RANK :]
+    )
+    units_own = geglu(gate_own, up_own).astype(jnp.bfloat16)
+    ffn_sum, low_sum = (
+        lax.psum_scatter(
+            matrix_product(units_own, feedforward_weight[:, 2, :]),
+            "dp",
+            scatter_dimension=0,
+            tiled=True,
+        ),
+        lax.psum_scatter(
+            matrix_product(units_own, ffn_own[:, :ADAPTER_RANK]),
+            "dp",
+            scatter_dimension=0,
+            tiled=True,
+        ),
+    )
+    down_lowrank = low_sum.astype(jnp.bfloat16)
+    complete_output = middle_state + active_mask * (
+        ffn_sum + matrix_product(down_lowrank, adapter_second[:, PROJECTED_WIDTH + MODEL_WIDTH :])
+    )
+    confidence = root_mean(residual_stream) / (
+        root_mean(residual_stream) + root_mean(complete_output - residual_stream)
+    )
+    conf_sum = jnp.sum(jnp.where(live_own, confidence, 0.0))
+    depth_hits = (
+        (token_exit_depth[0][:, None] == jnp.arange(loop_count + 1, dtype=jnp.int32)[None, :])
+        & live_own[:, None]
+    ).astype(jnp.float32)
+    conf_total, depth_total = lax.psum((conf_sum, jnp.sum(depth_hits, axis=0)), ("loop", "dp"))
+    mean_confidence = conf_total / jnp.sum(depth_total)
+    exit_counts = depth_total.astype(jnp.int32)
+    grad_out = layer_output_gradient[0].astype(jnp.float32)
+    feedforward_gradient = (active_mask * grad_out).astype(jnp.bfloat16)
+    lowrank_gradient = outer_columns(
+        feedforward_gradient, adapter_second[:, PROJECTED_WIDTH + MODEL_WIDTH :]
+    ).astype(jnp.bfloat16)
+    grad_ffn_all, grad_low_all = (
+        lax.all_gather(feedforward_gradient, "dp", axis=0, tiled=True),
+        lax.all_gather(lowrank_gradient, "dp", axis=0, tiled=True),
+    )
+    hidden_unit_gradient = outer_columns(grad_ffn_all, feedforward_weight[:, 2, :]) + outer_columns(
+        grad_low_all, ffn_own[:, :ADAPTER_RANK]
+    )
+    grad_gate_own, grad_up_own = jax.vjp(geglu, gate_own, up_own)[1](hidden_unit_gradient)
+    grad_gate_own = grad_gate_own.astype(jnp.bfloat16)
+    grad_up_own = grad_up_own.astype(jnp.bfloat16)
+    input_terms = matrix_product(grad_gate_own, feedforward_weight[:, 0, :]) + matrix_product(
+        grad_up_own, feedforward_weight[:, 1, :]
+    )
+    proj_terms = jnp.concatenate(
+        [
+            matrix_product(grad_gate_own, ffn_own[:, ADAPTER_RANK : 2 * ADAPTER_RANK]),
+            matrix_product(grad_up_own, ffn_own[:, 2 * ADAPTER_RANK :]),
+        ],
+        axis=1,
+    )
+    grad_norm_base, grad_proj = (
+        lax.psum_scatter(input_terms, "dp", scatter_dimension=0, tiled=True),
+        lax.psum_scatter(proj_terms, "dp", scatter_dimension=0, tiled=True),
+    )
+    ffn_grad = jnp.concatenate(
+        [
+            inner_rows(grad_gate_own, normed_all),
+            inner_rows(grad_up_own, normed_all),
+            inner_rows(units_own, grad_ffn_all),
+            inner_rows(units_own, grad_low_all),
+            inner_rows(grad_gate_own, proj_all[:, :ADAPTER_RANK]),
+            inner_rows(grad_up_own, proj_all[:, ADAPTER_RANK:]),
+        ],
+        axis=1,
+    )
+    lowrank_projection_gradient = grad_proj.astype(jnp.bfloat16)
+    second_normed_gradient = grad_norm_base + outer_columns(
+        lowrank_projection_gradient, adapter_first[:, 4 * ADAPTER_RANK :]
+    )
+    grad_middle_part, grad_gain_two = jax.vjp(norm_rows, middle_state, layer_norm_gains[1])[1](
+        second_normed_gradient
+    )
+    grad_middle = grad_out + grad_middle_part
+    branch_gradient = (active_mask * grad_middle).astype(jnp.bfloat16)
+    output_projection_gradient = outer_columns(
+        branch_gradient, adapter_second[:, PROJECTED_WIDTH : PROJECTED_WIDTH + MODEL_WIDTH]
+    ).astype(jnp.bfloat16)
+    grad_attended = (
+        outer_columns(branch_gradient, output_weight)
+        + outer_columns(
+            output_projection_gradient, adapter_first[:, 3 * ADAPTER_RANK : 4 * ADAPTER_RANK]
+        )
+    ).astype(jnp.bfloat16)
+    grad_att_rows = grad_attended.reshape(local_rows * HEADS, HEAD_SIZE)
+    prob = jnp.exp(score_rows() - top_score) / mass
+    grad_prob = outer_columns(grad_att_rows, values).reshape(local_rows, HEADS, key_total)
+    centre = jnp.sum(prob * grad_prob, axis=-1, keepdims=True)
+    grad_scores = (
+        (prob * (grad_prob - centre)).astype(jnp.bfloat16).reshape(local_rows * HEADS, key_total)
+    )
+    grad_queries = (matrix_product(grad_scores, keys) * scale).reshape(local_rows, HEADS, HEAD_SIZE)
+    prob_again = prob.astype(jnp.bfloat16).reshape(local_rows * HEADS, key_total)
+    kv_terms = jnp.concatenate(
+        [inner_rows(grad_scores, query_rows) * scale, inner_rows(prob_again, grad_att_rows)], axis=1
+    )
+    grad_kv = lax.psum_scatter(kv_terms, "dp", scatter_dimension=0, tiled=True)
+    query_linear_gradient = (
+        rotate_back(grad_queries, pos_own).reshape(local_rows, QUERY_WIDTH).astype(jnp.bfloat16)
+    )
+    key_linear_gradient = rotate_back(grad_kv[:, None, :HEAD_SIZE], pos_own)[:, 0].astype(
+        jnp.bfloat16
+    )
+    value_linear_gradient = grad_kv[:, HEAD_SIZE:].astype(jnp.bfloat16)
+    query_key_value_gradient = jnp.concatenate(
+        [query_linear_gradient, key_linear_gradient, value_linear_gradient], axis=1
+    )
+    attention_projection_gradient = jnp.concatenate(
+        [
+            outer_columns(query_linear_gradient, adapter_second[:, :QUERY_WIDTH]),
+            outer_columns(
+                key_linear_gradient, adapter_second[:, QUERY_WIDTH : QUERY_WIDTH + HEAD_SIZE]
+            ),
+            outer_columns(
+                value_linear_gradient, adapter_second[:, QUERY_WIDTH + HEAD_SIZE : PROJECTED_WIDTH]
+            ),
+        ],
+        axis=1,
+    ).astype(jnp.bfloat16)
+    normed_gradient = outer_columns(query_key_value_gradient, input_weight) + outer_columns(
+        attention_projection_gradient, adapter_first[:, : 3 * ADAPTER_RANK]
+    )
+    grad_resid_part, grad_gain_one = jax.vjp(norm_rows, residual_stream, layer_norm_gains[0])[1](
+        normed_gradient
+    )
+    hidden_grad = grad_middle + grad_resid_part
+    grad_w_in = inner_rows(normed_input, query_key_value_gradient)
+    grad_w_out = inner_rows(attended_rows, branch_gradient)
+    grad_gains = jnp.stack([grad_gain_one, grad_gain_two])
+    adapter_first_gradient = jnp.concatenate(
+        [
+            inner_rows(normed_input, attention_projection_gradient),
+            inner_rows(attended_rows, output_projection_gradient),
+            inner_rows(second_normed_input, lowrank_projection_gradient),
+        ],
+        axis=1,
+    )
+    adapter_second_gradient = jnp.concatenate(
+        [
+            inner_rows(lowrank_projection[:, :ADAPTER_RANK], query_linear_gradient),
+            inner_rows(lowrank_projection[:, ADAPTER_RANK : 2 * ADAPTER_RANK], key_linear_gradient),
+            inner_rows(lowrank_projection[:, 2 * ADAPTER_RANK :], value_linear_gradient),
+            inner_rows(output_projection, branch_gradient),
+            inner_rows(down_lowrank, feedforward_gradient),
+        ],
+        axis=1,
+    )
+    input_portion, output_portion, gain_portion, adapter_first_grads, adapter_second_grads = (
+        lax.psum_scatter(grad_w_in, "dp", scatter_dimension=0, tiled=True),
+        lax.psum_scatter(grad_w_out, "dp", scatter_dimension=0, tiled=True),
+        lax.psum_scatter(grad_gains, "dp", scatter_dimension=1, tiled=True),
+        lax.psum_scatter(adapter_first_gradient, "dp", scatter_dimension=0, tiled=True),
+        lax.psum_scatter(adapter_second_gradient, "dp", scatter_dimension=1, tiled=True),
+    )
+    mlp_part = ffn_grad[:, : 3 * MODEL_WIDTH].reshape(ffn_rows, 3, MODEL_WIDTH)
+    sum_in, sum_out, sum_gains, sum_mlp = (
+        lax.psum(input_portion.astype(jnp.bfloat16), "loop").astype(jnp.float32),
+        lax.psum(output_portion.astype(jnp.bfloat16), "loop").astype(jnp.float32),
+        lax.psum(gain_portion.astype(jnp.bfloat16), "loop").astype(jnp.float32),
+        lax.psum(mlp_part.astype(jnp.bfloat16), "loop").astype(jnp.float32),
+    )
+    return (
+        complete_output.astype(jnp.bfloat16)[None],
+        hidden_grad[None],
+        sum_in,
+        sum_out,
+        sum_mlp,
+        sum_gains,
+        adapter_first_grads[None],
+        adapter_second_grads[None],
+        ffn_grad[:, 3 * MODEL_WIDTH :][None],
+        exit_counts,
+        mean_confidence,
+    )
+
+
 def solution(mesh):
     return jax.shard_map(
-        per_device,
+        per_device if mesh.shape == {"loop": 2, "dp": LINE_DEVICES} else per_device_any,
         mesh=mesh,
         in_specs=(
             P("loop", "dp", None),

time: 706 us -> 654 us (0.926)
  matrix products: 26.8 us -> 1.32 us
  waiting for transfers between devices: 34.1 us -> 12.8 us
  Pallas kernels: 550 us -> 565 us
  between operations: 17.7 us -> 4 us
    dot_general x9 -> x0, matrix products: 22 us -> none  [matrix_product(): return jnp.dot(left, right, preferred_element_type=jnp.float32)]
    all_gather x1 -> x0, waiting for transfers between devices: 18.5 us -> none  [per_device(): lax.all_gather(feedforward_gradient, 'dp', axis=0, tiled=True)]
    pallas_call x2, Pallas kernels: 144 us -> 158 us  [the longest x1 81.3 us: opening(): pl.pallas_call(functools.partial(opening_body, count, shares, number), ou...]
  transfers between devices with their start and end apart: 7 -> 6, of which waited for: 3 -> 2; matrix products, arithmetic and copies ran while one was open for 10% -> 6% of each run, Pallas kernels for 35% -> 33%
where the time goes in v4:
time: 654 us; the launch traced here: 649 us
  Pallas kernels  565 us (86%)
  other arithmetic  45.2 us (7%)
  local copies, waits for them, and re-layouts  14.1 us (2%)
  waiting for transfers between devices  12.8 us (2%)
  starting transfers between devices  6.82 us (1%)
    pallas_call x1, Pallas kernels, closing(): pl.pallas_call(functools.partial(closing_body, count), out_shape=[jax.Sha...  135 us
    pallas_call x1, Pallas kernels, unit_grads(): pl.pallas_call(functools.partial(unit_grads_body, count, parts), out_shap...  121 us
    pallas_call x1, Pallas kernels, opening(): pl.pallas_call(functools.partial(opening_body, count, shares, number), ou...  81.3 us
    pallas_call x1, Pallas kernels, attention(): pl.pallas_call(functools.partial(attention_body, count), out_shape=[shape...  76.6 us
    pallas_call x1, Pallas kernels, attention_grads(): pl.pallas_call(functools.partial(attention_grads_body, count), out_shape=...  76.3 us
    pallas_call x1, Pallas kernels, hidden_units(): pl.pallas_call(functools.partial(hidden_body, count, parts), out_shape=[a...  73.6 us
    another operation x3, other arithmetic, per_device(): jnp.stack([gate_grad.astype(jnp.float32) + gate_other.astype(jnp.float32)...  23.6 us
  transfers between devices with their start and end apart: 6, of which 2 were waited for; matrix products, arithmetic and copies ran while one was open for 6% of the time, Pallas kernels for 33%

profile of v4, /device:TPU:0, one launch (start us, length us, event | category | flops | bytes accessed | tf_op | source)
XLA Modules:
  0.0 648.8 jit_solution(9533694726086311639)
XLA Ops:
  6.7 2.0 fusion.3.grads
  9.4 1.4 fusion.19
  11.5 1.3 compare_select_fusion
  12.9 1.0 multiply_sine_fusion
  13.8 81.3 %opening.1 = (bf16[16,128,2560]{2,1,0:T(8,128)(2,1)}, bf16[16,128,2048]{2,1,0:T(8,128)(2,1)}, bf16[3,1024,2048]{2,1,0:T(8,128)(2,1)}, bf16[128,2048]{1,0:T(8,128)(2,1)}, bf16[128,768]{1,0:T(8,128)(2,1)}) custom-call(bf16[128,2048]{1,0:T(8,128)(2,1)} %bitcast.71, f32[1,2048]{1,0:T(1,128)} %get-tuple-element.121.gain, bf16[128,2560]{1,0:T(8,128)(2,1)} %refs_0_.1, ...), custom_call_target="tpu_custom_call" | custom-call | tf_op jit(solution)/shard_map/opening/pallas_call | solution.py:456
  95.1 76.6 %attention.1 = (bf16[128,2048]{1,0:T(8,128)(2,1)}, bf16[128,2048]{1,0:T(8,128)(2,1)}, bf16[128,256]{1,0:T(8,128)(2,1)}, f32[4,256,128]{2,1,0:T(8,128)}, f32[128,...) custom-call(bf16[128,2048]{1,0:T(8,128)(2,1)} %get-tuple-element.73.nor, ...), custom_call_target="tpu_custom_call" | custom-call | tf_op jit(solution)/shard_map/attention/pallas_call | solution.py:644
  171.7 73.6 %hidden_units.1 = (bf16[2048,1024]{1,0:T(8,128)(2,1)}, bf16[2048,1024]{1,0:T(8,128)(2,1)}, bf16[2048,1024]{1,0:T(8,128)(2,1)}, bf16[16,128,2048]{2,1,0:T(8,128)(2,1)}) custom-call(bf16[128,2048]{1,0:T(8,128)(2,1)} %get-tuple-element.78.own, bf16[16,128,2048]{2,1,0:T(8,128)(2,1)} %get-tuple-element.79.grads.grads_all, ...), custom_call_target="tpu_custom_call" | custom-call | tf_op jit(solution)/shard_map/hidden_units/pallas_call | solution.py:868
  245.4 121.4 %unit_grads.1 = (f32[128,2048]{1,0:T(8,128)}, f32[128,2048]{1,0:T(8,128)}, bf16[1024,2048]{1,0:T(8,128)(2,1)}, bf16[1024,2048]{1,0:T(8,128)(2,1)}, bf16[1024,204...) custom-call(bf16[2048,1024]{1,0:T(8,128)(2,1)} %get-tuple-element.81.units, bf16[2048,1024]{1,0:T(8,128)(2,1)} %get-tuple-element.82.gate_grads, ...), custom_call_target="tpu_custom_call" | custom-call | tf_op jit(solution)/shard_map/unit_grads/pallas_call | solution.py:1201
  366.9 1.5 collective-permute-start.3
  369.0 2.3 slice.88
  371.3 1.5 collective-permute-start.2
  372.9 2.9 multiply_reduce_fusion
  377.7 1.5 multiply_convert_fusion
  379.2 76.3 %attention_grads.1 = (bf16[128,2560]{1,0:T(8,128)(2,1)}, bf16[128,768]{1,0:T(8,128)(2,1)}, f32[128,1536]{1,0:T(8,128)}) custom-call(bf16[128,2048]{1,0:T(8,128)(2,1)} %get-tuple-element.86.attended, bf16[128,2048]{1,0:T(8,128)(2,1)} %get-tuple-element.114.grad_rows, bf16[2048,2048]{1,0:T(8,128)(2,1)} %bitcast.69, ...), custom_call_target="tpu_custom_call" | custom-call | tf_op jit(solution)/shard_map/attention_grads/pallas_call | solution.py:1537
  455.5 135.3 %closing.1 = (f32[128,2560]{1,0:T(8,128)}, f32[128,512]{1,0:T(8,128)}, f32[416,256]{1,0:T(8,128)}, f32[128,512]{1,0:T(8,128)}, f32[8,128]{1,0:T(8,128)}, /*index=5*/f32[128,2048]{1,0:T(8,128)}, f32[1024,768]{1,0:T(8,128)}) custom-call(bf16[128,2048]{1,0:T(8,128)(2,1)} %get-tuple-element.73.normed, bf16[128,2560]{1,0:T(8,128)(2,1)} %get-tuple-element.91.joint_grads, ...), custom_call_target="tpu_custom_call" | custom-call | tf_op jit(solution)/shard_map/closing/pallas_call | solution.py:1778
  590.9 1.1 convert.8
  592.1 1.1 collective-permute-start.1
  593.2 1.4 convert_element_type.80
  594.6 1.1 collective-permute-start
  597.1 0.9 copy-done.16
  598.0 6.9 %collective-permute-done.1 = bf16[128,2048]{1,0:T(8,128)(2,1)S(1)} collective-permute-done((bf16[128,2048]{1,0:T(8,128)(2,1)S(1)}, bf16[128,2048]{1,0:T(8,128)(2,1)S(1)}, u32[]{:S(2)}, u32[]{:S(2)}) %collective-permute-start.1) | collective-permute-done | bytes 524320 | tf_op jit(solution)/shard_map/ppermute | solution.py:1807
  604.9 1.1 convert_add_fusion.2
  606.0 6.0 collective-permute-done
  611.9 1.2 convert_add_fusion.1
  613.1 1.1 collective-permute-start.5
  614.2 3.1 add_bitcast_fusion.2
  617.4 8.3 %add_bitcast_fusion = (f32[1024,1,2048]{2,0,1:T(8,128)S(1)}, f32[1024,1,2048]{2,0,1:T(8,128)}) fusion(bf16[1024,2048]{1,0:T(8,128)(2,1)} %collective-permute-done.4, bf16[1024,2048]{1,0:T(8,128)(2,1)} %get-tuple-element.96.down_grads, bf16[1024,2048]{1,0:T(8,128)(2,1)} %collective-permute-done.3, bf16[1024,2048]{1,0:T(8,128)(2,1)S(1)} %copy-done.2), kind=kLoop, calls=%fused_computation.1 | loop fusion | flops 12582912 | bytes 33554432 | tf_op jit(solution)/shard_map/stack | solution.py:1937
  625.7 12.2 %pad_maximum_fusion = f32[1024,3,2048]{2,0,1:T(8,128)} fusion(f32[1024,1,2048]{2,0,1:T(8,128)S(1)} %get-tuple-element.130, f32[1024,1,2048]{2,0,1:T(8,128)} %get-tuple-element.131, f32[1024,1,2048]{2,0,1:T(8,128)S(1)} %add_bitcast_fusion.2), kind=kLoop, calls=%fused_computation | loop fusion | flops 12582912 | bytes 50331648 | tf_op jit(solution)/shard_map/stack | solution.py:1937
  637.8 1.2 slice_reduce_fusion
  641.4 2.3 copy.41
  643.7 1.8 copy.42
  645.5 1.7 copy.43
  (69 shorter events, 12.6 us)
Async XLA Ops:
  245.4 127.4 %copy-start.3 = (f32[128,2048]{1,0:T(8,128)S(1)}, f32[128,2048]{1,0:T(8,128)}, u32[]{:S(2)}) copy-start(f32[128,2048]{1,0:T(8,128)} %get-tuple-element.77) | copy-start | bytes 3145732
  245.4 127.5 %copy-start.4 = (bf16[1,128,2048]{2,1,0:T(8,128)(2,1)S(1)}, bf16[1,128,2048]{2,1,0:T(8,128)(2,1)}, u32[]{:S(2)}) copy-start(bf16[1,128,2048]{2,1,0:T(8,128)(2,1)} %param.16) | copy-start | bytes 1572868
  245.4 127.5 %copy-start.13 = (f32[1,2048]{1,0:T(1,128)S(1)}, f32[1,2048]{1,0:T(1,128)}, u32[]{:S(2)}) copy-start(f32[1,2048]{1,0:T(1,128)} %get-tuple-element.120.gain) | copy-start | bytes 24580
  366.8 9.0 %copy-start.15 = (s32[1,128]{1,0:T(1,128)S(1)}, s32[1,128]{1,0:T(1,128)}, u32[]{:S(2)}) copy-start(s32[1,128]{1,0:T(1,128)} %param.27) | copy-start | bytes 1540
  366.9 10.8 %copy-start.6 = (f32[128,2048]{1,0:T(8,128)S(1)}, f32[128,2048]{1,0:T(8,128)}, u32[]{:S(2)}) copy-start(f32[128,2048]{1,0:T(8,128)} %get-tuple-element.87) | copy-start | bytes 3145732
  366.9 10.8 %copy-start.9 = (bf16[1,128,2048]{2,1,0:T(8,128)(2,1)S(1)}, bf16[1,128,2048]{2,1,0:T(8,128)(2,1)}, u32[]{:S(2)}) copy-start(bf16[1,128,2048]{2,1,0:T(8,128)(2,1)} %param.17) | copy-start | bytes 1572868
  366.9 246.2 %collective-permute-start.3 = (bf16[1024,2048]{1,0:T(8,128)(2,1)}, bf16[1024,2048]{1,0:T(8,128)(2,1)}, u32[]{:S(2)}, u32[]{:S(2)}) collective-permute-start(bf16[1024,2048]{1,0:T(8,128)(2,1)} %get-tuple-element.95.up_grads), channel_id=1, source_target_pairs={{0,16},{16,0},{1,17},{17,1},{2,18},{18,2},{3,19},{19,3},{4,20},{20... | collective-permute-start | bytes 12582920 | tf_op jit(solution)/shard_map/ppermute | solution.py:1807
  368.4 244.7 %collective-permute-start.4 = (bf16[1024,2048]{1,0:T(8,128)(2,1)}, bf16[1024,2048]{1,0:T(8,128)(2,1)}, u32[]{:S(2)}, u32[]{:S(2)}) collective-permute-start(bf16[1024,2048]{1,0:T(8,128)(2,1)} %get-tuple-element.96.down_grads), channel_id=1, source_target_pairs={{0,16},{16,0},{1,17},{17,1},{2,18},{18,2},{3,19},{19,3},{4,20},{20... | collective-permute-start | bytes 12582920 | tf_op jit(solution)/shard_map/ppermute | solution.py:1807
  371.3 241.8 %collective-permute-start.2 = (bf16[256,2048]{1,0:T(8,128)(2,1)}, bf16[256,2048]{1,0:T(8,128)(2,1)}, u32[]{:S(2)}, u32[]{:S(2)}) collective-permute-start(bf16[256,2048]{1,0:T(8,128)(2,1)} %slice.88), channel_id=1, source_target_pairs={{0,16},{16,0},{1,17},{17,1},{2,18},{18,2},{3,19},{19,3},{4,20},{20... | collective-permute-start | bytes 3145736 | tf_op jit(solution)/shard_map/ppermute | solution.py:1807
  377.6 77.9 %copy-start.12 = (f32[16,8,128]{2,1,0:T(8,128)}, f32[16,8,128]{2,1,0:T(8,128)S(1)}, u32[]{:S(2)}) copy-start(f32[16,8,128]{2,1,0:T(8,128)S(1)} %scatter.9.small) | copy-start | bytes 196612
  455.5 136.5 %copy-start.10 = (f32[128,1536]{1,0:T(8,128)S(1)}, f32[128,1536]{1,0:T(8,128)}, u32[]{:S(2)}) copy-start(f32[128,1536]{1,0:T(8,128)} %get-tuple-element.99) | copy-start | bytes 2359300
  590.9 4.8 copy-start
  592.1 5.0 copy-start.11
  592.1 12.7 %collective-permute-start.1 = (bf16[128,2048]{1,0:T(8,128)(2,1)S(1)}, bf16[128,2048]{1,0:T(8,128)(2,1)S(1)}, u32[]{:S(2)}, u32[]{:S(2)}) collective-permute-start(bf16[128,2048]{1,0:T(8,128)(2,1)S(1)} %pad_maximum_fusion.1), channel_id=1, source_target_pairs={{0,16},{16,0},{1,17},{17,1},{2,18},{18,2},{3,19},{19,3},{4,20},{20... | collective-permute-start | bytes 1572872 | tf_op jit(solution)/shard_map/ppermute | solution.py:1807
  594.6 17.3 %copy-start.5 = (f32[128,2560]{1,0:T(8,128)S(1)}, f32[128,2560]{1,0:T(8,128)}, u32[]{:S(2)}) copy-start(f32[128,2560]{1,0:T(8,128)} %get-tuple-element.98) | copy-start | bytes 3932164
  594.6 17.3 %collective-permute-start = (bf16[128,2560]{1,0:T(8,128)(2,1)S(1)}, bf16[128,2560]{1,0:T(8,128)(2,1)S(1)}, u32[]{:S(2)}, u32[]{:S(2)}) collective-permute-start(bf16[128,2560]{1,0:T(8,128)(2,1)S(1)} %convert_element_type.80), channel_id=1, source_target_pairs={{0,16},{16,0},{1,17},{17,1},{2,18},{18,2},{3,19},{19,3},{4,20},{20... | collective-permute-start | bytes 1966088 | tf_op jit(solution)/shard_map/ppermute | solution.py:1807
  596.6 16.6 %copy-start.14 = (f32[8,128]{1,0:T(8,128)S(1)}, f32[8,128]{1,0:T(8,128)}, u32[]{:S(2)}) copy-start(f32[8,128]{1,0:T(8,128)} %get-tuple-element.107) | copy-start | bytes 12292
  596.6 17.7 %copy-start.1 = (bf16[1024,2048]{1,0:T(8,128)(2,1)S(1)}, bf16[1024,2048]{1,0:T(8,128)(2,1)}, u32[]{:S(2)}) copy-start(bf16[1024,2048]{1,0:T(8,128)(2,1)} %get-tuple-element.94.gate_grads) | copy-start | bytes 12582916
  596.6 17.7 %copy-start.7 = (bf16[768,2048]{1,0:T(8,128)(2,1)S(1)}, bf16[768,2048]{1,0:T(8,128)(2,1)}, u32[]{:S(2)}) copy-start(bf16[768,2048]{1,0:T(8,128)(2,1)} %get-tuple-element.103) | copy-start | bytes 9437188
  597.1 0.9 copy-start.16
  613.1 4.2 copy-start.2
  613.1 24.7 %collective-permute-start.5 = (f32[8,128]{1,0:T(8,128)S(1)}, f32[8,128]{1,0:T(8,128)S(1)}, u32[]{:S(2)}, u32[]{:S(2)}) collective-permute-start(f32[8,128]{1,0:T(8,128)S(1)} %copy-done.14), channel_id=1, source_target_pairs={{0,16},{16,0},{1,17},{17,1},{2,18},{18,2},{3,19},{19,3},{4,20},{20... | collective-permute-start | bytes 12296 | tf_op jit(solution)/shard_map/ppermute | solution.py:1807
  625.6 19.9 %copy-start.8 = (f32[1024,768]{1,0:T(8,128)S(1)}, f32[1024,768]{1,0:T(8,128)}, u32[]{:S(2)}) copy-start(f32[1024,768]{1,0:T(8,128)} %get-tuple-element.110) | copy-start | bytes 9437188

commit v5 on v4

--- a/solution.py
+++ b/solution.py
@@ -136,8 +136,8 @@
     )
 
 
-def gather_plan(count, spans, own, full, sems, far_sems=None):
-    keep, recv, send_core, send_pair, send_right, send_left = sems
+def gather_plan(count, spans, own, full, sems, far_sems=None, twins=False):
+    keep, recv, send_core, send_pair, send_right, send_left, send_twin = sems
     arrays = len(own)
     me, depth, z, y, c = place(count)
     mate = me + 2 - 4 * y
@@ -171,6 +171,13 @@
         a, s = unit
         return copy(unit, block, me - 4, send_left.at[a, block // 4, s], first)
 
+    def to_twin(unit, block):
+        a, s = unit
+        return copy(unit, block, me + 4 - 8 * (z % 2), send_twin.at[a])
+
+    def shared(unit):
+        return twins and unit[1] == 1
+
     def to_far(a, block):
         rows = pl.ds(*spans[a][0])
         return pltpu.make_async_remote_copy(
@@ -229,7 +236,14 @@
             def _():
                 to_right(unit, block).start()
 
-            to_pair(unit, block).start()
+            if k == 1 and shared(unit):
+
+                @pl.when(z % 2 == 0)
+                def _():
+                    to_pair(unit, block).start()
+
+            else:
+                to_pair(unit, block).start()
             to_core(unit, block).start()
             cross(unit, block)
 
@@ -242,7 +256,14 @@
             def _():
                 to_left(unit, block).start()
 
-            to_pair(unit, block).start()
+            if k == 1 and shared(unit):
+
+                @pl.when(z % 2 == 1)
+                def _():
+                    to_pair(unit, block).start()
+
+            else:
+                to_pair(unit, block).start()
             to_core(unit, block).start()
             cross(unit, block)
 
@@ -254,6 +275,8 @@
     def from_pair(k, unit):
         if k == 0:
             pass_on(unit, mate)
+            if shared(unit):
+                to_twin(unit, mate).start()
             return
 
         @pl.when(z - k >= 0)
@@ -283,16 +306,17 @@
             far_on(a, me + 4 * k)
             far_on(a, mate + 4 * k)
 
-    def arrive():
+    def arrive(block=None, mine=True):
         for unit in units:
-            for j in range(count // 2):
-                to_core(unit, 2 * j + 1 - c).wait_recv()
+            for j in range(count // 2 if block is None else 1):
+                to_core(unit, 2 * j + 1 - c if block is None else block).wait_recv()
         if far_sems is not None:
             for a in range(arrays):
                 for j in range(count // 2):
                     far_core(a, 2 * j + 1 - c).wait_recv()
-        for item in local:
-            item.wait()
+        if mine:
+            for item in local:
+                item.wait()
 
     def finish():
         for unit in units:
@@ -300,7 +324,14 @@
                 to_core(unit, 2 * j + c).wait_send()
             for j in range(depth):
                 block = 4 * j + 2 * y + c
-                to_pair(unit, block).wait_send()
+                if shared(unit):
+
+                    @pl.when(j != z + 1 - 2 * (z % 2))
+                    def _():
+                        to_pair(unit, block).wait_send()
+
+                else:
+                    to_pair(unit, block).wait_send()
 
                 @pl.when((z >= j) & (z < depth - 1))
                 def _():
@@ -309,6 +340,9 @@
                 @pl.when((z <= j) & (z > 0))
                 def _():
                     to_left(unit, block).wait_send()
+
+            if shared(unit):
+                to_twin(unit, mate).wait_send()
 
         if far_sems is not None:
             for a in range(arrays):
@@ -332,6 +366,7 @@
         sem((number, depth, parts)),
         sem((number, depth, parts)),
         sem((number, depth, parts)),
+        sem((number,)),
     ]
 
 
@@ -370,7 +405,7 @@
             ]
         )
     units, begin, from_line, from_pair, from_far, arrive, finish = gather_plan(
-        count, spans, own, full, scratch[8:14], scratch[14:18]
+        count, spans, own, full, scratch[8:15], scratch[15:19]
     )
     begin()
     fills = [
@@ -511,10 +546,10 @@
     low = jnp.bfloat16
     greet(count)
     kv_units, kv_begin, kv_line, kv_pair, _, kv_arrive, kv_finish = gather_plan(
-        count, [even_spans(height, 1)], (kv_own,), (kv_full,), sems[:6]
+        count, [even_spans(height, 1)], (kv_own,), (kv_full,), sems[:7]
     )
     units, begin, from_line, from_pair, _, arrive, finish = gather_plan(
-        count, [even_spans(height, 2)], (grads,), (grads_all,), sems[6:]
+        count, [even_spans(height, 2)], (grads,), (grads_all,), sems[7:], twins=True
     )
     loads = [
         pltpu.make_async_copy(source, bank, load_sem.at[i])
@@ -528,6 +563,7 @@
             )
         )
     ]
+    begin()
     for item in loads:
         item.start()
     loads[0].wait()
@@ -542,7 +578,6 @@
     kv_own[:, :size] = turn(head(QUERY_WIDTH, 1), cosine[...], sine[...]).astype(low)
     kv_own[:, size:] = head(QUERY_WIDTH + size, 2).astype(low)
     kv_begin()
-    begin()
     heads = wide // size
 
     def some_heads(start, stop):
@@ -677,566 +712,10 @@
     )
 
 
-def line_order(z):
-    near = z < 2
-    return [z, z + 1 - 2 * (z % 2), jnp.where(near, 2, 1), jnp.where(near, 3, 0)]
-
-
-def unit_values(gate, up, grad):
-    slope = 0.7978845608028654
-    cubic = 0.044715
-    square = gate * gate
-    curve = jnp.tanh(slope * (gate + cubic * square * gate))
-    half = 0.5 * (1.0 + curve)
-    turned = gate * half
-    rise = half + 0.5 * gate * (1.0 - curve * curve) * slope * (1.0 + 3.0 * cubic * square)
-    low = jnp.bfloat16
-    return (turned * up).astype(low), (grad * up * rise).astype(low), (grad * turned).astype(low)
-
-
-def hidden_body(count, parts, own, grads, weights, units, gate_grads, up_grads, rows_out,
-                held, bank, coming, done, recv, send_core, send_pair, send_line, keep, bank_sem,
-                coming_sem, done_sem, rows_sem):
+def sum_plan(count, parts, mine, theirs, core_in, pair_in, line_in, twin_in, sems,
+             twins=True):
     me, depth, z, y, c = place(count)
-    height = own.shape[0]
-    width = bank.shape[1]
-    step = height // parts
-    tile = 512
-    core, mate = me + 1 - 2 * c, me + 2 - 4 * y
-    lines = line_order(z)
-    greet(count)
-
-    def hop(block, s, target, sem, first=False):
-        rows = pl.ds(s * step, step)
-        return pltpu.make_async_remote_copy(
-            src_ref=own.at[rows] if first else held.at[block, rows],
-            dst_ref=held.at[block, rows],
-            send_sem=sem,
-            recv_sem=recv.at[block, s],
-            device_id={"dp": target},
-            device_id_type=MESH,
-        )
-
-    def to_core(block, s, first=False):
-        return hop(block, s, core, send_core.at[block // 2, s], first)
-
-    def to_pair(block, s, first=False):
-        return hop(block, s, mate, send_pair.at[block // 4, s], first)
-
-    def to_right(block, s, first=False):
-        return hop(block, s, me + 4, send_line.at[0, block // 4, s], first)
-
-    def to_left(block, s, first=False):
-        return hop(block, s, me - 4, send_line.at[1, block // 4, s], first)
-
-    for s in range(parts):
-
-        @pl.when(z > 0)
-        def _():
-            to_left(me, s, True).start()
-
-        @pl.when(z < depth - 1)
-        def _():
-            to_right(me, s, True).start()
-
-        to_core(me, s, True).start()
-        to_pair(me, s, True).start()
-    mine = pltpu.make_async_copy(own, held.at[me], keep)
-    mine.start()
-    fills = [
-        pltpu.make_async_copy(weights.at[i], bank.at[i], bank_sem.at[i]) for i in range(3)
-    ]
-    for fill in fills:
-        fill.start()
-
-    def first_of(line, pair):
-        return 4 * line + 2 * pair
-
-    def fetch(line, pair, slot):
-        return pltpu.make_async_copy(
-            grads.at[pl.ds(first_of(line, pair), 2)], coming.at[slot], coming_sem.at[slot]
-        )
-
-    def store(line, pair, slot):
-        rows = pl.ds(first_of(line, pair) * height, 2 * height)
-        return [
-            pltpu.make_async_copy(done.at[slot, i], out.at[rows], done_sem.at[slot, i])
-            for i, out in enumerate((units, gate_grads, up_grads))
-        ]
-
-    def keep_rows(line, pair):
-        some = pl.ds(first_of(line, pair), 2)
-        return pltpu.make_async_copy(held.at[some], rows_out.at[some], rows_sem.at[line, pair])
-
-    def from_line(line):
-        block = first_of(line, y) + c
-        for s in range(parts):
-            hop(block, s, core, send_core.at[block // 2, s]).wait_recv()
-
-            @pl.when((line < z) & (z < depth - 1))
-            def _():
-                to_right(block, s).start()
-
-            @pl.when((line > z) & (z > 0))
-            def _():
-                to_left(block, s).start()
-
-            to_pair(block, s).start()
-            to_core(block, s).start()
-
-    def from_pair(line):
-        block = first_of(line, 1 - y) + c
-        for s in range(parts):
-            to_core(block, s).wait_recv()
-            to_core(block, s).start()
-
-    steps = [(line, pair) for line in lines for pair in (y, 1 - y)]
-
-    def work(index):
-        line, pair = steps[index]
-        slot = index % 2
-        for s in range(parts):
-            to_core(first_of(line, pair) + 1 - c, s).wait_recv()
-        if index == 0:
-            mine.wait()
-            fetch(line, pair, slot).start()
-            for fill in fills:
-                fill.wait()
-        if index + 1 < len(steps):
-            fetch(*steps[index + 1], 1 - slot).start()
-        fetch(line, pair, slot).wait()
-        keep_rows(line, pair).start()
-        if index >= 2:
-            for item in store(*steps[index - 2], slot):
-                item.wait()
-        some = pl.ds(first_of(line, pair), 2)
-
-        def inner(n, carry):
-            cols = pl.ds(pl.multiple_of(n * tile, tile), tile)
-            block = held[some].reshape(2 * height, held.shape[2])
-            gate = contract(block, bank[0, cols], 1, 1)
-            up = contract(block, bank[1, cols], 1, 1)
-            grad = contract(coming[slot].reshape(2 * height, held.shape[2]), bank[2, cols], 1, 1)
-            for i, value in enumerate(unit_values(gate, up, grad)):
-                done[slot, i, :, cols] = value
-            return carry
-
-        lax.fori_loop(0, width // tile, inner, 0)
-        for item in store(line, pair, slot):
-            item.start()
-
-    work(0)
-    from_pair(lines[0])
-    from_line(lines[1])
-    work(1)
-    for k in range(1, depth):
-        from_pair(lines[k])
-        work(2 * k)
-        if k + 1 < depth:
-            from_line(lines[k + 1])
-        work(2 * k + 1)
-
-    for index in (len(steps) - 2, len(steps) - 1):
-        for item in store(*steps[index], index % 2):
-            item.wait()
-    for line, pair in steps:
-        keep_rows(line, pair).wait()
-    for j in range(depth):
-        block = first_of(j, y) + c
-        for s in range(parts):
-            to_core(block, s).wait_send()
-            to_core(first_of(j, 1 - y) + c, s).wait_send()
-            to_pair(block, s).wait_send()
-
-            @pl.when((z >= j) & (z < depth - 1))
-            def _():
-                to_right(block, s).wait_send()
-
-            @pl.when((z <= j) & (z > 0))
-            def _():
-                to_left(block, s).wait_send()
-
-
-def hidden_units(count, ident, own, grads, weights, parts=2):
-    height, wide = own.shape
-    width = weights.shape[1]
-    depth = count // 4
-    low = jnp.bfloat16
-    sem = pltpu.SemaphoreType.DMA
-    anywhere = pl.BlockSpec(memory_space=pl.ANY)
-    acts = jax.ShapeDtypeStruct((count * height, width), low)
-    return pl.pallas_call(
-        functools.partial(hidden_body, count, parts),
-        out_shape=[acts, acts, acts, jax.ShapeDtypeStruct((count, height, wide), low)],
-        in_specs=[anywhere] * 3,
-        out_specs=[anywhere] * 4,
-        scratch_shapes=[
-            pltpu.VMEM((count, height, wide), low),
-            pltpu.VMEM((3, width, wide), low),
-            pltpu.VMEM((2, 2, height, wide), low),
-            pltpu.VMEM((2, 3, 2 * height, width), low),
-            sem((count, parts)),
-            sem((2 * depth, parts)),
-            sem((depth, parts)),
-            sem((2, depth, parts)),
-            sem,
-            sem((3,)),
-            sem((2,)),
-            sem((2, 3)),
-            sem((depth, 2)),
-        ],
-        compiler_params=kernel_params(ident),
-        name="hidden_units",
-    )(own, grads, weights)
-
-
-def unit_grads_body(count, parts, units, gate_grads, up_grads, weights, rows_all, grads_all,
-                    input_sum, output_sum, gate_out, up_out, down_out, gate_far,
-                    bank, rows_in, units_in, made, held, loaded, leaving, core_in, pair_in,
-                    line_in, bank_sem, rows_sem, fill_sems, units_sem, made_sem, core_send, core_recv,
-                    pair_send, pair_recv, line_send, line_recv,
-                    far_send, far_recv):
-    me, depth, z, y, c = place(count)
-    height, wide = input_sum.shape
-    width = weights.shape[1]
-    step = height // parts
-    low = jnp.bfloat16
-    core, mate = me + 1 - 2 * c, me + 2 - 4 * y
-    near = z < 2
-    order = [jnp.where(near, 3, 0), jnp.where(near, 0, 3), jnp.where(near, 2, 1),
-             jnp.where(near, 1, 2)]
-    greet(count, True)
-
-    def fill(source, at):
-        return pltpu.make_async_copy(source, bank.at[at], bank_sem.at[at])
-
-    blocks = width // height
-
-    def fill_rows(source, half, at):
-        return [
-            pltpu.make_async_copy(
-                source.at[half * blocks + i],
-                bank.at[at, pl.ds(i * height, height)],
-                fill_sems.at[at, i],
-            )
-            for i in range(blocks)
-        ]
-
-    first_fills = [fill(weights.at[i], i) for i in range(3)]
-    for item in first_fills:
-        item.start()
-    grad_tail = fill_rows(grads_all, 1, 3)
-    steps = [(line, pair) for line in order for pair in (1 - y, y)]
-
-    def fetch(line, pair, slot, sources):
-        rows = pl.ds((4 * line + 2 * pair) * height, 2 * height)
-        return [
-            pltpu.make_async_copy(source.at[rows], rows_in.at[slot, i], rows_sem.at[slot, i])
-            for i, source in enumerate(sources)
-        ]
-
-    def rows_of(s):
-        return pl.ds(s * step, step)
-
-    def to_core(a, line, pair, slot, s):
-        at = 2 * line + pair
-        return pltpu.make_async_remote_copy(
-            src_ref=leaving.at[a, slot, rows_of(s)],
-            dst_ref=core_in.at[a, at, rows_of(s)],
-            send_sem=core_send.at[a, slot, s],
-            recv_sem=core_recv.at[a, at, s],
-            device_id={"dp": core},
-            device_id_type=MESH,
-        )
-
-    def to_pair(a, line, s):
-        return pltpu.make_async_remote_copy(
-            src_ref=loaded.at[a, 2 * line + 1 - y, rows_of(s)],
-            dst_ref=pair_in.at[a, line, rows_of(s)],
-            send_sem=pair_send.at[a, line, s],
-            recv_sem=pair_recv.at[a, line, s],
-            device_id={"dp": mate},
-            device_id_type=MESH,
-        )
-
-    def along(a, line, slot, s, target):
-        return pltpu.make_async_remote_copy(
-            src_ref=loaded.at[a, 2 * line + y, rows_of(s)],
-            dst_ref=line_in.at[a, slot, rows_of(s)],
-            send_sem=line_send.at[a, line, s],
-            recv_sem=line_recv.at[a, slot, s],
-            device_id={"dp": target},
-            device_id_type=MESH,
-        )
-
-    def product(a, index):
-        line, pair = steps[index]
-        slot = index % 2
-        sources = (gate_grads, up_grads) if a == 0 else (units,)
-        if index == 0:
-            for item in fetch(line, pair, slot, sources):
-                item.start()
-        if index + 1 < len(steps):
-            for item in fetch(*steps[index + 1], 1 - slot, sources):
-                item.start()
-        if index >= 2:
-            for s in range(parts):
-                to_core(a, *steps[index - 2], slot, s).wait_send()
-        for item in fetch(line, pair, slot, sources):
-            item.wait()
-        tile = 512
-
-        def inner(n, carry):
-            cols = pl.ds(pl.multiple_of(n * tile, tile), tile)
-            if a == 0:
-                value = contract(rows_in[slot, 0], bank[0, :, cols], 1, 0)
-                value += contract(rows_in[slot, 1], bank[1, :, cols], 1, 0)
-            else:
-                value = contract(rows_in[slot, 0], bank[2, :, cols], 1, 0)
-            value = value.astype(low)
-
-            @pl.when(c == 0)
-            def _():
-                loaded[a, 2 * line + pair, :, cols] = value[:height]
-                leaving[a, slot, :, cols] = value[height:]
-
-            @pl.when(c == 1)
-            def _():
-                loaded[a, 2 * line + pair, :, cols] = value[height:]
-                leaving[a, slot, :, cols] = value[:height]
-
-            return carry
-
-        lax.fori_loop(0, wide // tile, inner, 0)
-        for s in range(parts):
-            to_core(a, line, pair, slot, s).start()
-
-    def finish_sends(a):
-        for index in (len(steps) - 2, len(steps) - 1):
-            for s in range(parts):
-                to_core(a, *steps[index], index % 2, s).wait_send()
-
-    def pair_step(a, k):
-        line = order[k]
-        at = 2 * line + 1 - y
-        for s in range(parts):
-            to_core(a, line, 1 - y, 0, s).wait_recv()
-            loaded[a, at, rows_of(s)] = loaded[a, at, rows_of(s)] + core_in[a, at, rows_of(s)]
-            to_pair(a, line, s).start()
-
-    def own_sum(a, line, s):
-        at = 2 * line + y
-        to_core(a, line, y, 0, s).wait_recv()
-        to_pair(a, line, s).wait_recv()
-        part = loaded[a, at, rows_of(s)].astype(jnp.float32)
-        part += core_in[a, at, rows_of(s)].astype(jnp.float32)
-        held[...] = part + pair_in[a, line, rows_of(s)].astype(jnp.float32)
-
-    def add_line(a, slot, s):
-        along(a, z, slot, s, me + 4).wait_recv()
-        held[...] += line_in[a, slot, rows_of(s)].astype(jnp.float32)
-
-    def line_step(a, k):
-        line = order[k]
-
-        @pl.when(line != z)
-        def _():
-            for s in range(parts):
-                own_sum(a, line, s)
-
-                @pl.when(((line > z) & (z > 0)) | ((line < z) & (z < depth - 1)))
-                def _():
-                    add_line(a, line, s)
-
-                loaded[a, 2 * line + y, rows_of(s)] = held[...].astype(low)
-
-                @pl.when(line > z)
-                def _():
-                    along(a, line, line, s, me + 4).start()
-
-                @pl.when(line < z)
-                def _():
-                    along(a, line, jnp.where(line == z - 1, depth, line), s, me - 4).start()
-
-    def last_step(a, total):
-        for s in range(parts):
-            own_sum(a, z, s)
-
-            @pl.when(z > 0)
-            def _():
-                add_line(a, z, s)
-
-            @pl.when(z < depth - 1)
-            def _():
-                add_line(a, depth, s)
-
-            total[rows_of(s)] = held[...]
-
-    tall = units_in.shape[2]
-    each = width // tall
-
-    def bring(g, slot):
-        source = (gate_grads, up_grads, units)[g // each]
-        cols = pl.ds((g % each) * tall, tall)
-        return pltpu.make_async_copy(source.at[:, cols], units_in.at[slot], units_sem.at[slot])
-
-    def put(g, slot):
-        rows = pl.ds((g % each) * tall, tall)
-        return pltpu.make_async_copy(
-            made.at[slot], (gate_out, up_out, down_out)[g // each].at[rows], made_sem.at[slot]
-        )
-
-    def swap(g):
-        rows = pl.ds(g * tall, tall)
-        return pltpu.make_async_remote_copy(
-            src_ref=gate_out.at[rows],
-            dst_ref=gate_far.at[rows],
-            send_sem=far_send.at[g],
-            recv_sem=far_recv.at[g],
-            device_id={"loop": 1 - lax.axis_index("loop")},
-            device_id_type=MESH,
-        )
-
-    number = 3 * each
-
-    def weight_product(g):
-        slot = g % 2
-        if g + 1 < number:
-            bring(g + 1, 1 - slot).start()
-        bring(g, slot).wait()
-        if g >= 2:
-            put(g - 2, slot).wait()
-            if g - 2 < FAR_TILES:
-                swap(g - 2).start()
-        at = 0 if g < 2 * each else 2
-        tile = 512
-
-        def inner(n, carry):
-            cols = pl.ds(pl.multiple_of(n * tile, tile), tile)
-            whole = bank[at : at + 2, :, cols].reshape(2 * width, tile)
-            made[slot, :, cols] = contract(units_in[slot], whole, 0, 0).astype(low)
-            return carry
-
-        lax.fori_loop(0, wide // tile, inner, 0)
-        put(g, slot).start()
-
-    for item in first_fills[:2]:
-        item.wait()
-    for index in range(8):
-        product(0, index)
-        if index >= 2 and index % 2 == 0:
-            pair_step(0, index // 2 - 1)
-    finish_sends(0)
-    row_fills = fill_rows(rows_all, 0, 0) + fill_rows(rows_all, 1, 1)
-    for item in row_fills:
-        item.start()
-    for item in grad_tail:
-        item.start()
-    bring(0, 0).start()
-    first_fills[2].wait()
-    product(1, 0)
-    pair_step(0, 3)
-    product(1, 1)
-    for item in row_fills:
-        item.wait()
-    weight_product(0)
-    weight_product(1)
-    line_step(0, 0)
-    weight_product(2)
-    weight_product(3)
-    line_step(0, 1)
-    for index in range(2, 8):
-        product(1, index)
-        if index % 2 == 0:
-            pair_step(1, index // 2 - 1)
-        if index == 6:
-            line_step(0, 2)
-    finish_sends(1)
-    grad_fills = fill_rows(grads_all, 0, 2)
-    for item in grad_fills:
-        item.start()
-    weight_product(4)
-    pair_step(1, 3)
-    line_step(0, 3)
-    weight_product(5)
-    last_step(0, input_sum)
-    weight_product(6)
-    weight_product(7)
-    line_step(1, 0)
-    for item in grad_tail + grad_fills:
-        item.wait()
-    weight_product(8)
-    weight_product(9)
-    line_step(1, 1)
-    weight_product(10)
-    weight_product(11)
-    line_step(1, 2)
-    line_step(1, 3)
-    last_step(1, output_sum)
-
-    for g in (number - 2, number - 1):
-        put(g, g % 2).wait()
-    for g in range(FAR_TILES):
-        swap(g).wait()
-    for a in range(2):
-        for line in range(depth):
-            for s in range(parts):
-                to_pair(a, line, s).wait_send()
-
-                @pl.when(z != line)
-                def _():
-                    along(a, line, line, s, me + 4).wait_send()
-
-
-def unit_grads(count, ident, units, gate_grads, up_grads, weights, rows_all, grads_all, parts=2):
-    width, wide = weights.shape[1:]
-    height = rows_all.shape[1]
-    depth = count // 4
-    low = jnp.bfloat16
-    sem = pltpu.SemaphoreType.DMA
-    anywhere = pl.BlockSpec(memory_space=pl.ANY)
-    inside = pl.BlockSpec(memory_space=pltpu.VMEM)
-    total = jax.ShapeDtypeStruct((height, wide), jnp.float32)
-
-    return pl.pallas_call(
-        functools.partial(unit_grads_body, count, parts),
-        out_shape=[total, total] + [jax.ShapeDtypeStruct((width, wide), low)] * 3
-        + [jax.ShapeDtypeStruct((FAR_TILES * 256, wide), low)],
-        in_specs=[anywhere] * 6,
-        out_specs=[inside, inside] + [anywhere] * 4,
-        scratch_shapes=[
-            pltpu.VMEM((4, width, wide), low),
-            pltpu.VMEM((2, 2, 2 * height, width), low),
-            pltpu.VMEM((2, count * height, 256), low),
-            pltpu.VMEM((2, 256, wide), low),
-            pltpu.VMEM((height // parts, wide), jnp.float32),
-            pltpu.VMEM((2, 2 * depth, height, wide), low),
-            pltpu.VMEM((2, 2, height, wide), low),
-            pltpu.VMEM((2, 2 * depth, height, wide), low),
-            pltpu.VMEM((2, depth, height, wide), low),
-            pltpu.VMEM((2, depth + 1, height, wide), low),
-            sem((4,)),
-            sem((2, 2)),
-            sem((4, width // height)),
-            sem((2,)),
-            sem((2,)),
-            sem((2, 2, parts)),
-            sem((2, 2 * depth, parts)),
-            sem((2, depth, parts)),
-            sem((2, depth, parts)),
-            sem((2, depth, parts)),
-            sem((2, depth + 1, parts)),
-            sem((FAR_TILES,)),
-            sem((FAR_TILES,)),
-        ],
-        compiler_params=kernel_params(ident),
-        name="unit_grads",
-    )(units, gate_grads, up_grads, weights, rows_all, grads_all)
-
-
-def sum_plan(count, parts, mine, theirs, core_in, pair_in, line_in, sems):
-    me, depth, z, y, c = place(count)
-    core_send, core_recv, pair_send, pair_recv, line_send, line_recv = sems
+    core_send, core_recv, pair_send, pair_recv, line_send, line_recv, twin_sem = sems
     rows = core_in.shape[1]
     step = rows // parts
     near = z < 2
@@ -1281,9 +760,31 @@
             device_id_type=MESH,
         )
 
+    twin = z + 1 - 2 * (z % 2)
+
+    def shared(s):
+        return twins and parts > 1 and s == parts - 1
+
+    def to_twin():
+        return pltpu.make_async_remote_copy(
+            src_ref=mine(2 * twin + 1 - y, rows_of(parts - 1)),
+            dst_ref=twin_in,
+            send_sem=twin_sem.at[0],
+            recv_sem=twin_sem.at[1],
+            device_id={"dp": me + 4 - 8 * (z % 2)},
+            device_id_type=MESH,
+        )
+
+    if shared(parts - 1):
+        pair_in[twin, rows_of(parts - 1)] = jnp.zeros((step, core_in.shape[2]), pair_in.dtype)
+
     def send_core(line, pair):
         for s in range(parts):
             to_core(line, pair, s).start()
+
+    def core_left(line, pair):
+        for s in range(parts):
+            to_core(line, pair, s).wait_send()
 
     def pair_step(k):
         line = order[k]
@@ -1292,12 +793,35 @@
             to_core(line, 1 - y, s).wait_recv()
             block = mine(at, rows_of(s))
             block[...] = block[...] + core_in[at, rows_of(s)]
-            to_pair(line, s).start()
+            if not shared(s):
+                to_pair(line, s).start()
+                continue
+
+            @pl.when(line == twin)
+            def _():
+                to_twin().start()
+
+            @pl.when((line != twin) & (line != z))
+            def _():
+                to_pair(line, s).start()
+
+    def twin_step():
+        block = mine(2 * z + 1 - y, rows_of(parts - 1))
+        to_twin().wait_recv()
+        block[...] = block[...] + twin_in[...]
+        to_pair(z, parts - 1).start()
 
     def own_sum(line, s):
         at = 2 * line + y
         to_core(line, y, s).wait_recv()
-        to_pair(line, s).wait_recv()
+        if shared(s):
+
+            @pl.when(line != twin)
+            def _():
+                to_pair(line, s).wait_recv()
+
+        else:
+            to_pair(line, s).wait_recv()
         part = mine(at, rows_of(s))[...].astype(jnp.float32)
         part += core_in[at, rows_of(s)].astype(jnp.float32)
         return part + pair_in[line, rows_of(s)].astype(jnp.float32)
@@ -1344,18 +868,27 @@
                 along(z, depth, s, me + 4).wait_recv()
                 total[rows_of(s)] += line_in[depth, rows_of(s)].astype(jnp.float32)
 
-    def finish():
+    def finish(cores=True):
+        if shared(parts - 1):
+            to_twin().wait_send()
         for line in range(depth):
             for s in range(parts):
-                for pair in range(2):
+                for pair in range(2 if cores else 0):
                     to_core(line, pair, s).wait_send()
-                to_pair(line, s).wait_send()
+                if shared(s):
+
+                    @pl.when(line != twin)
+                    def _():
+                        to_pair(line, s).wait_send()
+
+                else:
+                    to_pair(line, s).wait_send()
 
                 @pl.when(z != line)
                 def _():
                     along(line, line, s, me + 4).wait_send()
 
-    return order, send_core, pair_step, line_step, last_step, finish
+    return order, send_core, pair_step, line_step, last_step, finish, core_left, twin_step
 
 
 def sum_sems(count, parts):
@@ -1368,15 +901,17 @@
         sem((depth, parts)),
         sem((depth, parts)),
         sem((depth + 1, parts)),
+        sem((2,)),
     ]
 
 
-def sum_rooms(count, rows, cols, kind=jnp.bfloat16):
+def sum_rooms(count, rows, cols, kind=jnp.bfloat16, parts=2):
     depth = count // 4
     return [
         pltpu.VMEM((2 * depth, rows, cols), kind),
         pltpu.VMEM((depth, rows, cols), kind),
         pltpu.VMEM((depth + 1, rows, cols), kind),
+        pltpu.VMEM((rows // 2, cols) if parts > 1 else (16, 128), kind),
     ]
 
 
@@ -1404,7 +939,7 @@
                          cosine, sine, own_seq, own_order, all_seq, all_order, first, second,
                          joint_grads, lowrank_grads, out_sum,
                          weight_in, out_first, both_second, grad_att, allowed, kv_total, kv_terms, kv_sum, out_terms,
-                         out_core, out_pair, out_line, kv_core, kv_pair, kv_line,
+                         out_core, out_pair, out_line, out_twin, kv_core, kv_pair, kv_line, kv_twin,
                          weight_sem, *sems):
     me, depth, z, y, c = place(count)
     height, wide = grad_rows.shape
@@ -1425,11 +960,11 @@
     ]
     for item in loads:
         item.start()
-    order, send_out, pair_out, line_out, last_out, finish_out = sum_terms(
-        count, 2, out_terms, (out_core, out_pair, out_line), sems[:6]
-    )
-    _, send_kv, pair_kv, line_kv, last_kv, finish_kv = sum_terms(
-        count, 1, kv_terms, (kv_core, kv_pair, kv_line), sems[6:]
+    order, send_out, pair_out, line_out, last_out, finish_out, _, twin_out = sum_terms(
+        count, 2, out_terms, (out_core, out_pair, out_line, out_twin), sems[:7]
+    )
+    _, send_kv, pair_kv, line_kv, last_kv, finish_kv, _, _ = sum_terms(
+        count, 1, kv_terms, (kv_core, kv_pair, kv_line, kv_twin), sems[7:]
     )
     feature, some = out_terms.shape[1:]
 
@@ -1500,6 +1035,8 @@
 
     for pair in range(wide // size // 2):
         heads(pair)
+        if pair == 0:
+            twin_out()
     for block in range(count):
         kv_terms[block] = kv_total[block * height : (block + 1) * height].astype(low)
     for pair in (1 - y, y):
@@ -1555,7 +1092,7 @@
             pltpu.VMEM((count, feature, OUT_SPLIT), low),
         ]
         + sum_rooms(count, feature, OUT_SPLIT)
-        + sum_rooms(count, height, both)
+        + sum_rooms(count, height, both, parts=1)
         + [pltpu.SemaphoreType.DMA((3,))]
         + sum_sems(count, 2)
         + sum_sems(count, 1),
@@ -1578,9 +1115,9 @@
     rank = ADAPTER_RANK
     width = gate_grads.shape[0]
     low = jnp.bfloat16
-    rooms = [scratch[3 * i : 3 * i + 3] for i in range(5)]
-    weight_sem, grads_sem, factor_sem, made_sem, side_sem = scratch[15:20]
-    sems = [scratch[20 + 6 * i : 26 + 6 * i] for i in range(5)]
+    rooms = [scratch[4 * i : 4 * i + 4] for i in range(5)]
+    weight_sem, grads_sem, factor_sem, made_sem, side_sem = scratch[20:25]
+    sems = [scratch[25 + 7 * i : 32 + 7 * i] for i in range(5)]
     greet(count)
     halves = [
         pltpu.make_async_copy(weight.at[pl.ds(i * width, width)], bank, weight_sem.at[i])
@@ -1671,11 +1208,13 @@
         pair_step[0](k)
     in_load.wait()
     half_product(0)
+    plans[0][7]()
     block_products(1, attended, grad_rows, OUT_SPLIT)
     for k in range(depth):
         pair_step[1](k)
     for i in range(1, len(halves)):
         half_product(i)
+    plans[1][7]()
     first_load.start()
     side_load.start()
 
@@ -1773,7 +1312,7 @@
     sem = pltpu.SemaphoreType.DMA
     rooms, sems = [], []
     for (rows, cols, kind), parts in zip(shapes, (2, 2, 1, 1, 1)):
-        rooms += sum_rooms(count, rows, cols, kind)
+        rooms += sum_rooms(count, rows, cols, kind, parts)
         sems += sum_sems(count, parts)
     return pl.pallas_call(
         functools.partial(closing_body, count),
@@ -1803,12 +1342,439 @@
     )
 
 
+def line_order(z):
+    near = z < 2
+    return [z, z + 1 - 2 * (z % 2), jnp.where(near, 2, 1), jnp.where(near, 3, 0)]
+
+
+def unit_values(gate, up, grad):
+    slope = 0.7978845608028654
+    cubic = 0.044715
+    square = gate * gate
+    curve = jnp.tanh(slope * (gate + cubic * square * gate))
+    half = 0.5 * (1.0 + curve)
+    turned = gate * half
+    rise = half + 0.5 * gate * (1.0 - curve * curve) * slope * (1.0 + 3.0 * cubic * square)
+    low = jnp.bfloat16
+    return (turned * up).astype(low), (grad * up * rise).astype(low), (grad * turned).astype(low)
+
+
+def hidden_body(count, parts, own, grads, weights, units, gate_grads, up_grads, rows_out,
+                held, bank, coming, done, bank_sem, coming_sem, done_sem, rows_sem, *sems):
+    me, depth, z, y, c = place(count)
+    height, wide = own.shape
+    width = bank.shape[1]
+    tile = 512
+    lines = line_order(z)
+    greet(count)
+    pieces, begin, from_line, from_pair, _, arrive, finish = gather_plan(
+        count, [even_spans(height, parts)], (own,), (held,), sems
+    )
+    begin()
+    fills = [
+        pltpu.make_async_copy(weights.at[i], bank.at[i], bank_sem.at[i]) for i in range(3)
+    ]
+    for fill in fills:
+        fill.start()
+
+    def first_of(line, pair):
+        return 4 * line + 2 * pair
+
+    steps = [(line, pair) for line in lines for pair in (y, 1 - y)]
+
+    def fetch(index):
+        some = pl.ds(first_of(*steps[index]), 2)
+        return pltpu.make_async_copy(
+            grads.at[some], coming.at[index % 2], coming_sem.at[index % 2]
+        )
+
+    def store(index):
+        rows = pl.ds(first_of(*steps[index]) * height, 2 * height)
+        slot = index % 2
+        return [
+            pltpu.make_async_copy(done.at[slot, i], out.at[rows], done_sem.at[slot, i])
+            for i, out in enumerate((units, gate_grads, up_grads))
+        ]
+
+    def keep_rows(index):
+        some = pl.ds(first_of(*steps[index]), 2)
+        return pltpu.make_async_copy(held.at[some], rows_out.at[some], rows_sem.at[index])
+
+    def work(index):
+        line, pair = steps[index]
+        slot = index % 2
+        arrive(first_of(line, pair) + 1 - c, index == 0)
+        if index == 0:
+            fetch(0).start()
+            for fill in fills:
+                fill.wait()
+        if index + 1 < len(steps):
+            fetch(index + 1).start()
+        fetch(index).wait()
+        keep_rows(index).start()
+        if index >= 2:
+            for item in store(index - 2):
+                item.wait()
+        some = pl.ds(first_of(line, pair), 2)
+
+        def inner(n, carry):
+            cols = pl.ds(pl.multiple_of(n * tile, tile), tile)
+            block = held[some].reshape(2 * height, wide)
+            gate = contract(block, bank[0, cols], 1, 1)
+            up = contract(block, bank[1, cols], 1, 1)
+            grad = contract(coming[slot].reshape(2 * height, wide), bank[2, cols], 1, 1)
+            for i, value in enumerate(unit_values(gate, up, grad)):
+                done[slot, i, :, cols] = value
+            return carry
+
+        lax.fori_loop(0, width // tile, inner, 0)
+        for item in store(index):
+            item.start()
+
+    work(0)
+    for k in range(1, depth + 1):
+        for piece in pieces:
+            if k < depth:
+                from_line(k, piece)
+            from_pair(k - 1, piece)
+        work(2 * k - 1)
+        if k < depth:
+            work(2 * k)
+
+    for index in (len(steps) - 2, len(steps) - 1):
+        for item in store(index):
+            item.wait()
+    for index in range(len(steps)):
+        keep_rows(index).wait()
+    finish()
+
+
+def hidden_units(count, ident, own, grads, weights, parts=2):
+    height, wide = own.shape
+    width = weights.shape[1]
+    low = jnp.bfloat16
+    sem = pltpu.SemaphoreType.DMA
+    anywhere = pl.BlockSpec(memory_space=pl.ANY)
+    acts = jax.ShapeDtypeStruct((count * height, width), low)
+    return pl.pallas_call(
+        functools.partial(hidden_body, count, parts),
+        out_shape=[acts, acts, acts, jax.ShapeDtypeStruct((count, height, wide), low)],
+        in_specs=[anywhere] * 3,
+        out_specs=[anywhere] * 4,
+        scratch_shapes=[
+            pltpu.VMEM((count, height, wide), low),
+            pltpu.VMEM((3, width, wide), low),
+            pltpu.VMEM((2, 2, height, wide), low),
+            pltpu.VMEM((2, 3, 2 * height, width), low),
+            sem((3,)),
+            sem((2,)),
+            sem((2, 3)),
+            sem((count // 2,)),
+        ]
+        + gather_sems(count, 1, parts),
+        compiler_params=kernel_params(ident),
+        name="hidden_units",
+    )(own, grads, weights)
+
+
+def unit_grads_body(count, parts, units, gate_grads, up_grads, weights, rows_all, grads_all,
+                    input_sum, output_sum, gate_out, up_out, down_out, gate_far,
+                    bank, rows_in, units_in, made, loaded, leaving, core_in, pair_in, line_in,
+                    twin_in, bank_sem, rows_sem, fill_sems, units_sem, made_sem, far_send,
+                    far_recv, *sems):
+    me, depth, z, y, c = place(count)
+    height, wide = input_sum.shape
+    width = weights.shape[1]
+    step = height // parts
+    low = jnp.bfloat16
+    core, mate = me + 1 - 2 * c, me + 2 - 4 * y
+    near = z < 2
+    order = [jnp.where(near, 3, 0), jnp.where(near, 0, 3), jnp.where(near, 2, 1),
+             jnp.where(near, 1, 2)]
+    greet(count, True)
+
+    def fill(source, at):
+        return pltpu.make_async_copy(source, bank.at[at], bank_sem.at[at])
+
+    blocks = width // height
+
+    def fill_rows(source, half, at):
+        return [
+            pltpu.make_async_copy(
+                source.at[half * blocks + i],
+                bank.at[at, pl.ds(i * height, height)],
+                fill_sems.at[at, i],
+            )
+            for i in range(blocks)
+        ]
+
+    first_fills = [fill(weights.at[i], i) for i in range(3)]
+    for item in first_fills:
+        item.start()
+    grad_tail = fill_rows(grads_all, 1, 3)
+    steps = [(line, pair) for line in order for pair in (1 - y, y)]
+
+    def fetch(line, pair, slot, sources):
+        rows = pl.ds((4 * line + 2 * pair) * height, 2 * height)
+        return [
+            pltpu.make_async_copy(source.at[rows], rows_in.at[slot, i], rows_sem.at[slot, i])
+            for i, source in enumerate(sources)
+        ]
+
+    def plan(a):
+        def mine(at, rows):
+            return loaded.at[a, at, rows]
+
+        def theirs(at, rows):
+            return leaving.at[a, jnp.where(at % 2 == y, 1, 0), rows]
+
+        return sum_plan(
+            count, parts, mine, theirs, core_in.at[a], pair_in.at[a], line_in.at[a],
+            twin_in.at[a], sems[7 * a : 7 * a + 7],
+        )
+
+    plans = [plan(a) for a in range(2)]
+
+    def pair_step(a, k):
+        plans[a][2](k)
+
+    def line_step(a, k):
+        plans[a][3](k)
+
+    def last_step(a, total):
+        plans[a][4](total)
+
+    def to_core(a, line, pair):
+        plans[a][1](line, pair)
+
+    def core_left(a, line, pair):
+        plans[a][6](line, pair)
+
+    def product(a, index):
+        line, pair = steps[index]
+        slot = index % 2
+        sources = (gate_grads, up_grads) if a == 0 else (units,)
+        if index == 0:
+            for item in fetch(line, pair, slot, sources):
+                item.start()
+        if index + 1 < len(steps):
+            for item in fetch(*steps[index + 1], 1 - slot, sources):
+                item.start()
+        if index >= 2:
+            core_left(a, *steps[index - 2])
+        for item in fetch(line, pair, slot, sources):
+            item.wait()
+        tile = 512
+
+        def inner(n, carry):
+            cols = pl.ds(pl.multiple_of(n * tile, tile), tile)
+            if a == 0:
+                value = contract(rows_in[slot, 0], bank[0, :, cols], 1, 0)
+                value += contract(rows_in[slot, 1], bank[1, :, cols], 1, 0)
+            else:
+                value = contract(rows_in[slot, 0], bank[2, :, cols], 1, 0)
+            value = value.astype(low)
+
+            @pl.when(c == 0)
+            def _():
+                loaded[a, 2 * line + pair, :, cols] = value[:height]
+                leaving[a, slot, :, cols] = value[height:]
+
+            @pl.when(c == 1)
+            def _():
+                loaded[a, 2 * line + pair, :, cols] = value[height:]
+                leaving[a, slot, :, cols] = value[:height]
+
+            return carry
+
+        lax.fori_loop(0, wide // tile, inner, 0)
+        to_core(a, line, pair)
+
+    def finish_sends(a):
+        for index in (len(steps) - 2, len(steps) - 1):
+            core_left(a, *steps[index])
+
+    tall = units_in.shape[2]
+    each = width // tall
+
+    def bring(g, slot):
+        source = (gate_grads, up_grads, units)[g // each]
+        cols = pl.ds((g % each) * tall, tall)
+        return pltpu.make_async_copy(source.at[:, cols], units_in.at[slot], units_sem.at[slot])
+
+    def put(g, slot):
+        rows = pl.ds((g % each) * tall, tall)
+        return pltpu.make_async_copy(
+            made.at[slot], (gate_out, up_out, down_out)[g // each].at[rows], made_sem.at[slot]
+        )
+
+    def swap(g):
+        rows = pl.ds(g * tall, tall)
+        return pltpu.make_async_remote_copy(
+            src_ref=gate_out.at[rows],
+            dst_ref=gate_far.at[rows],
+            send_sem=far_send.at[g],
+            recv_sem=far_recv.at[g],
+            device_id={"loop": 1 - lax.axis_index("loop")},
+            device_id_type=MESH,
+        )
+
+    number = 3 * each
+
+    def weight_product(g):
+        slot = g % 2
+        if g + 1 < number:
+            bring(g + 1, 1 - slot).start()
+        bring(g, slot).wait()
+        if g >= 2:
+            put(g - 2, slot).wait()
+            if g - 2 < FAR_TILES:
+                swap(g - 2).start()
+        at = 0 if g < 2 * each else 2
+        tile = 512
+
+        def inner(n, carry):
+            cols = pl.ds(pl.multiple_of(n * tile, tile), tile)
+            whole = bank[at : at + 2, :, cols].reshape(2 * width, tile)
+            made[slot, :, cols] = contract(units_in[slot], whole, 0, 0).astype(low)
+            return carry
+
+        lax.fori_loop(0, wide // tile, inner, 0)
+        put(g, slot).start()
+
+    for item in first_fills[:2]:
+        item.wait()
+    for index in range(8):
+        product(0, index)
+        if index >= 2 and index % 2 == 0:
+            pair_step(0, index // 2 - 1)
+    finish_sends(0)
+    row_fills = fill_rows(rows_all, 0, 0) + fill_rows(rows_all, 1, 1)
+    for item in row_fills:
+        item.start()
+    for item in grad_tail:
+        item.start()
+    bring(0, 0).start()
+    first_fills[2].wait()
+    product(1, 0)
+    pair_step(0, 3)
+    product(1, 1)
+    plans[0][7]()
+    for item in row_fills:
+        item.wait()
+    weight_product(0)
+    weight_product(1)
+    line_step(0, 0)
+    weight_product(2)
+    weight_product(3)
+    line_step(0, 1)
+    for index in range(2, 8):
+        product(1, index)
+        if index % 2 == 0:
+            pair_step(1, index // 2 - 1)
+        if index == 6:
+            line_step(0, 2)
+    finish_sends(1)
+    grad_fills = fill_rows(grads_all, 0, 2)
+    for item in grad_fills:
+        item.start()
+    weight_product(4)
+    pair_step(1, 3)
+    line_step(0, 3)
+    weight_product(5)
+    plans[1][7]()
+    last_step(0, input_sum)
+    weight_product(6)
+    weight_product(7)
+    line_step(1, 0)
+    for item in grad_tail + grad_fills:
+        item.wait()
+    weight_product(8)
+    weight_product(9)
+    line_step(1, 1)
+    weight_product(10)
+    weight_product(11)
+    line_step(1, 2)
+    line_step(1, 3)
+    last_step(1, output_sum)
+
+    for g in (number - 2, number - 1):
+        put(g, g % 2).wait()
+    for g in range(FAR_TILES):
+        swap(g).wait()
+    for a in range(2):
+        plans[a][5](False)
+
+
+def unit_grads(count, ident, units, gate_grads, up_grads, weights, rows_all, grads_all, parts=2):
+    width, wide = weights.shape[1:]
+    height = rows_all.shape[1]
+    depth = count // 4
+    low = jnp.bfloat16
+    sem = pltpu.SemaphoreType.DMA
+    anywhere = pl.BlockSpec(memory_space=pl.ANY)
+    inside = pl.BlockSpec(memory_space=pltpu.VMEM)
+    total = jax.ShapeDtypeStruct((height, wide), jnp.float32)
+
+    return pl.pallas_call(
+        functools.partial(unit_grads_body, count, parts),
+        out_shape=[total, total] + [jax.ShapeDtypeStruct((width, wide), low)] * 3
+        + [jax.ShapeDtypeStruct((FAR_TILES * 256, wide), low)],
+        in_specs=[anywhere] * 6,
+        out_specs=[inside, inside] + [anywhere] * 4,
+        scratch_shapes=[
+            pltpu.VMEM((4, width, wide), low),
+            pltpu.VMEM((2, 2, 2 * height, width), low),
+            pltpu.VMEM((2, count * height, 256), low),
+            pltpu.VMEM((2, 256, wide), low),
+            pltpu.VMEM((2, 2 * depth, height, wide), low),
+            pltpu.VMEM((2, 2, height, wide), low),
+            pltpu.VMEM((2, 2 * depth, height, wide), low),
+            pltpu.VMEM((2, depth, height, wide), low),
+            pltpu.VMEM((2, depth + 1, height, wide), low),
+            pltpu.VMEM((2, height // 2, wide), low),
+            sem((4,)),
+            sem((2, 2)),
+            sem((4, width // height)),
+            sem((2,)),
+            sem((2,)),
+            sem((FAR_TILES,)),
+            sem((FAR_TILES,)),
+        ]
+        + sum_sems(count, parts)
+        + sum_sems(count, parts),
+        compiler_params=kernel_params(ident),
+        name="unit_grads",
+    )(units, gate_grads, up_grads, weights, rows_all, grads_all)
+
+
 def swap_loops(values):
     return lax.ppermute(values, "loop", [(0, 1), (1, 0)])
 
 
-def both_loops(values):
-    return values.astype(jnp.float32) + swap_loops(values).astype(jnp.float32)
+def add_body(*refs):
+    left, right, out = refs[-3], refs[-2], refs[-1]
+    out[0] = left[...].astype(jnp.float32) + right[...].astype(jnp.float32)
+
+
+def add_into(held, left, right, whole, which, skip):
+    rows, wide = right.shape
+    step = 256
+    before = [] if held is None else [held]
+    return pl.pallas_call(
+        add_body,
+        grid=(rows // step,),
+        out_shape=jax.ShapeDtypeStruct(whole, jnp.float32),
+        in_specs=[pl.BlockSpec(memory_space=pl.ANY)] * len(before)
+        + [
+            pl.BlockSpec((step, wide), lambda r: (r + skip // step, 0)),
+            pl.BlockSpec((step, wide), lambda r: (r, 0)),
+        ],
+        out_specs=pl.BlockSpec((1, step, wide), lambda r: (which, r + skip // step, 0)),
+        input_output_aliases={0: 0} if before else {},
+        compiler_params=pltpu.CompilerParams(vmem_limit_bytes=VMEM_LIMIT),
+        name="add_loops",
+    )(*before, left, right)
 
 
 def per_device(
@@ -1916,9 +1882,14 @@
     gate_other, gate_last, up_other, down_other, small_sum = lax.optimization_barrier(
         (gate_other, gate_last, up_other, down_other, small_sum)
     )
-    gate_other = jnp.concatenate([gate_other, gate_last], axis=0)
     in_low = in_portion.astype(low)
     out_low = jnp.concatenate([out_first, out_last], axis=1).astype(low)
+    in_far, out_far, small_far = swap_loops(in_low), swap_loops(out_low), swap_loops(small_sum)
+    whole = ffn_weight.shape
+    sum_mlp = add_into(None, gate_grad, gate_other, whole, 0, 0)
+    sum_mlp = add_into(sum_mlp, gate_grad, gate_last, whole, 0, FAR_TILES * 256)
+    sum_mlp = add_into(sum_mlp, up_grad, up_other, whole, 1, 0)
+    sum_mlp = add_into(sum_mlp, down_grad, down_other, whole, 2, 0)
     adapter_first_gradient = jnp.concatenate(
         [
             outer_columns(in_low[:, :key_at], adapter_second[:, :key_at]),
@@ -1929,25 +1900,20 @@
         ],
         axis=1,
     )
-    small_total = both_loops(small_sum)
+    in_far, out_far, small_far, sum_mlp, adapter_first_gradient = lax.optimization_barrier(
+        (in_far, out_far, small_far, sum_mlp, adapter_first_gradient)
+    )
+    small_total = small_sum + small_far
     sum_gains = small_total[:2, :width_own]
     depth_total = small_total[2, 1 : loop_count + 2]
     mean_confidence = small_total[2, 0] / jnp.sum(depth_total)
     exit_counts = depth_total.astype(jnp.int32)
-    sum_mlp = jnp.stack(
-        [
-            gate_grad.astype(jnp.float32) + gate_other.astype(jnp.float32),
-            up_grad.astype(jnp.float32) + up_other.astype(jnp.float32),
-            down_grad.astype(jnp.float32) + down_other.astype(jnp.float32),
-        ],
-        axis=1,
-    )
     return (
         complete_output.astype(low)[None],
         hidden_grad[None],
-        both_loops(in_low),
-        both_loops(out_low),
-        sum_mlp,
+        in_low.astype(jnp.float32) + in_far.astype(jnp.float32),
+        out_low.astype(jnp.float32) + out_far.astype(jnp.float32),
+        jnp.swapaxes(sum_mlp, 0, 1),
         sum_gains,
         adapter_first_gradient[None],
         jnp.swapaxes(second_grad, 0, 1)[None],

time: 654 us -> 622 us (0.951)
  other arithmetic: 45.2 us -> 23.7 us
  waiting for transfers between devices: 12.8 us -> 0.02 us
    pallas_call x0 -> x4, Pallas kernels: none -> 24.2 us  [add_into(): pl.pallas_call(add_body, grid=(rows // step,), out_shape=jax.ShapeDtypeSt...]
    another operation x6 -> x3, other arithmetic: 25.6 us -> 1.99 us  [the longest x3 23.6 us: per_device(): jnp.stack([gate_grad.astype(jnp.float32) + gate_other.astype(jnp.float32)...]
    pallas_call x1, Pallas kernels: 73.6 us -> 55.1 us  [hidden_units(): pl.pallas_call(functools.partial(hidden_body, count, parts), out_shape=[a...]
    ppermute x6, waiting for transfers between devices: 12.8 us -> 0.02 us  [swap_loops(): return lax.ppermute(values, 'loop', [(0, 1), (1, 0)])]
    pallas_call x1, Pallas kernels: 121 us -> 134 us  [unit_grads(): pl.pallas_call(functools.partial(unit_grads_body, count, parts), out_shap...]
    pallas_call x1, Pallas kernels: 135 us -> 127 us  [closing(): pl.pallas_call(functools.partial(closing_body, count), out_shape=[jax.Sha...]
  transfers between devices with their start and end apart: 6 -> 6, of which waited for: 2 -> 0; matrix products, arithmetic and copies ran while one was open for 6% -> 2% of each run, Pallas kernels for 33% -> 36%
where the time goes in v5:
time: 622 us; the launch traced here: 616 us
  Pallas kernels  567 us (91%)
  other arithmetic  23.7 us (4%)
  local copies, waits for them, and re-layouts  12.9 us (2%)
  starting transfers between devices  6.41 us (1%)
    pallas_call x1, Pallas kernels, unit_grads(): pl.pallas_call(functools.partial(unit_grads_body, count, parts), out_shap...  134 us
    pallas_call x1, Pallas kernels, closing(): pl.pallas_call(functools.partial(closing_body, count), out_shape=[jax.Sha...  127 us
    pallas_call x1, Pallas kernels, opening(): pl.pallas_call(functools.partial(opening_body, count, shares, number), ou...  81.3 us
    pallas_call x1, Pallas kernels, attention_grads(): pl.pallas_call(functools.partial(attention_grads_body, count), out_shape=...  73.2 us
    pallas_call x1, Pallas kernels, attention(): pl.pallas_call(functools.partial(attention_body, count), out_shape=[shape...  72.8 us
    pallas_call x1, Pallas kernels, hidden_units(): pl.pallas_call(functools.partial(hidden_body, count, parts), out_shape=[a...  55.1 us
    pallas_call x4, Pallas kernels, add_into(): pl.pallas_call(add_body, grid=(rows // step,), out_shape=jax.ShapeDtypeSt...  24.2 us
  transfers between devices with their start and end apart: 6, of which 0 were waited for; matrix products, arithmetic and copies ran while one was open for 2% of the time, Pallas kernels for 36%

profile of v5, /device:TPU:0, one launch (start us, length us, event | category | flops | bytes accessed | tf_op | source)
XLA Modules:
  0.0 615.6 jit_solution(13137189309486738285)
XLA Ops:
  1.4 0.8 reduce-window.4
  2.9 0.8 convert_reduce_fusion
  3.6 0.8 select_bitcast_fusion
  4.5 0.8 fusion.13
  6.7 2.0 fusion.3.grads
  9.4 1.4 fusion.19
  11.5 1.3 compare_select_fusion
  12.9 1.0 multiply_sine_fusion
  13.8 81.3 %opening.1 = (bf16[16,128,2560]{2,1,0:T(8,128)(2,1)}, bf16[16,128,2048]{2,1,0:T(8,128)(2,1)}, bf16[3,1024,2048]{2,1,0:T(8,128)(2,1)}, bf16[128,2048]{1,0:T(8,128)(2,1)}, bf16[128,768]{1,0:T(8,128)(2,1)}) custom-call(bf16[128,2048]{1,0:T(8,128)(2,1)} %bitcast.67, f32[1,2048]{1,0:T(1,128)} %get-tuple-element.131.gain, bf16[128,2560]{1,0:T(8,128)(2,1)} %refs_0_.1, ...), custom_call_target="tpu_custom_call" | custom-call | tf_op jit(solution)/shard_map/opening/pallas_call | solution.py:491
  95.1 72.8 %attention.1 = (bf16[128,2048]{1,0:T(8,128)(2,1)}, bf16[128,2048]{1,0:T(8,128)(2,1)}, bf16[128,256]{1,0:T(8,128)(2,1)}, f32[4,256,128]{2,1,0:T(8,128)}, f32[128,...) custom-call(bf16[128,2048]{1,0:T(8,128)(2,1)} %get-tuple-element.78.nor, ...), custom_call_target="tpu_custom_call" | custom-call | tf_op jit(solution)/shard_map/attention/pallas_call | solution.py:679
  167.9 55.1 %hidden_units.1 = (bf16[2048,1024]{1,0:T(8,128)(2,1)}, bf16[2048,1024]{1,0:T(8,128)(2,1)}, bf16[2048,1024]{1,0:T(8,128)(2,1)}, bf16[16,128,2048]{2,1,0:T(8,128)(2,1)}) custom-call(bf16[128,2048]{1,0:T(8,128)(2,1)} %get-tuple-element.83.own, bf16[16,128,2048]{2,1,0:T(8,128)(2,1)} %get-tuple-element.84.grads.grads_all, ...), custom_call_target="tpu_custom_call" | custom-call | tf_op jit(solution)/shard_map/hidden_units/pallas_call | solution.py:1459
  223.0 134.2 %unit_grads.1 = (f32[128,2048]{1,0:T(8,128)}, f32[128,2048]{1,0:T(8,128)}, bf16[1024,2048]{1,0:T(8,128)(2,1)}, bf16[1024,2048]{1,0:T(8,128)(2,1)}, bf16[1024,204...) custom-call(bf16[2048,1024]{1,0:T(8,128)(2,1)} %get-tuple-element.86.units, bf16[2048,1024]{1,0:T(8,128)(2,1)} %get-tuple-element.87.gate_grads, ...), custom_call_target="tpu_custom_call" | custom-call | tf_op jit(solution)/shard_map/unit_grads/pallas_call | solution.py:1719
  357.3 1.6 collective-permute-start.3
  359.4 2.3 slice.88
  361.7 1.5 collective-permute-start.2
  363.4 2.9 multiply_reduce_fusion
  368.1 1.5 multiply_convert_fusion
  369.6 73.2 %attention_grads.1 = (bf16[128,2560]{1,0:T(8,128)(2,1)}, bf16[128,768]{1,0:T(8,128)(2,1)}, f32[128,1536]{1,0:T(8,128)}) custom-call(bf16[128,2048]{1,0:T(8,128)(2,1)} %get-tuple-element.91.attended, bf16[128,2048]{1,0:T(8,128)(2,1)} %get-tuple-element.124.grad_rows, bf16[2048,2048]{1,0:T(8,128)(2,1)} %bitcast.65, ...), custom_call_target="tpu_custom_call" | custom-call | tf_op jit(solution)/shard_map/attention_grads/pallas_call | solution.py:1074
  442.8 126.8 %closing.1 = (f32[128,2560]{1,0:T(8,128)}, f32[128,512]{1,0:T(8,128)}, f32[416,256]{1,0:T(8,128)}, f32[128,512]{1,0:T(8,128)}, f32[8,128]{1,0:T(8,128)}, /*index=5*/f32[128,2048]{1,0:T(8,128)}, f32[1024,768]{1,0:T(8,128)}) custom-call(bf16[128,2048]{1,0:T(8,128)(2,1)} %get-tuple-element.78.normed, bf16[128,2560]{1,0:T(8,128)(2,1)} %get-tuple-element.96.joint_grads, ...), custom_call_target="tpu_custom_call" | custom-call | tf_op jit(solution)/shard_map/closing/pallas_call | solution.py:1317
  569.7 1.1 convert.8
  571.6 1.4 convert_element_type.62
  573.0 1.5 collective-permute-start
  576.6 6.7 %add_loops.4.refs_0_ = f32[3,1024,2048]{2,1,0:T(8,128)} custom-call(bf16[1024,2048]{1,0:T(8,128)(2,1)} %get-tuple-element.99.gate_grads.refs_0_.refs_1_, bf16[768,2048]{1,0:T(8,128)(2,1)} %get-tuple-element.109.refs_1_), custom_call_target="tpu_custom_call" | custom-call | tf_op jit(solution)/shard_map/add_loops/pallas_call | solution.py:1764
  583.3 3.1 add_loops.5.refs_0_
  586.4 7.1 %add_loops.6.refs_0_ = f32[3,1024,2048]{2,1,0:T(8,128)} custom-call(f32[3,1024,2048]{2,1,0:T(8,128)} %add_loops.5.refs_0_, bf16[1024,2048]{1,0:T(8,128)(2,1)} %get-tuple-element.100.up_grads.refs_1_, bf16[1024,2048]{1,0:T(8,128)(2,1)} %collective-permute-done.3.refs_2_), custom_call_target="tpu_custom_call", output_to_operand_aliasing={{}: (0, {})} | custom-call | tf_op jit(solution)/shard_map/add_loops/pallas_call | solution.py:1764
  593.5 7.2 %add_loops.7 = f32[3,1024,2048]{2,1,0:T(8,128)} custom-call(f32[3,1024,2048]{2,1,0:T(8,128)} %add_loops.6.refs_0_, bf16[1024,2048]{1,0:T(8,128)(2,1)} %get-tuple-element.101.down_grads.refs_1_, bf16[1024,2048]{1,0:T(8,128)(2,1)} %collective-permute-done.4.refs_2_), custom_call_target="tpu_custom_call", output_to_operand_aliasing={{}: (0, {})} | custom-call | tf_op jit(solution)/shard_map/add_loops/pallas_call | solution.py:1764
  600.8 1.2 slice_reduce_fusion
  603.0 2.1 convert_add_fusion.2
  605.2 2.3 convert_add_fusion.1
  608.8 1.0 copy.47
  609.8 0.8 copy.48
  610.5 3.8 copy.49
  (65 shorter events, 10.8 us)
Async XLA Ops:
  223.0 140.2 %copy-start.1 = (f32[128,2048]{1,0:T(8,128)S(1)}, f32[128,2048]{1,0:T(8,128)}, u32[]{:S(2)}) copy-start(f32[128,2048]{1,0:T(8,128)} %get-tuple-element.82) | copy-start | bytes 3145732
  223.0 140.4 %copy-start.2 = (bf16[1,128,2048]{2,1,0:T(8,128)(2,1)S(1)}, bf16[1,128,2048]{2,1,0:T(8,128)(2,1)}, u32[]{:S(2)}) copy-start(bf16[1,128,2048]{2,1,0:T(8,128)(2,1)} %param.16) | copy-start | bytes 1572868
  223.0 140.4 %copy-start.11 = (f32[1,2048]{1,0:T(1,128)S(1)}, f32[1,2048]{1,0:T(1,128)}, u32[]{:S(2)}) copy-start(f32[1,2048]{1,0:T(1,128)} %get-tuple-element.130.gain) | copy-start | bytes 24580
  357.3 9.0 %copy-start.13 = (s32[1,128]{1,0:T(1,128)S(1)}, s32[1,128]{1,0:T(1,128)}, u32[]{:S(2)}) copy-start(s32[1,128]{1,0:T(1,128)} %param.27) | copy-start | bytes 1540
  357.3 10.8 %copy-start.4 = (f32[128,2048]{1,0:T(8,128)S(1)}, f32[128,2048]{1,0:T(8,128)}, u32[]{:S(2)}) copy-start(f32[128,2048]{1,0:T(8,128)} %get-tuple-element.92) | copy-start | bytes 3145732
  357.3 10.8 %copy-start.5 = (bf16[1,128,2048]{2,1,0:T(8,128)(2,1)S(1)}, bf16[1,128,2048]{2,1,0:T(8,128)(2,1)}, u32[]{:S(2)}) copy-start(bf16[1,128,2048]{2,1,0:T(8,128)(2,1)} %param.17) | copy-start | bytes 1572868
  357.3 218.6 %collective-permute-start.3 = (bf16[1024,2048]{1,0:T(8,128)(2,1)}, bf16[1024,2048]{1,0:T(8,128)(2,1)}, u32[]{:S(2)}, u32[]{:S(2)}) collective-permute-start(bf16[1024,2048]{1,0:T(8,128)(2,1)} %get-tuple-element.100.up_grads.refs_1_), channel_id=1, source_target_pairs={{0,16},{16,0},{1,17},{17,1},{2,18},{18,2},{3,19},{19,3},{4,20},{20... | collective-permute-start | bytes 12582920 | tf_op jit(solution)/shard_map/ppermute | solution.py:1752
  358.9 217.0 %collective-permute-start.4 = (bf16[1024,2048]{1,0:T(8,128)(2,1)}, bf16[1024,2048]{1,0:T(8,128)(2,1)}, u32[]{:S(2)}, u32[]{:S(2)}) collective-permute-start(bf16[1024,2048]{1,0:T(8,128)(2,1)} %get-tuple-element.101.down_grads.refs_1_), channel_id=1, source_target_pairs={{0,16},{16,0},{1,17},{17,1},{2,18},{18,2},{3,19},{19,3},{4,20},{20... | collective-permute-start | bytes 12582920 | tf_op jit(solution)/shard_map/ppermute | solution.py:1752
  361.7 214.2 %collective-permute-start.2 = (bf16[256,2048]{1,0:T(8,128)(2,1)}, bf16[256,2048]{1,0:T(8,128)(2,1)}, u32[]{:S(2)}, u32[]{:S(2)}) collective-permute-start(bf16[256,2048]{1,0:T(8,128)(2,1)} %slice.88), channel_id=1, source_target_pairs={{0,16},{16,0},{1,17},{17,1},{2,18},{18,2},{3,19},{19,3},{4,20},{20... | collective-permute-start | bytes 3145736 | tf_op jit(solution)/shard_map/ppermute | solution.py:1752
  368.1 74.7 %copy-start.10 = (f32[16,8,128]{2,1,0:T(8,128)}, f32[16,8,128]{2,1,0:T(8,128)S(1)}, u32[]{:S(2)}) copy-start(f32[16,8,128]{2,1,0:T(8,128)S(1)} %scatter.9.small) | copy-start | bytes 196612
  442.8 128.0 %copy-start.7 = (f32[128,1536]{1,0:T(8,128)S(1)}, f32[128,1536]{1,0:T(8,128)}, u32[]{:S(2)}) copy-start(f32[128,1536]{1,0:T(8,128)} %get-tuple-element.104) | copy-start | bytes 2359300
  569.7 4.8 copy-start
  570.9 5.0 copy-start.12
  570.9 5.7 copy-start.9
  570.9 29.8 %collective-permute-start.1 = (bf16[128,2048]{1,0:T(8,128)(2,1)S(1)}, bf16[128,2048]{1,0:T(8,128)(2,1)}, u32[]{:S(2)}, u32[]{:S(2)}) collective-permute-start(bf16[128,2048]{1,0:T(8,128)(2,1)S(1)} %pad_maximum_fusion), channel_id=1, source_target_pairs={{0,16},{16,0},{1,17},{17,1},{2,18},{18,2},{3,19},{19,3},{4,20},{20... | collective-permute-start | bytes 1572872 | tf_op jit(solution)/shard_map/ppermute | solution.py:1752
  573.0 27.8 %collective-permute-start = (bf16[128,2560]{1,0:T(8,128)(2,1)S(1)}, bf16[128,2560]{1,0:T(8,128)(2,1)}, u32[]{:S(2)}, u32[]{:S(2)}) collective-permute-start(bf16[128,2560]{1,0:T(8,128)(2,1)S(1)} %convert_element_type.62), channel_id=1, source_target_pairs={{0,16},{16,0},{1,17},{17,1},{2,18},{18,2},{3,19},{19,3},{4,20},{20... | collective-permute-start | bytes 1966088 | tf_op jit(solution)/shard_map/ppermute | solution.py:1752
  575.9 24.9 %collective-permute-start.5 = (f32[8,128]{1,0:T(8,128)S(1)}, f32[8,128]{1,0:T(8,128)S(1)}, u32[]{:S(2)}, u32[]{:S(2)}) collective-permute-start(f32[8,128]{1,0:T(8,128)S(1)} %copy-done.12), channel_id=1, source_target_pairs={{0,16},{16,0},{1,17},{17,1},{2,18},{18,2},{3,19},{19,3},{4,20},{20... | collective-permute-start | bytes 12296 | tf_op jit(solution)/shard_map/ppermute | solution.py:1752
  576.6 6.7 %copy-start.14 = (f32[128,1536]{1,0:T(8,128)}, f32[128,1536]{1,0:T(8,128)S(1)}, u32[]{:S(2)}) copy-start(f32[128,1536]{1,0:T(8,128)S(1)} %constant_dynamic-update-slice_fusion) | copy-start | bytes 2359300
  593.5 11.7 %copy-start.3 = (f32[128,2560]{1,0:T(8,128)S(1)}, f32[128,2560]{1,0:T(8,128)}, u32[]{:S(2)}) copy-start(f32[128,2560]{1,0:T(8,128)} %get-tuple-element.103) | copy-start | bytes 3932164
  600.7 8.1 %copy-start.6 = (f32[128,2048]{1,0:T(8,128)S(1)}, f32[128,2048]{1,0:T(8,128)}, u32[]{:S(2)}) copy-start(f32[128,2048]{1,0:T(8,128)} %get-tuple-element.102) | copy-start | bytes 3145732
  600.7 9.0 %copy-start.8 = (f32[416,256]{1,0:T(8,128)S(1)}, f32[416,256]{1,0:T(8,128)}, u32[]{:S(2)}) copy-start(f32[416,256]{1,0:T(8,128)} %get-tuple-element.119) | copy-start | bytes 1277956

commit v6 on v5

--- a/solution.py
+++ b/solution.py
@@ -24,6 +24,8 @@
 OUT_SPLIT = 1536
 IN_SHARE = 48
 OUT_SHARE = 32
+AB_PARTS = 2
+CLOSING_PARTS = (2, 2, 1, 1, 1)
 
 
 def matrix_product(left, right):
@@ -380,12 +382,15 @@
     )
 
 
-def opening_body(count, shares, arrays, stream, gain, *refs):
+def opening_body(count, shares, arrays, stream, gain, tokens, depths, lengths, grads, *refs):
     own = refs[:arrays]
     weights, factors, first, second = refs[arrays : arrays + 4]
     full = refs[arrays + 4 : 2 * arrays + 4]
     folded, normed, lowrank = refs[2 * arrays + 4 : 2 * arrays + 7]
-    scratch = refs[2 * arrays + 7 :]
+    all_seq, all_order, own_seq, own_order, own_place, active, live, masked = refs[
+        2 * arrays + 7 : 2 * arrays + 15
+    ]
+    scratch = refs[2 * arrays + 15 :]
     (bank, factor_bank, first_bank, in_bank, second_bank, bank_sem, factor_sem, out_sem) = scratch[
         :8
     ]
@@ -451,6 +456,44 @@
 
         lax.fori_loop(0, (width // high) * (wide // tile), inner, 0)
         put(i).start()
+
+    starts, total = [], 0
+    for i in range(lengths.shape[1]):
+        starts.append(total)
+        total = total + lengths[0, i]
+    ends = starts[1:] + [total]
+
+    def facts(token, row):
+        alive = token >= 0
+        sequence = sum((token >= end).astype(jnp.int32) for end in ends)
+        start = sum(jnp.where(sequence == i, item, 0) for i, item in enumerate(starts))
+        return (
+            alive,
+            jnp.where(alive, sequence, -1 - row),
+            jnp.where(alive, token, 0),
+            jnp.where(alive, token - start, 0),
+        )
+
+    every = tokens[...]
+    _, all_seq[...], all_order[...], _ = facts(
+        every, lax.broadcasted_iota(jnp.int32, every.shape, 1)
+    )
+    height = stream.shape[0]
+    square = (height, height)
+    on = lax.broadcasted_iota(jnp.int32, square, 0) == lax.broadcasted_iota(jnp.int32, square, 1)
+
+    def upright(row):
+        return jnp.sum(jnp.where(on, row, 0), axis=1, keepdims=True)
+
+    token = upright(tokens[:, pl.ds(pl.multiple_of(me * height, height), height)])
+    alive, own_seq[...], own_order[...], own_place[...] = facts(
+        token, me * height + lax.broadcasted_iota(jnp.int32, token.shape, 0)
+    )
+    depth_own = upright(depths[...])
+    live[...] = jnp.where(alive, 1.0, 0.0)
+    moving = jnp.where(alive & (depth_own > loop), 1.0, 0.0)
+    active[...] = moving
+    masked[...] = (moving * grads[...].astype(jnp.float32)).astype(masked.dtype)
 
     rows = stream[...].astype(jnp.float32)
     inverse = lax.rsqrt(jnp.mean(rows * rows, axis=-1, keepdims=True) + EPSILON)
@@ -480,7 +523,8 @@
         put(i).wait()
 
 
-def opening(count, ident, stream, gain, arrays, shares, weights, factors, first, second):
+def opening(count, ident, stream, gain, tokens, depths, lengths, grads, arrays, shares, weights,
+            factors, first, second):
     number = len(arrays)
     _, width, wide = weights.shape
     low = jnp.bfloat16
@@ -497,9 +541,16 @@
             jax.ShapeDtypeStruct(weights.shape, low),
             jax.ShapeDtypeStruct(stream.shape, low),
             jax.ShapeDtypeStruct((stream.shape[0], 3 * rank), low),
-        ],
-        in_specs=[inside] * 2 + [anywhere] * (number + 4),
-        out_specs=[anywhere] * (number + 1) + [inside] * 2,
+            jax.ShapeDtypeStruct(tokens.shape, jnp.int32),
+            jax.ShapeDtypeStruct(tokens.shape, jnp.int32),
+        ]
+        + [jax.ShapeDtypeStruct((stream.shape[0], 1), jnp.int32)] * 3
+        + [jax.ShapeDtypeStruct((stream.shape[0], 1), jnp.float32)] * 2
+        + [jax.ShapeDtypeStruct(grads.shape, low)],
+        in_specs=[inside] * 4
+        + [pl.BlockSpec(memory_space=pltpu.SMEM), inside]
+        + [anywhere] * (number + 4),
+        out_specs=[anywhere] * (number + 1) + [inside] * 10,
         scratch_shapes=[
             pltpu.VMEM(weights.shape, low),
             pltpu.VMEM((width, factors.shape[1]), low),
@@ -519,7 +570,7 @@
         ],
         compiler_params=kernel_params(ident),
         name="opening",
-    )(stream, gain, *arrays, weights, factors, first, second)
+    )(stream, gain, tokens, depths, lengths, grads, *arrays, weights, factors, first, second)
     return [
         item.reshape((count * item.shape[1],) + item.shape[2:]) for item in out[:number]
     ] + list(out[number:])
@@ -589,17 +640,18 @@
     (kv_unit,) = kv_units
     kv_line(1, kv_unit)
     kv_pair(0, kv_unit)
+    from_line(1, units[0])
+    from_pair(0, units[0])
     some_heads(4, heads)
     same = own_seq[...] == all_seq[...]
     allowed[...] = jnp.where(same & (all_order[...] <= own_order[...]), 1.0, 0.0)
     kv_line(2, kv_unit)
     kv_pair(1, kv_unit)
+    from_line(1, units[1])
+    from_pair(0, units[1])
     kv_line(3, kv_unit)
     kv_pair(2, kv_unit)
     kv_pair(3, kv_unit)
-    for unit in units:
-        from_line(1, unit)
-        from_pair(0, unit)
     kv_arrive()
     put_kv = pltpu.make_async_copy(kv_full, keys_values, put_sem)
     put_kv.start()
@@ -911,7 +963,7 @@
         pltpu.VMEM((2 * depth, rows, cols), kind),
         pltpu.VMEM((depth, rows, cols), kind),
         pltpu.VMEM((depth + 1, rows, cols), kind),
-        pltpu.VMEM((rows // 2, cols) if parts > 1 else (16, 128), kind),
+        pltpu.VMEM((rows // parts, cols) if parts > 1 else (16, 128), kind),
     ]
 
 
@@ -961,7 +1013,7 @@
     for item in loads:
         item.start()
     order, send_out, pair_out, line_out, last_out, finish_out, _, twin_out = sum_terms(
-        count, 2, out_terms, (out_core, out_pair, out_line, out_twin), sems[:7]
+        count, AB_PARTS, out_terms, (out_core, out_pair, out_line, out_twin), sems[:7]
     )
     _, send_kv, pair_kv, line_kv, last_kv, finish_kv, _, _ = sum_terms(
         count, 1, kv_terms, (kv_core, kv_pair, kv_line, kv_twin), sems[7:]
@@ -1044,10 +1096,12 @@
             send_kv(line, pair)
     for k in range(depth):
         pair_kv(k)
-    for k in range(depth):
-        line_out(k)
+    line_out(0)
+    line_out(1)
     for k in range(depth):
         line_kv(k)
+        if k + 2 < depth:
+            line_out(k + 2)
     last_kv(kv_sum)
     part = turn_back(kv_sum[:, :size], cosine[...], sine[...])
     joint_grads[:, wide : wide + size] = part.astype(low)
@@ -1091,10 +1145,10 @@
             pltpu.VMEM((height, both), jnp.float32),
             pltpu.VMEM((count, feature, OUT_SPLIT), low),
         ]
-        + sum_rooms(count, feature, OUT_SPLIT)
+        + sum_rooms(count, feature, OUT_SPLIT, parts=AB_PARTS)
         + sum_rooms(count, height, both, parts=1)
         + [pltpu.SemaphoreType.DMA((3,))]
-        + sum_sems(count, 2)
+        + sum_sems(count, AB_PARTS)
         + sum_sems(count, 1),
         compiler_params=kernel_params(ident),
         name="attention_grads",
@@ -1144,7 +1198,7 @@
     for item in [in_load] + loads:
         item.start()
     terms = (in_terms, out_terms, second_terms, first_terms, small_terms)
-    parts = (2, 2, 1, 1, 1)
+    parts = CLOSING_PARTS
     plans = [sum_terms(count, parts[i], terms[i], rooms[i], sems[i]) for i in range(5)]
     order = plans[0][0]
     send = [plan[1] for plan in plans]
@@ -1278,11 +1332,15 @@
         PROJECTED_WIDTH + MODEL_WIDTH, contract(held[...], factor_bank[...], 0, 0)
     )
     send_all(2)
+    if parts[3] > 1:
+        plans[3][7]()
     line_step[0](3)
     for k in range(depth):
         line_step[1](k)
     last_step[0](in_sum)
     last_step[1](out_sum)
+    if parts[2] > 1:
+        plans[2][7]()
     for i, total in ((4, small_sum), (3, first_sum), (2, second_sum)):
         for k in range(depth):
             line_step[i](k)
@@ -1311,7 +1369,7 @@
     ]
     sem = pltpu.SemaphoreType.DMA
     rooms, sems = [], []
-    for (rows, cols, kind), parts in zip(shapes, (2, 2, 1, 1, 1)):
+    for (rows, cols, kind), parts in zip(shapes, CLOSING_PARTS):
         rooms += sum_rooms(count, rows, cols, kind, parts)
         sems += sum_sems(count, parts)
     return pl.pallas_call(
@@ -1753,28 +1811,63 @@
 
 
 def add_body(*refs):
-    left, right, out = refs[-3], refs[-2], refs[-1]
-    out[0] = left[...].astype(jnp.float32) + right[...].astype(jnp.float32)
-
-
-def add_into(held, left, right, whole, which, skip):
-    rows, wide = right.shape
+    lefts, rights, out = refs[:3], refs[3:7], refs[7]
+    left, right, made, load_sem, made_sem = refs[8:]
+    step = made.shape[1]
+    each = left.shape[1] // step
+    chunks = [(i, n) for i in range(3) for n in range(each)]
+
+    def loads(i, n):
+        rows = pl.ds(n * step, step)
+        far = rights[i + 1].at[rows] if i else rights[0].at[rows] if n < FAR_TILES else None
+        if far is None:
+            far = rights[1].at[pl.ds((n - FAR_TILES) * step, step)]
+        return [
+            pltpu.make_async_copy(lefts[i].at[rows], left.at[i, rows], load_sem.at[i, n, 0]),
+            pltpu.make_async_copy(far, right.at[i, rows], load_sem.at[i, n, 1]),
+        ]
+
+    def put(at):
+        i, n = chunks[at]
+        return pltpu.make_async_copy(
+            made.at[at % 2], out.at[i, pl.ds(n * step, step)], made_sem.at[at % 2]
+        )
+
+    for i, n in chunks:
+        for item in loads(i, n):
+            item.start()
+    for at, (i, n) in enumerate(chunks):
+        for item in loads(i, n):
+            item.wait()
+        if at >= 2:
+            put(at - 2).wait()
+        rows = pl.ds(n * step, step)
+        made[at % 2] = left[i, rows].astype(jnp.float32) + right[i, rows].astype(jnp.float32)
+        put(at).start()
+    for at in (len(chunks) - 2, len(chunks) - 1):
+        put(at).wait()
+
+
+def add_loops(lefts, rights):
+    rows, wide = lefts[0].shape
     step = 256
-    before = [] if held is None else [held]
+    anywhere = pl.BlockSpec(memory_space=pl.ANY)
+    sem = pltpu.SemaphoreType.DMA
     return pl.pallas_call(
         add_body,
-        grid=(rows // step,),
-        out_shape=jax.ShapeDtypeStruct(whole, jnp.float32),
-        in_specs=[pl.BlockSpec(memory_space=pl.ANY)] * len(before)
-        + [
-            pl.BlockSpec((step, wide), lambda r: (r + skip // step, 0)),
-            pl.BlockSpec((step, wide), lambda r: (r, 0)),
+        out_shape=jax.ShapeDtypeStruct((3, rows, wide), jnp.float32),
+        in_specs=[anywhere] * 7,
+        out_specs=anywhere,
+        scratch_shapes=[
+            pltpu.VMEM((3, rows, wide), jnp.bfloat16),
+            pltpu.VMEM((3, rows, wide), jnp.bfloat16),
+            pltpu.VMEM((2, step, wide), jnp.float32),
+            sem((3, rows // step, 2)),
+            sem((2,)),
         ],
-        out_specs=pl.BlockSpec((1, step, wide), lambda r: (which, r + skip // step, 0)),
-        input_output_aliases={0: 0} if before else {},
         compiler_params=pltpu.CompilerParams(vmem_limit_bytes=VMEM_LIMIT),
         name="add_loops",
-    )(*before, left, right)
+    )(*lefts, *rights)
 
 
 def per_device(
@@ -1791,8 +1884,6 @@
     token_per_row,
     token_exit_depth,
 ):
-    current_loop = lax.axis_index("loop")
-    dp_index = lax.axis_index("dp")
     loop_count = lax.axis_size("loop")
     count = lax.axis_size("dp")
     local_rows = layer_input_stream.shape[1]
@@ -1800,35 +1891,28 @@
     key_at = QUERY_WIDTH
     value_at = QUERY_WIDTH + HEAD_SIZE
     down_at = PROJECTED_WIDTH + MODEL_WIDTH
-    live_all, seq_all, order_all, pos_all = token_facts(token_per_row[0], group_sequence_lengths[0])
-    first_row = dp_index * local_rows
-
-    def own_slice(values):
-        return lax.dynamic_slice_in_dim(values, first_row, local_rows, 0)
-
-    live_own = own_slice(live_all)
-    seq_own = own_slice(seq_all)
-    order_own = own_slice(order_all)
-    pos_own = own_slice(pos_all)
-    active_mask = (live_own & (token_exit_depth[0] > current_loop)).astype(jnp.float32)[:, None]
     stream = layer_input_stream[0]
     residual_stream = stream.astype(jnp.float32)
     grad_out = layer_output_gradient[0].astype(jnp.float32)
     adapter_first = adapter_first_factors[0]
     adapter_second = adapter_second_factors[0]
     ffn_weight = jnp.swapaxes(feedforward_weight, 0, 1)
-    feedforward_gradient = (active_mask * grad_out).astype(low)
-
-    input_weight, output_weight, ffn_folded, normed_input, lowrank_projection = opening(
-        count, 1, stream, layer_norm_gains[:1], (attention_in_weight, attention_out_weight),
-        (IN_SHARE, OUT_SHARE), ffn_weight, adapter_hidden_factors[0], adapter_first,
-        adapter_second,
-    )
+
+    (
+        input_weight, output_weight, ffn_folded, normed_input, lowrank_projection, seq_all,
+        order_all, seq_own, order_own, pos_own, active_mask, live_mask, feedforward_gradient,
+    ) = opening(
+        count, 1, stream, layer_norm_gains[:1], token_per_row, token_exit_depth,
+        group_sequence_lengths, layer_output_gradient[0],
+        (attention_in_weight, attention_out_weight), (IN_SHARE, OUT_SHARE), ffn_weight,
+        adapter_hidden_factors[0], adapter_first, adapter_second,
+    )
+    live_own = live_mask[:, 0] > 0.5
     half = HEAD_SIZE // 2
     freqs = 10000.0 ** (-jnp.arange(half, dtype=jnp.float32) / half)
-    angles = pos_own.astype(jnp.float32)[:, None] * freqs
+    angles = pos_own.astype(jnp.float32) * freqs
     cosine, sine = jnp.cos(angles), jnp.sin(angles)
-    facts = (cosine, sine, seq_own[:, None], order_own[:, None], seq_all[None], order_all[None])
+    facts = (cosine, sine, seq_own, order_own, seq_all, order_all)
     (
         queries, attended_rows, output_projection, level, middle_state, second_normed_input,
         kv_blocks, grad_blocks,
@@ -1885,11 +1969,9 @@
     in_low = in_portion.astype(low)
     out_low = jnp.concatenate([out_first, out_last], axis=1).astype(low)
     in_far, out_far, small_far = swap_loops(in_low), swap_loops(out_low), swap_loops(small_sum)
-    whole = ffn_weight.shape
-    sum_mlp = add_into(None, gate_grad, gate_other, whole, 0, 0)
-    sum_mlp = add_into(sum_mlp, gate_grad, gate_last, whole, 0, FAR_TILES * 256)
-    sum_mlp = add_into(sum_mlp, up_grad, up_other, whole, 1, 0)
-    sum_mlp = add_into(sum_mlp, down_grad, down_other, whole, 2, 0)
+    sum_mlp = add_loops(
+        (gate_grad, up_grad, down_grad), (gate_other, gate_last, up_other, down_other)
+    )
     adapter_first_gradient = jnp.concatenate(
         [
             outer_columns(in_low[:, :key_at], adapter_second[:, :key_at]),

time: 622 us -> 608 us (0.977)
  other arithmetic: 23.7 us -> 15.1 us
    pallas_call x4 -> x1, Pallas kernels: 24.2 us -> 17.5 us  [add_loops(): pl.pallas_call(add_body, out_shape=jax.ShapeDtypeStruct((3, rows, wide),...]
  transfers between devices with their start and end apart: 6 -> 6, of which waited for: 0 -> 0; matrix products, arithmetic and copies ran while one was open for 2% -> 2% of each run, Pallas kernels for 36% -> 37%
where the time goes in v6:
time: 608 us; the launch traced here: 603 us
  Pallas kernels  564 us (93%)
  other arithmetic  15.1 us (2%)
  local copies, waits for them, and re-layouts  11.9 us (2%)
  starting transfers between devices  6.63 us (1%)
    pallas_call x1, Pallas kernels, unit_grads(): pl.pallas_call(functools.partial(unit_grads_body, count, parts), out_shap...  134 us
    pallas_call x1, Pallas kernels, closing(): pl.pallas_call(functools.partial(closing_body, count), out_shape=[jax.Sha...  133 us
    pallas_call x1, Pallas kernels, opening(): pl.pallas_call(functools.partial(opening_body, count, shares, number), ou...  82 us
    pallas_call x1, Pallas kernels, attention(): pl.pallas_call(functools.partial(attention_body, count), out_shape=[shape...  72.3 us
    pallas_call x1, Pallas kernels, attention_grads(): pl.pallas_call(functools.partial(attention_grads_body, count), out_shape=...  69.8 us
    pallas_call x1, Pallas kernels, hidden_units(): pl.pallas_call(functools.partial(hidden_body, count, parts), out_shape=[a...  55.2 us
    pallas_call x1, Pallas kernels, add_loops(): pl.pallas_call(add_body, out_shape=jax.ShapeDtypeStruct((3, rows, wide),...  17.5 us
  transfers between devices with their start and end apart: 6, of which 0 were waited for; matrix products, arithmetic and copies ran while one was open for 2% of the time, Pallas kernels for 37%

profile of v6, /device:TPU:0, one launch (start us, length us, event | category | flops | bytes accessed | tf_op | source)
XLA Modules:
  0.0 602.5 jit_solution(3355093558025038660)
XLA Ops:
  0.7 1.4 fusion.16
  2.1 82.0 %opening.1 = (bf16[16,128,2560]{2,1,0:T(8,128)(2,1)}, bf16[16,128,2048]{2,1,0:T(8,128)(2,1)}, bf16[3,1024,2048]{2,1,0:T(8,128)(2,1)}, bf16[128,2048]{1,0:T(8,128...) custom-call(bf16[128,2048]{1,0:T(8,128)(2,1)} %bitcast.49, ...), custom_call_target="tpu_custom_call" | custom-call | tf_op jit(solution)/shard_map/opening/pallas_call | solution.py:535
  84.0 0.9 convert_reduce_fusion
  85.0 1.0 multiply_sine_fusion
  86.0 72.3 %attention.1 = (bf16[128,2048]{1,0:T(8,128)(2,1)}, bf16[128,2048]{1,0:T(8,128)(2,1)}, bf16[128,256]{1,0:T(8,128)(2,1)}, f32[4,256,128]{2,1,0:T(8,128)}, f32[128,...) custom-call(bf16[128,2048]{1,0:T(8,128)(2,1)} %get-tuple-element.86.nor, ...), custom_call_target="tpu_custom_call" | custom-call | tf_op jit(solution)/shard_map/attention/pallas_call | solution.py:731
  158.2 55.2 %hidden_units.1 = (bf16[2048,1024]{1,0:T(8,128)(2,1)}, bf16[2048,1024]{1,0:T(8,128)(2,1)}, bf16[2048,1024]{1,0:T(8,128)(2,1)}, bf16[16,128,2048]{2,1,0:T(8,128)(2,1)}) custom-call(bf16[128,2048]{1,0:T(8,128)(2,1)} %get-tuple-element.98.own, bf16[16,128,2048]{2,1,0:T(8,128)(2,1)} %get-tuple-element.99.grads.grads_all, ...), custom_call_target="tpu_custom_call" | custom-call | tf_op jit(solution)/shard_map/hidden_units/pallas_call | solution.py:1517
  213.4 134.1 %unit_grads.1 = (f32[128,2048]{1,0:T(8,128)}, f32[128,2048]{1,0:T(8,128)}, bf16[1024,2048]{1,0:T(8,128)(2,1)}, bf16[1024,2048]{1,0:T(8,128)(2,1)}, bf16[1024,204...) custom-call(bf16[2048,1024]{1,0:T(8,128)(2,1)} %get-tuple-element.101.units, bf16[2048,1024]{1,0:T(8,128)(2,1)} %get-tuple-element.102.gate_grads, ...), custom_call_target="tpu_custom_call" | custom-call | tf_op jit(solution)/shard_map/unit_grads/pallas_call | solution.py:1777
  347.6 1.5 collective-permute-start.3
  349.1 0.6 collective-permute-start.4
  349.7 2.4 slice.88
  352.0 1.5 collective-permute-start.2
  353.8 2.5 multiply_reduce_fusion
  356.6 0.6 multiply_multiply_fusion
  357.3 0.7 pad_maximum_fusion.1
  358.4 1.5 multiply_convert_fusion
  359.9 69.8 %attention_grads.1 = (bf16[128,2560]{1,0:T(8,128)(2,1)}, bf16[128,768]{1,0:T(8,128)(2,1)}, f32[128,1536]{1,0:T(8,128)}) custom-call(bf16[128,2048]{1,0:T(8,128)(2,1)} %get-tuple-element.106.attended, bf16[128,2048]{1,0:T(8,128)(2,1)} %get-tuple-element.140.grad_rows, bf16[2048,2048]{1,0:T(8,128)(2,1)} %bitcast.46, ...), custom_call_target="tpu_custom_call" | custom-call | tf_op jit(solution)/shard_map/attention_grads/pallas_call | solution.py:1128
  429.8 132.6 %closing.1 = (f32[128,2560]{1,0:T(8,128)}, f32[128,512]{1,0:T(8,128)}, f32[416,256]{1,0:T(8,128)}, f32[128,512]{1,0:T(8,128)}, f32[8,128]{1,0:T(8,128)}, /*index=5*/f32[128,2048]{1,0:T(8,128)}, f32[1024,768]{1,0:T(8,128)}) custom-call(bf16[128,2048]{1,0:T(8,128)(2,1)} %get-tuple-element.86.normed, bf16[128,2560]{1,0:T(8,128)(2,1)} %get-tuple-element.111.joint_grads, ...), custom_call_target="tpu_custom_call" | custom-call | tf_op jit(solution)/shard_map/closing/pallas_call | solution.py:1375
  562.4 1.1 convert.7
  563.7 0.9 collective-permute-start.1
  564.6 1.4 convert_element_type.46
  566.0 1.2 collective-permute-start
  568.7 0.9 collective-permute-start.5
  569.6 0.9 copy-done.15
  570.5 17.5 %add_loops.1 = f32[3,1024,2048]{2,1,0:T(8,128)} custom-call(bf16[1024,2048]{1,0:T(8,128)(2,1)} %get-tuple-element.115.gate_grads.refs_0_, bf16[1024,2048]{1,0:T(8,128)(2,1)} %get-tuple-element.116.up_grads.refs_1_, bf16[1024,2048]{1,0:T(8,128)(2,1)} %get-tuple-element.117.down_grads.refs_2_, bf16[768,2048]{1,0:T(8,128)(2,1)} %get-tuple-element.125.refs_3_, ...), custom_call_target="tpu_custom_call" | custom-call | tf_op jit(solution)/shard_map/add_loops/pallas_call | solution.py:1856
  588.1 0.5 slice.98
  588.6 0.6 slice.96
  589.2 1.2 slice_reduce_fusion
  590.3 1.2 convert_add_fusion
  591.5 2.3 convert_add_fusion.1
  595.2 2.3 copy.31
  597.4 1.8 copy.32
  599.2 1.7 copy.33
  (54 shorter events, 2.4 us)
Async XLA Ops:
  213.4 140.1 %copy-start.8 = (f32[128,1]{1,0:T(8,128)S(1)}, f32[128,1]{1,0:T(8,128)}, u32[]{:S(2)}) copy-start(f32[128,1]{1,0:T(8,128)} %get-tuple-element.88.active) | copy-start | bytes 1540
  213.4 140.2 %copy-start.1 = (f32[128,2048]{1,0:T(8,128)S(1)}, f32[128,2048]{1,0:T(8,128)}, u32[]{:S(2)}) copy-start(f32[128,2048]{1,0:T(8,128)} %get-tuple-element.97) | copy-start | bytes 3145732
  213.4 140.4 %copy-start.11 = (f32[1,2048]{1,0:T(1,128)S(1)}, f32[1,2048]{1,0:T(1,128)}, u32[]{:S(2)}) copy-start(f32[1,2048]{1,0:T(1,128)} %get-tuple-element.144.gain) | copy-start | bytes 24580
  347.6 6.3 %copy-start.2 = (bf16[1,128,2048]{2,1,0:T(8,128)(2,1)S(1)}, bf16[1,128,2048]{2,1,0:T(8,128)(2,1)}, u32[]{:S(2)}) copy-start(bf16[1,128,2048]{2,1,0:T(8,128)(2,1)} %param.16) | copy-start | bytes 1572868
  347.6 6.3 %copy-start.4 = (f32[128,2048]{1,0:T(8,128)S(1)}, f32[128,2048]{1,0:T(8,128)}, u32[]{:S(2)}) copy-start(f32[128,2048]{1,0:T(8,128)} %get-tuple-element.107) | copy-start | bytes 3145732
  347.6 221.1 %collective-permute-start.3 = (bf16[1024,2048]{1,0:T(8,128)(2,1)}, bf16[1024,2048]{1,0:T(8,128)(2,1)}, u32[]{:S(2)}, u32[]{:S(2)}) collective-permute-start(bf16[1024,2048]{1,0:T(8,128)(2,1)} %get-tuple-element.116.up_grads.refs_1_), channel_id=1, source_target_pairs={{0,16},{16,0},{1,17},{17,1},{2,18},{18,2},{3,19},{19,3},{4,20},{20... | collective-permute-start | bytes 12582920 | tf_op jit(solution)/shard_map/ppermute | solution.py:1810
  349.1 219.5 %collective-permute-start.4 = (bf16[1024,2048]{1,0:T(8,128)(2,1)}, bf16[1024,2048]{1,0:T(8,128)(2,1)}, u32[]{:S(2)}, u32[]{:S(2)}) collective-permute-start(bf16[1024,2048]{1,0:T(8,128)(2,1)} %get-tuple-element.117.down_grads.refs_2_), channel_id=1, source_target_pairs={{0,16},{16,0},{1,17},{17,1},{2,18},{18,2},{3,19},{19,3},{4,20},{20... | collective-permute-start | bytes 12582920 | tf_op jit(solution)/shard_map/ppermute | solution.py:1810
  349.7 6.7 %copy-start.12 = (f32[128,1]{1,0:T(8,128)S(1)}, f32[128,1]{1,0:T(8,128)}, u32[]{:S(2)}) copy-start(f32[128,1]{1,0:T(8,128)} %get-tuple-element.113) | copy-start | bytes 1540
  349.7 6.8 %copy-start.14 = (s32[1,128]{1,0:T(1,128)S(1)}, s32[1,128]{1,0:T(1,128)}, u32[]{:S(2)}) copy-start(s32[1,128]{1,0:T(1,128)} %depths.1) | copy-start | bytes 1540
  349.7 8.7 %copy-start.6 = (bf16[1,128,2048]{2,1,0:T(8,128)(2,1)S(1)}, bf16[1,128,2048]{2,1,0:T(8,128)(2,1)}, u32[]{:S(2)}) copy-start(bf16[1,128,2048]{2,1,0:T(8,128)(2,1)} %param.17) | copy-start | bytes 1572868
  352.0 216.6 %collective-permute-start.2 = (bf16[256,2048]{1,0:T(8,128)(2,1)}, bf16[256,2048]{1,0:T(8,128)(2,1)}, u32[]{:S(2)}, u32[]{:S(2)}) collective-permute-start(bf16[256,2048]{1,0:T(8,128)(2,1)} %slice.88), channel_id=1, source_target_pairs={{0,16},{16,0},{1,17},{17,1},{2,18},{18,2},{3,19},{19,3},{4,20},{20... | collective-permute-start | bytes 3145736 | tf_op jit(solution)/shard_map/ppermute | solution.py:1810
  358.3 71.4 %copy-start.10 = (f32[16,8,128]{2,1,0:T(8,128)}, f32[16,8,128]{2,1,0:T(8,128)S(1)}, u32[]{:S(2)}) copy-start(f32[16,8,128]{2,1,0:T(8,128)S(1)} %scatter.9.small) | copy-start | bytes 196612
  429.8 133.8 %copy-start.7 = (f32[128,1536]{1,0:T(8,128)S(1)}, f32[128,1536]{1,0:T(8,128)}, u32[]{:S(2)}) copy-start(f32[128,1536]{1,0:T(8,128)} %get-tuple-element.120) | copy-start | bytes 2359300
  562.4 4.8 copy-start
  563.7 24.4 %collective-permute-start.1 = (bf16[128,2048]{1,0:T(8,128)(2,1)S(1)}, bf16[128,2048]{1,0:T(8,128)(2,1)}, u32[]{:S(2)}, u32[]{:S(2)}) collective-permute-start(bf16[128,2048]{1,0:T(8,128)(2,1)S(1)} %pad_maximum_fusion), channel_id=1, source_target_pairs={{0,16},{16,0},{1,17},{17,1},{2,18},{18,2},{3,19},{19,3},{4,20},{20... | collective-permute-start | bytes 1572872 | tf_op jit(solution)/shard_map/ppermute | solution.py:1810
  564.6 4.1 copy-start.13
  564.6 5.0 copy-start.9
  566.0 22.0 %collective-permute-start = (bf16[128,2560]{1,0:T(8,128)(2,1)S(1)}, bf16[128,2560]{1,0:T(8,128)(2,1)S(1)}, u32[]{:S(2)}, u32[]{:S(2)}) collective-permute-start(bf16[128,2560]{1,0:T(8,128)(2,1)S(1)} %convert_element_type.46), channel_id=1, source_target_pairs={{0,16},{16,0},{1,17},{17,1},{2,18},{18,2},{3,19},{19,3},{4,20},{20... | collective-permute-start | bytes 1966088 | tf_op jit(solution)/shard_map/ppermute | solution.py:1810
  568.7 19.4 %collective-permute-start.5 = (f32[8,128]{1,0:T(8,128)S(1)}, f32[8,128]{1,0:T(8,128)S(1)}, u32[]{:S(2)}, u32[]{:S(2)}) collective-permute-start(f32[8,128]{1,0:T(8,128)S(1)} %copy-done.13), channel_id=1, source_target_pairs={{0,16},{16,0},{1,17},{17,1},{2,18},{18,2},{3,19},{19,3},{4,20},{20... | collective-permute-start | bytes 12296 | tf_op jit(solution)/shard_map/ppermute | solution.py:1810
  569.6 0.9 copy-start.15
  570.5 19.8 %copy-start.3 = (f32[128,2560]{1,0:T(8,128)S(1)}, f32[128,2560]{1,0:T(8,128)}, u32[]{:S(2)}) copy-start(f32[128,2560]{1,0:T(8,128)} %get-tuple-element.119) | copy-start | bytes 3932164
  591.5 7.7 %copy-start.5 = (f32[1024,768]{1,0:T(8,128)S(1)}, f32[1024,768]{1,0:T(8,128)}, u32[]{:S(2)}) copy-start(f32[1024,768]{1,0:T(8,128)} %get-tuple-element.136) | copy-start | bytes 9437188

commit v7 on v6

--- a/solution.py
+++ b/solution.py
@@ -1537,9 +1537,10 @@
 
 def unit_grads_body(count, parts, units, gate_grads, up_grads, weights, rows_all, grads_all,
                     input_sum, output_sum, gate_out, up_out, down_out, gate_far,
+                    gate_tail,
                     bank, rows_in, units_in, made, loaded, leaving, core_in, pair_in, line_in,
                     twin_in, bank_sem, rows_sem, fill_sems, units_sem, made_sem, far_send,
-                    far_recv, *sems):
+                    far_recv, tail_sem, *sems):
     me, depth, z, y, c = place(count)
     height, wide = input_sum.shape
     width = weights.shape[1]
@@ -1666,6 +1667,9 @@
             made.at[slot], (gate_out, up_out, down_out)[g // each].at[rows], made_sem.at[slot]
         )
 
+    def put_tail(slot):
+        return pltpu.make_async_copy(made.at[slot], gate_tail, tail_sem)
+
     def swap(g):
         rows = pl.ds(g * tall, tall)
         return pltpu.make_async_remote_copy(
@@ -1686,6 +1690,8 @@
         bring(g, slot).wait()
         if g >= 2:
             put(g - 2, slot).wait()
+            if g - 2 == FAR_TILES:
+                put_tail(slot).wait()
             if g - 2 < FAR_TILES:
                 swap(g - 2).start()
         at = 0 if g < 2 * each else 2
@@ -1699,6 +1705,8 @@
 
         lax.fori_loop(0, wide // tile, inner, 0)
         put(g, slot).start()
+        if g == FAR_TILES:
+            put_tail(slot).start()
 
     for item in first_fills[:2]:
         item.wait()
@@ -1777,9 +1785,12 @@
     return pl.pallas_call(
         functools.partial(unit_grads_body, count, parts),
         out_shape=[total, total] + [jax.ShapeDtypeStruct((width, wide), low)] * 3
-        + [jax.ShapeDtypeStruct((FAR_TILES * 256, wide), low)],
+        + [
+            jax.ShapeDtypeStruct((FAR_TILES * 256, wide), low),
+            jax.ShapeDtypeStruct((width - FAR_TILES * 256, wide), low),
+        ],
         in_specs=[anywhere] * 6,
-        out_specs=[inside, inside] + [anywhere] * 4,
+        out_specs=[inside, inside] + [anywhere] * 5,
         scratch_shapes=[
             pltpu.VMEM((4, width, wide), low),
             pltpu.VMEM((2, 2, 2 * height, width), low),
@@ -1798,6 +1809,7 @@
             sem((2,)),
             sem((FAR_TILES,)),
             sem((FAR_TILES,)),
+            sem,
         ]
         + sum_sems(count, parts)
         + sum_sems(count, parts),
@@ -1923,10 +1935,10 @@
     units_own, grad_gate_own, grad_up_own, normed_blocks = hidden_units(
         count, 3, second_normed_input, grad_blocks, ffn_folded
     )
-    second_normed_gradient, ffn_sum, gate_grad, up_grad, down_grad, gate_other = unit_grads(
+    second_normed_gradient, ffn_sum, gate_grad, up_grad, down_grad, gate_other, gate_tail = unit_grads(
         count, 4, units_own, grad_gate_own, grad_up_own, ffn_folded, normed_blocks, grad_blocks
     )
-    gate_last = swap_loops(gate_grad[FAR_TILES * 256 :])
+    gate_last = swap_loops(gate_tail)
     up_other = swap_loops(up_grad)
     down_other = swap_loops(down_grad)
 

time: 608 us -> 606 us (level)
  no operation moved by 1% of the time
where the time goes in v7:
time: 606 us; the launch traced here: 600 us
  Pallas kernels  563 us (93%)
  other arithmetic  15.4 us (3%)
  local copies, waits for them, and re-layouts  9.56 us (2%)
  starting transfers between devices  6.38 us (1%)
    pallas_call x1, Pallas kernels, unit_grads(): pl.pallas_call(functools.partial(unit_grads_body, count, parts), out_shap...  134 us
    pallas_call x1, Pallas kernels, closing(): pl.pallas_call(functools.partial(closing_body, count), out_shape=[jax.Sha...  133 us
    pallas_call x1, Pallas kernels, opening(): pl.pallas_call(functools.partial(opening_body, count, shares, number), ou...  81.8 us
    pallas_call x1, Pallas kernels, attention(): pl.pallas_call(functools.partial(attention_body, count), out_shape=[shape...  72.3 us
    pallas_call x1, Pallas kernels, attention_grads(): pl.pallas_call(functools.partial(attention_grads_body, count), out_shape=...  69.8 us
    pallas_call x1, Pallas kernels, hidden_units(): pl.pallas_call(functools.partial(hidden_body, count, parts), out_shape=[a...  55.2 us
    pallas_call x1, Pallas kernels, add_loops(): pl.pallas_call(add_body, out_shape=jax.ShapeDtypeStruct((3, rows, wide),...  17.5 us
  transfers between devices with their start and end apart: 6, of which 0 were waited for; matrix products, arithmetic and copies ran while one was open for 2% of the time, Pallas kernels for 37%

profile of v7, /device:TPU:0, one launch (start us, length us, event | category | flops | bytes accessed | tf_op | source)
XLA Modules:
  0.0 600.2 jit_solution(10496034783372440534)
XLA Ops:
  0.7 1.4 fusion.16
  2.1 81.8 %opening.1 = (bf16[16,128,2560]{2,1,0:T(8,128)(2,1)}, bf16[16,128,2048]{2,1,0:T(8,128)(2,1)}, bf16[3,1024,2048]{2,1,0:T(8,128)(2,1)}, bf16[128,2048]{1,0:T(8,128...) custom-call(bf16[128,2048]{1,0:T(8,128)(2,1)} %bitcast.49, ...), custom_call_target="tpu_custom_call" | custom-call | tf_op jit(solution)/shard_map/opening/pallas_call | solution.py:535
  83.9 0.9 convert_reduce_fusion
  84.9 1.0 multiply_sine_fusion
  85.8 72.3 %attention.1 = (bf16[128,2048]{1,0:T(8,128)(2,1)}, bf16[128,2048]{1,0:T(8,128)(2,1)}, bf16[128,256]{1,0:T(8,128)(2,1)}, f32[4,256,128]{2,1,0:T(8,128)}, f32[128,...) custom-call(bf16[128,2048]{1,0:T(8,128)(2,1)} %get-tuple-element.87.nor, ...), custom_call_target="tpu_custom_call" | custom-call | tf_op jit(solution)/shard_map/attention/pallas_call | solution.py:731
  158.2 55.2 %hidden_units.1 = (bf16[2048,1024]{1,0:T(8,128)(2,1)}, bf16[2048,1024]{1,0:T(8,128)(2,1)}, bf16[2048,1024]{1,0:T(8,128)(2,1)}, bf16[16,128,2048]{2,1,0:T(8,128)(2,1)}) custom-call(bf16[128,2048]{1,0:T(8,128)(2,1)} %get-tuple-element.99.own, bf16[16,128,2048]{2,1,0:T(8,128)(2,1)} %get-tuple-element.100.grads.grads_all, ...), custom_call_target="tpu_custom_call" | custom-call | tf_op jit(solution)/shard_map/hidden_units/pallas_call | solution.py:1517
  213.4 134.1 %unit_grads.1 = (f32[128,2048]{1,0:T(8,128)}, f32[128,2048]{1,0:T(8,128)}, bf16[1024,2048]{1,0:T(8,128)(2,1)}, bf16[1024,2048]{1,0:T(8,128)(2,1)}, bf16[1024,204...) custom-call(bf16[2048,1024]{1,0:T(8,128)(2,1)} %get-tuple-element.102.units, ...), custom_call_target="tpu_custom_call" | custom-call | tf_op jit(solution)/shard_map/unit_grads/pallas_call | solution.py:1785
  347.5 1.5 collective-permute-start.3
  349.1 0.6 collective-permute-start.4
  349.6 1.5 collective-permute-start.2
  351.4 2.9 multiply_reduce_fusion
  354.5 0.6 multiply_multiply_fusion
  355.1 0.7 pad_maximum_fusion.1
  356.3 1.5 multiply_convert_fusion
  357.8 69.8 %attention_grads.1 = (bf16[128,2560]{1,0:T(8,128)(2,1)}, bf16[128,768]{1,0:T(8,128)(2,1)}, f32[128,1536]{1,0:T(8,128)}) custom-call(bf16[128,2048]{1,0:T(8,128)(2,1)} %get-tuple-element.107.attended, bf16[128,2048]{1,0:T(8,128)(2,1)} %get-tuple-element.142.grad_rows, bf16[2048,2048]{1,0:T(8,128)(2,1)} %bitcast.46, ...), custom_call_target="tpu_custom_call" | custom-call | tf_op jit(solution)/shard_map/attention_grads/pallas_call | solution.py:1128
  427.6 132.7 %closing.1 = (f32[128,2560]{1,0:T(8,128)}, f32[128,512]{1,0:T(8,128)}, f32[416,256]{1,0:T(8,128)}, f32[128,512]{1,0:T(8,128)}, f32[8,128]{1,0:T(8,128)}, /*index=5*/f32[128,2048]{1,0:T(8,128)}, f32[1024,768]{1,0:T(8,128)}) custom-call(bf16[128,2048]{1,0:T(8,128)(2,1)} %get-tuple-element.87.normed, bf16[128,2560]{1,0:T(8,128)(2,1)} %get-tuple-element.112.joint_grads, ...), custom_call_target="tpu_custom_call" | custom-call | tf_op jit(solution)/shard_map/closing/pallas_call | solution.py:1375
  560.3 1.1 convert.7
  561.5 0.7 collective-permute-start.1
  562.2 1.4 convert_element_type.46
  563.6 1.5 collective-permute-start
  566.0 0.5 convolution_dynamic-update-slice_fusion.2
  566.5 0.7 collective-permute-start.5
  567.2 0.9 copy-done.15
  568.1 17.5 %add_loops.1 = f32[3,1024,2048]{2,1,0:T(8,128)} custom-call(bf16[1024,2048]{1,0:T(8,128)(2,1)} %get-tuple-element.116.gate_grads.refs_0_, bf16[1024,2048]{1,0:T(8,128)(2,1)} %get-tuple-element.117.up_grads.refs_1_, bf16[1024,2048]{1,0:T(8,128)(2,1)} %get-tuple-element.118.down_grads.refs_2_, bf16[768,2048]{1,0:T(8,128)(2,1)} %get-tuple-element.127.refs_3_, ...), custom_call_target="tpu_custom_call" | custom-call | tf_op jit(solution)/shard_map/add_loops/pallas_call | solution.py:1868
  585.7 0.5 slice.94
  586.2 0.6 slice.92
  586.8 1.2 slice_reduce_fusion
  588.0 1.2 convert_add_fusion
  589.1 2.3 convert_add_fusion.1
  592.8 2.3 copy.31
  595.1 1.8 copy.32
  596.9 1.7 copy.33
  (53 shorter events, 1.9 us)
Async XLA Ops:
  213.4 137.7 %copy-start.8 = (f32[128,1]{1,0:T(8,128)S(1)}, f32[128,1]{1,0:T(8,128)}, u32[]{:S(2)}) copy-start(f32[128,1]{1,0:T(8,128)} %get-tuple-element.89.active) | copy-start | bytes 1540
  213.4 137.8 %copy-start.1 = (f32[128,2048]{1,0:T(8,128)S(1)}, f32[128,2048]{1,0:T(8,128)}, u32[]{:S(2)}) copy-start(f32[128,2048]{1,0:T(8,128)} %get-tuple-element.98) | copy-start | bytes 3145732
  213.4 138.0 %copy-start.2 = (bf16[1,128,2048]{2,1,0:T(8,128)(2,1)S(1)}, bf16[1,128,2048]{2,1,0:T(8,128)(2,1)}, u32[]{:S(2)}) copy-start(bf16[1,128,2048]{2,1,0:T(8,128)(2,1)} %param.16) | copy-start | bytes 1572868
  213.4 138.0 %copy-start.11 = (f32[1,2048]{1,0:T(1,128)S(1)}, f32[1,2048]{1,0:T(1,128)}, u32[]{:S(2)}) copy-start(f32[1,2048]{1,0:T(1,128)} %get-tuple-element.146.gain) | copy-start | bytes 24580
  347.5 6.8 %copy-start.12 = (f32[128,1]{1,0:T(8,128)S(1)}, f32[128,1]{1,0:T(8,128)}, u32[]{:S(2)}) copy-start(f32[128,1]{1,0:T(8,128)} %get-tuple-element.114) | copy-start | bytes 1540
  347.5 6.9 %copy-start.14 = (s32[1,128]{1,0:T(1,128)S(1)}, s32[1,128]{1,0:T(1,128)}, u32[]{:S(2)}) copy-start(s32[1,128]{1,0:T(1,128)} %depths.1) | copy-start | bytes 1540
  347.5 8.7 %copy-start.4 = (f32[128,2048]{1,0:T(8,128)S(1)}, f32[128,2048]{1,0:T(8,128)}, u32[]{:S(2)}) copy-start(f32[128,2048]{1,0:T(8,128)} %get-tuple-element.108) | copy-start | bytes 3145732
  347.5 8.7 %copy-start.6 = (bf16[1,128,2048]{2,1,0:T(8,128)(2,1)S(1)}, bf16[1,128,2048]{2,1,0:T(8,128)(2,1)}, u32[]{:S(2)}) copy-start(bf16[1,128,2048]{2,1,0:T(8,128)(2,1)} %param.17) | copy-start | bytes 1572868
  347.5 219.0 %collective-permute-start.3 = (bf16[1024,2048]{1,0:T(8,128)(2,1)}, bf16[1024,2048]{1,0:T(8,128)(2,1)}, u32[]{:S(2)}, u32[]{:S(2)}) collective-permute-start(bf16[1024,2048]{1,0:T(8,128)(2,1)} %get-tuple-element.117.up_grads.refs_1_), channel_id=1, source_target_pairs={{0,16},{16,0},{1,17},{17,1},{2,18},{18,2},{3,19},{19,3},{4,20},{20... | collective-permute-start | bytes 12582920 | tf_op jit(solution)/shard_map/ppermute | solution.py:1822
  349.1 217.5 %collective-permute-start.4 = (bf16[1024,2048]{1,0:T(8,128)(2,1)}, bf16[1024,2048]{1,0:T(8,128)(2,1)}, u32[]{:S(2)}, u32[]{:S(2)}) collective-permute-start(bf16[1024,2048]{1,0:T(8,128)(2,1)} %get-tuple-element.118.down_grads.refs_2_), channel_id=1, source_target_pairs={{0,16},{16,0},{1,17},{17,1},{2,18},{18,2},{3,19},{19,3},{4,20},{20... | collective-permute-start | bytes 12582920 | tf_op jit(solution)/shard_map/ppermute | solution.py:1822
  349.6 216.9 %collective-permute-start.2 = (bf16[256,2048]{1,0:T(8,128)(2,1)}, bf16[256,2048]{1,0:T(8,128)(2,1)}, u32[]{:S(2)}, u32[]{:S(2)}) collective-permute-start(bf16[256,2048]{1,0:T(8,128)(2,1)} %get-tuple-element.124), channel_id=1, source_target_pairs={{0,16},{16,0},{1,17},{17,1},{2,18},{18,2},{3,19},{19,3},{4,20},{20... | collective-permute-start | bytes 3145736 | tf_op jit(solution)/shard_map/ppermute | solution.py:1822
  356.2 71.4 %copy-start.10 = (f32[16,8,128]{2,1,0:T(8,128)}, f32[16,8,128]{2,1,0:T(8,128)S(1)}, u32[]{:S(2)}) copy-start(f32[16,8,128]{2,1,0:T(8,128)S(1)} %scatter.9.small) | copy-start | bytes 196612
  427.6 133.8 %copy-start.7 = (f32[128,1536]{1,0:T(8,128)S(1)}, f32[128,1536]{1,0:T(8,128)}, u32[]{:S(2)}) copy-start(f32[128,1536]{1,0:T(8,128)} %get-tuple-element.121) | copy-start | bytes 2359300
  560.3 4.8 copy-start
  561.5 24.1 %collective-permute-start.1 = (bf16[128,2048]{1,0:T(8,128)(2,1)S(1)}, bf16[128,2048]{1,0:T(8,128)(2,1)}, u32[]{:S(2)}, u32[]{:S(2)}) collective-permute-start(bf16[128,2048]{1,0:T(8,128)(2,1)S(1)} %pad_maximum_fusion), channel_id=1, source_target_pairs={{0,16},{16,0},{1,17},{17,1},{2,18},{18,2},{3,19},{19,3},{4,20},{20... | collective-permute-start | bytes 1572872 | tf_op jit(solution)/shard_map/ppermute | solution.py:1822
  562.2 4.3 copy-start.13
  562.2 5.0 copy-start.9
  563.6 22.0 %collective-permute-start = (bf16[128,2560]{1,0:T(8,128)(2,1)S(1)}, bf16[128,2560]{1,0:T(8,128)(2,1)S(1)}, u32[]{:S(2)}, u32[]{:S(2)}) collective-permute-start(bf16[128,2560]{1,0:T(8,128)(2,1)S(1)} %convert_element_type.46), channel_id=1, source_target_pairs={{0,16},{16,0},{1,17},{17,1},{2,18},{18,2},{3,19},{19,3},{4,20},{20... | collective-permute-start | bytes 1966088 | tf_op jit(solution)/shard_map/ppermute | solution.py:1822
  566.5 19.1 %collective-permute-start.5 = (f32[8,128]{1,0:T(8,128)S(1)}, f32[8,128]{1,0:T(8,128)S(1)}, u32[]{:S(2)}, u32[]{:S(2)}) collective-permute-start(f32[8,128]{1,0:T(8,128)S(1)} %copy-done.13), channel_id=1, source_target_pairs={{0,16},{16,0},{1,17},{17,1},{2,18},{18,2},{3,19},{19,3},{4,20},{20... | collective-permute-start | bytes 12296 | tf_op jit(solution)/shard_map/ppermute | solution.py:1822
  567.2 0.9 copy-start.15
  568.1 19.8 %copy-start.3 = (f32[128,2560]{1,0:T(8,128)S(1)}, f32[128,2560]{1,0:T(8,128)}, u32[]{:S(2)}) copy-start(f32[128,2560]{1,0:T(8,128)} %get-tuple-element.120) | copy-start | bytes 3932164
  589.1 7.7 %copy-start.5 = (f32[1024,768]{1,0:T(8,128)S(1)}, f32[1024,768]{1,0:T(8,128)}, u32[]{:S(2)}) copy-start(f32[1024,768]{1,0:T(8,128)} %get-tuple-element.138) | copy-start | bytes 9437188
